TPU v7x, 32 devices: a whole 2x2x4 slice. The times are simulated.
32 devices in a mesh: row: 8 (over z, y), col: 4 (over x, core).
Axes of the slice: x: 2, y: 2, z: 4, core: 2. Of those that a mesh axis runs over, the one named last changes fastest.
Arguments:
- features: bfloat16 [128, 64, 384], P('row', 'col'), may hold values from -6 to 6
- norm_gain: float32 [384], replicated, may hold values from 0.5 to 1.5
- in_weight: bfloat16 [384, 1536], replicated, may hold values from -0.3125 to 0.3125
- conv_weight: float32 [3, 3, 768], replicated, may hold values from -2 to 2
- conv_bias: float32 [768], replicated, may hold values from -3 to 3
- proj_weight: bfloat16 [4, 768, 56], replicated, may hold values from -0.21875 to 0.21875
- step_weight: float32 [4, 24, 768], replicated, may hold values from -1.25 to 1.25
- step_bias: float32 [4, 768], replicated, may hold values from -9 to 2
- decay_log: float32 [4, 768, 16], replicated, may hold values from -3 to 0
- skip_gain: float32 [4, 768], replicated, may hold values from 0.02 to 0.2
- out_gain: float32 [768], replicated, may hold values from 0.5 to 1.5
- out_weight: bfloat16 [768, 384], replicated, may hold values from -0.21875 to 0.21875
Outputs:
- block_out: bfloat16 [128, 64, 384], P('row', 'col')
All inputs are finite; a program needn't handle non-finite values.
Results may differ from a plain program's by a relative error of at most 0.014.
Values may be sent and summed in bfloat16 or wider, within the bound.
No kernel may reach another device: no remote copies, remote signals or barrier semaphores. Data moves between devices by JAX's collectives and lax.ppermute only.
A program may use at most 192 MiB of HBM per device.

v0:
```python
import functools

import jax
import jax.numpy as jnp
from jax import lax
from jax.experimental import pallas as pl
from jax.experimental.pallas import tpu as pltpu
from jax.sharding import PartitionSpec as P

F32 = jnp.float32
BF16 = jnp.bfloat16
LANES = 128
SLOTS = 8
LOG2E = 1.4426950408889634


def bits(value):
    assert value & (value - 1) == 0
    return value.bit_length() - 1


def one_hot(targets, width):
    lane = lax.broadcasted_iota(jnp.int32, targets[0].shape, 1)
    blocks = []
    for block in range(width // LANES):
        hit = targets[0] == lane + block * LANES
        for other in targets[1:]:
            hit = jnp.logical_or(hit, other == lane + block * LANES)
        blocks.append(jnp.where(hit, 1.0, 0.0).astype(BF16))
    return jnp.concatenate(blocks, axis=1)


def rows_of(count, start=0):
    return lax.broadcasted_iota(jnp.int32, (count, LANES), 0) + start


def dot(a, b):
    return jnp.dot(a, b, preferred_element_type=F32)


def layer_norm(values, scale_gain):
    centred = values - jnp.mean(values, axis=-1, keepdims=True)
    spread = jnp.mean(centred * centred, axis=-1, keepdims=True)
    return centred * lax.rsqrt(spread + 1e-05) * scale_gain


def cut_kernel(feat_ref, top_ref, bottom_ref, left_ref, right_ref, gain_ref, norm_ref, rows_ref, cols_ref):
    height, width, channels = feat_ref.shape
    gain = gain_ref[...]

    def normed(values):
        return layer_norm(values.astype(F32), gain).astype(BF16)

    tile = normed(feat_ref[...].reshape(height * width, channels))
    norm_ref[...] = tile
    top, bottom = normed(top_ref[...]), normed(bottom_ref[...])
    left, right = normed(left_ref[...]), normed(right_ref[...])
    row = rows_of(height * width)
    turned = dot(one_hot([((row & (height - 1)) << bits(width)) + (row >> bits(height))], height * width), tile).astype(
        BF16
    )

    def cut(out_ref, first, body, last, lines, length):
        parts, reach = out_ref.shape[0], out_ref.shape[1]
        for part in range(parts):
            for line in range(reach):
                at = part * (reach - 2) + line - 1
                if at < 0:
                    out_ref[part, line] = first
                elif at >= lines:
                    out_ref[part, line] = last
                else:
                    out_ref[part, line] = body[at * length : (at + 1) * length]

    cut(rows_ref, top, tile, bottom, height, width)
    cut(cols_ref, left, turned, right, width, height)


def gate_kernel(norm_ref, weight_ref, gate_ref):
    gate_ref[...] = dot(norm_ref[...], weight_ref[...]).astype(BF16)


def line_kernel(
    lines,
    x_ref,
    weight_ref,
    conv_ref,
    conv_bias_ref,
    proj_ref,
    step_ref,
    bias_ref,
    rate_ref,
    skip_ref,
    out_ref,
    inner_ref,
    active_ref,
    proj_out_ref,
    s_ref,
    v_ref,
    y_ref,
):
    parts, reach, length, channels = x_ref.shape
    time = parts * length
    low = time // SLOTS
    width = weight_ref.shape[1]
    chunk = s_ref.shape[2]
    halves = width // chunk
    slot_lines = SLOTS // (2 * halves)
    states = rate_ref.shape[0]

    row = rows_of(reach * time)
    when = (row & (time - 1)) >> 3
    when = ((row & 7) << bits(low)) + when
    line = row >> bits(time)
    source = (when >> bits(length)) * (reach * length) + line * length + (when & (length - 1))
    tokens = dot(one_hot([source], reach * time), x_ref[...].reshape(parts * reach * length, channels)).astype(BF16)
    inner = dot(tokens, weight_ref[...]).astype(BF16).astype(F32)
    inner = inner.reshape(reach, low, SLOTS, width)
    inner_ref[:, 1 : low + 1] = inner
    place = lax.broadcasted_iota(jnp.int32, (SLOTS, width), 0)
    for line in range(reach):
        inner_ref[line, 0] = jnp.where(place == 0, 0.0, pltpu.roll(inner[line, low - 1], 1, 0))
        inner_ref[line, low + 1] = jnp.where(place == SLOTS - 1, 0.0, pltpu.roll(inner[line, 0], SLOTS - 1, 0))

    for line in range(lines):
        for half in range(halves):
            cells = pl.ds(half * chunk, chunk)
            total = jnp.zeros((low, SLOTS, chunk), F32) + conv_bias_ref[:, cells]
            for across in range(3):
                for along in range(3):
                    tap = conv_ref[across, along, cells].reshape(1, 1, chunk)
                    total = total + inner_ref[line + across, along : along + low, :, cells] * tap
            total = total / (1.0 + jnp.exp(-total))
            active_ref[pl.ds((half * lines + line) * time, time), :] = total.reshape(time, chunk).astype(BF16)

    piece = 256
    for first in range(0, time * SLOTS, piece):
        row = rows_of(piece, first)
        now = row >> 3
        slot = row & 7
        line = slot & (slot_lines - 1)
        back = (slot >> bits(slot_lines)) & 1
        half = slot >> bits(2 * slot_lines)
        when = jnp.where(back == 1, time - 1 - now, now)
        source = half * (lines * time) + line * time + ((when & (low - 1)) << 3) + (when >> bits(low))
        if slot_lines > lines:
            source = jnp.where(line < lines, source, -1)
        u = dot(one_hot([source], halves * lines * time), active_ref[...])
        kind = slot >> bits(slot_lines)
        projected = dot(u.astype(BF16), proj_ref[...])
        p = projected[:, :LANES]
        for other in range(1, 2 * halves):
            p = jnp.where(kind == other, projected[:, other * LANES : (other + 1) * LANES], p)
        if halves == 2:
            p = p.reshape(piece // SLOTS, SLOTS, LANES)
            p = p + pltpu.roll(p, SLOTS // 2, 1)
            p = p.reshape(piece, LANES)
        steps = pl.ds(first // SLOTS, piece // SLOTS)
        proj_out_ref[steps] = p.reshape(piece // SLOTS, SLOTS, LANES)
        high = p.astype(BF16).astype(F32)
        lane = lax.broadcasted_iota(jnp.int32, p.shape, 1)
        rank = RANK
        mixed = jnp.where(jnp.logical_and(lane >= rank, lane < 2 * rank), p - high, high)
        stacked = jnp.concatenate([jnp.where(kind == k, mixed, 0.0).astype(BF16) for k in range(2 * halves)], axis=1)
        before = dot(stacked, step_ref[...]).reshape(piece // SLOTS, SLOTS, chunk) + bias_ref[...]
        small = jnp.exp(-jnp.abs(before))
        log1p = jnp.where(small < 0.01, small * (1.0 + small * (-0.5 + small * (1.0 / 3.0 - 0.25 * small))), jnp.log(1.0 + small))
        step = jnp.maximum(before, 0.0) + log1p
        u = u.reshape(piece // SLOTS, SLOTS, chunk)
        s_ref[steps] = step
        v_ref[steps] = step * u
        y_ref[steps] = skip_ref[...] * u

    groups = chunk // LANES
    at_once = max(1, 12 // groups)
    unroll = 8
    for first in range(0, states, at_once):
        rates = [
            [rate_ref[n, :, g * LANES : (g + 1) * LANES] for g in range(groups)] for n in range(first, first + at_once)
        ]

        def advance(lap, hidden):
            hidden = list(hidden)
            for sub in range(unroll):
                t = lap * unroll + sub
                coefs = proj_out_ref[t]
                enter = []
                leave = []
                for n in range(at_once):
                    lane = 3 * RANK + first + n
                    enter.append(jnp.broadcast_to(coefs[:, lane : lane + 1], (SLOTS, LANES)))
                    lane = lane + states
                    leave.append(jnp.broadcast_to(coefs[:, lane : lane + 1], (SLOTS, LANES)))
                for g in range(groups):
                    cells = pl.ds(g * LANES, LANES)
                    step = s_ref[t, :, cells]
                    value = v_ref[t, :, cells]
                    y = y_ref[t, :, cells]
                    for n in range(at_once):
                        k = n * groups + g
                        h = jnp.exp2(step * rates[n][g]) * hidden[k] + value * enter[n]
                        hidden[k] = h
                        y = y + h * leave[n]
                    y_ref[t, :, cells] = y
            return tuple(hidden)

        zero = jnp.zeros((SLOTS, LANES), F32)
        lax.fori_loop(0, time // unroll, advance, (zero,) * (at_once * groups))

    row = rows_of(lines * time)
    line = (row >> bits(length)) & (lines - 1)
    now = ((row >> bits(lines * length)) << bits(length)) + (row & (length - 1))
    scanned = y_ref[...].reshape(time * SLOTS, chunk).astype(BF16)
    for half in range(halves):
        ahead = now * SLOTS + (half * 2 * slot_lines) + line
        behind = (time - 1 - now) * SLOTS + (half * 2 * slot_lines + slot_lines) + line
        joined = dot(one_hot([ahead, behind], time * SLOTS), scanned)
        out_ref[:, half * chunk : (half + 1) * chunk] = joined.astype(BF16)


RANK = 24


def lines_of(x, in_weight, conv, conv_bias, proj, step_weight, step_bias, decay_log, skip):
    parts, reach, length, channels = x.shape
    lines = reach - 2
    time = parts * length
    width = conv.shape[2]
    rank = step_weight.shape[1]
    states = decay_log.shape[2]
    assert rank == RANK
    halves = 1 if lines >= 4 else 2
    slot_lines = SLOTS // (2 * halves)
    assert lines <= slot_lines
    chunk = width // halves

    def by_half(a):
        return jnp.swapaxes(a.reshape(a.shape[:-1] + (halves, chunk)), 0, -2)

    def slots(a):
        a = jnp.swapaxes(a.reshape(2, halves, 1, chunk), 0, 1)
        return jnp.broadcast_to(a, (halves, 2, slot_lines, chunk)).reshape(SLOTS, chunk)

    ranks = proj[:, :, :rank]
    wide = jnp.concatenate(
        [ranks, ranks, ranks, proj[:, :, rank:], jnp.zeros((2, width, LANES - 3 * rank - 2 * states), proj.dtype)],
        axis=2,
    )
    wide = wide.reshape(2, halves, chunk, LANES).transpose(2, 1, 0, 3).reshape(chunk, halves * 2 * LANES)
    high = lax.reduce_precision(step_weight, 8, 7)
    rest = step_weight - high
    tall = jnp.concatenate(
        [high, high, rest, jnp.zeros((2, LANES - 3 * rank, width), step_weight.dtype)], axis=1
    ).astype(BF16)
    tall = tall.reshape(2, LANES, halves, chunk).transpose(2, 0, 1, 3).reshape(halves * 2 * LANES, chunk)
    rates = -jnp.exp(decay_log) * LOG2E
    rates = rates.transpose(2, 0, 1).reshape(states, 2, halves, 1, chunk).transpose(0, 2, 1, 3, 4)
    rates = jnp.broadcast_to(rates, (states, halves, 2, slot_lines, chunk)).reshape(states, SLOTS, chunk)

    whole = pl.BlockSpec(memory_space=pltpu.VMEM)
    flops = 2 * time * (reach * channels * width + SLOTS * width * 256)
    return pl.pallas_call(
        functools.partial(line_kernel, lines),
        out_shape=jax.ShapeDtypeStruct((parts * lines * length, width), BF16),
        grid=(1,),
        in_specs=[whole, pl.BlockSpec((channels, width), lambda i: (0, 0))] + [whole] * 7,
        out_specs=whole,
        scratch_shapes=[
            pltpu.VMEM((reach, time // SLOTS + 2, SLOTS, width), F32),
            pltpu.VMEM((halves * lines * time, chunk), BF16),
            pltpu.VMEM((time, SLOTS, LANES), F32),
            pltpu.VMEM((time, SLOTS, chunk), F32),
            pltpu.VMEM((time, SLOTS, chunk), F32),
            pltpu.VMEM((time, SLOTS, chunk), F32),
        ],
        compiler_params=pltpu.CompilerParams(vmem_limit_bytes=50 * 1024 * 1024),
        cost_estimate=pl.CostEstimate(
            flops=flops, bytes_accessed=4 * 1024 * 1024, transcendentals=time * SLOTS * chunk * states
        ),
    )(x, in_weight, conv, conv_bias.reshape(1, width), wide, tall, slots(step_bias), rates, slots(skip))


def end_kernel(rows_ref, cols_ref, gate_ref, gain_ref, weight_ref, out_ref):
    height, width, channels = out_ref.shape
    row = rows_of(height * width)
    source = ((row & (width - 1)) << bits(height)) + (row >> bits(width))
    combined = rows_ref[...].astype(F32) + dot(one_hot([source], height * width), cols_ref[...])
    gate = gate_ref[...].astype(F32)
    gated = layer_norm(combined, gain_ref[...]) * (gate / (1.0 + jnp.exp(-gate)))
    out = dot(gated.astype(BF16), weight_ref[...]).astype(BF16)
    out_ref[...] = out.reshape(height, width, channels)


def both_ways(array, axis, dim):
    count = lax.axis_size(axis)
    size = array.shape[dim]
    head = lax.index_in_dim(array, 0, dim, False)
    tail = lax.index_in_dim(array, size - 1, dim, False)
    up = [(i, i + 1) for i in range(count - 1)]
    down = [(i + 1, i) for i in range(count - 1)]
    return lax.ppermute(tail, axis, up), lax.ppermute(head, axis, down)


def local(
    features,
    norm_gain,
    in_weight,
    conv_weight,
    conv_bias,
    proj_weight,
    step_weight,
    step_bias,
    decay_log,
    skip_gain,
    out_gain,
    out_weight,
):
    height, width, channels = features.shape
    inner = out_weight.shape[0]
    tokens = height * width
    row_lines = height // lax.axis_size("col")
    col_lines = width // lax.axis_size("row")
    top, bottom = both_ways(features, "row", 0)
    left, right = both_ways(features, "col", 1)

    normed, row_send, col_send = pl.pallas_call(
        cut_kernel,
        out_shape=(
            jax.ShapeDtypeStruct((tokens, channels), BF16),
            jax.ShapeDtypeStruct((lax.axis_size("col"), row_lines + 2, width, channels), BF16),
            jax.ShapeDtypeStruct((lax.axis_size("row"), col_lines + 2, height, channels), BF16),
        ),
    )(features, top, bottom, left, right, norm_gain.reshape(1, channels))
    row_x = lax.all_to_all(row_send, "col", 0, 0, tiled=True)
    col_x = lax.all_to_all(col_send, "row", 0, 0, tiled=True)
    gate = pl.pallas_call(
        gate_kernel,
        out_shape=jax.ShapeDtypeStruct((tokens, inner), BF16),
        grid=(1,),
        in_specs=[
            pl.BlockSpec((tokens, channels), lambda i: (0, 0)),
            pl.BlockSpec((channels, inner), lambda i: (0, 1)),
        ],
        out_specs=pl.BlockSpec((tokens, inner), lambda i: (0, 0)),
        cost_estimate=pl.CostEstimate(flops=2 * tokens * channels * inner, bytes_accessed=1 << 20, transcendentals=0),
    )(normed, in_weight)
    row_y = lines_of(
        row_x,
        in_weight,
        conv_weight,
        conv_bias,
        proj_weight[:2],
        step_weight[:2],
        step_bias[:2],
        decay_log[:2],
        skip_gain[:2],
    )
    row_y = lax.all_to_all(row_y.reshape(lax.axis_size("col"), -1, inner), "col", 0, 0, tiled=True)
    col_y = lines_of(
        col_x,
        in_weight,
        jnp.swapaxes(conv_weight, 0, 1),
        conv_bias,
        proj_weight[2:],
        step_weight[2:],
        step_bias[2:],
        decay_log[2:],
        skip_gain[2:],
    )
    col_y = lax.all_to_all(col_y.reshape(lax.axis_size("row"), -1, inner), "row", 0, 0, tiled=True)
    return pl.pallas_call(
        end_kernel,
        out_shape=jax.ShapeDtypeStruct(features.shape, BF16),
    )(row_y.reshape(tokens, inner), col_y.reshape(tokens, inner), gate, out_gain.reshape(1, inner), out_weight)


def solution(mesh):
    in_specs = (P("row", "col", None), P(), P(), P(), P(), P(), P(), P(), P(), P(), P(), P())
    out_specs = P("row", "col", None)
    return jax.shard_map(local, mesh=mesh, in_specs=in_specs, out_specs=out_specs, check_vma=False)
```

profile of v0, /device:TPU:0, one launch (start us, length us, event | category | flops | bytes accessed | tf_op | source)
XLA Modules:
  0.0 95.6 jit_solution(4474463710503160706)
XLA Ops:
  0.0 1.0 %fusion.4 = (bf16[16,1,384]{2,1,0:T(2,128)(2,1)S(1)}, bf16[16,1,384]{2,1,0:T(2,128)(2,1)S(1)}) fusion(bf16[16,16,384]{2,1,0:T(8,128)(2,1)} %feat_ref.1), kind=kLoop, calls=%fused_computation.21 | loop fusion | bytes 49152 | tf_op jit(solution)/shard_map/slice | solution.py:297
  1.0 2.4 %collective-permute-start.2 = (bf16[16,384]{1,0:T(8,128)(2,1)S(1)}, bf16[16,384]{1,0:T(8,128)(2,1)S(1)}, u32[]{:S(2)}, u32[]{:S(2)}) collective-permute-start(bf16[16,384]{1,0:T(8,128)(2,1)S(1)} %bitcast.62), channel_id=1, source_target_pairs={{0,1},{1,2},{2,3},{4,5},{5,6},{6,7},{8,9},{9,10},{10,11},{12,13},{... | collective-permute-start | bytes 36872 | tf_op jit(solution)/shard_map/ppermute | solution.py:301
  3.4 1.3 %collective-permute-start.3 = (bf16[16,384]{1,0:T(8,128)(2,1)S(1)}, bf16[16,384]{1,0:T(8,128)(2,1)S(1)}, u32[]{:S(2)}, u32[]{:S(2)}) collective-permute-start(bf16[16,384]{1,0:T(8,128)(2,1)S(1)} %bitcast.63), channel_id=1, source_target_pairs={{1,0},{2,1},{3,2},{5,4},{6,5},{7,6},{9,8},{10,9},{11,10},{13,12},{... | collective-permute-start | bytes 36872 | tf_op jit(solution)/shard_map/ppermute | solution.py:301
  4.7 0.7 slice_bitcast_fusion
  5.4 4.2 %collective-permute-start = (bf16[16,384]{1,0:T(8,128)(2,1)S(1)}, bf16[16,384]{1,0:T(8,128)(2,1)S(1)}, u32[]{:S(2)}, u32[]{:S(2)}) collective-permute-start(bf16[16,384]{1,0:T(8,128)(2,1)S(1)} %get-tuple-element.24), channel_id=1, source_target_pairs={{0,4},{4,8},{8,12},{12,16},{16,20},{20,24},{24,28},{1,5},{5,9},{9,... | collective-permute-start | bytes 36872 | tf_op jit(solution)/shard_map/ppermute | solution.py:301
  9.7 1.3 %collective-permute-start.1 = (bf16[16,384]{1,0:T(8,128)(2,1)S(1)}, bf16[16,384]{1,0:T(8,128)(2,1)S(1)}, u32[]{:S(2)}, u32[]{:S(2)}) collective-permute-start(bf16[16,384]{1,0:T(8,128)(2,1)S(1)} %get-tuple-element.23), channel_id=1, source_target_pairs={{4,0},{8,4},{12,8},{16,12},{20,16},{24,20},{28,24},{5,1},{9,5},{13... | collective-permute-start | bytes 36872 | tf_op jit(solution)/shard_map/ppermute | solution.py:301
  11.0 1.0 %fusion.3 = (bf16[2,768,56]{1,2,0:T(8,128)(2,1)S(1)}, bf16[2,768,56]{1,2,0:T(8,128)(2,1)S(1)}) fusion(bf16[4,768,56]{1,2,0:T(8,128)(2,1)} %param.17), kind=kLoop, calls=%fused_computation.20 | loop fusion | bytes 688128 | tf_op jit(solution)/shard_map/slice | solution.py:244
  12.1 0.9 fusion.2
  13.5 0.6 reshape.78.gain_ref
  14.2 0.7 copy.18
  16.2 0.6 copy-done.10
  16.8 2.2 %shard_map.118 = (bf16[256,384]{1,0:T(8,128)(2,1)}, bf16[4,6,16,384]{3,2,1,0:T(8,128)(2,1)}, bf16[8,4,16,384]{3,2,1,0:T(8,128)(2,1)}) custom-call(bf16[16,16,384]{2,1,0:T(8,128)(2,1)} %feat_ref.1, bf16[16,384]{1,0:T(8,128)(2,1)} %copy-done.9, bf16[16,384]{1,0:T(8,128)(2,1)} %copy-done.10, bf16[16,384]{1,0:T(8,128)(2,1)} %copy-done.7, ...), custom_call_target="tpu_custom_call" | custom-call | tf_op jit(solution)/shard_map/pallas_call | solution.py:326
  19.0 5.3 %all-to-all-start = ((bf16[4,6,16,384]{3,2,1,0:T(8,128)(2,1)}), bf16[4,6,16,384]{3,2,1,0:T(8,128)(2,1)S(1)}, u32[]{:S(2)}, u32[]{:S(2)}) async-start(bf16[4,6,16,384]{3,2,1,0:T(8,128)(2,1)} %get-tuple-element.8), calls=%async_computation | async-start | bytes 589824 | tf_op jit(solution)/shard_map/all_to_all | solution.py:334
  25.0 5.7 %all-to-all-done.x_ref = bf16[4,6,16,384]{3,2,1,0:T(8,128)(2,1)S(1)} async-done(((bf16[4,6,16,384]{3,2,1,0:T(8,128)(2,1)}), bf16[4,6,16,384]{3,2,1,0:T(8,128)(2,1)S(1)}, u32[]{:S(2)}, u32[]{:S(2)}) %all-to-all-start) | async-done | bytes 294944 | tf_op jit(solution)/shard_map/all_to_all | solution.py:334
  30.7 7.0 %all-to-all-start.2 = ((bf16[8,4,16,384]{3,2,1,0:T(8,128)(2,1)}), bf16[8,4,16,384]{3,2,1,0:T(8,128)(2,1)S(1)}, u32[]{:S(2)}, u32[]{:S(2)}) async-start(bf16[8,4,16,384]{3,2,1,0:T(8,128)(2,1)} %get-tuple-element.9), calls=%async_computation.2 | async-start | bytes 786432 | tf_op jit(solution)/shard_map/all_to_all | solution.py:335
  37.6 1.0 %reduce-precision_convert_fusion = (bf16[2,24,768]{2,1,0:T(8,128)(2,1)S(1)}, bf16[2,24,768]{2,1,0:T(8,128)(2,1)S(1)}, bf16[2,24,768]{2,1,0:T(8,128)(2,1)S(1)}, bf16[2,24,768]{2,1,0:T(8,128)(2,1)S(1)}) fusion(f32[4,24,768]{2,1,0:T(8,128)} %param.18), kind=kLoop, calls=%fused_computation.5 | loop fusion | flops 294912 | bytes 589824 | tf_op jit(solution)/shard_map/convert
  38.8 13.3 %shard_map.119 = bf16[256,768]{1,0:T(8,128)(2,1)} custom-call(bf16[4,6,16,384]{3,2,1,0:T(8,128)(2,1)S(1)} %all-to-all-done.x_ref, bf16[384,1536]{1,0:T(8,128)(2,1)S(1)} %copy-done, f32[3,3,768]{2,1,0:T(4,128)S(1)} %copy-done.1, f32[1,768]{1,0:T(1,128)S(1)} %reshape.79.conv_bias_ref, bf16[768,256]{1,0:T(8,128)(2,1)S(1)} %copy.25.proj_ref, ...), custom_call_target="tpu_custom_call" | custom-call | flops 427819008 | bytes 4194304 | tf_op jit(solution)/shard_map/pallas_call | solution.py:262
  52.1 3.6 %all-to-all-start.1 = ((bf16[4,64,768]{2,1,0:T(8,128)(2,1)}), bf16[4,64,768]{2,1,0:T(8,128)(2,1)S(1)}, u32[]{:S(2)}, u32[]{:S(2)}) async-start(bf16[4,64,768]{2,1,0:T(8,128)(2,1)} %bitcast.9), calls=%async_computation.1 | async-start | bytes 786432 | tf_op jit(solution)/shard_map/all_to_all | solution.py:358
  55.9 17.8 %shard_map.120 = bf16[256,768]{1,0:T(8,128)(2,1)} custom-call(bf16[8,4,16,384]{3,2,1,0:T(8,128)(2,1)S(1)} %all-to-all-done.2.x_ref, bf16[384,1536]{1,0:T(8,128)(2,1)S(1)} %copy-done, f32[3,3,768]{2,1,0:T(4,128)S(1)} %bitcast.52, f32[1,768]{1,0:T(1,128)S(1)} %reshape.79.conv_bias_ref, bf16[384,512]{1,0:T(8,128)(2,1)S(1)} %reshape.85.proj_ref, ...), custom_call_target="tpu_custom_call" | custom-call | flops 704643072 | bytes 4194304 | tf_op jit(solution)/shard_map/pallas_call | solution.py:262
  73.7 6.0 %all-to-all-start.3 = ((bf16[8,32,768]{2,1,0:T(8,128)(2,1)}), bf16[8,32,768]{2,1,0:T(8,128)(2,1)S(1)}, u32[]{:S(2)}, u32[]{:S(2)}) async-start(bf16[8,32,768]{2,1,0:T(8,128)(2,1)} %bitcast.22), calls=%async_computation.3 | async-start | bytes 786432 | tf_op jit(solution)/shard_map/all_to_all | solution.py:370
  80.3 2.3 %shard_map.121.gate_ref = bf16[256,768]{1,0:T(8,128)(2,1)} custom-call(bf16[256,384]{1,0:T(8,128)(2,1)} %get-tuple-element.10.norm_ref, bf16[384,1536]{1,0:T(8,128)(2,1)} %weight_ref.6), custom_call_target="tpu_custom_call" | custom-call | flops 150994944 | bytes 1048576 | tf_op jit(solution)/shard_map/pallas_call | solution.py:336
  82.6 9.2 %all-to-all-done.3 = bf16[8,32,768]{2,1,0:T(8,128)(2,1)S(1)} async-done(((bf16[8,32,768]{2,1,0:T(8,128)(2,1)}), bf16[8,32,768]{2,1,0:T(8,128)(2,1)S(1)}, u32[]{:S(2)}, u32[]{:S(2)}) %all-to-all-start.3) | async-done | bytes 393248 | tf_op jit(solution)/shard_map/all_to_all | solution.py:370
  91.8 0.7 copy-done.3
  92.6 3.0 %shard_map.122 = bf16[16,16,384]{2,1,0:T(8,128)(2,1)} custom-call(bf16[256,768]{1,0:T(8,128)(2,1)} %bitcast.55, bf16[256,768]{1,0:T(8,128)(2,1)} %bitcast.56, bf16[256,768]{1,0:T(8,128)(2,1)} %shard_map.121.gate_ref, f32[1,768]{1,0:T(1,128)} %reshape.95.gain_ref, bf16[768,384]{1,0:T(8,128)(2,1)} %weight_ref.7), custom_call_target="tpu_custom_call" | custom-call | tf_op jit(solution)/shard_map/pallas_call | solution.py:371
  (70 shorter events, 3.2 us)
Async XLA Ops:
  0.0 13.0 %copy-start.4 = (f32[4,768,16]{1,2,0:T(8,128)S(1)}, f32[4,768,16]{1,2,0:T(8,128)}, u32[]{:S(2)}) copy-start(f32[4,768,16]{1,2,0:T(8,128)} %param.20) | copy-start | bytes 589828
  1.0 14.5 %collective-permute-start.2 = (bf16[16,384]{1,0:T(8,128)(2,1)S(1)}, bf16[16,384]{1,0:T(8,128)(2,1)S(1)}, u32[]{:S(2)}, u32[]{:S(2)}) collective-permute-start(bf16[16,384]{1,0:T(8,128)(2,1)S(1)} %bitcast.62), channel_id=1, source_target_pairs={{0,1},{1,2},{2,3},{4,5},{5,6},{6,7},{8,9},{9,10},{10,11},{12,13},{... | collective-permute-start | bytes 36872 | tf_op jit(solution)/shard_map/ppermute | solution.py:301
  3.4 12.2 %collective-permute-start.3 = (bf16[16,384]{1,0:T(8,128)(2,1)S(1)}, bf16[16,384]{1,0:T(8,128)(2,1)S(1)}, u32[]{:S(2)}, u32[]{:S(2)}) collective-permute-start(bf16[16,384]{1,0:T(8,128)(2,1)S(1)} %bitcast.63), channel_id=1, source_target_pairs={{1,0},{2,1},{3,2},{5,4},{6,5},{7,6},{9,8},{10,9},{11,10},{13,12},{... | collective-permute-start | bytes 36872 | tf_op jit(solution)/shard_map/ppermute | solution.py:301
  5.4 10.2 %collective-permute-start = (bf16[16,384]{1,0:T(8,128)(2,1)S(1)}, bf16[16,384]{1,0:T(8,128)(2,1)S(1)}, u32[]{:S(2)}, u32[]{:S(2)}) collective-permute-start(bf16[16,384]{1,0:T(8,128)(2,1)S(1)} %get-tuple-element.24), channel_id=1, source_target_pairs={{0,4},{4,8},{8,12},{12,16},{16,20},{20,24},{24,28},{1,5},{5,9},{9,... | collective-permute-start | bytes 36872 | tf_op jit(solution)/shard_map/ppermute | solution.py:301
  9.7 3.7 %copy-start.5 = (f32[4,768]{1,0:T(4,128)S(1)}, f32[4,768]{1,0:T(4,128)}, u32[]{:S(2)}) copy-start(f32[4,768]{1,0:T(4,128)} %param.19) | copy-start | bytes 36868
  9.7 3.8 %copy-start.13 = (f32[384]{0:T(512)S(1)}, f32[384]{0:T(512)}, u32[]{:S(2)}) copy-start(f32[384]{0:T(512)} %param.13) | copy-start | bytes 4612
  9.7 5.9 %collective-permute-start.1 = (bf16[16,384]{1,0:T(8,128)(2,1)S(1)}, bf16[16,384]{1,0:T(8,128)(2,1)S(1)}, u32[]{:S(2)}, u32[]{:S(2)}) collective-permute-start(bf16[16,384]{1,0:T(8,128)(2,1)S(1)} %get-tuple-element.23), channel_id=1, source_target_pairs={{4,0},{8,4},{12,8},{16,12},{20,16},{24,20},{28,24},{5,1},{9,5},{13... | collective-permute-start | bytes 36872 | tf_op jit(solution)/shard_map/ppermute | solution.py:301
  15.1 9.2 %copy-start.6 = (f32[4,768]{1,0:T(4,128)S(1)}, f32[4,768]{1,0:T(4,128)}, u32[]{:S(2)}) copy-start(f32[4,768]{1,0:T(4,128)} %param.21) | copy-start | bytes 36868
  15.1 9.2 %copy-start.11 = (f32[768]{0:T(1024)S(1)}, f32[768]{0:T(1024)}, u32[]{:S(2)}) copy-start(f32[768]{0:T(1024)} %param.16) | copy-start | bytes 9220
  15.1 9.2 %copy-start.1 = (f32[3,3,768]{2,1,0:T(4,128)S(1)}, f32[3,3,768]{2,1,0:T(4,128)}, u32[]{:S(2)}) copy-start(f32[3,3,768]{2,1,0:T(4,128)} %conv_ref.1) | copy-start | bytes 82948
  15.6 0.6 copy-start.7
  15.6 0.6 copy-start.8
  15.6 0.6 copy-start.9
  16.2 0.6 copy-start.10
  19.0 11.7 %all-to-all-start = ((bf16[4,6,16,384]{3,2,1,0:T(8,128)(2,1)}), bf16[4,6,16,384]{3,2,1,0:T(8,128)(2,1)S(1)}, u32[]{:S(2)}, u32[]{:S(2)}) async-start(bf16[4,6,16,384]{3,2,1,0:T(8,128)(2,1)} %get-tuple-element.8), calls=%async_computation | async-start | bytes 589824 | tf_op jit(solution)/shard_map/all_to_all | solution.py:334
  24.9 13.9 %copy-start = (bf16[384,1536]{1,0:T(8,128)(2,1)S(1)}, bf16[384,1536]{1,0:T(8,128)(2,1)}, u32[]{:S(2)}) copy-start(bf16[384,1536]{1,0:T(8,128)(2,1)} %weight_ref.6) | copy-start | bytes 3538948
  30.7 21.4 %all-to-all-start.2 = ((bf16[8,4,16,384]{3,2,1,0:T(8,128)(2,1)}), bf16[8,4,16,384]{3,2,1,0:T(8,128)(2,1)S(1)}, u32[]{:S(2)}, u32[]{:S(2)}) async-start(bf16[8,4,16,384]{3,2,1,0:T(8,128)(2,1)} %get-tuple-element.9), calls=%async_computation.2 | async-start | bytes 786432 | tf_op jit(solution)/shard_map/all_to_all | solution.py:335
  52.1 21.6 %all-to-all-start.1 = ((bf16[4,64,768]{2,1,0:T(8,128)(2,1)}), bf16[4,64,768]{2,1,0:T(8,128)(2,1)S(1)}, u32[]{:S(2)}, u32[]{:S(2)}) async-start(bf16[4,64,768]{2,1,0:T(8,128)(2,1)} %bitcast.9), calls=%async_computation.1 | async-start | bytes 786432 | tf_op jit(solution)/shard_map/all_to_all | solution.py:358
  55.9 23.8 %copy-start.12 = (f32[768]{0:T(1024)S(1)}, f32[768]{0:T(1024)}, u32[]{:S(2)}) copy-start(f32[768]{0:T(1024)} %param.22) | copy-start | bytes 9220
  73.7 8.9 %copy-start.2 = (bf16[4,64,768]{2,1,0:T(8,128)(2,1)}, bf16[4,64,768]{2,1,0:T(8,128)(2,1)S(1)}, u32[]{:S(2)}) copy-start(bf16[4,64,768]{2,1,0:T(8,128)(2,1)S(1)} %all-to-all-done.1) | copy-start | bytes 1179652
  73.7 18.1 %all-to-all-start.3 = ((bf16[8,32,768]{2,1,0:T(8,128)(2,1)}), bf16[8,32,768]{2,1,0:T(8,128)(2,1)S(1)}, u32[]{:S(2)}, u32[]{:S(2)}) async-start(bf16[8,32,768]{2,1,0:T(8,128)(2,1)} %bitcast.22), calls=%async_computation.3 | async-start | bytes 786432 | tf_op jit(solution)/shard_map/all_to_all | solution.py:370
  91.8 0.8 copy-start.3
where the time goes:
time: 96.3 us; the launch traced here: 95.6 us
  Pallas kernels  38.6 us (40%)
  starting transfers between devices  31.1 us (32%)
  waiting for transfers between devices  14.9 us (15%)
  local copies, waits for them, and re-layouts  8.98 us (9%)
  other arithmetic  1.55 us (2%)
    pallas_call x2, Pallas kernels, lines_of(): pl.pallas_call(functools.partial(line_kernel, lines), out_shape=jax.Shape...  31.1 us
    all_to_all x1, waiting for transfers between devices, local(): lax.all_to_all(col_y.reshape(lax.axis_size('row'), -1, inner), 'row', 0,...  9.22 us
    ppermute x4, starting transfers between devices, both_ways(): return (lax.ppermute(tail, axis, up), lax.ppermute(head, axis, down))  9.18 us
    all_to_all x1, starting transfers between devices, local(): col_x = lax.all_to_all(col_send, 'row', 0, 0, tiled=True)  6.96 us
    all_to_all x1, starting transfers between devices, local(): lax.all_to_all(col_y.reshape(lax.axis_size('row'), -1, inner), 'row', 0,...  6.01 us
    all_to_all x1, waiting for transfers between devices, local(): row_x = lax.all_to_all(row_send, 'col', 0, 0, tiled=True)  5.7 us
    all_to_all x1, starting transfers between devices, local(): row_x = lax.all_to_all(row_send, 'col', 0, 0, tiled=True)  5.29 us
    all_to_all x1, starting transfers between devices, local(): lax.all_to_all(row_y.reshape(lax.axis_size('col'), -1, inner), 'col', 0,...  3.64 us
  transfers between devices with their start and end apart: 8, of which 2 were waited for; matrix products, arithmetic and copies ran while one was open for 8% of the time, Pallas kernels for 35%

commit v1 on v0

--- a/solution.py
+++ b/solution.py
@@ -22,12 +22,12 @@
 def one_hot(targets, width):
     lane = lax.broadcasted_iota(jnp.int32, targets[0].shape, 1)
     blocks = []
-    for block in range(width // LANES):
+    for block in range(pl.cdiv(width, LANES)):
         hit = targets[0] == lane + block * LANES
         for other in targets[1:]:
             hit = jnp.logical_or(hit, other == lane + block * LANES)
         blocks.append(jnp.where(hit, 1.0, 0.0).astype(BF16))
-    return jnp.concatenate(blocks, axis=1)
+    return jnp.concatenate(blocks, axis=1)[:, :width]
 
 
 def rows_of(count, start=0):
@@ -44,36 +44,27 @@
     return centred * lax.rsqrt(spread + 1e-05) * scale_gain
 
 
-def cut_kernel(feat_ref, top_ref, bottom_ref, left_ref, right_ref, gain_ref, norm_ref, rows_ref, cols_ref):
+def cut_kernel(feat_ref, gain_ref, norm_ref, rows_ref, cols_ref):
     height, width, channels = feat_ref.shape
-    gain = gain_ref[...]
-
-    def normed(values):
-        return layer_norm(values.astype(F32), gain).astype(BF16)
-
-    tile = normed(feat_ref[...].reshape(height * width, channels))
+    tile = layer_norm(feat_ref[...].reshape(height * width, channels).astype(F32), gain_ref[...]).astype(BF16)
     norm_ref[...] = tile
-    top, bottom = normed(top_ref[...]), normed(bottom_ref[...])
-    left, right = normed(left_ref[...]), normed(right_ref[...])
     row = rows_of(height * width)
     turned = dot(one_hot([((row & (height - 1)) << bits(width)) + (row >> bits(height))], height * width), tile).astype(
         BF16
     )
 
-    def cut(out_ref, first, body, last, lines, length):
+    def cut(out_ref, body, lines, length):
         parts, reach = out_ref.shape[0], out_ref.shape[1]
         for part in range(parts):
             for line in range(reach):
                 at = part * (reach - 2) + line - 1
-                if at < 0:
-                    out_ref[part, line] = first
-                elif at >= lines:
-                    out_ref[part, line] = last
+                if 0 <= at < lines:
+                    out_ref[part, line] = body[at * length : (at + 1) * length]
                 else:
-                    out_ref[part, line] = body[at * length : (at + 1) * length]
-
-    cut(rows_ref, top, tile, bottom, height, width)
-    cut(cols_ref, left, turned, right, width, height)
+                    out_ref[part, line] = jnp.zeros((length, channels), BF16)
+
+    cut(rows_ref, tile, height, width)
+    cut(cols_ref, turned, width, height)
 
 
 def gate_kernel(norm_ref, weight_ref, gate_ref):
@@ -83,6 +74,8 @@
 def line_kernel(
     lines,
     x_ref,
+    seam_ref,
+    ends_ref,
     weight_ref,
     conv_ref,
     conv_bias_ref,
@@ -108,30 +101,48 @@
     slot_lines = SLOTS // (2 * halves)
     states = rate_ref.shape[0]
 
-    row = rows_of(reach * time)
-    when = (row & (time - 1)) >> 3
-    when = ((row & 7) << bits(low)) + when
-    line = row >> bits(time)
-    source = (when >> bits(length)) * (reach * length) + line * length + (when & (length - 1))
-    tokens = dot(one_hot([source], reach * time), x_ref[...].reshape(parts * reach * length, channels)).astype(BF16)
-    inner = dot(tokens, weight_ref[...]).astype(BF16).astype(F32)
-    inner = inner.reshape(reach, low, SLOTS, width)
-    inner_ref[:, 1 : low + 1] = inner
+    row = rows_of(time)
+    order = one_hot([((row & 7) << bits(low)) + (row >> 3)], time)
     place = lax.broadcasted_iota(jnp.int32, (SLOTS, width), 0)
     for line in range(reach):
-        inner_ref[line, 0] = jnp.where(place == 0, 0.0, pltpu.roll(inner[line, low - 1], 1, 0))
-        inner_ref[line, low + 1] = jnp.where(place == SLOTS - 1, 0.0, pltpu.roll(inner[line, 0], SLOTS - 1, 0))
-
-    for line in range(lines):
-        for half in range(halves):
-            cells = pl.ds(half * chunk, chunk)
-            total = jnp.zeros((low, SLOTS, chunk), F32) + conv_bias_ref[:, cells]
+        x = x_ref[:, line].reshape(time, channels)
+        if line == 0 or line == reach - 1:
+            missing = ends_ref[0 if line == 0 else 1] == 1
+            x = jnp.where(missing, seam_ref[...].reshape(time, channels), x)
+        tokens = dot(order, x).astype(BF16)
+        inner = dot(tokens, weight_ref[...]).astype(BF16).astype(F32).reshape(low, SLOTS, width)
+        inner_ref[line, 1 : low + 1] = inner
+        inner_ref[line, 0] = jnp.where(place == 0, 0.0, pltpu.roll(inner[low - 1], 1, 0))
+        inner_ref[line, low + 1] = jnp.where(place == SLOTS - 1, 0.0, pltpu.roll(inner[0], SLOTS - 1, 0))
+
+    def convolve(pair, _):
+        for group in range(width // (2 * LANES)):
+            cells = slice(group * 2 * LANES, (group + 1) * 2 * LANES)
+            half = (group * 2 * LANES) // chunk
+            base = group * 2 * LANES - half * chunk
+            bias = jnp.broadcast_to(conv_bias_ref[:, cells], (SLOTS, 2 * LANES))
+            totals = [[bias for _ in range(2)] for _ in range(lines)]
             for across in range(3):
                 for along in range(3):
-                    tap = conv_ref[across, along, cells].reshape(1, 1, chunk)
-                    total = total + inner_ref[line + across, along : along + low, :, cells] * tap
-            total = total / (1.0 + jnp.exp(-total))
-            active_ref[pl.ds((half * lines + line) * time, time), :] = total.reshape(time, chunk).astype(BF16)
+                    tap = jnp.broadcast_to(conv_ref[across, along : along + 1, cells], (SLOTS, 2 * LANES))
+                    for line in range(lines):
+                        for sub in range(2):
+                            totals[line][sub] += inner_ref[line + across, 2 * pair + sub + along, :, cells] * tap
+            for line in range(lines):
+                value = jnp.concatenate(totals[line], axis=0)
+                value = 0.5 * value
+                value = value * jnp.tanh(value) + value
+                value = value.astype(BF16)
+                for piece in range(2):
+                    at = base + piece * LANES
+                    start = ((half + at // chunk) * lines + line) * time
+                    start = pl.multiple_of(start + pair * (2 * SLOTS), 2 * SLOTS)
+                    active_ref[pl.ds(start, 2 * SLOTS), at % chunk : at % chunk + LANES] = value[
+                        :, piece * LANES : (piece + 1) * LANES
+                    ]
+        return 0
+
+    lax.fori_loop(0, low // 2, convolve, 0)
 
     piece = 256
     for first in range(0, time * SLOTS, piece):
@@ -146,6 +157,8 @@
         if slot_lines > lines:
             source = jnp.where(line < lines, source, -1)
         u = dot(one_hot([source], halves * lines * time), active_ref[...])
+        steps = pl.ds(first // SLOTS, piece // SLOTS)
+        v_ref[steps] = u.reshape(piece // SLOTS, SLOTS, chunk)
         kind = slot >> bits(slot_lines)
         projected = dot(u.astype(BF16), proj_ref[...])
         p = projected[:, :LANES]
@@ -155,21 +168,29 @@
             p = p.reshape(piece // SLOTS, SLOTS, LANES)
             p = p + pltpu.roll(p, SLOTS // 2, 1)
             p = p.reshape(piece, LANES)
-        steps = pl.ds(first // SLOTS, piece // SLOTS)
         proj_out_ref[steps] = p.reshape(piece // SLOTS, SLOTS, LANES)
         high = p.astype(BF16).astype(F32)
         lane = lax.broadcasted_iota(jnp.int32, p.shape, 1)
-        rank = RANK
-        mixed = jnp.where(jnp.logical_and(lane >= rank, lane < 2 * rank), p - high, high)
+        mixed = jnp.where(jnp.logical_and(lane >= RANK, lane < 2 * RANK), p - high, high)
         stacked = jnp.concatenate([jnp.where(kind == k, mixed, 0.0).astype(BF16) for k in range(2 * halves)], axis=1)
-        before = dot(stacked, step_ref[...]).reshape(piece // SLOTS, SLOTS, chunk) + bias_ref[...]
-        small = jnp.exp(-jnp.abs(before))
-        log1p = jnp.where(small < 0.01, small * (1.0 + small * (-0.5 + small * (1.0 / 3.0 - 0.25 * small))), jnp.log(1.0 + small))
-        step = jnp.maximum(before, 0.0) + log1p
-        u = u.reshape(piece // SLOTS, SLOTS, chunk)
-        s_ref[steps] = step
-        v_ref[steps] = step * u
-        y_ref[steps] = skip_ref[...] * u
+        s_ref[steps] = dot(stacked, step_ref[...]).reshape(piece // SLOTS, SLOTS, chunk)
+
+    def soften(lap, _):
+        for sub in range(4):
+            t = lap * 4 + sub
+            for g in range(chunk // LANES):
+                cells = slice(g * LANES, (g + 1) * LANES)
+                before = s_ref[t, :, cells] + bias_ref[:, cells]
+                small = jnp.exp(-jnp.abs(before))
+                series = small * (1.0 + small * (-0.5 + small * (1.0 / 3.0 - 0.25 * small)))
+                step = jnp.maximum(before, 0.0) + jnp.where(small < 0.01, series, jnp.log(1.0 + small))
+                u = v_ref[t, :, cells]
+                s_ref[t, :, cells] = step
+                v_ref[t, :, cells] = step * u
+                y_ref[t, :, cells] = skip_ref[:, cells] * u
+        return 0
+
+    lax.fori_loop(0, time // 4, soften, 0)
 
     groups = chunk // LANES
     at_once = max(1, 12 // groups)
@@ -221,7 +242,7 @@
 RANK = 24
 
 
-def lines_of(x, in_weight, conv, conv_bias, proj, step_weight, step_bias, decay_log, skip):
+def lines_of(x, seam, ends, in_weight, conv, conv_bias, proj, step_weight, step_bias, decay_log, skip):
     parts, reach, length, channels = x.shape
     lines = reach - 2
     time = parts * length
@@ -263,7 +284,8 @@
         functools.partial(line_kernel, lines),
         out_shape=jax.ShapeDtypeStruct((parts * lines * length, width), BF16),
         grid=(1,),
-        in_specs=[whole, pl.BlockSpec((channels, width), lambda i: (0, 0))] + [whole] * 7,
+        in_specs=[whole, whole, pl.BlockSpec(memory_space=pltpu.SMEM), pl.BlockSpec((channels, width), lambda i: (0, 0))]
+        + [whole] * 7,
         out_specs=whole,
         scratch_shapes=[
             pltpu.VMEM((reach, time // SLOTS + 2, SLOTS, width), F32),
@@ -277,7 +299,7 @@
         cost_estimate=pl.CostEstimate(
             flops=flops, bytes_accessed=4 * 1024 * 1024, transcendentals=time * SLOTS * chunk * states
         ),
-    )(x, in_weight, conv, conv_bias.reshape(1, width), wide, tall, slots(step_bias), rates, slots(skip))
+    )(x, seam, ends, in_weight, conv, conv_bias.reshape(1, width), wide, tall, slots(step_bias), rates, slots(skip))
 
 
 def end_kernel(rows_ref, cols_ref, gate_ref, gain_ref, weight_ref, out_ref):
@@ -291,14 +313,17 @@
     out_ref[...] = out.reshape(height, width, channels)
 
 
-def both_ways(array, axis, dim):
-    count = lax.axis_size(axis)
-    size = array.shape[dim]
-    head = lax.index_in_dim(array, 0, dim, False)
-    tail = lax.index_in_dim(array, size - 1, dim, False)
-    up = [(i, i + 1) for i in range(count - 1)]
-    down = [(i + 1, i) for i in range(count - 1)]
-    return lax.ppermute(tail, axis, up), lax.ppermute(head, axis, down)
+def send_lines(send, axis):
+    x = lax.all_to_all(send, axis, 0, 0, tiled=True)
+    count, place = lax.axis_size(axis), lax.axis_index(axis)
+    height, breadth = lax.axis_size("row"), lax.axis_size("col")
+    if axis == "row":
+        ends = [((count - 1) * breadth + c, c + 1) for c in range(breadth - 1)]
+    else:
+        ends = [(r * breadth + count - 1, (r + 1) * breadth) for r in range(height - 1)]
+    pairs = ends + [(b, a) for a, b in ends]
+    seam = lax.ppermute(jnp.where(place == 0, x[:, 1], x[:, -2]), ("row", "col"), pairs)
+    return x, seam, jnp.stack([place == 0, place == count - 1]).astype(jnp.int32)
 
 
 def local(
@@ -320,8 +345,6 @@
     tokens = height * width
     row_lines = height // lax.axis_size("col")
     col_lines = width // lax.axis_size("row")
-    top, bottom = both_ways(features, "row", 0)
-    left, right = both_ways(features, "col", 1)
 
     normed, row_send, col_send = pl.pallas_call(
         cut_kernel,
@@ -330,9 +353,19 @@
             jax.ShapeDtypeStruct((lax.axis_size("col"), row_lines + 2, width, channels), BF16),
             jax.ShapeDtypeStruct((lax.axis_size("row"), col_lines + 2, height, channels), BF16),
         ),
-    )(features, top, bottom, left, right, norm_gain.reshape(1, channels))
-    row_x = lax.all_to_all(row_send, "col", 0, 0, tiled=True)
-    col_x = lax.all_to_all(col_send, "row", 0, 0, tiled=True)
+    )(features, norm_gain.reshape(1, channels))
+    normed, conv_weight, proj_weight, step_weight, step_bias, decay_log, skip_gain = lax.optimization_barrier(
+        (normed, conv_weight, proj_weight, step_weight, step_bias, decay_log, skip_gain)
+    )
+
+    def along(sent, ks, conv):
+        return lines_of(
+            *sent, in_weight, conv, conv_bias, proj_weight[ks], step_weight[ks], step_bias[ks], decay_log[ks], skip_gain[ks]
+        )
+
+    col_sent = send_lines(col_send, "row")
+    row_send, _ = lax.optimization_barrier((row_send, col_sent[0]))
+    row_sent = send_lines(row_send, "col")
     gate = pl.pallas_call(
         gate_kernel,
         out_shape=jax.ShapeDtypeStruct((tokens, inner), BF16),
@@ -344,30 +377,11 @@
         out_specs=pl.BlockSpec((tokens, inner), lambda i: (0, 0)),
         cost_estimate=pl.CostEstimate(flops=2 * tokens * channels * inner, bytes_accessed=1 << 20, transcendentals=0),
     )(normed, in_weight)
-    row_y = lines_of(
-        row_x,
-        in_weight,
-        conv_weight,
-        conv_bias,
-        proj_weight[:2],
-        step_weight[:2],
-        step_bias[:2],
-        decay_log[:2],
-        skip_gain[:2],
-    )
+    col_y = along(col_sent, slice(2, 4), jnp.swapaxes(conv_weight, 0, 1))
+    row_sent, _ = lax.optimization_barrier((row_sent, col_y))
+    col_y = lax.all_to_all(col_y.reshape(lax.axis_size("row"), -1, inner), "row", 0, 0, tiled=True)
+    row_y = along(row_sent, slice(0, 2), conv_weight)
     row_y = lax.all_to_all(row_y.reshape(lax.axis_size("col"), -1, inner), "col", 0, 0, tiled=True)
-    col_y = lines_of(
-        col_x,
-        in_weight,
-        jnp.swapaxes(conv_weight, 0, 1),
-        conv_bias,
-        proj_weight[2:],
-        step_weight[2:],
-        step_bias[2:],
-        decay_log[2:],
-        skip_gain[2:],
-    )
-    col_y = lax.all_to_all(col_y.reshape(lax.axis_size("row"), -1, inner), "row", 0, 0, tiled=True)
     return pl.pallas_call(
         end_kernel,
         out_shape=jax.ShapeDtypeStruct(features.shape, BF16),

time: 96.3 us -> 104 us (1.080)
  starting transfers between devices: 31.1 us -> 16.1 us
  blocking collectives: 0 us -> 14.5 us
  other arithmetic: 1.55 us -> 3.9 us
  waiting for transfers between devices: 14.9 us -> 17.2 us
  Pallas kernels: 38.6 us -> 40.7 us
    all_to_all x0 -> x1, blocking collectives: none -> 14.5 us  [local(): lax.all_to_all(row_y.reshape(lax.axis_size('col'), -1, inner), 'col', 0,...]
    ppermute x4 -> x2, starting transfers between devices: 9.18 us -> 1.95 us  [send_lines(): lax.ppermute(jnp.where(place == 0, x[:, 1], x[:, -2]), ('row', 'col'), pa...]
    all_to_all x3 -> x2, starting transfers between devices: 15.9 us -> 10.7 us  [send_lines(): x = lax.all_to_all(send, axis, 0, 0, tiled=True)]
    all_to_all x3 -> x2, waiting for transfers between devices: 5.71 us -> 8.53 us  [send_lines(): x = lax.all_to_all(send, axis, 0, 0, tiled=True)]
    all_to_all x1, starting transfers between devices: 6.01 us -> 3.45 us  [local(): lax.all_to_all(col_y.reshape(lax.axis_size('row'), -1, inner), 'row', 0,...]
    pallas_call x2, Pallas kernels: 31.1 us -> 33.3 us  [lines_of(): pl.pallas_call(functools.partial(line_kernel, lines), out_shape=jax.Shape...]
    unnamed x31 -> x36, local copies, waits for them, and re-layouts: 2 us -> 4.09 us
    slice x2, local copies, waits for them, and re-layouts: 1.97 us -> 0.04 us  [lines_of(): ranks = proj[:, :, :rank]]
  transfers between devices with their start and end apart: 8 -> 5, of which waited for: 2 -> 3; matrix products, arithmetic and copies ran while one was open for 8% -> 8% of each run, Pallas kernels for 35% -> 21%
where the time goes in v1:
time: 104 us; the launch traced here: 103 us
  Pallas kernels  40.7 us (39%)
  waiting for transfers between devices  17.2 us (17%)
  starting transfers between devices  16.1 us (15%)
  blocking collectives  14.5 us (14%)
  local copies, waits for them, and re-layouts  10 us (10%)
  other arithmetic  3.9 us (4%)
    pallas_call x2, Pallas kernels, lines_of(): pl.pallas_call(functools.partial(line_kernel, lines), out_shape=jax.Shape...  33.3 us
    all_to_all x1, blocking collectives, local(): lax.all_to_all(row_y.reshape(lax.axis_size('col'), -1, inner), 'col', 0,...  14.5 us
    all_to_all x2, starting transfers between devices, send_lines(): x = lax.all_to_all(send, axis, 0, 0, tiled=True)  10.7 us
    all_to_all x1, waiting for transfers between devices, local(): lax.all_to_all(col_y.reshape(lax.axis_size('row'), -1, inner), 'row', 0,...  8.64 us
    all_to_all x2, waiting for transfers between devices, send_lines(): x = lax.all_to_all(send, axis, 0, 0, tiled=True)  8.53 us
    unnamed x36, local copies, waits for them, and re-layouts  4.09 us
    all_to_all x1, starting transfers between devices, local(): lax.all_to_all(col_y.reshape(lax.axis_size('row'), -1, inner), 'row', 0,...  3.45 us
    pallas_call x1, Pallas kernels, local(): pl.pallas_call(end_kernel, out_shape=jax.ShapeDtypeStruct(features.shape,...  2.98 us
  transfers between devices with their start and end apart: 5, of which 3 were waited for; matrix products, arithmetic and copies ran while one was open for 8% of the time, Pallas kernels for 21%

profile of v1, /device:TPU:0, one launch (start us, length us, event | category | flops | bytes accessed | tf_op | source)
XLA Modules:
  0.0 102.8 jit_solution(16448649684287773194)
XLA Ops:
  0.0 1.3 %reshape.82.gain_ref = f32[1,384]{1,0:T(1,128)} reshape(f32[384]{0:T(512)} %param.13) | data formatting | bytes 3072 | tf_op jit(solution)/shard_map/reshape | solution.py:356
  1.3 2.1 %shard_map.118 = (bf16[256,384]{1,0:T(8,128)(2,1)}, bf16[4,6,16,384]{3,2,1,0:T(8,128)(2,1)}, bf16[8,4,16,384]{3,2,1,0:T(8,128)(2,1)}) custom-call(bf16[16,16,384]{2,1,0:T(8,128)(2,1)} %feat_ref.1, f32[1,384]{1,0:T(1,128)} %reshape.82.gain_ref), custom_call_target="tpu_custom_call" | custom-call | tf_op jit(solution)/shard_map/pallas_call | solution.py:349
  3.4 7.3 %all-to-all-start = ((bf16[8,4,16,384]{3,2,1,0:T(8,128)(2,1)}), bf16[8,4,16,384]{3,2,1,0:T(8,128)(2,1)S(1)}, u32[]{:S(2)}, u32[]{:S(2)}) async-start(bf16[8,4,16,384]{3,2,1,0:T(8,128)(2,1)} %get-tuple-element.20), calls=%async_computation | async-start | bytes 786432 | tf_op jit(solution)/shard_map/all_to_all | solution.py:317
  11.4 0.7 copy.32
  13.3 0.8 reshape.90.rate_ref
  16.7 0.9 maximum_maximum_fusion.1
  17.6 0.7 maximum_maximum_fusion.3
  18.3 4.1 %all-to-all-done.x_ref = bf16[8,4,16,384]{3,2,1,0:T(8,128)(2,1)S(1)} async-done(((bf16[8,4,16,384]{3,2,1,0:T(8,128)(2,1)}), bf16[8,4,16,384]{3,2,1,0:T(8,128)(2,1)S(1)}, u32[]{:S(2)}, u32[]{:S(2)}) %all-to-all-start) | async-done | bytes 393248 | tf_op jit(solution)/shard_map/all_to_all | solution.py:317
  22.4 3.5 %all-to-all-start.1 = ((bf16[4,6,16,384]{3,2,1,0:T(8,128)(2,1)}), bf16[4,6,16,384]{3,2,1,0:T(8,128)(2,1)S(1)}, u32[]{:S(2)}, u32[]{:S(2)}) async-start(bf16[4,6,16,384]{3,2,1,0:T(8,128)(2,1)} %get-tuple-element.21), calls=%async_computation.1 | async-start | bytes 589824 | tf_op jit(solution)/shard_map/all_to_all | solution.py:317
  26.5 1.3 %collective-permute-start.1 = (bf16[8,16,384]{2,1,0:T(8,128)(2,1)}, bf16[8,16,384]{2,1,0:T(8,128)(2,1)}, u32[]{:S(2)}, u32[]{:S(2)}) collective-permute-start(bf16[8,16,384]{2,1,0:T(8,128)(2,1)} %fusion.3), channel_id=1, source_target_pairs={{28,1},{29,2},{30,3},{1,28},{2,29},{3,30}} | collective-permute-start | bytes 294920 | tf_op jit(solution)/shard_map/ppermute | solution.py:325
  27.8 4.4 %all-to-all-done.1.x_ref = bf16[4,6,16,384]{3,2,1,0:T(8,128)(2,1)S(1)} async-done(((bf16[4,6,16,384]{3,2,1,0:T(8,128)(2,1)}), bf16[4,6,16,384]{3,2,1,0:T(8,128)(2,1)S(1)}, u32[]{:S(2)}, u32[]{:S(2)}) %all-to-all-start.1) | async-done | bytes 294944 | tf_op jit(solution)/shard_map/all_to_all | solution.py:317
  32.2 0.7 collective-permute-start
  32.9 1.0 copy-done.1
  33.9 0.9 copy-done.3
  34.8 0.7 copy-done.6
  35.6 0.7 copy-done.8
  36.2 19.0 %shard_map.119 = bf16[256,768]{1,0:T(8,128)(2,1)S(1)} custom-call(bf16[8,4,16,384]{3,2,1,0:T(8,128)(2,1)S(1)} %all-to-all-done.x_ref, bf16[8,16,384]{2,1,0:T(8,128)(2,1)} %collective-permute-done.1.seam_ref, s32[2]{0:T(128)S(1)} %copy-done.8, bf16[384,1536]{1,0:T(8,128)(2,1)S(1)} %copy-done, f32[3,3,768]{2,1,0:T(4,128)S(1)} %bitcast.72, ...), custom_call_target="tpu_custom_call" | custom-call | flops 704643072 | bytes 4194304 | tf_op jit(solution)/shard_map/pallas_call | solution.py:283
  55.2 14.3 %shard_map.120 = bf16[256,768]{1,0:T(8,128)(2,1)S(1)} custom-call(bf16[4,6,16,384]{3,2,1,0:T(8,128)(2,1)S(1)} %all-to-all-done.1.x_ref, bf16[4,16,384]{2,1,0:T(8,128)(2,1)S(1)} %collective-permute-done.seam_ref, s32[2]{0:T(128)S(1)} %copy-done.7, bf16[384,1536]{1,0:T(8,128)(2,1)S(1)} %copy-done, f32[3,3,768]{2,1,0:T(4,128)S(1)} %copy-done.4, ...), custom_call_target="tpu_custom_call" | custom-call | flops 427819008 | bytes 4194304 | tf_op jit(solution)/shard_map/pallas_call | solution.py:283
  69.6 14.5 %all_to_all.20 = bf16[4,64,768]{2,1,0:T(8,128)(2,1)} all-to-all(bf16[4,64,768]{2,1,0:T(8,128)(2,1)S(1)} %bitcast.71), channel_id=1, replica_groups=mesh['row'=8,'col'=4] {'col'}, dimensions={0} | all-to-all | bytes 786432 | tf_op jit(solution)/shard_map/all_to_all | solution.py:384
  84.1 3.5 %all-to-all-start.3 = ((bf16[8,32,768]{2,1,0:T(8,128)(2,1)}), bf16[8,32,768]{2,1,0:T(8,128)(2,1)S(1)}, u32[]{:S(2)}, u32[]{:S(2)}) async-start(bf16[8,32,768]{2,1,0:T(8,128)(2,1)} %bitcast.70), calls=%async_computation.3 | async-start | bytes 786432 | tf_op jit(solution)/shard_map/all_to_all | solution.py:382
  88.2 2.3 %shard_map.121.gate_ref = bf16[256,768]{1,0:T(8,128)(2,1)} custom-call(bf16[256,384]{1,0:T(8,128)(2,1)} %get-tuple-element.32.norm_ref, bf16[384,1536]{1,0:T(8,128)(2,1)} %weight_ref.6), custom_call_target="tpu_custom_call" | custom-call | flops 150994944 | bytes 1048576 | tf_op jit(solution)/shard_map/pallas_call | solution.py:369
  90.5 8.6 %all-to-all-done.3 = bf16[8,32,768]{2,1,0:T(8,128)(2,1)S(1)} async-done(((bf16[8,32,768]{2,1,0:T(8,128)(2,1)}), bf16[8,32,768]{2,1,0:T(8,128)(2,1)S(1)}, u32[]{:S(2)}, u32[]{:S(2)}) %all-to-all-start.3) | async-done | bytes 393248 | tf_op jit(solution)/shard_map/all_to_all | solution.py:382
  99.1 0.7 copy-done.9
  99.8 3.0 %shard_map.122 = bf16[16,16,384]{2,1,0:T(8,128)(2,1)} custom-call(bf16[256,768]{1,0:T(8,128)(2,1)} %bitcast.75, bf16[256,768]{1,0:T(8,128)(2,1)} %bitcast.76, bf16[256,768]{1,0:T(8,128)(2,1)} %shard_map.121.gate_ref, f32[1,768]{1,0:T(1,128)} %reshape.99.gain_ref, bf16[768,384]{1,0:T(8,128)(2,1)} %weight_ref.7), custom_call_target="tpu_custom_call" | custom-call | tf_op jit(solution)/shard_map/pallas_call | solution.py:385
  (72 shorter events, 5.4 us)
Async XLA Ops:
  0.0 10.7 %copy-start.10 = (bf16[4,768,56]{1,2,0:T(8,128)(2,1)S(1)}, bf16[4,768,56]{1,2,0:T(8,128)(2,1)}, u32[]{:S(2)}) copy-start(bf16[4,768,56]{1,2,0:T(8,128)(2,1)} %param.17) | copy-start | bytes 1032196
  0.0 10.8 %copy-start.11 = (f32[4,24,768]{2,1,0:T(8,128)S(1)}, f32[4,24,768]{2,1,0:T(8,128)}, u32[]{:S(2)}) copy-start(f32[4,24,768]{2,1,0:T(8,128)} %param.18) | copy-start | bytes 884740
  3.4 19.0 %all-to-all-start = ((bf16[8,4,16,384]{3,2,1,0:T(8,128)(2,1)}), bf16[8,4,16,384]{3,2,1,0:T(8,128)(2,1)S(1)}, u32[]{:S(2)}, u32[]{:S(2)}) async-start(bf16[8,4,16,384]{3,2,1,0:T(8,128)(2,1)} %get-tuple-element.20), calls=%async_computation | async-start | bytes 786432 | tf_op jit(solution)/shard_map/all_to_all | solution.py:317
  10.9 5.8 %copy-start.17 = (bf16[128]{0:T(256)(128)(2,1)}, bf16[128]{0:T(256)(128)(2,1)S(1)}, u32[]{:S(2)}) copy-start(bf16[128]{0:T(256)(128)(2,1)S(1)} %pad.11.clone) | copy-start | bytes 772
  11.3 1.0 %copy-start.13 = (f32[4,768]{1,0:T(4,128)S(1)}, f32[4,768]{1,0:T(4,128)}, u32[]{:S(2)}) copy-start(f32[4,768]{1,0:T(4,128)} %param.21) | copy-start | bytes 36868
  11.3 1.0 %copy-start.14 = (f32[4,768]{1,0:T(4,128)S(1)}, f32[4,768]{1,0:T(4,128)}, u32[]{:S(2)}) copy-start(f32[4,768]{1,0:T(4,128)} %param.19) | copy-start | bytes 36868
  11.3 1.8 %copy-start.12 = (f32[4,768,16]{1,2,0:T(8,128)S(1)}, f32[4,768,16]{1,2,0:T(8,128)}, u32[]{:S(2)}) copy-start(f32[4,768,16]{1,2,0:T(8,128)} %param.20) | copy-start | bytes 589828
  12.1 2.0 %copy-start.4 = (f32[3,3,768]{2,1,0:T(4,128)S(1)}, f32[3,3,768]{2,1,0:T(4,128)}, u32[]{:S(2)}) copy-start(f32[3,3,768]{2,1,0:T(4,128)} %conv_ref) | copy-start | bytes 82948
  12.2 2.0 %copy-start.15 = (f32[768]{0:T(1024)S(1)}, f32[768]{0:T(1024)}, u32[]{:S(2)}) copy-start(f32[768]{0:T(1024)} %param.16) | copy-start | bytes 9220
  16.6 16.3 %copy-start = (bf16[384,1536]{1,0:T(8,128)(2,1)S(1)}, bf16[384,1536]{1,0:T(8,128)(2,1)}, u32[]{:S(2)}) copy-start(bf16[384,1536]{1,0:T(8,128)(2,1)} %weight_ref.6) | copy-start | bytes 3538948
  22.4 9.8 %all-to-all-start.1 = ((bf16[4,6,16,384]{3,2,1,0:T(8,128)(2,1)}), bf16[4,6,16,384]{3,2,1,0:T(8,128)(2,1)S(1)}, u32[]{:S(2)}, u32[]{:S(2)}) async-start(bf16[4,6,16,384]{3,2,1,0:T(8,128)(2,1)} %get-tuple-element.21), calls=%async_computation.1 | async-start | bytes 589824 | tf_op jit(solution)/shard_map/all_to_all | solution.py:317
  26.5 6.4 %collective-permute-start.1 = (bf16[8,16,384]{2,1,0:T(8,128)(2,1)}, bf16[8,16,384]{2,1,0:T(8,128)(2,1)}, u32[]{:S(2)}, u32[]{:S(2)}) collective-permute-start(bf16[8,16,384]{2,1,0:T(8,128)(2,1)} %fusion.3), channel_id=1, source_target_pairs={{28,1},{29,2},{30,3},{1,28},{2,29},{3,30}} | collective-permute-start | bytes 294920 | tf_op jit(solution)/shard_map/ppermute | solution.py:325
  32.2 23.0 %collective-permute-start = (bf16[4,16,384]{2,1,0:T(8,128)(2,1)S(1)}, bf16[4,16,384]{2,1,0:T(8,128)(2,1)S(1)}, u32[]{:S(2)}, u32[]{:S(2)}) collective-permute-start(bf16[4,16,384]{2,1,0:T(8,128)(2,1)S(1)} %fusion.5), channel_id=1, source_target_pairs={{3,4},{7,8},{11,12},{15,16},{19,20},{23,24},{27,28},{4,3},{8,7},{1... | collective-permute-start | bytes 147464 | tf_op jit(solution)/shard_map/ppermute | solution.py:325
  32.9 1.0 copy-start.1
  33.9 0.9 copy-start.3
  34.8 0.7 copy-start.6
  35.6 0.7 copy-start.8
  36.2 19.0 %copy-start.5 = (f32[8,768]{1,0:T(8,128)S(1)}, f32[8,768]{1,0:T(8,128)}, u32[]{:S(2)}) copy-start(f32[8,768]{1,0:T(8,128)} %broadcast_in_dim.53.skip_ref) | copy-start | bytes 73732
  36.2 19.0 %copy-start.7 = (s32[2]{0:T(128)S(1)}, s32[2]{0:T(128)}, u32[]{:S(2)}) copy-start(s32[2]{0:T(128)} %add_convert_fusion.ends_ref) | copy-start | bytes 28
  55.2 14.4 %copy-start.2 = (bf16[256,768]{1,0:T(8,128)(2,1)}, bf16[256,768]{1,0:T(8,128)(2,1)S(1)}, u32[]{:S(2)}) copy-start(bf16[256,768]{1,0:T(8,128)(2,1)S(1)} %shard_map.119) | copy-start | bytes 1179652
  69.6 18.0 %copy-start.16 = (f32[768]{0:T(1024)S(1)}, f32[768]{0:T(1024)}, u32[]{:S(2)}) copy-start(f32[768]{0:T(1024)} %param.22) | copy-start | bytes 9220
  84.1 15.0 %all-to-all-start.3 = ((bf16[8,32,768]{2,1,0:T(8,128)(2,1)}), bf16[8,32,768]{2,1,0:T(8,128)(2,1)S(1)}, u32[]{:S(2)}, u32[]{:S(2)}) async-start(bf16[8,32,768]{2,1,0:T(8,128)(2,1)} %bitcast.70), calls=%async_computation.3 | async-start | bytes 786432 | tf_op jit(solution)/shard_map/all_to_all | solution.py:382
  99.1 0.7 copy-start.9

commit v2 on v1

--- a/solution.py
+++ b/solution.py
@@ -73,24 +73,31 @@
 
 def line_kernel(
     lines,
+    axis,
+    after_ref,
     x_ref,
     seam_ref,
-    ends_ref,
     weight_ref,
     conv_ref,
     conv_bias_ref,
+    proj_raw_ref,
+    step_raw_ref,
+    bias_raw_ref,
+    decay_ref,
+    skip_raw_ref,
+    out_ref,
+    token_ref,
+    inner_ref,
+    active_ref,
     proj_ref,
     step_ref,
     bias_ref,
-    rate_ref,
     skip_ref,
-    out_ref,
-    inner_ref,
-    active_ref,
     proj_out_ref,
     s_ref,
     v_ref,
     y_ref,
+    spread_ref,
 ):
     parts, reach, length, channels = x_ref.shape
     time = parts * length
@@ -99,21 +106,54 @@
     chunk = s_ref.shape[2]
     halves = width // chunk
     slot_lines = SLOTS // (2 * halves)
-    states = rate_ref.shape[0]
+    states = decay_ref.shape[1]
+    if axis == "row":
+        across_first = lambda across, along: (along, across)
+    else:
+        across_first = lambda across, along: (across, along)
+
+    place = lax.broadcasted_iota(jnp.int32, (SLOTS, chunk), 0)
+
+    def by_slot(rows):
+        found = None
+        for half in range(halves):
+            for way in range(2):
+                row = rows(half, way)
+                row = jnp.broadcast_to(row, (SLOTS, row.shape[1]))
+                kind = half * 2 + way
+                found = row if found is None else jnp.where(place[:, : row.shape[1]] >= kind * slot_lines, row, found)
+        return found
+
+    bias_ref[...] = by_slot(lambda half, way: bias_raw_ref[way : way + 1, half * chunk : (half + 1) * chunk])
+    skip_ref[...] = by_slot(lambda half, way: skip_raw_ref[way : way + 1, half * chunk : (half + 1) * chunk])
+    for half in range(halves):
+        cells = slice(half * chunk, (half + 1) * chunk)
+        for way in range(2):
+            kind = slice((half * 2 + way) * LANES, (half * 2 + way + 1) * LANES)
+            w = proj_raw_ref[way, :, cells].astype(F32)
+            ranks = w[:RANK]
+            rest = jnp.zeros((LANES - 3 * RANK - 2 * states, chunk), F32)
+            w = jnp.concatenate([ranks, ranks, ranks, w[RANK:], rest], axis=0)
+            proj_ref[:, kind] = w.T.astype(BF16)
+            w = step_raw_ref[way, :, cells]
+            high = w.astype(BF16).astype(F32)
+            rest = jnp.zeros((LANES - 3 * RANK, chunk), F32)
+            step_ref[kind, :] = jnp.concatenate([high, high, w - high, rest], axis=0).astype(BF16)
 
     row = rows_of(time)
     order = one_hot([((row & 7) << bits(low)) + (row >> 3)], time)
-    place = lax.broadcasted_iota(jnp.int32, (SLOTS, width), 0)
     for line in range(reach):
         x = x_ref[:, line].reshape(time, channels)
         if line == 0 or line == reach - 1:
-            missing = ends_ref[0 if line == 0 else 1] == 1
+            missing = lax.axis_index(axis) == (0 if line == 0 else lax.axis_size(axis) - 1)
             x = jnp.where(missing, seam_ref[...].reshape(time, channels), x)
-        tokens = dot(order, x).astype(BF16)
-        inner = dot(tokens, weight_ref[...]).astype(BF16).astype(F32).reshape(low, SLOTS, width)
-        inner_ref[line, 1 : low + 1] = inner
-        inner_ref[line, 0] = jnp.where(place == 0, 0.0, pltpu.roll(inner[low - 1], 1, 0))
-        inner_ref[line, low + 1] = jnp.where(place == SLOTS - 1, 0.0, pltpu.roll(inner[0], SLOTS - 1, 0))
+        token_ref[line * time : (line + 1) * time] = dot(order, x).astype(BF16)
+    inner = dot(token_ref[...], weight_ref[...]).astype(BF16).astype(F32)
+    inner_ref[:, 1 : low + 1] = inner.reshape(reach, low, SLOTS, width)
+    place = lax.broadcasted_iota(jnp.int32, (SLOTS, width), 0)
+    for line in range(reach):
+        inner_ref[line, 0] = jnp.where(place == 0, 0.0, pltpu.roll(inner_ref[line, low], 1, 0))
+        inner_ref[line, low + 1] = jnp.where(place == SLOTS - 1, 0.0, pltpu.roll(inner_ref[line, 1], SLOTS - 1, 0))
 
     def convolve(pair, _):
         for group in range(width // (2 * LANES)):
@@ -124,7 +164,8 @@
             totals = [[bias for _ in range(2)] for _ in range(lines)]
             for across in range(3):
                 for along in range(3):
-                    tap = jnp.broadcast_to(conv_ref[across, along : along + 1, cells], (SLOTS, 2 * LANES))
+                    first, second = across_first(across, along)
+                    tap = jnp.broadcast_to(conv_ref[first, second : second + 1, cells], (SLOTS, 2 * LANES))
                     for line in range(lines):
                         for sub in range(2):
                             totals[line][sub] += inner_ref[line + across, 2 * pair + sub + along, :, cells] * tap
@@ -195,23 +236,40 @@
     groups = chunk // LANES
     at_once = max(1, 12 // groups)
     unroll = 8
+    laps = time // unroll
+    place = lax.broadcasted_iota(jnp.int32, (SLOTS, LANES), 0)
     for first in range(0, states, at_once):
-        rates = [
-            [rate_ref[n, :, g * LANES : (g + 1) * LANES] for g in range(groups)] for n in range(first, first + at_once)
-        ]
+        rates = []
+        for n in range(first, first + at_once):
+            rates.append([])
+            for g in range(groups):
+                rate = by_slot(
+                    lambda half, way: decay_ref[way, n : n + 1, half * chunk + g * LANES : half * chunk + (g + 1) * LANES]
+                )
+                rates[-1].append(-LOG2E * jnp.exp(rate))
+
+        def spread(lap):
+            found = []
+            for sub in range(unroll):
+                coefs = proj_out_ref[lap * unroll + sub]
+                for kind in range(2):
+                    for n in range(at_once):
+                        lane = 3 * RANK + kind * states + first + n
+                        found.append(jnp.broadcast_to(coefs[:, lane : lane + 1], (SLOTS, LANES)))
+            return found
+
+        def keep(slot, found):
+            for k, value in enumerate(found):
+                spread_ref[slot, k] = value
 
         def advance(lap, hidden):
             hidden = list(hidden)
+            slot = lap & 1
+            ahead = spread(jnp.minimum(lap + 1, laps - 1))
             for sub in range(unroll):
                 t = lap * unroll + sub
-                coefs = proj_out_ref[t]
-                enter = []
-                leave = []
-                for n in range(at_once):
-                    lane = 3 * RANK + first + n
-                    enter.append(jnp.broadcast_to(coefs[:, lane : lane + 1], (SLOTS, LANES)))
-                    lane = lane + states
-                    leave.append(jnp.broadcast_to(coefs[:, lane : lane + 1], (SLOTS, LANES)))
+                enter = [spread_ref[slot, sub * 2 * at_once + n] for n in range(at_once)]
+                leave = [spread_ref[slot, sub * 2 * at_once + at_once + n] for n in range(at_once)]
                 for g in range(groups):
                     cells = pl.ds(g * LANES, LANES)
                     step = s_ref[t, :, cells]
@@ -223,83 +281,114 @@
                         hidden[k] = h
                         y = y + h * leave[n]
                     y_ref[t, :, cells] = y
+            keep(1 - slot, ahead)
             return tuple(hidden)
 
+        keep(0, spread(0))
         zero = jnp.zeros((SLOTS, LANES), F32)
-        lax.fori_loop(0, time // unroll, advance, (zero,) * (at_once * groups))
-
+        lax.fori_loop(0, laps, advance, (zero,) * (at_once * groups))
+
+    out_ref[...] = y_ref[...].reshape(time * SLOTS, chunk).astype(BF16)
+
+
+def join_kernel(parts, lines, after_ref, scanned_ref, out_ref):
+    length = out_ref.shape[0] // (parts * lines)
+    time = parts * length
+    chunk = scanned_ref.shape[1]
+    halves = out_ref.shape[1] // chunk
+    slot_lines = SLOTS // (2 * halves)
     row = rows_of(lines * time)
     line = (row >> bits(length)) & (lines - 1)
     now = ((row >> bits(lines * length)) << bits(length)) + (row & (length - 1))
-    scanned = y_ref[...].reshape(time * SLOTS, chunk).astype(BF16)
     for half in range(halves):
         ahead = now * SLOTS + (half * 2 * slot_lines) + line
         behind = (time - 1 - now) * SLOTS + (half * 2 * slot_lines + slot_lines) + line
-        joined = dot(one_hot([ahead, behind], time * SLOTS), scanned)
+        joined = dot(one_hot([ahead, behind], time * SLOTS), scanned_ref[...])
         out_ref[:, half * chunk : (half + 1) * chunk] = joined.astype(BF16)
 
 
+def join(scanned, parts, lines, length, width, after):
+    return pl.pallas_call(
+        functools.partial(join_kernel, parts, lines),
+        out_shape=jax.ShapeDtypeStruct((parts * lines * length, width), BF16),
+        in_specs=[pl.BlockSpec(memory_space=pl.ANY), pl.BlockSpec(memory_space=pltpu.VMEM)],
+        out_specs=pl.BlockSpec(memory_space=pltpu.VMEM),
+        compiler_params=pltpu.CompilerParams(vmem_limit_bytes=50 * 1024 * 1024),
+    )(after, scanned)
+
+
 RANK = 24
 
 
-def lines_of(x, seam, ends, in_weight, conv, conv_bias, proj, step_weight, step_bias, decay_log, skip):
+def lines_of(axis, after, x, seam, in_weight, conv, conv_bias, proj, step_weight, step_bias, decay_log, skip):
     parts, reach, length, channels = x.shape
     lines = reach - 2
     time = parts * length
     width = conv.shape[2]
-    rank = step_weight.shape[1]
     states = decay_log.shape[2]
-    assert rank == RANK
+    assert step_weight.shape[1] == RANK
     halves = 1 if lines >= 4 else 2
-    slot_lines = SLOTS // (2 * halves)
-    assert lines <= slot_lines
+    assert lines <= SLOTS // (2 * halves)
     chunk = width // halves
-
-    def by_half(a):
-        return jnp.swapaxes(a.reshape(a.shape[:-1] + (halves, chunk)), 0, -2)
-
-    def slots(a):
-        a = jnp.swapaxes(a.reshape(2, halves, 1, chunk), 0, 1)
-        return jnp.broadcast_to(a, (halves, 2, slot_lines, chunk)).reshape(SLOTS, chunk)
-
-    ranks = proj[:, :, :rank]
-    wide = jnp.concatenate(
-        [ranks, ranks, ranks, proj[:, :, rank:], jnp.zeros((2, width, LANES - 3 * rank - 2 * states), proj.dtype)],
-        axis=2,
-    )
-    wide = wide.reshape(2, halves, chunk, LANES).transpose(2, 1, 0, 3).reshape(chunk, halves * 2 * LANES)
-    high = lax.reduce_precision(step_weight, 8, 7)
-    rest = step_weight - high
-    tall = jnp.concatenate(
-        [high, high, rest, jnp.zeros((2, LANES - 3 * rank, width), step_weight.dtype)], axis=1
-    ).astype(BF16)
-    tall = tall.reshape(2, LANES, halves, chunk).transpose(2, 0, 1, 3).reshape(halves * 2 * LANES, chunk)
-    rates = -jnp.exp(decay_log) * LOG2E
-    rates = rates.transpose(2, 0, 1).reshape(states, 2, halves, 1, chunk).transpose(0, 2, 1, 3, 4)
-    rates = jnp.broadcast_to(rates, (states, halves, 2, slot_lines, chunk)).reshape(states, SLOTS, chunk)
-
-    whole = pl.BlockSpec(memory_space=pltpu.VMEM)
+    way = 0 if axis == "col" else 1
+    at_once = max(1, 12 // (chunk // LANES))
+
+    def all_of(*shape):
+        return pl.BlockSpec(shape, lambda i: (0,) * len(shape))
+
+    def pair(*shape):
+        return pl.BlockSpec((2,) + shape, lambda i: (way,) + (0,) * len(shape))
+
     flops = 2 * time * (reach * channels * width + SLOTS * width * 256)
     return pl.pallas_call(
-        functools.partial(line_kernel, lines),
-        out_shape=jax.ShapeDtypeStruct((parts * lines * length, width), BF16),
+        functools.partial(line_kernel, lines, axis),
+        out_shape=jax.ShapeDtypeStruct((time * SLOTS, chunk), BF16),
         grid=(1,),
-        in_specs=[whole, whole, pl.BlockSpec(memory_space=pltpu.SMEM), pl.BlockSpec((channels, width), lambda i: (0, 0))]
-        + [whole] * 7,
-        out_specs=whole,
+        in_specs=[
+            pl.BlockSpec(memory_space=pl.ANY),
+            all_of(parts, reach, length, channels),
+            all_of(parts, length, channels),
+            all_of(channels, width),
+            all_of(3, 3, width),
+            all_of(1, width),
+            pair(RANK + 2 * states, width),
+            pair(RANK, width),
+            pl.BlockSpec((None, 2, width), lambda i: (way, 0, 0)),
+            pair(states, width),
+            pl.BlockSpec((None, 2, width), lambda i: (way, 0, 0)),
+        ],
+        out_specs=all_of(time * SLOTS, chunk),
         scratch_shapes=[
+            pltpu.VMEM((reach * time, channels), BF16),
             pltpu.VMEM((reach, time // SLOTS + 2, SLOTS, width), F32),
             pltpu.VMEM((halves * lines * time, chunk), BF16),
+            pltpu.VMEM((chunk, halves * 2 * LANES), BF16),
+            pltpu.VMEM((halves * 2 * LANES, chunk), BF16),
+            pltpu.VMEM((SLOTS, chunk), F32),
+            pltpu.VMEM((SLOTS, chunk), F32),
             pltpu.VMEM((time, SLOTS, LANES), F32),
             pltpu.VMEM((time, SLOTS, chunk), F32),
             pltpu.VMEM((time, SLOTS, chunk), F32),
             pltpu.VMEM((time, SLOTS, chunk), F32),
+            pltpu.VMEM((2, 8 * 2 * at_once, SLOTS, LANES), F32),
         ],
         compiler_params=pltpu.CompilerParams(vmem_limit_bytes=50 * 1024 * 1024),
         cost_estimate=pl.CostEstimate(
             flops=flops, bytes_accessed=4 * 1024 * 1024, transcendentals=time * SLOTS * chunk * states
         ),
-    )(x, seam, ends, in_weight, conv, conv_bias.reshape(1, width), wide, tall, slots(step_bias), rates, slots(skip))
+    )(
+        after,
+        x,
+        seam,
+        in_weight,
+        conv,
+        conv_bias.reshape(1, width),
+        jnp.swapaxes(proj, 1, 2),
+        step_weight,
+        step_bias.reshape(2, 2, width),
+        jnp.swapaxes(decay_log, 1, 2),
+        skip.reshape(2, 2, width),
+    )
 
 
 def end_kernel(rows_ref, cols_ref, gate_ref, gain_ref, weight_ref, out_ref):
@@ -323,7 +412,7 @@
         ends = [(r * breadth + count - 1, (r + 1) * breadth) for r in range(height - 1)]
     pairs = ends + [(b, a) for a, b in ends]
     seam = lax.ppermute(jnp.where(place == 0, x[:, 1], x[:, -2]), ("row", "col"), pairs)
-    return x, seam, jnp.stack([place == 0, place == count - 1]).astype(jnp.int32)
+    return x, seam
 
 
 def local(
@@ -354,17 +443,8 @@
             jax.ShapeDtypeStruct((lax.axis_size("row"), col_lines + 2, height, channels), BF16),
         ),
     )(features, norm_gain.reshape(1, channels))
-    normed, conv_weight, proj_weight, step_weight, step_bias, decay_log, skip_gain = lax.optimization_barrier(
-        (normed, conv_weight, proj_weight, step_weight, step_bias, decay_log, skip_gain)
-    )
-
-    def along(sent, ks, conv):
-        return lines_of(
-            *sent, in_weight, conv, conv_bias, proj_weight[ks], step_weight[ks], step_bias[ks], decay_log[ks], skip_gain[ks]
-        )
-
+    weights = (in_weight, conv_weight, conv_bias, proj_weight, step_weight, step_bias, decay_log, skip_gain)
     col_sent = send_lines(col_send, "row")
-    row_send, _ = lax.optimization_barrier((row_send, col_sent[0]))
     row_sent = send_lines(row_send, "col")
     gate = pl.pallas_call(
         gate_kernel,
@@ -377,11 +457,14 @@
         out_specs=pl.BlockSpec((tokens, inner), lambda i: (0, 0)),
         cost_estimate=pl.CostEstimate(flops=2 * tokens * channels * inner, bytes_accessed=1 << 20, transcendentals=0),
     )(normed, in_weight)
-    col_y = along(col_sent, slice(2, 4), jnp.swapaxes(conv_weight, 0, 1))
-    row_sent, _ = lax.optimization_barrier((row_sent, col_y))
-    col_y = lax.all_to_all(col_y.reshape(lax.axis_size("row"), -1, inner), "row", 0, 0, tiled=True)
-    row_y = along(row_sent, slice(0, 2), conv_weight)
-    row_y = lax.all_to_all(row_y.reshape(lax.axis_size("col"), -1, inner), "col", 0, 0, tiled=True)
+    parts = lax.axis_size("row")
+    col_y = lines_of("row", normed, *col_sent, *weights)
+    joined = join(col_y, parts, col_lines, height, inner, normed)
+    col_y = lax.all_to_all(joined.reshape(parts, -1, inner), "row", 0, 0, tiled=True)
+    parts = lax.axis_size("col")
+    row_y = lines_of("col", joined, *row_sent, *weights)
+    row_y = join(row_y, parts, row_lines, width, inner, col_y)
+    row_y = lax.all_to_all(row_y.reshape(parts, -1, inner), "col", 0, 0, tiled=True)
     return pl.pallas_call(
         end_kernel,
         out_shape=jax.ShapeDtypeStruct(features.shape, BF16),

time: 104 us -> 106 us (1.019)
  the two profiles are of different devices: /device:TPU:0 before, /device:TPU:16 now
where the time goes in v2:
time: 106 us; the launch traced here: 105 us
  Pallas kernels  45.4 us (43%)
  starting transfers between devices  31.8 us (30%)
  waiting for transfers between devices  22.6 us (21%)
  local copies, waits for them, and re-layouts  5.49 us (5%)
    pallas_call x2, Pallas kernels, lines_of(): pl.pallas_call(functools.partial(line_kernel, lines, axis), out_shape=jax...  35.4 us
    all_to_all x1, starting transfers between devices, local(): lax.all_to_all(joined.reshape(parts, -1, inner), 'row', 0, 0, tiled=True)  13.6 us
    all_to_all x2, starting transfers between devices, send_lines(): x = lax.all_to_all(send, axis, 0, 0, tiled=True)  9.75 us
    all_to_all x2, waiting for transfers between devices, send_lines(): x = lax.all_to_all(send, axis, 0, 0, tiled=True)  9.58 us
    ppermute x2, waiting for transfers between devices, send_lines(): lax.ppermute(jnp.where(place == 0, x[:, 1], x[:, -2]), ('row', 'col'), pa...  8.47 us
    ppermute x2, starting transfers between devices, send_lines(): lax.ppermute(jnp.where(place == 0, x[:, 1], x[:, -2]), ('row', 'col'), pa...  4.97 us
    all_to_all x1, waiting for transfers between devices, local(): lax.all_to_all(row_y.reshape(parts, -1, inner), 'col', 0, 0, tiled=True)  4.55 us
    unnamed x30, local copies, waits for them, and re-layouts  3.47 us
  transfers between devices with their start and end apart: 6, of which 3 were waited for; matrix products, arithmetic and copies ran while one was open for 1% of the time, Pallas kernels for 37%

profile of v2, /device:TPU:16, one launch (start us, length us, event | category | flops | bytes accessed | tf_op | source)
XLA Modules:
  0.0 105.5 jit_solution(14142255261611851797)
XLA Ops:
  0.0 0.0 copy-start.6
  0.0 0.0 copy-start.1
  0.0 1.4 %reshape.34.gain_ref = f32[1,384]{1,0:T(1,128)} reshape(f32[384]{0:T(512)} %param.13) | data formatting | bytes 3072 | tf_op jit(solution)/shard_map/reshape | solution.py:445
  1.4 2.1 %shard_map.118 = (bf16[256,384]{1,0:T(8,128)(2,1)}, bf16[4,6,16,384]{3,2,1,0:T(8,128)(2,1)}, bf16[8,4,16,384]{3,2,1,0:T(8,128)(2,1)}) custom-call(bf16[16,16,384]{2,1,0:T(8,128)(2,1)} %feat_ref.1, f32[1,384]{1,0:T(1,128)} %reshape.34.gain_ref), custom_call_target="tpu_custom_call" | custom-call | tf_op jit(solution)/shard_map/pallas_call | solution.py:438
  3.6 6.3 %all-to-all-start = ((bf16[8,4,16,384]{3,2,1,0:T(8,128)(2,1)}), bf16[8,4,16,384]{3,2,1,0:T(8,128)(2,1)S(1)}, u32[]{:S(2)}, u32[]{:S(2)}) async-start(bf16[8,4,16,384]{3,2,1,0:T(8,128)(2,1)} %get-tuple-element.9), calls=%async_computation | async-start | bytes 786432 | tf_op jit(solution)/shard_map/all_to_all | solution.py:406
  9.8 9.6 %all-to-all-done.x_ref = bf16[8,4,16,384]{3,2,1,0:T(8,128)(2,1)S(1)} async-done(((bf16[8,4,16,384]{3,2,1,0:T(8,128)(2,1)}), bf16[8,4,16,384]{3,2,1,0:T(8,128)(2,1)S(1)}, u32[]{:S(2)}, u32[]{:S(2)}) %all-to-all-start) | async-done | bytes 393248 | tf_op jit(solution)/shard_map/all_to_all | solution.py:406
  19.4 3.5 %all-to-all-start.2 = ((bf16[4,6,16,384]{3,2,1,0:T(8,128)(2,1)}), bf16[4,6,16,384]{3,2,1,0:T(8,128)(2,1)S(1)}, u32[]{:S(2)}, u32[]{:S(2)}) async-start(bf16[4,6,16,384]{3,2,1,0:T(8,128)(2,1)} %get-tuple-element.10), calls=%async_computation.2 | async-start | bytes 589824 | tf_op jit(solution)/shard_map/all_to_all | solution.py:406
  22.9 0.7 collective-permute-start
  23.7 1.0 copy-done.4
  24.7 0.8 copy-done.8
  25.5 21.4 %shard_map.119.scanned_ref = bf16[1024,384]{1,0:T(8,128)(2,1)S(1)} custom-call(bf16[256,384]{1,0:T(8,128)(2,1)S(1)} %copy-done.2, bf16[8,4,16,384]{3,2,1,0:T(8,128)(2,1)S(1)} %all-to-all-done.x_ref, bf16[8,16,384]{2,1,0:T(8,128)(2,1)S(1)} %collective-permute-done.seam_ref, bf16[384,1536]{1,0:T(8,128)(2,1)S(1)} %copy-done.1, f32[3,3,768]{2,1,0:T(4,128)S(1)} %copy-done.8, ...), custom_call_target="tpu_custom_call" | custom-call | flops 704643072 | bytes 4194304 | tf_op jit(solution)/shard_map/pallas_call | solution.py:343
  46.9 1.5 %shard_map.120.after_ref = bf16[256,768]{1,0:T(8,128)(2,1)} custom-call(bf16[256,384]{1,0:T(8,128)(2,1)S(1)} %copy-done.2, bf16[1024,384]{1,0:T(8,128)(2,1)S(1)} %shard_map.119.scanned_ref), custom_call_target="tpu_custom_call" | custom-call | tf_op jit(solution)/shard_map/pallas_call | solution.py:311
  48.3 13.6 %all-to-all-start.1 = ((bf16[8,32,768]{2,1,0:T(8,128)(2,1)}), bf16[8,32,768]{2,1,0:T(8,128)(2,1)S(1)}, u32[]{:S(2)}, u32[]{:S(2)}) async-start(bf16[8,32,768]{2,1,0:T(8,128)(2,1)} %bitcast.3), calls=%async_computation.1 | async-start | bytes 786432 | tf_op jit(solution)/shard_map/all_to_all | solution.py:463
  61.9 4.3 %collective-permute-start.1 = (bf16[4,16,384]{2,1,0:T(8,128)(2,1)S(1)}, bf16[4,16,384]{2,1,0:T(8,128)(2,1)S(1)}, u32[]{:S(2)}, u32[]{:S(2)}) collective-permute-start(bf16[4,16,384]{2,1,0:T(8,128)(2,1)S(1)} %fusion.3), channel_id=1, source_target_pairs={{3,4},{7,8},{11,12},{15,16},{19,20},{23,24},{27,28},{4,3},{8,7},{1... | collective-permute-start | bytes 147464 | tf_op jit(solution)/shard_map/ppermute | solution.py:414
  66.2 8.5 %collective-permute-done.1.seam_ref = bf16[4,16,384]{2,1,0:T(8,128)(2,1)S(1)} collective-permute-done((bf16[4,16,384]{2,1,0:T(8,128)(2,1)S(1)}, bf16[4,16,384]{2,1,0:T(8,128)(2,1)S(1)}, u32[]{:S(2)}, u32[]{:S(2)}) %collective-permute-start.1) | collective-permute-done | bytes 49184 | tf_op jit(solution)/shard_map/ppermute | solution.py:414
  74.7 0.9 copy-done.7
  75.7 14.0 %shard_map.121.scanned_ref = bf16[512,768]{1,0:T(8,128)(2,1)S(1)} custom-call(bf16[256,768]{1,0:T(8,128)(2,1)} %shard_map.120.after_ref, bf16[4,6,16,384]{3,2,1,0:T(8,128)(2,1)S(1)} %all-to-all-done.2.x_ref, bf16[4,16,384]{2,1,0:T(8,128)(2,1)S(1)} %collective-permute-done.1.seam_ref, bf16[384,1536]{1,0:T(8,128)(2,1)S(1)} %copy-done.1, ...), custom_call_target="tpu_custom_call" | custom-call | flops 427819008 | bytes 4194304 | tf_op jit(solution)/shard_map/pallas_call | solution.py:343
  89.7 1.2 %shard_map.122 = bf16[256,768]{1,0:T(8,128)(2,1)} custom-call(bf16[8,32,768]{2,1,0:T(8,128)(2,1)S(1)} %all-to-all-done.1.after_ref, bf16[512,768]{1,0:T(8,128)(2,1)S(1)} %shard_map.121.scanned_ref), custom_call_target="tpu_custom_call" | custom-call | tf_op jit(solution)/shard_map/pallas_call | solution.py:311
  90.9 3.5 %all-to-all-start.3 = ((bf16[4,64,768]{2,1,0:T(8,128)(2,1)}), bf16[4,64,768]{2,1,0:T(8,128)(2,1)S(1)}, u32[]{:S(2)}, u32[]{:S(2)}) async-start(bf16[4,64,768]{2,1,0:T(8,128)(2,1)} %bitcast.5), calls=%async_computation.3 | async-start | bytes 786432 | tf_op jit(solution)/shard_map/all_to_all | solution.py:467
  94.3 0.6 reshape.42.gain_ref
  94.9 2.3 %shard_map.123.gate_ref = bf16[256,768]{1,0:T(8,128)(2,1)} custom-call(bf16[256,384]{1,0:T(8,128)(2,1)} %get-tuple-element.8.after_ref.norm_ref, bf16[384,1536]{1,0:T(8,128)(2,1)} %weight_ref.6), custom_call_target="tpu_custom_call" | custom-call | flops 150994944 | bytes 1048576 | tf_op jit(solution)/shard_map/pallas_call | solution.py:449
  97.2 4.5 %all-to-all-done.3 = bf16[4,64,768]{2,1,0:T(8,128)(2,1)S(1)} async-done(((bf16[4,64,768]{2,1,0:T(8,128)(2,1)}), bf16[4,64,768]{2,1,0:T(8,128)(2,1)S(1)}, u32[]{:S(2)}, u32[]{:S(2)}) %all-to-all-start.3) | async-done | bytes 393248 | tf_op jit(solution)/shard_map/all_to_all | solution.py:467
  101.7 0.8 copy-done.10
  102.5 3.0 %shard_map.124 = bf16[16,16,384]{2,1,0:T(8,128)(2,1)} custom-call(bf16[256,768]{1,0:T(8,128)(2,1)} %bitcast.35, bf16[256,768]{1,0:T(8,128)(2,1)} %bitcast.30, bf16[256,768]{1,0:T(8,128)(2,1)} %shard_map.123.gate_ref, f32[1,768]{1,0:T(1,128)} %reshape.42.gain_ref, bf16[768,384]{1,0:T(8,128)(2,1)} %weight_ref.7), custom_call_target="tpu_custom_call" | custom-call | tf_op jit(solution)/shard_map/pallas_call | solution.py:468
  (32 shorter events, 0.1 us)
Async XLA Ops:
  0.0 23.6 %copy-start.11 = (f32[4,768]{1,0:T(4,128)S(1)}, f32[4,768]{1,0:T(4,128)}, u32[]{:S(2)}) copy-start(f32[4,768]{1,0:T(4,128)} %param.19) | copy-start | bytes 36868
  0.0 23.6 %copy-start.12 = (f32[4,768]{1,0:T(4,128)S(1)}, f32[4,768]{1,0:T(4,128)}, u32[]{:S(2)}) copy-start(f32[4,768]{1,0:T(4,128)} %param.21) | copy-start | bytes 36868
  0.0 23.6 %copy-start.13 = (f32[768]{0:T(1024)S(1)}, f32[768]{0:T(1024)}, u32[]{:S(2)}) copy-start(f32[768]{0:T(1024)} %param.16) | copy-start | bytes 9220
  0.0 23.7 %copy-start.3 = (bf16[4,768,56]{1,2,0:T(8,128)(2,1)S(1)}, bf16[4,768,56]{1,2,0:T(8,128)(2,1)}, u32[]{:S(2)}) copy-start(bf16[4,768,56]{1,2,0:T(8,128)(2,1)} %param.17) | copy-start | bytes 1032196
  0.0 23.7 %copy-start.6 = (f32[4,768,16]{1,2,0:T(8,128)S(1)}, f32[4,768,16]{1,2,0:T(8,128)}, u32[]{:S(2)}) copy-start(f32[4,768,16]{1,2,0:T(8,128)} %param.20) | copy-start | bytes 589828
  0.0 23.7 %copy-start.1 = (bf16[384,1536]{1,0:T(8,128)(2,1)S(1)}, bf16[384,1536]{1,0:T(8,128)(2,1)}, u32[]{:S(2)}) copy-start(bf16[384,1536]{1,0:T(8,128)(2,1)} %weight_ref.6) | copy-start | bytes 3538948
  3.5 20.2 %copy-start.2 = (bf16[256,384]{1,0:T(8,128)(2,1)S(1)}, bf16[256,384]{1,0:T(8,128)(2,1)}, u32[]{:S(2)}) copy-start(bf16[256,384]{1,0:T(8,128)(2,1)} %get-tuple-element.8.after_ref.norm_ref) | copy-start | bytes 589828
  3.6 15.9 %all-to-all-start = ((bf16[8,4,16,384]{3,2,1,0:T(8,128)(2,1)}), bf16[8,4,16,384]{3,2,1,0:T(8,128)(2,1)S(1)}, u32[]{:S(2)}, u32[]{:S(2)}) async-start(bf16[8,4,16,384]{3,2,1,0:T(8,128)(2,1)} %get-tuple-element.9), calls=%async_computation | async-start | bytes 786432 | tf_op jit(solution)/shard_map/all_to_all | solution.py:406
  19.4 28.9 %all-to-all-start.2 = ((bf16[4,6,16,384]{3,2,1,0:T(8,128)(2,1)}), bf16[4,6,16,384]{3,2,1,0:T(8,128)(2,1)S(1)}, u32[]{:S(2)}, u32[]{:S(2)}) async-start(bf16[4,6,16,384]{3,2,1,0:T(8,128)(2,1)} %get-tuple-element.10), calls=%async_computation.2 | async-start | bytes 589824 | tf_op jit(solution)/shard_map/all_to_all | solution.py:406
  22.9 0.8 collective-permute-start
  23.7 1.0 copy-start.4
  24.7 0.8 copy-start.8
  46.9 27.9 %copy-start.5 = (f32[4,24,768]{2,1,0:T(8,128)S(1)}, f32[4,24,768]{2,1,0:T(8,128)}, u32[]{:S(2)}) copy-start(f32[4,24,768]{2,1,0:T(8,128)} %step_raw_ref.3) | copy-start | bytes 884740
  46.9 27.8 %copy-start.9 = (f32[3,3,768]{2,1,0:T(4,128)S(1)}, f32[3,3,768]{2,1,0:T(4,128)}, u32[]{:S(2)}) copy-start(f32[3,3,768]{2,1,0:T(4,128)} %conv_ref.3) | copy-start | bytes 82948
  48.3 41.3 %all-to-all-start.1 = ((bf16[8,32,768]{2,1,0:T(8,128)(2,1)}), bf16[8,32,768]{2,1,0:T(8,128)(2,1)S(1)}, u32[]{:S(2)}, u32[]{:S(2)}) async-start(bf16[8,32,768]{2,1,0:T(8,128)(2,1)} %bitcast.3), calls=%async_computation.1 | async-start | bytes 786432 | tf_op jit(solution)/shard_map/all_to_all | solution.py:463
  61.9 12.8 %collective-permute-start.1 = (bf16[4,16,384]{2,1,0:T(8,128)(2,1)S(1)}, bf16[4,16,384]{2,1,0:T(8,128)(2,1)S(1)}, u32[]{:S(2)}, u32[]{:S(2)}) collective-permute-start(bf16[4,16,384]{2,1,0:T(8,128)(2,1)S(1)} %fusion.3), channel_id=1, source_target_pairs={{3,4},{7,8},{11,12},{15,16},{19,20},{23,24},{27,28},{4,3},{8,7},{1... | collective-permute-start | bytes 147464 | tf_op jit(solution)/shard_map/ppermute | solution.py:414
  74.7 0.9 copy-start.7
  89.7 4.7 %copy-start.14 = (f32[768]{0:T(1024)S(1)}, f32[768]{0:T(1024)}, u32[]{:S(2)}) copy-start(f32[768]{0:T(1024)} %param.22) | copy-start | bytes 9220
  89.7 1.2 %copy-start = (bf16[8,32,768]{2,1,0:T(8,128)(2,1)}, bf16[8,32,768]{2,1,0:T(8,128)(2,1)S(1)}, u32[]{:S(2)}) copy-start(bf16[8,32,768]{2,1,0:T(8,128)(2,1)S(1)} %all-to-all-done.1.after_ref) | copy-start | bytes 1179652
  90.9 10.9 %all-to-all-start.3 = ((bf16[4,64,768]{2,1,0:T(8,128)(2,1)}), bf16[4,64,768]{2,1,0:T(8,128)(2,1)S(1)}, u32[]{:S(2)}, u32[]{:S(2)}) async-start(bf16[4,64,768]{2,1,0:T(8,128)(2,1)} %bitcast.5), calls=%async_computation.3 | async-start | bytes 786432 | tf_op jit(solution)/shard_map/all_to_all | solution.py:467
  101.7 0.8 copy-start.10

commit v3 on v2

--- a/solution.py
+++ b/solution.py
@@ -44,27 +44,34 @@
     return centred * lax.rsqrt(spread + 1e-05) * scale_gain
 
 
+def flip(axis):
+    other = "col" if axis == "row" else "row"
+    return (lax.axis_index(other) & 1) * (lax.axis_size(axis) - 1)
+
+
 def cut_kernel(feat_ref, gain_ref, norm_ref, rows_ref, cols_ref):
     height, width, channels = feat_ref.shape
-    tile = layer_norm(feat_ref[...].reshape(height * width, channels).astype(F32), gain_ref[...]).astype(BF16)
+    tile = layer_norm(feat_ref[...].reshape(height * width, channels).astype(F32), gain_ref[...][None]).astype(BF16)
     norm_ref[...] = tile
     row = rows_of(height * width)
     turned = dot(one_hot([((row & (height - 1)) << bits(width)) + (row >> bits(height))], height * width), tile).astype(
         BF16
     )
 
-    def cut(out_ref, body, lines, length):
+    def cut(axis, out_ref, body, lines, length):
         parts, reach = out_ref.shape[0], out_ref.shape[1]
+        turn = flip(axis)
         for part in range(parts):
+            to = part ^ turn
             for line in range(reach):
                 at = part * (reach - 2) + line - 1
                 if 0 <= at < lines:
-                    out_ref[part, line] = body[at * length : (at + 1) * length]
+                    out_ref[to, line] = body[at * length : (at + 1) * length]
                 else:
-                    out_ref[part, line] = jnp.zeros((length, channels), BF16)
-
-    cut(rows_ref, tile, height, width)
-    cut(cols_ref, turned, width, height)
+                    out_ref[to, line] = jnp.zeros((length, channels), BF16)
+
+    cut("col", rows_ref, tile, height, width)
+    cut("row", cols_ref, turned, width, height)
 
 
 def gate_kernel(norm_ref, weight_ref, gate_ref):
@@ -97,7 +104,6 @@
     s_ref,
     v_ref,
     y_ref,
-    spread_ref,
 ):
     parts, reach, length, channels = x_ref.shape
     time = parts * length
@@ -145,7 +151,8 @@
     for line in range(reach):
         x = x_ref[:, line].reshape(time, channels)
         if line == 0 or line == reach - 1:
-            missing = lax.axis_index(axis) == (0 if line == 0 else lax.axis_size(axis) - 1)
+            place = lax.axis_index(axis) ^ flip(axis)
+            missing = place == (0 if line == 0 else lax.axis_size(axis) - 1)
             x = jnp.where(missing, seam_ref[...].reshape(time, channels), x)
         token_ref[line * time : (line + 1) * time] = dot(order, x).astype(BF16)
     inner = dot(token_ref[...], weight_ref[...]).astype(BF16).astype(F32)
@@ -217,21 +224,21 @@
         s_ref[steps] = dot(stacked, step_ref[...]).reshape(piece // SLOTS, SLOTS, chunk)
 
     def soften(lap, _):
-        for sub in range(4):
-            t = lap * 4 + sub
+        for sub in range(8):
+            t = lap * 8 + sub
             for g in range(chunk // LANES):
                 cells = slice(g * LANES, (g + 1) * LANES)
                 before = s_ref[t, :, cells] + bias_ref[:, cells]
                 small = jnp.exp(-jnp.abs(before))
-                series = small * (1.0 + small * (-0.5 + small * (1.0 / 3.0 - 0.25 * small)))
-                step = jnp.maximum(before, 0.0) + jnp.where(small < 0.01, series, jnp.log(1.0 + small))
+                log1p = jnp.where(small < 0.001, small - 0.5 * small * small, jnp.log(1.0 + small))
+                step = jnp.maximum(before, 0.0) + log1p
                 u = v_ref[t, :, cells]
                 s_ref[t, :, cells] = step
                 v_ref[t, :, cells] = step * u
                 y_ref[t, :, cells] = skip_ref[:, cells] * u
         return 0
 
-    lax.fori_loop(0, time // 4, soften, 0)
+    lax.fori_loop(0, time // 8, soften, 0)
 
     groups = chunk // LANES
     at_once = max(1, 12 // groups)
@@ -248,28 +255,17 @@
                 )
                 rates[-1].append(-LOG2E * jnp.exp(rate))
 
-        def spread(lap):
-            found = []
-            for sub in range(unroll):
-                coefs = proj_out_ref[lap * unroll + sub]
-                for kind in range(2):
-                    for n in range(at_once):
-                        lane = 3 * RANK + kind * states + first + n
-                        found.append(jnp.broadcast_to(coefs[:, lane : lane + 1], (SLOTS, LANES)))
-            return found
-
-        def keep(slot, found):
-            for k, value in enumerate(found):
-                spread_ref[slot, k] = value
-
         def advance(lap, hidden):
             hidden = list(hidden)
-            slot = lap & 1
-            ahead = spread(jnp.minimum(lap + 1, laps - 1))
             for sub in range(unroll):
                 t = lap * unroll + sub
-                enter = [spread_ref[slot, sub * 2 * at_once + n] for n in range(at_once)]
-                leave = [spread_ref[slot, sub * 2 * at_once + at_once + n] for n in range(at_once)]
+                coefs = proj_out_ref[t]
+
+                def spread(lane):
+                    return jnp.broadcast_to(coefs[:, lane : lane + 1], (SLOTS, LANES))
+
+                enter = [spread(3 * RANK + first + n) for n in range(at_once)]
+                leave = [spread(3 * RANK + states + first + n) for n in range(at_once)]
                 for g in range(groups):
                     cells = pl.ds(g * LANES, LANES)
                     step = s_ref[t, :, cells]
@@ -281,10 +277,8 @@
                         hidden[k] = h
                         y = y + h * leave[n]
                     y_ref[t, :, cells] = y
-            keep(1 - slot, ahead)
             return tuple(hidden)
 
-        keep(0, spread(0))
         zero = jnp.zeros((SLOTS, LANES), F32)
         lax.fori_loop(0, laps, advance, (zero,) * (at_once * groups))
 
@@ -331,7 +325,6 @@
     assert lines <= SLOTS // (2 * halves)
     chunk = width // halves
     way = 0 if axis == "col" else 1
-    at_once = max(1, 12 // (chunk // LANES))
 
     def all_of(*shape):
         return pl.BlockSpec(shape, lambda i: (0,) * len(shape))
@@ -370,7 +363,6 @@
             pltpu.VMEM((time, SLOTS, chunk), F32),
             pltpu.VMEM((time, SLOTS, chunk), F32),
             pltpu.VMEM((time, SLOTS, chunk), F32),
-            pltpu.VMEM((2, 8 * 2 * at_once, SLOTS, LANES), F32),
         ],
         compiler_params=pltpu.CompilerParams(vmem_limit_bytes=50 * 1024 * 1024),
         cost_estimate=pl.CostEstimate(
@@ -394,23 +386,29 @@
 def end_kernel(rows_ref, cols_ref, gate_ref, gain_ref, weight_ref, out_ref):
     height, width, channels = out_ref.shape
     row = rows_of(height * width)
-    source = ((row & (width - 1)) << bits(height)) + (row >> bits(width))
-    combined = rows_ref[...].astype(F32) + dot(one_hot([source], height * width), cols_ref[...])
+    turn = flip("row") * (width // lax.axis_size("row"))
+    source = (((row & (width - 1)) ^ turn) << bits(height)) + (row >> bits(width))
+    turn = flip("col")
+    rows = jnp.concatenate([rows_ref[part ^ turn] for part in range(rows_ref.shape[0])], axis=0)
+    combined = rows.astype(F32) + dot(one_hot([source], height * width), cols_ref[...])
     gate = gate_ref[...].astype(F32)
-    gated = layer_norm(combined, gain_ref[...]) * (gate / (1.0 + jnp.exp(-gate)))
+    gated = layer_norm(combined, gain_ref[...][None]) * (gate / (1.0 + jnp.exp(-gate)))
     out = dot(gated.astype(BF16), weight_ref[...]).astype(BF16)
     out_ref[...] = out.reshape(height, width, channels)
 
 
 def send_lines(send, axis):
     x = lax.all_to_all(send, axis, 0, 0, tiled=True)
-    count, place = lax.axis_size(axis), lax.axis_index(axis)
+    count = lax.axis_size(axis)
     height, breadth = lax.axis_size("row"), lax.axis_size("col")
     if axis == "row":
-        ends = [((count - 1) * breadth + c, c + 1) for c in range(breadth - 1)]
+        at = lambda group: (0 if group & 1 else count - 1) * breadth
+        ends = [(at(c) + c, at(c) + c + 1) for c in range(breadth - 1)]
     else:
-        ends = [(r * breadth + count - 1, (r + 1) * breadth) for r in range(height - 1)]
+        at = lambda group: 0 if group & 1 else count - 1
+        ends = [(at(r) + r * breadth, at(r) + (r + 1) * breadth) for r in range(height - 1)]
     pairs = ends + [(b, a) for a, b in ends]
+    place = lax.axis_index(axis) ^ flip(axis)
     seam = lax.ppermute(jnp.where(place == 0, x[:, 1], x[:, -2]), ("row", "col"), pairs)
     return x, seam
 
@@ -442,7 +440,7 @@
             jax.ShapeDtypeStruct((lax.axis_size("col"), row_lines + 2, width, channels), BF16),
             jax.ShapeDtypeStruct((lax.axis_size("row"), col_lines + 2, height, channels), BF16),
         ),
-    )(features, norm_gain.reshape(1, channels))
+    )(features, norm_gain)
     weights = (in_weight, conv_weight, conv_bias, proj_weight, step_weight, step_bias, decay_log, skip_gain)
     col_sent = send_lines(col_send, "row")
     row_sent = send_lines(row_send, "col")
@@ -459,7 +457,7 @@
     )(normed, in_weight)
     parts = lax.axis_size("row")
     col_y = lines_of("row", normed, *col_sent, *weights)
-    joined = join(col_y, parts, col_lines, height, inner, normed)
+    joined = join(col_y, parts, col_lines, height, inner, row_sent[1])
     col_y = lax.all_to_all(joined.reshape(parts, -1, inner), "row", 0, 0, tiled=True)
     parts = lax.axis_size("col")
     row_y = lines_of("col", joined, *row_sent, *weights)
@@ -468,7 +466,7 @@
     return pl.pallas_call(
         end_kernel,
         out_shape=jax.ShapeDtypeStruct(features.shape, BF16),
-    )(row_y.reshape(tokens, inner), col_y.reshape(tokens, inner), gate, out_gain.reshape(1, inner), out_weight)
+    )(row_y, col_y.reshape(tokens, inner), gate, out_gain, out_weight)
 
 
 def solution(mesh):

time: 106 us -> 87.1 us (0.82)
  the two profiles are of different devices: /device:TPU:16 before, /device:TPU:0 now
where the time goes in v3:
time: 87.1 us; the launch traced here: 86.4 us
  Pallas kernels  40 us (46%)
  starting transfers between devices  21.1 us (24%)
  waiting for transfers between devices  20.3 us (23%)
  local copies, waits for them, and re-layouts  4.82 us (6%)
    pallas_call x2, Pallas kernels, lines_of(): pl.pallas_call(functools.partial(line_kernel, lines, axis), out_shape=jax...  29.8 us
    all_to_all x2, waiting for transfers between devices, send_lines(): x = lax.all_to_all(send, axis, 0, 0, tiled=True)  15.2 us
    all_to_all x2, starting transfers between devices, send_lines(): x = lax.all_to_all(send, axis, 0, 0, tiled=True)  10.9 us
    all_to_all x1, starting transfers between devices, local(): lax.all_to_all(joined.reshape(parts, -1, inner), 'row', 0, 0, tiled=True)  5.43 us
    all_to_all x1, waiting for transfers between devices, local(): lax.all_to_all(row_y.reshape(parts, -1, inner), 'col', 0, 0, tiled=True)  5.12 us
    all_to_all x1, starting transfers between devices, local(): lax.all_to_all(row_y.reshape(parts, -1, inner), 'col', 0, 0, tiled=True)  3.46 us
    pallas_call x1, Pallas kernels, local(): pl.pallas_call(end_kernel, out_shape=jax.ShapeDtypeStruct(features.shape,...  2.99 us
    unnamed x20, local copies, waits for them, and re-layouts  2.68 us
  transfers between devices with their start and end apart: 6, of which 3 were waited for; matrix products, arithmetic and copies ran while one was open for 3% of the time, Pallas kernels for 37%

profile of v3, /device:TPU:0, one launch (start us, length us, event | category | flops | bytes accessed | tf_op | source)
XLA Modules:
  0.0 86.4 jit_solution(318759683184910363)
XLA Ops:
  0.0 2.3 %shard_map.118 = (bf16[256,384]{1,0:T(8,128)(2,1)}, bf16[4,6,16,384]{3,2,1,0:T(8,128)(2,1)}, bf16[8,4,16,384]{3,2,1,0:T(8,128)(2,1)}) custom-call(bf16[16,16,384]{2,1,0:T(8,128)(2,1)} %feat_ref.1, f32[384]{0:T(512)} %gain_ref.2), custom_call_target="tpu_custom_call" | custom-call | tf_op jit(solution)/shard_map/pallas_call | solution.py:436
  2.3 7.4 %all-to-all-start.1 = ((bf16[8,4,16,384]{3,2,1,0:T(8,128)(2,1)}), bf16[8,4,16,384]{3,2,1,0:T(8,128)(2,1)S(1)}, u32[]{:S(2)}, u32[]{:S(2)}) async-start(bf16[8,4,16,384]{3,2,1,0:T(8,128)(2,1)} %get-tuple-element.10), calls=%async_computation.1 | async-start | bytes 786432 | tf_op jit(solution)/shard_map/all_to_all | solution.py:401
  9.7 0.7 reshape.26.bias_raw_ref
  10.4 0.7 reshape.27.skip_raw_ref
  11.1 0.7 reshape.25.conv_bias_ref
  11.8 9.5 %all-to-all-done.1.x_ref = bf16[8,4,16,384]{3,2,1,0:T(8,128)(2,1)S(1)} async-done(((bf16[8,4,16,384]{3,2,1,0:T(8,128)(2,1)}), bf16[8,4,16,384]{3,2,1,0:T(8,128)(2,1)S(1)}, u32[]{:S(2)}, u32[]{:S(2)}) %all-to-all-start.1) | async-done | bytes 393248 | tf_op jit(solution)/shard_map/all_to_all | solution.py:401
  21.4 3.5 %all-to-all-start = ((bf16[4,6,16,384]{3,2,1,0:T(8,128)(2,1)}), bf16[4,6,16,384]{3,2,1,0:T(8,128)(2,1)S(1)}, u32[]{:S(2)}, u32[]{:S(2)}) async-start(bf16[4,6,16,384]{3,2,1,0:T(8,128)(2,1)} %get-tuple-element.8), calls=%async_computation | async-start | bytes 589824 | tf_op jit(solution)/shard_map/all_to_all | solution.py:401
  24.9 0.7 collective-permute-start.1
  25.5 5.7 %all-to-all-done.x_ref = bf16[4,6,16,384]{3,2,1,0:T(8,128)(2,1)S(1)} async-done(((bf16[4,6,16,384]{3,2,1,0:T(8,128)(2,1)}), bf16[4,6,16,384]{3,2,1,0:T(8,128)(2,1)S(1)}, u32[]{:S(2)}, u32[]{:S(2)}) %all-to-all-start) | async-done | bytes 294944 | tf_op jit(solution)/shard_map/all_to_all | solution.py:401
  31.2 0.7 collective-permute-start
  32.0 0.9 %copy-done.6 = f32[4,768,16]{1,2,0:T(8,128)S(1)} copy-done((f32[4,768,16]{1,2,0:T(8,128)S(1)}, f32[4,768,16]{1,2,0:T(8,128)}, u32[]{:S(2)}) %copy-start.6) | copy-done | bytes 196632
  32.9 17.1 %shard_map.119.scanned_ref = bf16[1024,384]{1,0:T(8,128)(2,1)S(1)} custom-call(bf16[256,384]{1,0:T(8,128)(2,1)S(1)} %copy-done.2, bf16[8,4,16,384]{3,2,1,0:T(8,128)(2,1)S(1)} %all-to-all-done.1.x_ref, bf16[8,16,384]{2,1,0:T(8,128)(2,1)S(1)} %collective-permute-done.1.seam_ref, bf16[384,1536]{1,0:T(8,128)(2,1)S(1)} %copy-done.1, f32[3,3,768]{2,1,0:T(4,128)S(1)} %copy-done.8, ...), custom_call_target="tpu_custom_call" | custom-call | flops 704643072 | bytes 4194304 | tf_op jit(solution)/shard_map/pallas_call | solution.py:336
  50.0 0.0 copy-start.7
  50.0 1.5 %shard_map.120.after_ref = bf16[256,768]{1,0:T(8,128)(2,1)} custom-call(bf16[4,16,384]{2,1,0:T(8,128)(2,1)S(1)} %collective-permute-done.after_ref.seam_ref, bf16[1024,384]{1,0:T(8,128)(2,1)S(1)} %shard_map.119.scanned_ref), custom_call_target="tpu_custom_call" | custom-call | tf_op jit(solution)/shard_map/pallas_call | solution.py:305
  51.5 5.4 %all-to-all-start.2 = ((bf16[8,32,768]{2,1,0:T(8,128)(2,1)}), bf16[8,32,768]{2,1,0:T(8,128)(2,1)S(1)}, u32[]{:S(2)}, u32[]{:S(2)}) async-start(bf16[8,32,768]{2,1,0:T(8,128)(2,1)} %bitcast.4), calls=%async_computation.2 | async-start | bytes 786432 | tf_op jit(solution)/shard_map/all_to_all | solution.py:461
  56.9 0.0 copy-start.5
  56.9 1.0 %copy-done.5 = f32[4,24,768]{2,1,0:T(8,128)S(1)} copy-done((f32[4,24,768]{2,1,0:T(8,128)S(1)}, f32[4,24,768]{2,1,0:T(8,128)}, u32[]{:S(2)}) %copy-start.5) | copy-done | bytes 294936
  57.9 12.7 %shard_map.121.scanned_ref = bf16[512,768]{1,0:T(8,128)(2,1)S(1)} custom-call(bf16[256,768]{1,0:T(8,128)(2,1)} %shard_map.120.after_ref, bf16[4,6,16,384]{3,2,1,0:T(8,128)(2,1)S(1)} %all-to-all-done.x_ref, bf16[4,16,384]{2,1,0:T(8,128)(2,1)S(1)} %collective-permute-done.after_ref.seam_ref, bf16[384,1536]{1,0:T(8,128)(2,1)S(1)} %copy-done.1, ...), custom_call_target="tpu_custom_call" | custom-call | flops 427819008 | bytes 4194304 | tf_op jit(solution)/shard_map/pallas_call | solution.py:336
  70.6 1.2 %shard_map.122 = bf16[256,768]{1,0:T(8,128)(2,1)} custom-call(bf16[8,32,768]{2,1,0:T(8,128)(2,1)S(1)} %all-to-all-done.2.after_ref, bf16[512,768]{1,0:T(8,128)(2,1)S(1)} %shard_map.121.scanned_ref), custom_call_target="tpu_custom_call" | custom-call | tf_op jit(solution)/shard_map/pallas_call | solution.py:305
  71.8 3.5 %all-to-all-start.3 = ((bf16[4,64,768]{2,1,0:T(8,128)(2,1)}), bf16[4,64,768]{2,1,0:T(8,128)(2,1)S(1)}, u32[]{:S(2)}, u32[]{:S(2)}) async-start(bf16[4,64,768]{2,1,0:T(8,128)(2,1)} %bitcast.5), calls=%async_computation.3 | async-start | bytes 786432 | tf_op jit(solution)/shard_map/all_to_all | solution.py:465
  75.2 2.3 %shard_map.123.gate_ref = bf16[256,768]{1,0:T(8,128)(2,1)} custom-call(bf16[256,384]{1,0:T(8,128)(2,1)} %get-tuple-element.9.after_ref.norm_ref, bf16[384,1536]{1,0:T(8,128)(2,1)} %weight_ref.6), custom_call_target="tpu_custom_call" | custom-call | flops 150994944 | bytes 1048576 | tf_op jit(solution)/shard_map/pallas_call | solution.py:447
  77.5 5.1 %all-to-all-done.3.rows_ref = bf16[4,64,768]{2,1,0:T(8,128)(2,1)S(1)} async-done(((bf16[4,64,768]{2,1,0:T(8,128)(2,1)}), bf16[4,64,768]{2,1,0:T(8,128)(2,1)S(1)}, u32[]{:S(2)}, u32[]{:S(2)}) %all-to-all-start.3) | async-done | bytes 393248 | tf_op jit(solution)/shard_map/all_to_all | solution.py:465
  82.6 0.8 copy-done.9
  83.4 3.0 %shard_map.124 = bf16[16,16,384]{2,1,0:T(8,128)(2,1)} custom-call(bf16[4,64,768]{2,1,0:T(8,128)(2,1)} %copy-done.9, bf16[256,768]{1,0:T(8,128)(2,1)} %bitcast.29, bf16[256,768]{1,0:T(8,128)(2,1)} %shard_map.123.gate_ref, f32[768]{0:T(1024)} %gain_ref.3, bf16[768,384]{1,0:T(8,128)(2,1)} %weight_ref.7), custom_call_target="tpu_custom_call" | custom-call | tf_op jit(solution)/shard_map/pallas_call | solution.py:466
  (20 shorter events, 0.1 us)
Async XLA Ops:
  0.0 31.9 %copy-start.3 = (bf16[4,768,56]{1,2,0:T(8,128)(2,1)S(1)}, bf16[4,768,56]{1,2,0:T(8,128)(2,1)}, u32[]{:S(2)}) copy-start(bf16[4,768,56]{1,2,0:T(8,128)(2,1)} %param.17) | copy-start | bytes 1032196
  0.0 31.9 %copy-start.1 = (bf16[384,1536]{1,0:T(8,128)(2,1)S(1)}, bf16[384,1536]{1,0:T(8,128)(2,1)}, u32[]{:S(2)}) copy-start(bf16[384,1536]{1,0:T(8,128)(2,1)} %weight_ref.6) | copy-start | bytes 3538948
  0.0 31.9 %copy-start.8 = (f32[3,3,768]{2,1,0:T(4,128)S(1)}, f32[3,3,768]{2,1,0:T(4,128)}, u32[]{:S(2)}) copy-start(f32[3,3,768]{2,1,0:T(4,128)} %conv_ref.3) | copy-start | bytes 82948
  0.0 31.9 %copy-start.4 = (f32[4,24,768]{2,1,0:T(8,128)S(1)}, f32[4,24,768]{2,1,0:T(8,128)}, u32[]{:S(2)}) copy-start(f32[4,24,768]{2,1,0:T(8,128)} %step_raw_ref.3) | copy-start | bytes 884740
  2.3 29.7 %copy-start.2 = (bf16[256,384]{1,0:T(8,128)(2,1)S(1)}, bf16[256,384]{1,0:T(8,128)(2,1)}, u32[]{:S(2)}) copy-start(bf16[256,384]{1,0:T(8,128)(2,1)} %get-tuple-element.9.after_ref.norm_ref) | copy-start | bytes 589828
  2.3 19.1 %all-to-all-start.1 = ((bf16[8,4,16,384]{3,2,1,0:T(8,128)(2,1)}), bf16[8,4,16,384]{3,2,1,0:T(8,128)(2,1)S(1)}, u32[]{:S(2)}, u32[]{:S(2)}) async-start(bf16[8,4,16,384]{3,2,1,0:T(8,128)(2,1)} %get-tuple-element.10), calls=%async_computation.1 | async-start | bytes 786432 | tf_op jit(solution)/shard_map/all_to_all | solution.py:401
  21.4 9.8 %all-to-all-start = ((bf16[4,6,16,384]{3,2,1,0:T(8,128)(2,1)}), bf16[4,6,16,384]{3,2,1,0:T(8,128)(2,1)S(1)}, u32[]{:S(2)}, u32[]{:S(2)}) async-start(bf16[4,6,16,384]{3,2,1,0:T(8,128)(2,1)} %get-tuple-element.8), calls=%async_computation | async-start | bytes 589824 | tf_op jit(solution)/shard_map/all_to_all | solution.py:401
  24.9 7.0 %collective-permute-start.1 = (bf16[8,16,384]{2,1,0:T(8,128)(2,1)S(1)}, bf16[8,16,384]{2,1,0:T(8,128)(2,1)S(1)}, u32[]{:S(2)}, u32[]{:S(2)}) collective-permute-start(bf16[8,16,384]{2,1,0:T(8,128)(2,1)S(1)} %fusion.1), channel_id=1, source_target_pairs={{28,29},{1,2},{30,31},{29,28},{2,1},{31,30}} | collective-permute-start | bytes 294920 | tf_op jit(solution)/shard_map/ppermute | solution.py:412
  31.2 18.8 %collective-permute-start = (bf16[4,16,384]{2,1,0:T(8,128)(2,1)S(1)}, bf16[4,16,384]{2,1,0:T(8,128)(2,1)S(1)}, u32[]{:S(2)}, u32[]{:S(2)}) collective-permute-start(bf16[4,16,384]{2,1,0:T(8,128)(2,1)S(1)} %fusion.3), channel_id=1, source_target_pairs={{3,7},{4,8},{11,15},{12,16},{19,23},{20,24},{27,31},{7,3},{8,4},{1... | collective-permute-start | bytes 147464 | tf_op jit(solution)/shard_map/ppermute | solution.py:412
  31.9 0.9 %copy-start.6 = (f32[4,768,16]{1,2,0:T(8,128)S(1)}, f32[4,768,16]{1,2,0:T(8,128)}, u32[]{:S(2)}) copy-start(f32[4,768,16]{1,2,0:T(8,128)} %param.20) | copy-start | bytes 589828
  50.0 6.9 %copy-start.7 = (f32[4,768,16]{1,2,0:T(8,128)S(1)}, f32[4,768,16]{1,2,0:T(8,128)}, u32[]{:S(2)}) copy-start(f32[4,768,16]{1,2,0:T(8,128)} %param.20) | copy-start | bytes 589828
  51.5 19.1 %all-to-all-start.2 = ((bf16[8,32,768]{2,1,0:T(8,128)(2,1)}), bf16[8,32,768]{2,1,0:T(8,128)(2,1)S(1)}, u32[]{:S(2)}, u32[]{:S(2)}) async-start(bf16[8,32,768]{2,1,0:T(8,128)(2,1)} %bitcast.4), calls=%async_computation.2 | async-start | bytes 786432 | tf_op jit(solution)/shard_map/all_to_all | solution.py:461
  56.9 1.0 %copy-start.5 = (f32[4,24,768]{2,1,0:T(8,128)S(1)}, f32[4,24,768]{2,1,0:T(8,128)}, u32[]{:S(2)}) copy-start(f32[4,24,768]{2,1,0:T(8,128)} %step_raw_ref.3) | copy-start | bytes 884740
  70.6 1.2 %copy-start = (bf16[8,32,768]{2,1,0:T(8,128)(2,1)}, bf16[8,32,768]{2,1,0:T(8,128)(2,1)S(1)}, u32[]{:S(2)}) copy-start(bf16[8,32,768]{2,1,0:T(8,128)(2,1)S(1)} %all-to-all-done.2.after_ref) | copy-start | bytes 1179652
  71.8 10.9 %all-to-all-start.3 = ((bf16[4,64,768]{2,1,0:T(8,128)(2,1)}), bf16[4,64,768]{2,1,0:T(8,128)(2,1)S(1)}, u32[]{:S(2)}, u32[]{:S(2)}) async-start(bf16[4,64,768]{2,1,0:T(8,128)(2,1)} %bitcast.5), calls=%async_computation.3 | async-start | bytes 786432 | tf_op jit(solution)/shard_map/all_to_all | solution.py:465
  82.6 0.8 copy-start.9

commit v4 on v3

--- a/solution.py
+++ b/solution.py
@@ -49,40 +49,51 @@
     return (lax.axis_index(other) & 1) * (lax.axis_size(axis) - 1)
 
 
-def cut_kernel(feat_ref, gain_ref, norm_ref, rows_ref, cols_ref):
+def cut_kernel(feat_ref, gain_ref, norm_ref, cols_ref, *row_refs):
     height, width, channels = feat_ref.shape
     tile = layer_norm(feat_ref[...].reshape(height * width, channels).astype(F32), gain_ref[...][None]).astype(BF16)
     norm_ref[...] = tile
+    reach = row_refs[0].shape[0]
+    turn = flip("col") ^ lax.axis_index("col")
+    for part, row_ref in enumerate(row_refs):
+        for line in range(reach):
+            at = jnp.clip((part ^ turn) * (reach - 2) + line - 1, 0, height - 1)
+            row_ref[line] = norm_ref[pl.ds(pl.multiple_of(at * width, width), width)]
     row = rows_of(height * width)
     turned = dot(one_hot([((row & (height - 1)) << bits(width)) + (row >> bits(height))], height * width), tile).astype(
         BF16
     )
-
-    def cut(axis, out_ref, body, lines, length):
-        parts, reach = out_ref.shape[0], out_ref.shape[1]
-        turn = flip(axis)
-        for part in range(parts):
-            to = part ^ turn
-            for line in range(reach):
-                at = part * (reach - 2) + line - 1
-                if 0 <= at < lines:
-                    out_ref[to, line] = body[at * length : (at + 1) * length]
-                else:
-                    out_ref[to, line] = jnp.zeros((length, channels), BF16)
-
-    cut("col", rows_ref, tile, height, width)
-    cut("row", cols_ref, turned, width, height)
+    reach = cols_ref.shape[1]
+    turn = flip("row")
+    for part in range(cols_ref.shape[0]):
+        for line in range(reach):
+            at = min(max(part * (reach - 2) + line - 1, 0), width - 1)
+            cols_ref[part ^ turn, line] = turned[at * height : (at + 1) * height]
 
 
 def gate_kernel(norm_ref, weight_ref, gate_ref):
     gate_ref[...] = dot(norm_ref[...], weight_ref[...]).astype(BF16)
 
 
-def line_kernel(
+def by_slot(halves, rows):
+    found = None
+    for kind in range(halves * 2):
+        row = rows(kind >> 1, kind & 1)
+        row = jnp.broadcast_to(row, (SLOTS, row.shape[1]))
+        slot = lax.broadcasted_iota(jnp.int32, row.shape, 0)
+        found = row if found is None else jnp.where(slot >= kind * (SLOTS // (halves * 2)), row, found)
+    return found
+
+
+def prepare_kernel(
     lines,
     axis,
+    swapped,
     after_ref,
-    x_ref,
+    *refs,
+):
+    x_refs, refs = refs[:-16], refs[-16:]
+    (
     seam_ref,
     weight_ref,
     conv_ref,
@@ -90,48 +101,31 @@
     proj_raw_ref,
     step_raw_ref,
     bias_raw_ref,
-    decay_ref,
-    skip_raw_ref,
-    out_ref,
+    proj_out_ref,
+    s_ref,
+    v_ref,
     token_ref,
     inner_ref,
     active_ref,
     proj_ref,
     step_ref,
     bias_ref,
-    skip_ref,
-    proj_out_ref,
-    s_ref,
-    v_ref,
-    y_ref,
-):
-    parts, reach, length, channels = x_ref.shape
+    ) = refs
+    parts, length, channels = seam_ref.shape
+    reach = lines + 2
+    states = (proj_raw_ref.shape[1] - RANK) // 2
     time = parts * length
     low = time // SLOTS
     width = weight_ref.shape[1]
     chunk = s_ref.shape[2]
     halves = width // chunk
     slot_lines = SLOTS // (2 * halves)
-    states = decay_ref.shape[1]
     if axis == "row":
         across_first = lambda across, along: (along, across)
     else:
         across_first = lambda across, along: (across, along)
 
-    place = lax.broadcasted_iota(jnp.int32, (SLOTS, chunk), 0)
-
-    def by_slot(rows):
-        found = None
-        for half in range(halves):
-            for way in range(2):
-                row = rows(half, way)
-                row = jnp.broadcast_to(row, (SLOTS, row.shape[1]))
-                kind = half * 2 + way
-                found = row if found is None else jnp.where(place[:, : row.shape[1]] >= kind * slot_lines, row, found)
-        return found
-
-    bias_ref[...] = by_slot(lambda half, way: bias_raw_ref[way : way + 1, half * chunk : (half + 1) * chunk])
-    skip_ref[...] = by_slot(lambda half, way: skip_raw_ref[way : way + 1, half * chunk : (half + 1) * chunk])
+    bias_ref[...] = by_slot(halves, lambda half, way: bias_raw_ref[way : way + 1, half * chunk : (half + 1) * chunk])
     for half in range(halves):
         cells = slice(half * chunk, (half + 1) * chunk)
         for way in range(2):
@@ -147,9 +141,15 @@
             step_ref[kind, :] = jnp.concatenate([high, high, w - high, rest], axis=0).astype(BF16)
 
     row = rows_of(time)
-    order = one_hot([((row & 7) << bits(low)) + (row >> 3)], time)
+    source = ((row & 7) << bits(low)) + (row >> 3)
+    if swapped:
+        source = source ^ (lax.axis_index(axis) << bits(length))
+    order = one_hot([source], time)
     for line in range(reach):
-        x = x_ref[:, line].reshape(time, channels)
+        if swapped:
+            x = jnp.concatenate([x_ref[line] for x_ref in x_refs], axis=0)
+        else:
+            x = x_refs[0][:, line].reshape(time, channels)
         if line == 0 or line == reach - 1:
             place = lax.axis_index(axis) ^ flip(axis)
             missing = place == (0 if line == 0 else lax.axis_size(axis) - 1)
@@ -232,34 +232,46 @@
                 small = jnp.exp(-jnp.abs(before))
                 log1p = jnp.where(small < 0.001, small - 0.5 * small * small, jnp.log(1.0 + small))
                 step = jnp.maximum(before, 0.0) + log1p
-                u = v_ref[t, :, cells]
                 s_ref[t, :, cells] = step
-                v_ref[t, :, cells] = step * u
-                y_ref[t, :, cells] = skip_ref[:, cells] * u
         return 0
 
     lax.fori_loop(0, time // 8, soften, 0)
 
+
+def scan_kernel(after_ref, coef_ref, s_ref, u_ref, decay_ref, skip_raw_ref, out_ref, v_ref, y_ref):
+    time, _, chunk = s_ref.shape
+    halves = decay_ref.shape[2] // chunk
+    states = decay_ref.shape[1]
     groups = chunk // LANES
     at_once = max(1, 12 // groups)
     unroll = 8
     laps = time // unroll
-    place = lax.broadcasted_iota(jnp.int32, (SLOTS, LANES), 0)
     for first in range(0, states, at_once):
         rates = []
         for n in range(first, first + at_once):
             rates.append([])
             for g in range(groups):
                 rate = by_slot(
-                    lambda half, way: decay_ref[way, n : n + 1, half * chunk + g * LANES : half * chunk + (g + 1) * LANES]
+                    halves,
+                    lambda half, way: decay_ref[way, n : n + 1, half * chunk + g * LANES : half * chunk + (g + 1) * LANES],
                 )
                 rates[-1].append(-LOG2E * jnp.exp(rate))
+        if first == 0:
+            skips = [
+                by_slot(
+                    halves,
+                    lambda half, way: skip_raw_ref[
+                        way : way + 1, half * chunk + g * LANES : half * chunk + (g + 1) * LANES
+                    ],
+                )
+                for g in range(groups)
+            ]
 
         def advance(lap, hidden):
             hidden = list(hidden)
             for sub in range(unroll):
                 t = lap * unroll + sub
-                coefs = proj_out_ref[t]
+                coefs = coef_ref[t]
 
                 def spread(lane):
                     return jnp.broadcast_to(coefs[:, lane : lane + 1], (SLOTS, LANES))
@@ -269,8 +281,14 @@
                 for g in range(groups):
                     cells = pl.ds(g * LANES, LANES)
                     step = s_ref[t, :, cells]
-                    value = v_ref[t, :, cells]
-                    y = y_ref[t, :, cells]
+                    if first == 0:
+                        u = u_ref[t, :, cells]
+                        value = step * u
+                        v_ref[t, :, cells] = value
+                        y = skips[g] * u
+                    else:
+                        value = v_ref[t, :, cells]
+                        y = y_ref[t, :, cells]
                     for n in range(at_once):
                         k = n * groups + g
                         h = jnp.exp2(step * rates[n][g]) * hidden[k] + value * enter[n]
@@ -285,37 +303,46 @@
     out_ref[...] = y_ref[...].reshape(time * SLOTS, chunk).astype(BF16)
 
 
-def join_kernel(parts, lines, after_ref, scanned_ref, out_ref):
-    length = out_ref.shape[0] // (parts * lines)
+def join_kernel(parts, lines, axis, after_ref, scanned_ref, *out_refs):
+    length = sum(out_ref.shape[0] for out_ref in out_refs) // (parts * lines)
     time = parts * length
     chunk = scanned_ref.shape[1]
-    halves = out_ref.shape[1] // chunk
+    halves = out_refs[0].shape[1] // chunk
     slot_lines = SLOTS // (2 * halves)
     row = rows_of(lines * time)
     line = (row >> bits(length)) & (lines - 1)
-    now = ((row >> bits(lines * length)) << bits(length)) + (row & (length - 1))
+    part = row >> bits(lines * length)
+    if len(out_refs) > 1:
+        part = part ^ lax.axis_index(axis)
+    now = (part << bits(length)) + (row & (length - 1))
     for half in range(halves):
         ahead = now * SLOTS + (half * 2 * slot_lines) + line
         behind = (time - 1 - now) * SLOTS + (half * 2 * slot_lines + slot_lines) + line
-        joined = dot(one_hot([ahead, behind], time * SLOTS), scanned_ref[...])
-        out_ref[:, half * chunk : (half + 1) * chunk] = joined.astype(BF16)
-
-
-def join(scanned, parts, lines, length, width, after):
+        joined = dot(one_hot([ahead, behind], time * SLOTS), scanned_ref[...]).astype(BF16)
+        at = 0
+        for out_ref in out_refs:
+            out_ref[:, half * chunk : (half + 1) * chunk] = joined[at : at + out_ref.shape[0]]
+            at += out_ref.shape[0]
+
+
+def join(axis, scanned, parts, lines, length, width, after, apart):
+    count = parts if apart else 1
     return pl.pallas_call(
-        functools.partial(join_kernel, parts, lines),
-        out_shape=jax.ShapeDtypeStruct((parts * lines * length, width), BF16),
+        functools.partial(join_kernel, parts, lines, axis),
+        out_shape=[jax.ShapeDtypeStruct((parts * lines * length // count, width), BF16)] * count,
         in_specs=[pl.BlockSpec(memory_space=pl.ANY), pl.BlockSpec(memory_space=pltpu.VMEM)],
-        out_specs=pl.BlockSpec(memory_space=pltpu.VMEM),
-        compiler_params=pltpu.CompilerParams(vmem_limit_bytes=50 * 1024 * 1024),
+        out_specs=[pl.BlockSpec(memory_space=pltpu.VMEM)] * count,
+        compiler_params=pltpu.CompilerParams(vmem_limit_bytes=24 * 1024 * 1024),
     )(after, scanned)
 
 
 RANK = 24
 
 
-def lines_of(axis, after, x, seam, in_weight, conv, conv_bias, proj, step_weight, step_bias, decay_log, skip):
-    parts, reach, length, channels = x.shape
+def prepare(axis, after, xs, seam, in_weight, conv, conv_bias, proj, step_weight, step_bias, decay_log, skip):
+    swapped = len(xs) > 1
+    parts, length, channels = seam.shape
+    reach = xs[0].shape[-3]
     lines = reach - 2
     time = parts * length
     width = conv.shape[2]
@@ -332,14 +359,19 @@
     def pair(*shape):
         return pl.BlockSpec((2,) + shape, lambda i: (way,) + (0,) * len(shape))
 
+    vmem = pl.BlockSpec(memory_space=pltpu.VMEM)
     flops = 2 * time * (reach * channels * width + SLOTS * width * 256)
     return pl.pallas_call(
-        functools.partial(line_kernel, lines, axis),
-        out_shape=jax.ShapeDtypeStruct((time * SLOTS, chunk), BF16),
+        functools.partial(prepare_kernel, lines, axis, swapped),
+        out_shape=[
+            jax.ShapeDtypeStruct((time, SLOTS, LANES), F32),
+            jax.ShapeDtypeStruct((time, SLOTS, chunk), F32),
+            jax.ShapeDtypeStruct((time, SLOTS, chunk), F32),
+        ],
         grid=(1,),
-        in_specs=[
-            pl.BlockSpec(memory_space=pl.ANY),
-            all_of(parts, reach, length, channels),
+        in_specs=[pl.BlockSpec(memory_space=pl.ANY)]
+        + [all_of(*x.shape) for x in xs]
+        + [
             all_of(parts, length, channels),
             all_of(channels, width),
             all_of(3, 3, width),
@@ -347,10 +379,8 @@
             pair(RANK + 2 * states, width),
             pair(RANK, width),
             pl.BlockSpec((None, 2, width), lambda i: (way, 0, 0)),
-            pair(states, width),
-            pl.BlockSpec((None, 2, width), lambda i: (way, 0, 0)),
         ],
-        out_specs=all_of(time * SLOTS, chunk),
+        out_specs=[vmem, vmem, vmem],
         scratch_shapes=[
             pltpu.VMEM((reach * time, channels), BF16),
             pltpu.VMEM((reach, time // SLOTS + 2, SLOTS, width), F32),
@@ -358,19 +388,12 @@
             pltpu.VMEM((chunk, halves * 2 * LANES), BF16),
             pltpu.VMEM((halves * 2 * LANES, chunk), BF16),
             pltpu.VMEM((SLOTS, chunk), F32),
-            pltpu.VMEM((SLOTS, chunk), F32),
-            pltpu.VMEM((time, SLOTS, LANES), F32),
-            pltpu.VMEM((time, SLOTS, chunk), F32),
-            pltpu.VMEM((time, SLOTS, chunk), F32),
-            pltpu.VMEM((time, SLOTS, chunk), F32),
         ],
-        compiler_params=pltpu.CompilerParams(vmem_limit_bytes=50 * 1024 * 1024),
-        cost_estimate=pl.CostEstimate(
-            flops=flops, bytes_accessed=4 * 1024 * 1024, transcendentals=time * SLOTS * chunk * states
-        ),
+        compiler_params=pltpu.CompilerParams(vmem_limit_bytes=24 * 1024 * 1024),
+        cost_estimate=pl.CostEstimate(flops=4 * flops, bytes_accessed=4 * 1024 * 1024, transcendentals=time * SLOTS * chunk),
     )(
         after,
-        x,
+        *xs,
         seam,
         in_weight,
         conv,
@@ -378,27 +401,78 @@
         jnp.swapaxes(proj, 1, 2),
         step_weight,
         step_bias.reshape(2, 2, width),
-        jnp.swapaxes(decay_log, 1, 2),
-        skip.reshape(2, 2, width),
     )
 
 
-def end_kernel(rows_ref, cols_ref, gate_ref, gain_ref, weight_ref, out_ref):
+def scan(axis, after, coefs, steps, u, decay_log, skip):
+    time, _, chunk = steps.shape
+    width, states = decay_log.shape[1:]
+    way = 0 if axis == "col" else 1
+    vmem = pl.BlockSpec(memory_space=pltpu.VMEM)
+    return pl.pallas_call(
+        scan_kernel,
+        out_shape=jax.ShapeDtypeStruct((time * SLOTS, chunk), BF16),
+        grid=(1,),
+        in_specs=[
+            pl.BlockSpec(memory_space=pl.ANY),
+            vmem,
+            vmem,
+            vmem,
+            pl.BlockSpec((2, states, width), lambda i: (way, 0, 0)),
+            pl.BlockSpec((None, 2, width), lambda i: (way, 0, 0)),
+        ],
+        out_specs=vmem,
+        scratch_shapes=[pltpu.VMEM((time, SLOTS, chunk), F32), pltpu.VMEM((time, SLOTS, chunk), F32)],
+        compiler_params=pltpu.CompilerParams(vmem_limit_bytes=24 * 1024 * 1024),
+        cost_estimate=pl.CostEstimate(
+            flops=8 * time * SLOTS * chunk * states,
+            bytes_accessed=4 * 1024 * 1024,
+            transcendentals=time * SLOTS * chunk * states,
+        ),
+    )(after, coefs, steps, u, jnp.swapaxes(decay_log, 1, 2), skip.reshape(2, 2, width))
+
+
+def end_kernel(cols_ref, gate_ref, gain_ref, weight_ref, *refs):
+    row_refs, out_ref, gated_ref = refs[:-2], refs[-2], refs[-1]
     height, width, channels = out_ref.shape
+    size = row_refs[0].shape[0]
+    lines = size // width
+    swap = flip("col") ^ lax.axis_index("col")
+    turn = flip("row") * (width // lax.axis_size("row"))
     row = rows_of(height * width)
-    turn = flip("row") * (width // lax.axis_size("row"))
-    source = (((row & (width - 1)) ^ turn) << bits(height)) + (row >> bits(width))
-    turn = flip("col")
-    rows = jnp.concatenate([rows_ref[part ^ turn] for part in range(rows_ref.shape[0])], axis=0)
-    combined = rows.astype(F32) + dot(one_hot([source], height * width), cols_ref[...])
-    gate = gate_ref[...].astype(F32)
-    gated = layer_norm(combined, gain_ref[...][None]) * (gate / (1.0 + jnp.exp(-gate)))
-    out = dot(gated.astype(BF16), weight_ref[...]).astype(BF16)
+    line = (row >> bits(width)) ^ (swap * lines)
+    source = (((row & (width - 1)) ^ turn) << bits(height)) + line
+    rows = jnp.concatenate([row_ref[...] for row_ref in row_refs], axis=0)
+    combined = layer_norm(rows.astype(F32) + dot(one_hot([source], height * width), cols_ref[...]), gain_ref[...][None])
+    for part in range(len(row_refs)):
+        cells = pl.ds(pl.multiple_of((part ^ swap) * size, size), size)
+        gate = gate_ref[cells].astype(F32)
+        gated_ref[cells] = (combined[part * size : (part + 1) * size] * (gate / (1.0 + jnp.exp(-gate)))).astype(BF16)
+    out = dot(gated_ref[...], weight_ref[...]).astype(BF16)
     out_ref[...] = out.reshape(height, width, channels)
 
 
-def send_lines(send, axis):
-    x = lax.all_to_all(send, axis, 0, 0, tiled=True)
+def swap_blocks(blocks, axis):
+    count = lax.axis_size(axis)
+    blocks = list(blocks)
+    return blocks[:1] + [lax.ppermute(blocks[k], axis, [(i, i ^ k) for i in range(count)]) for k in range(1, count)]
+
+
+def pick_kernel(axis, after_ref, x_ref, out_ref):
+    place = lax.axis_index(axis) ^ flip(axis)
+    out_ref[...] = x_ref[:, jnp.where(place == 0, 1, x_ref.shape[1] - 2)]
+
+
+def pick(axis, after, x):
+    return pl.pallas_call(
+        functools.partial(pick_kernel, axis),
+        out_shape=jax.ShapeDtypeStruct((x.shape[0],) + x.shape[2:], x.dtype),
+        in_specs=[pl.BlockSpec(memory_space=pl.ANY), pl.BlockSpec(memory_space=pltpu.VMEM)],
+        out_specs=pl.BlockSpec(memory_space=pltpu.VMEM),
+    )(after, x)
+
+
+def seam_of(axis, line):
     count = lax.axis_size(axis)
     height, breadth = lax.axis_size("row"), lax.axis_size("col")
     if axis == "row":
@@ -408,9 +482,7 @@
         at = lambda group: 0 if group & 1 else count - 1
         ends = [(at(r) + r * breadth, at(r) + (r + 1) * breadth) for r in range(height - 1)]
     pairs = ends + [(b, a) for a, b in ends]
-    place = lax.axis_index(axis) ^ flip(axis)
-    seam = lax.ppermute(jnp.where(place == 0, x[:, 1], x[:, -2]), ("row", "col"), pairs)
-    return x, seam
+    return lax.ppermute(line, ("row", "col"), pairs)
 
 
 def local(
@@ -433,17 +505,16 @@
     row_lines = height // lax.axis_size("col")
     col_lines = width // lax.axis_size("row")
 
-    normed, row_send, col_send = pl.pallas_call(
+    rows, cols = lax.axis_size("row"), lax.axis_size("col")
+    normed, col_send, *row_send = pl.pallas_call(
         cut_kernel,
-        out_shape=(
+        out_shape=[
             jax.ShapeDtypeStruct((tokens, channels), BF16),
-            jax.ShapeDtypeStruct((lax.axis_size("col"), row_lines + 2, width, channels), BF16),
-            jax.ShapeDtypeStruct((lax.axis_size("row"), col_lines + 2, height, channels), BF16),
-        ),
+            jax.ShapeDtypeStruct((rows, col_lines + 2, height, channels), BF16),
+        ]
+        + [jax.ShapeDtypeStruct((row_lines + 2, width, channels), BF16)] * cols,
     )(features, norm_gain)
     weights = (in_weight, conv_weight, conv_bias, proj_weight, step_weight, step_bias, decay_log, skip_gain)
-    col_sent = send_lines(col_send, "row")
-    row_sent = send_lines(row_send, "col")
     gate = pl.pallas_call(
         gate_kernel,
         out_shape=jax.ShapeDtypeStruct((tokens, inner), BF16),
@@ -455,18 +526,24 @@
         out_specs=pl.BlockSpec((tokens, inner), lambda i: (0, 0)),
         cost_estimate=pl.CostEstimate(flops=2 * tokens * channels * inner, bytes_accessed=1 << 20, transcendentals=0),
     )(normed, in_weight)
-    parts = lax.axis_size("row")
-    col_y = lines_of("row", normed, *col_sent, *weights)
-    joined = join(col_y, parts, col_lines, height, inner, row_sent[1])
-    col_y = lax.all_to_all(joined.reshape(parts, -1, inner), "row", 0, 0, tiled=True)
-    parts = lax.axis_size("col")
-    row_y = lines_of("col", joined, *row_sent, *weights)
-    row_y = join(row_y, parts, row_lines, width, inner, col_y)
-    row_y = lax.all_to_all(row_y.reshape(parts, -1, inner), "col", 0, 0, tiled=True)
+
+    row_x = swap_blocks(row_send, "col")
+    col_x = lax.all_to_all(col_send, "row", 0, 0, tiled=True)
+    start = lax.axis_index("col") == flip("col")
+    row_seam = seam_of("col", jnp.stack([jnp.where(start, x[1], x[-2]) for x in row_x]))
+    row_steps = prepare("col", normed, row_x, row_seam, *weights)
+    col_seam = seam_of("row", pick("row", row_steps[0], col_x))
+    col_steps = prepare("row", row_steps[0], [col_x], col_seam, *weights)
+    col_y = scan("row", normed, *col_steps, decay_log, skip_gain)
+    (joined,) = join("row", col_y, rows, col_lines, height, inner, normed, False)
+    col_y = lax.all_to_all(joined.reshape(rows, -1, inner), "row", 0, 0, tiled=True)
+    row_y = scan("col", joined, *row_steps, decay_log, skip_gain)
+    row_y = swap_blocks(join("col", row_y, cols, row_lines, width, inner, col_y, True), "col")
     return pl.pallas_call(
         end_kernel,
         out_shape=jax.ShapeDtypeStruct(features.shape, BF16),
-    )(row_y, col_y.reshape(tokens, inner), gate, out_gain, out_weight)
+        scratch_shapes=[pltpu.VMEM((tokens, inner), BF16)],
+    )(col_y.reshape(tokens, inner), gate, out_gain, out_weight, *row_y)
 
 
 def solution(mesh):

time: 87.1 us -> 87.1 us (level)
  waiting for transfers between devices: 20.3 us -> 2.8 us
  local copies, waits for them, and re-layouts: 4.82 us -> 17 us
  starting transfers between devices: 21.1 us -> 24.7 us
    all_to_all x4 -> x2, waiting for transfers between devices: 20.3 us -> 0.01 us  [the longest x1 0.01 us: local(): col_x = lax.all_to_all(col_send, 'row', 0, 0, tiled=True)]
    unnamed x20 -> x54, local copies, waits for them, and re-layouts: 2.68 us -> 15.6 us
    ppermute x2 -> x8, starting transfers between devices: 1.33 us -> 6.25 us  [the longest x6 4.93 us: swap_blocks(): lax.ppermute(blocks[k], axis, [(i, i ^ k) for i in range(count)])]
    ppermute x2 -> x8, waiting for transfers between devices: 0.01 us -> 2.79 us  [the longest x6 2.79 us: swap_blocks(): lax.ppermute(blocks[k], axis, [(i, i ^ k) for i in range(count)])]
    all_to_all x4 -> x2, starting transfers between devices: 19.8 us -> 18.5 us  [the longest x1 12.4 us: local(): lax.all_to_all(joined.reshape(rows, -1, inner), 'row', 0, 0, tiled=True)]
    pallas_call x5 -> x8, Pallas kernels: 34.7 us -> 35.1 us  [the longest x2 21 us: scan(): pl.pallas_call(scan_kernel, out_shape=jax.ShapeDtypeStruct((time * SLOTS,...]
  transfers between devices with their start and end apart: 6 -> 10, of which waited for: 3 -> 2; matrix products, arithmetic and copies ran while one was open for 3% -> 3% of each run, Pallas kernels for 37% -> 17%
where the time goes in v4:
time: 87.1 us; the launch traced here: 86.1 us
  Pallas kernels  40.5 us (46%)
  starting transfers between devices  24.7 us (28%)
  local copies, waits for them, and re-layouts  17 us (20%)
  waiting for transfers between devices  2.8 us (3%)
    pallas_call x2, Pallas kernels, scan(): pl.pallas_call(scan_kernel, out_shape=jax.ShapeDtypeStruct((time * SLOTS,...  21 us
    unnamed x54, local copies, waits for them, and re-layouts  15.6 us
    all_to_all x1, starting transfers between devices, local(): lax.all_to_all(joined.reshape(rows, -1, inner), 'row', 0, 0, tiled=True)  12.4 us
    pallas_call x2, Pallas kernels, prepare(): pl.pallas_call(functools.partial(prepare_kernel, lines, axis, swapped), o...  8.5 us
    all_to_all x1, starting transfers between devices, local(): col_x = lax.all_to_all(col_send, 'row', 0, 0, tiled=True)  6.08 us
    ppermute x6, starting transfers between devices, swap_blocks(): lax.ppermute(blocks[k], axis, [(i, i ^ k) for i in range(count)])  4.93 us
    pallas_call x1, Pallas kernels, local(): pl.pallas_call(end_kernel, out_shape=jax.ShapeDtypeStruct(features.shape,...  3.14 us
    ppermute x6, waiting for transfers between devices, swap_blocks(): lax.ppermute(blocks[k], axis, [(i, i ^ k) for i in range(count)])  2.79 us
  transfers between devices with their start and end apart: 10, of which 2 were waited for; matrix products, arithmetic and copies ran while one was open for 3% of the time, Pallas kernels for 17%

profile of v4, /device:TPU:0, one launch (start us, length us, event | category | flops | bytes accessed | tf_op | source)
XLA Modules:
  0.0 86.1 jit_solution(1154806645956729518)
XLA Ops:
  0.0 2.1 %shard_map.118 = (bf16[256,384]{1,0:T(8,128)(2,1)}, bf16[8,4,16,384]{3,2,1,0:T(8,128)(2,1)}, bf16[6,16,384]{2,1,0:T(8,128)(2,1)}, bf16[6,16,384]{2,1,0:T(8,128)(...) custom-call(bf16[16,16,384]{2,1,0:T(8,128)(2,1)} %feat_ref.1, f32[384]{0:T(512)} %gain_ref.2), custom_call_target="tpu_custom_call" | custom-call | tf_op jit(solution)/shard_map/pallas_call | solution.py:509
  2.1 2.4 %collective-permute-start.2 = (bf16[6,16,384]{2,1,0:T(8,128)(2,1)}, bf16[6,16,384]{2,1,0:T(8,128)(2,1)S(1)}, u32[]{:S(2)}, u32[]{:S(2)}) collective-permute-start(bf16[6,16,384]{2,1,0:T(8,128)(2,1)} %get-tuple-element.25), channel_id=1, source_target_pairs={{0,3},{1,2},{2,1},{3,0},{4,7},{5,6},{6,5},{7,4},{8,11},{9,10},{10,... | collective-permute-start | bytes 221192 | tf_op jit(solution)/shard_map/ppermute | solution.py:458
  5.2 6.1 %all-to-all-start = ((bf16[8,4,16,384]{3,2,1,0:T(8,128)(2,1)}), bf16[8,4,16,384]{3,2,1,0:T(8,128)(2,1)S(1)}, u32[]{:S(2)}, u32[]{:S(2)}) async-start(bf16[8,4,16,384]{3,2,1,0:T(8,128)(2,1)} %get-tuple-element.27), calls=%async_computation | async-start | bytes 786432 | tf_op jit(solution)/shard_map/all_to_all | solution.py:531
  14.2 1.3 %copy-done.3 = bf16[384,1536]{1,0:T(8,128)(2,1)S(1)} copy-done((bf16[384,1536]{1,0:T(8,128)(2,1)S(1)}, bf16[384,1536]{1,0:T(8,128)(2,1)}, u32[]{:S(2)}) %copy-start.3) | copy-done | bytes 1179672
  17.3 1.0 %copy-done.12 = bf16[4,768,56]{1,2,0:T(8,128)(2,1)S(1)} copy-done((bf16[4,768,56]{1,2,0:T(8,128)(2,1)S(1)}, bf16[4,768,56]{1,2,0:T(8,128)(2,1)}, u32[]{:S(2)}) %copy-start.12) | copy-done | bytes 344088
  18.2 1.0 %copy-done.14 = f32[4,24,768]{2,1,0:T(8,128)S(1)} copy-done((f32[4,24,768]{2,1,0:T(8,128)S(1)}, f32[4,24,768]{2,1,0:T(8,128)}, u32[]{:S(2)}) %copy-start.14) | copy-done | bytes 294936
  20.0 3.5 %shard_map.119 = (f32[64,8,128]{2,1,0:T(8,128)S(1)}, f32[64,8,768]{2,1,0:T(8,128)S(1)}, f32[64,8,768]{2,1,0:T(8,128)S(1)}) custom-call(bf16[256,384]{1,0:T(8,128)(2,1)S(1)} %copy-done.5, bf16[6,16,384]{2,1,0:T(8,128)(2,1)S(1)} %copy-done.11, bf16[6,16,384]{2,1,0:T(8,128)(2,1)S(1)} %collective-permute-done.refs_1_, ...), custom_call_target="tpu_custom_call" | custom-call | flops 1711276032 | bytes 4194304 | tf_op jit(solution)/shard_map/pallas_call | solution.py:364
  24.2 1.2 %copy-done.19 = f32[64,8,768]{2,1,0:T(8,128)} copy-done((f32[64,8,768]{2,1,0:T(8,128)}, f32[64,8,768]{2,1,0:T(8,128)S(1)}, u32[]{:S(2)}) %copy-start.19) | copy-done | bytes 1572888
  25.3 1.2 %copy-done.21 = f32[64,8,768]{2,1,0:T(8,128)} copy-done((f32[64,8,768]{2,1,0:T(8,128)}, f32[64,8,768]{2,1,0:T(8,128)S(1)}, u32[]{:S(2)}) %copy-start.21) | copy-done | bytes 1572888
  27.3 1.6 %shard_map.120 = bf16[8,16,384]{2,1,0:T(8,128)(2,1)} custom-call(f32[64,8,128]{2,1,0:T(8,128)} %copy-done.7, bf16[8,4,16,384]{3,2,1,0:T(8,128)(2,1)} %copy-done.1), custom_call_target="tpu_custom_call" | custom-call | tf_op jit(solution)/shard_map/pallas_call | solution.py:467
  29.6 1.0 %copy-done.2 = bf16[8,4,16,384]{3,2,1,0:T(8,128)(2,1)S(1)} copy-done((bf16[8,4,16,384]{3,2,1,0:T(8,128)(2,1)S(1)}, bf16[8,4,16,384]{3,2,1,0:T(8,128)(2,1)}, u32[]{:S(2)}) %copy-start.2) | copy-done | bytes 393240
  30.6 0.9 %copy-done.8 = f32[64,8,128]{2,1,0:T(8,128)S(1)} copy-done((f32[64,8,128]{2,1,0:T(8,128)S(1)}, f32[64,8,128]{2,1,0:T(8,128)}, u32[]{:S(2)}) %copy-start.8) | copy-done | bytes 262168
  31.6 5.0 %shard_map.121 = (f32[128,8,128]{2,1,0:T(8,128)S(1)}, f32[128,8,384]{2,1,0:T(8,128)S(1)}, f32[128,8,384]{2,1,0:T(8,128)S(1)}) custom-call(f32[64,8,128]{2,1,0:T(8,128)S(1)} %copy-done.8, bf16[8,4,16,384]{3,2,1,0:T(8,128)(2,1)S(1)} %copy-done.2, bf16[8,16,384]{2,1,0:T(8,128)(2,1)S(1)} %collective-permute-done.4.refs_1_, bf16[384,1536]{1,0:T(8,128)(2,1)S(1)} %copy-done.4, ...), custom_call_target="tpu_custom_call" | custom-call | flops 2818572288 | bytes 4194304 | tf_op jit(solution)/shard_map/pallas_call | solution.py:364
  36.7 11.7 %shard_map.122.scanned_ref = bf16[1024,384]{1,0:T(8,128)(2,1)S(1)} custom-call(bf16[256,384]{1,0:T(8,128)(2,1)S(1)} %copy-done.6, f32[128,8,128]{2,1,0:T(8,128)S(1)} %get-tuple-element.28.coef_ref, f32[128,8,384]{2,1,0:T(8,128)S(1)} %get-tuple-element.29.s_ref, f32[128,8,384]{2,1,0:T(8,128)S(1)} %get-tuple-element.30.u_ref, f32[4,16,768]{2,1,0:T(8,128)S(1)} %bitcast.7, ...), custom_call_target="tpu_custom_call" | custom-call | flops 50331648 | bytes 4194304 | tf_op jit(solution)/shard_map/pallas_call | solution.py:412
  48.4 1.5 %shard_map.123.after_ref = bf16[256,768]{1,0:T(8,128)(2,1)} custom-call(bf16[256,384]{1,0:T(8,128)(2,1)S(1)} %copy-done.6, bf16[1024,384]{1,0:T(8,128)(2,1)S(1)} %shard_map.122.scanned_ref), custom_call_target="tpu_custom_call" | custom-call | tf_op jit(solution)/shard_map/pallas_call | solution.py:330
  49.8 12.4 %all-to-all-start.1 = ((bf16[8,32,768]{2,1,0:T(8,128)(2,1)}), bf16[8,32,768]{2,1,0:T(8,128)(2,1)S(1)}, u32[]{:S(2)}, u32[]{:S(2)}) async-start(bf16[8,32,768]{2,1,0:T(8,128)(2,1)} %bitcast.2), calls=%async_computation.1 | async-start | bytes 786432 | tf_op jit(solution)/shard_map/all_to_all | solution.py:539
  62.3 1.4 %copy-done.20 = f32[64,8,768]{2,1,0:T(8,128)S(1)} copy-done((f32[64,8,768]{2,1,0:T(8,128)S(1)}, f32[64,8,768]{2,1,0:T(8,128)}, u32[]{:S(2)}) %copy-start.20) | copy-done | bytes 1572888
  63.7 1.4 %copy-done.22 = f32[64,8,768]{2,1,0:T(8,128)S(1)} copy-done((f32[64,8,768]{2,1,0:T(8,128)S(1)}, f32[64,8,768]{2,1,0:T(8,128)}, u32[]{:S(2)}) %copy-start.22) | copy-done | bytes 1572888
  65.1 9.3 %shard_map.125.scanned_ref = bf16[512,768]{1,0:T(8,128)(2,1)S(1)} custom-call(bf16[256,768]{1,0:T(8,128)(2,1)} %shard_map.123.after_ref, f32[64,8,128]{2,1,0:T(8,128)S(1)} %copy-done.9, f32[64,8,768]{2,1,0:T(8,128)S(1)} %copy-done.20, f32[64,8,768]{2,1,0:T(8,128)S(1)} %copy-done.22, f32[4,16,768]{2,1,0:T(8,128)S(1)} %bitcast.8, ...), custom_call_target="tpu_custom_call" | custom-call | flops 50331648 | bytes 4194304 | tf_op jit(solution)/shard_map/pallas_call | solution.py:412
  75.5 1.8 %collective-permute-start.7 = (bf16[64,768]{1,0:T(8,128)(2,1)S(1)}, bf16[64,768]{1,0:T(8,128)(2,1)S(1)}, u32[]{:S(2)}, u32[]{:S(2)}) collective-permute-start(bf16[64,768]{1,0:T(8,128)(2,1)S(1)} %get-tuple-element.36), channel_id=1, source_target_pairs={{0,3},{1,2},{2,1},{3,0},{4,7},{5,6},{6,5},{7,4},{8,11},{9,10},{10,... | collective-permute-start | bytes 294920 | tf_op jit(solution)/shard_map/ppermute | solution.py:458
  77.3 2.3 %shard_map.124.gate_ref = bf16[256,768]{1,0:T(8,128)(2,1)} custom-call(bf16[256,384]{1,0:T(8,128)(2,1)} %get-tuple-element.21.after_ref.norm_ref, bf16[384,1536]{1,0:T(8,128)(2,1)} %weight_ref.2), custom_call_target="tpu_custom_call" | custom-call | flops 150994944 | bytes 1048576 | tf_op jit(solution)/shard_map/pallas_call | solution.py:518
  79.6 1.4 %collective-permute-done.6.refs_2_ = bf16[64,768]{1,0:T(8,128)(2,1)S(1)} collective-permute-done((bf16[64,768]{1,0:T(8,128)(2,1)S(1)}, bf16[64,768]{1,0:T(8,128)(2,1)S(1)}, u32[]{:S(2)}, u32[]{:S(2)}) %collective-permute-start.6) | collective-permute-done | bytes 98336 | tf_op jit(solution)/shard_map/ppermute | solution.py:458
  81.0 1.4 %collective-permute-done.7.refs_3_ = bf16[64,768]{1,0:T(8,128)(2,1)S(1)} collective-permute-done((bf16[64,768]{1,0:T(8,128)(2,1)S(1)}, bf16[64,768]{1,0:T(8,128)(2,1)S(1)}, u32[]{:S(2)}, u32[]{:S(2)}) %collective-permute-start.7) | collective-permute-done | bytes 98336 | tf_op jit(solution)/shard_map/ppermute | solution.py:458
  83.0 3.1 %shard_map.127 = bf16[16,16,384]{2,1,0:T(8,128)(2,1)} custom-call(bf16[256,768]{1,0:T(8,128)(2,1)} %bitcast.4, bf16[256,768]{1,0:T(8,128)(2,1)} %shard_map.124.gate_ref, f32[768]{0:T(1024)} %gain_ref.3, bf16[768,384]{1,0:T(8,128)(2,1)} %weight_ref.3, bf16[64,768]{1,0:T(8,128)(2,1)} %copy-done.10, bf16[64,768]{1,0:T(8,128)(2,1)} %copy-done.23, ...), custom_call_target="tpu_custom_call" | custom-call | tf_op jit(solution)/shard_map/pallas_call | solution.py:542
  (68 shorter events, 10.0 us)
Async XLA Ops:
  2.1 9.9 %collective-permute-start.2 = (bf16[6,16,384]{2,1,0:T(8,128)(2,1)}, bf16[6,16,384]{2,1,0:T(8,128)(2,1)S(1)}, u32[]{:S(2)}, u32[]{:S(2)}) collective-permute-start(bf16[6,16,384]{2,1,0:T(8,128)(2,1)} %get-tuple-element.25), channel_id=1, source_target_pairs={{0,3},{1,2},{2,1},{3,0},{4,7},{5,6},{6,5},{7,4},{8,11},{9,10},{10,... | collective-permute-start | bytes 221192 | tf_op jit(solution)/shard_map/ppermute | solution.py:458
  4.5 7.5 %collective-permute-start.1 = (bf16[6,16,384]{2,1,0:T(8,128)(2,1)}, bf16[6,16,384]{2,1,0:T(8,128)(2,1)S(1)}, u32[]{:S(2)}, u32[]{:S(2)}) collective-permute-start(bf16[6,16,384]{2,1,0:T(8,128)(2,1)} %get-tuple-element.24), channel_id=1, source_target_pairs={{0,2},{1,3},{2,0},{3,1},{4,6},{5,7},{6,4},{7,5},{8,10},{9,11},{10,... | collective-permute-start | bytes 221192 | tf_op jit(solution)/shard_map/ppermute | solution.py:458
  5.1 6.9 %collective-permute-start = (bf16[6,16,384]{2,1,0:T(8,128)(2,1)}, bf16[6,16,384]{2,1,0:T(8,128)(2,1)S(1)}, u32[]{:S(2)}, u32[]{:S(2)}) collective-permute-start(bf16[6,16,384]{2,1,0:T(8,128)(2,1)} %get-tuple-element.23), channel_id=1, source_target_pairs={{0,1},{1,0},{2,3},{3,2},{4,5},{5,4},{6,7},{7,6},{8,9},{9,8},{10,11... | collective-permute-start | bytes 221192 | tf_op jit(solution)/shard_map/ppermute | solution.py:458
  5.2 21.3 %all-to-all-start = ((bf16[8,4,16,384]{3,2,1,0:T(8,128)(2,1)}), bf16[8,4,16,384]{3,2,1,0:T(8,128)(2,1)S(1)}, u32[]{:S(2)}, u32[]{:S(2)}) async-start(bf16[8,4,16,384]{3,2,1,0:T(8,128)(2,1)} %get-tuple-element.27), calls=%async_computation | async-start | bytes 786432 | tf_op jit(solution)/shard_map/all_to_all | solution.py:531
  12.1 2.1 %collective-permute-start.3 = (bf16[4,16,384]{2,1,0:T(8,128)(2,1)S(1)}, bf16[4,16,384]{2,1,0:T(8,128)(2,1)S(1)}, u32[]{:S(2)}, u32[]{:S(2)}) collective-permute-start(bf16[4,16,384]{2,1,0:T(8,128)(2,1)S(1)} %pad_maximum_fusion), channel_id=1, source_target_pairs={{3,7},{4,8},{11,15},{12,16},{19,23},{20,24},{27,31},{7,3},{8,4},{1... | collective-permute-start | bytes 147464 | tf_op jit(solution)/shard_map/ppermute | solution.py:485
  14.2 1.3 %copy-start.3 = (bf16[384,1536]{1,0:T(8,128)(2,1)S(1)}, bf16[384,1536]{1,0:T(8,128)(2,1)}, u32[]{:S(2)}) copy-start(bf16[384,1536]{1,0:T(8,128)(2,1)} %weight_ref.2) | copy-start | bytes 3538948
  20.0 9.6 %copy-start.26 = (f32[4,768]{1,0:T(4,128)S(1)}, f32[4,768]{1,0:T(4,128)}, u32[]{:S(2)}) copy-start(f32[4,768]{1,0:T(4,128)} %param.21) | copy-start | bytes 36868
  20.0 9.6 %copy-start.4 = (bf16[384,1536]{1,0:T(8,128)(2,1)S(1)}, bf16[384,1536]{1,0:T(8,128)(2,1)}, u32[]{:S(2)}) copy-start(bf16[384,1536]{1,0:T(8,128)(2,1)} %weight_ref.2) | copy-start | bytes 3538948
  20.0 9.6 %copy-start.13 = (bf16[4,768,56]{1,2,0:T(8,128)(2,1)S(1)}, bf16[4,768,56]{1,2,0:T(8,128)(2,1)}, u32[]{:S(2)}) copy-start(bf16[4,768,56]{1,2,0:T(8,128)(2,1)} %param.17) | copy-start | bytes 1032196
  20.0 9.6 %copy-start.15 = (f32[4,24,768]{2,1,0:T(8,128)S(1)}, f32[4,24,768]{2,1,0:T(8,128)}, u32[]{:S(2)}) copy-start(f32[4,24,768]{2,1,0:T(8,128)} %refs_6_.3) | copy-start | bytes 884740
  20.0 9.6 %copy-start.18 = (f32[3,3,768]{2,1,0:T(4,128)S(1)}, f32[3,3,768]{2,1,0:T(4,128)}, u32[]{:S(2)}) copy-start(f32[3,3,768]{2,1,0:T(4,128)} %refs_3_.1) | copy-start | bytes 82948
  28.9 0.7 collective-permute-start.4
  31.6 5.1 %copy-start.6 = (bf16[256,384]{1,0:T(8,128)(2,1)S(1)}, bf16[256,384]{1,0:T(8,128)(2,1)}, u32[]{:S(2)}) copy-start(bf16[256,384]{1,0:T(8,128)(2,1)} %get-tuple-element.21.after_ref.norm_ref) | copy-start | bytes 589828
  31.6 5.1 %copy-start.16 = (f32[4,768,16]{1,2,0:T(8,128)S(1)}, f32[4,768,16]{1,2,0:T(8,128)}, u32[]{:S(2)}) copy-start(f32[4,768,16]{1,2,0:T(8,128)} %param.20) | copy-start | bytes 589828
  48.4 13.9 %copy-start.9 = (f32[64,8,128]{2,1,0:T(8,128)S(1)}, f32[64,8,128]{2,1,0:T(8,128)}, u32[]{:S(2)}) copy-start(f32[64,8,128]{2,1,0:T(8,128)} %copy-done.7) | copy-start | bytes 786436
  49.8 24.5 %all-to-all-start.1 = ((bf16[8,32,768]{2,1,0:T(8,128)(2,1)}), bf16[8,32,768]{2,1,0:T(8,128)(2,1)S(1)}, u32[]{:S(2)}, u32[]{:S(2)}) async-start(bf16[8,32,768]{2,1,0:T(8,128)(2,1)} %bitcast.2), calls=%async_computation.1 | async-start | bytes 786432 | tf_op jit(solution)/shard_map/all_to_all | solution.py:539
  62.3 1.4 %copy-start.20 = (f32[64,8,768]{2,1,0:T(8,128)S(1)}, f32[64,8,768]{2,1,0:T(8,128)}, u32[]{:S(2)}) copy-start(f32[64,8,768]{2,1,0:T(8,128)} %copy-done.19) | copy-start | bytes 4718596
  63.7 1.4 %copy-start.22 = (f32[64,8,768]{2,1,0:T(8,128)S(1)}, f32[64,8,768]{2,1,0:T(8,128)}, u32[]{:S(2)}) copy-start(f32[64,8,768]{2,1,0:T(8,128)} %copy-done.21) | copy-start | bytes 4718596
  74.4 8.0 %copy-start = (bf16[8,32,768]{2,1,0:T(8,128)(2,1)}, bf16[8,32,768]{2,1,0:T(8,128)(2,1)S(1)}, u32[]{:S(2)}) copy-start(bf16[8,32,768]{2,1,0:T(8,128)(2,1)S(1)} %all-to-all-done.1.after_ref) | copy-start | bytes 1179652
  75.4 4.2 %collective-permute-start.5 = (bf16[64,768]{1,0:T(8,128)(2,1)S(1)}, bf16[64,768]{1,0:T(8,128)(2,1)S(1)}, u32[]{:S(2)}, u32[]{:S(2)}) collective-permute-start(bf16[64,768]{1,0:T(8,128)(2,1)S(1)} %get-tuple-element.34), channel_id=1, source_target_pairs={{0,1},{1,0},{2,3},{3,2},{4,5},{5,4},{6,7},{7,6},{8,9},{9,8},{10,11... | collective-permute-start | bytes 294920 | tf_op jit(solution)/shard_map/ppermute | solution.py:458
  75.4 5.6 %collective-permute-start.6 = (bf16[64,768]{1,0:T(8,128)(2,1)S(1)}, bf16[64,768]{1,0:T(8,128)(2,1)S(1)}, u32[]{:S(2)}, u32[]{:S(2)}) collective-permute-start(bf16[64,768]{1,0:T(8,128)(2,1)S(1)} %get-tuple-element.35), channel_id=1, source_target_pairs={{0,2},{1,3},{2,0},{3,1},{4,6},{5,7},{6,4},{7,5},{8,10},{9,11},{10,... | collective-permute-start | bytes 294920 | tf_op jit(solution)/shard_map/ppermute | solution.py:458
  75.5 6.9 %collective-permute-start.7 = (bf16[64,768]{1,0:T(8,128)(2,1)S(1)}, bf16[64,768]{1,0:T(8,128)(2,1)S(1)}, u32[]{:S(2)}, u32[]{:S(2)}) collective-permute-start(bf16[64,768]{1,0:T(8,128)(2,1)S(1)} %get-tuple-element.36), channel_id=1, source_target_pairs={{0,3},{1,2},{2,1},{3,0},{4,7},{5,6},{6,5},{7,4},{8,11},{9,10},{10,... | collective-permute-start | bytes 294920 | tf_op jit(solution)/shard_map/ppermute | solution.py:458
  79.6 2.8 %copy-start.23 = (bf16[64,768]{1,0:T(8,128)(2,1)}, bf16[64,768]{1,0:T(8,128)(2,1)S(1)}, u32[]{:S(2)}) copy-start(bf16[64,768]{1,0:T(8,128)(2,1)S(1)} %collective-permute-done.5.refs_1_) | copy-start | bytes 294916
  81.0 1.4 %copy-start.24 = (bf16[64,768]{1,0:T(8,128)(2,1)}, bf16[64,768]{1,0:T(8,128)(2,1)S(1)}, u32[]{:S(2)}) copy-start(bf16[64,768]{1,0:T(8,128)(2,1)S(1)} %collective-permute-done.6.refs_2_) | copy-start | bytes 294916
  (13 other events, 11.5 us)

commit v5 on v4

--- a/solution.py
+++ b/solution.py
@@ -49,7 +49,8 @@
     return (lax.axis_index(other) & 1) * (lax.axis_size(axis) - 1)
 
 
-def cut_kernel(feat_ref, gain_ref, norm_ref, cols_ref, *row_refs):
+def cut_kernel(columns, feat_ref, gain_ref, norm_ref, *refs):
+    col_refs, row_refs, turned_ref = refs[:columns], refs[columns:-1], refs[-1]
     height, width, channels = feat_ref.shape
     tile = layer_norm(feat_ref[...].reshape(height * width, channels).astype(F32), gain_ref[...][None]).astype(BF16)
     norm_ref[...] = tile
@@ -63,12 +64,13 @@
     turned = dot(one_hot([((row & (height - 1)) << bits(width)) + (row >> bits(height))], height * width), tile).astype(
         BF16
     )
-    reach = cols_ref.shape[1]
-    turn = flip("row")
-    for part in range(cols_ref.shape[0]):
+    turned_ref[...] = turned
+    reach = col_refs[0].shape[0]
+    turn = flip("row") ^ lax.axis_index("row")
+    for part, col_ref in enumerate(col_refs):
         for line in range(reach):
-            at = min(max(part * (reach - 2) + line - 1, 0), width - 1)
-            cols_ref[part ^ turn, line] = turned[at * height : (at + 1) * height]
+            at = jnp.clip((part ^ turn) * (reach - 2) + line - 1, 0, width - 1)
+            col_ref[line] = turned_ref[pl.ds(pl.multiple_of(at * height, height), height)]
 
 
 def gate_kernel(norm_ref, weight_ref, gate_ref):
@@ -88,29 +90,51 @@
 def prepare_kernel(
     lines,
     axis,
-    swapped,
     after_ref,
     *refs,
 ):
-    x_refs, refs = refs[:-16], refs[-16:]
+    x_refs, refs = refs[:-23], refs[-23:]
     (
-    seam_ref,
-    weight_ref,
-    conv_ref,
-    conv_bias_ref,
-    proj_raw_ref,
-    step_raw_ref,
-    bias_raw_ref,
-    proj_out_ref,
-    s_ref,
-    v_ref,
-    token_ref,
-    inner_ref,
-    active_ref,
-    proj_ref,
-    step_ref,
-    bias_ref,
+        seam_ref,
+        weight_hbm,
+        conv_hbm,
+        conv_bias_hbm,
+        proj_hbm,
+        step_hbm,
+        bias_hbm,
+        proj_out_ref,
+        s_ref,
+        v_ref,
+        weight_ref,
+        conv_ref,
+        conv_bias_ref,
+        proj_raw_ref,
+        step_raw_ref,
+        bias_raw_ref,
+        token_ref,
+        inner_ref,
+        active_ref,
+        proj_ref,
+        step_ref,
+        bias_ref,
+        copied,
     ) = refs
+    pair = pl.ds(0 if axis == "col" else 2, 2)
+    copies = [
+        pltpu.make_async_copy(source, to, copied.at[k])
+        for k, (source, to) in enumerate(
+            [
+                (weight_hbm.at[:, pl.ds(0, weight_ref.shape[1])], weight_ref),
+                (conv_hbm, conv_ref),
+                (conv_bias_hbm, conv_bias_ref),
+                (proj_hbm.at[pair], proj_raw_ref),
+                (step_hbm.at[pair], step_raw_ref),
+                (bias_hbm, bias_raw_ref),
+            ]
+        )
+    ]
+    for copy in copies:
+        copy.start()
     parts, length, channels = seam_ref.shape
     reach = lines + 2
     states = (proj_raw_ref.shape[1] - RANK) // 2
@@ -125,36 +149,19 @@
     else:
         across_first = lambda across, along: (across, along)
 
-    bias_ref[...] = by_slot(halves, lambda half, way: bias_raw_ref[way : way + 1, half * chunk : (half + 1) * chunk])
-    for half in range(halves):
-        cells = slice(half * chunk, (half + 1) * chunk)
-        for way in range(2):
-            kind = slice((half * 2 + way) * LANES, (half * 2 + way + 1) * LANES)
-            w = proj_raw_ref[way, :, cells].astype(F32)
-            ranks = w[:RANK]
-            rest = jnp.zeros((LANES - 3 * RANK - 2 * states, chunk), F32)
-            w = jnp.concatenate([ranks, ranks, ranks, w[RANK:], rest], axis=0)
-            proj_ref[:, kind] = w.T.astype(BF16)
-            w = step_raw_ref[way, :, cells]
-            high = w.astype(BF16).astype(F32)
-            rest = jnp.zeros((LANES - 3 * RANK, chunk), F32)
-            step_ref[kind, :] = jnp.concatenate([high, high, w - high, rest], axis=0).astype(BF16)
-
     row = rows_of(time)
     source = ((row & 7) << bits(low)) + (row >> 3)
-    if swapped:
-        source = source ^ (lax.axis_index(axis) << bits(length))
+    source = source ^ (lax.axis_index(axis) << bits(length))
     order = one_hot([source], time)
     for line in range(reach):
-        if swapped:
-            x = jnp.concatenate([x_ref[line] for x_ref in x_refs], axis=0)
-        else:
-            x = x_refs[0][:, line].reshape(time, channels)
+        x = jnp.concatenate([x_ref[line] for x_ref in x_refs], axis=0)
         if line == 0 or line == reach - 1:
             place = lax.axis_index(axis) ^ flip(axis)
             missing = place == (0 if line == 0 else lax.axis_size(axis) - 1)
             x = jnp.where(missing, seam_ref[...].reshape(time, channels), x)
         token_ref[line * time : (line + 1) * time] = dot(order, x).astype(BF16)
+    for copy in copies:
+        copy.wait()
     inner = dot(token_ref[...], weight_ref[...]).astype(BF16).astype(F32)
     inner_ref[:, 1 : low + 1] = inner.reshape(reach, low, SLOTS, width)
     place = lax.broadcasted_iota(jnp.int32, (SLOTS, width), 0)
@@ -162,12 +169,14 @@
         inner_ref[line, 0] = jnp.where(place == 0, 0.0, pltpu.roll(inner_ref[line, low], 1, 0))
         inner_ref[line, low + 1] = jnp.where(place == SLOTS - 1, 0.0, pltpu.roll(inner_ref[line, 1], SLOTS - 1, 0))
 
+    conv_bias = conv_bias_ref[...][None]
+
     def convolve(pair, _):
         for group in range(width // (2 * LANES)):
             cells = slice(group * 2 * LANES, (group + 1) * 2 * LANES)
             half = (group * 2 * LANES) // chunk
             base = group * 2 * LANES - half * chunk
-            bias = jnp.broadcast_to(conv_bias_ref[:, cells], (SLOTS, 2 * LANES))
+            bias = jnp.broadcast_to(conv_bias[:, cells], (SLOTS, 2 * LANES))
             totals = [[bias for _ in range(2)] for _ in range(lines)]
             for across in range(3):
                 for along in range(3):
@@ -191,6 +200,21 @@
         return 0
 
     lax.fori_loop(0, low // 2, convolve, 0)
+
+    bias_ref[...] = by_slot(halves, lambda half, way: bias_raw_ref[pair.start + way : pair.start + way + 1, half * chunk : (half + 1) * chunk])
+    for half in range(halves):
+        cells = slice(half * chunk, (half + 1) * chunk)
+        for way in range(2):
+            kind = slice((half * 2 + way) * LANES, (half * 2 + way + 1) * LANES)
+            w = proj_raw_ref[way, :, cells].astype(F32)
+            ranks = w[:RANK]
+            rest = jnp.zeros((LANES - 3 * RANK - 2 * states, chunk), F32)
+            w = jnp.concatenate([ranks, ranks, ranks, w[RANK:], rest], axis=0)
+            proj_ref[:, kind] = w.T.astype(BF16)
+            w = step_raw_ref[way, :, cells]
+            high = w.astype(BF16).astype(F32)
+            rest = jnp.zeros((LANES - 3 * RANK, chunk), F32)
+            step_ref[kind, :] = jnp.concatenate([high, high, w - high, rest], axis=0).astype(BF16)
 
     piece = 256
     for first in range(0, time * SLOTS, piece):
@@ -238,7 +262,22 @@
     lax.fori_loop(0, time // 8, soften, 0)
 
 
-def scan_kernel(after_ref, coef_ref, s_ref, u_ref, decay_ref, skip_raw_ref, out_ref, v_ref, y_ref):
+def scan_kernel(
+    axis,
+    after_ref,
+    coef_ref,
+    s_ref,
+    u_ref,
+    decay_hbm,
+    skip_hbm,
+    out_ref,
+    v_ref,
+    y_ref,
+    spread_ref,
+    decay_ref,
+    skip_raw_ref,
+    copied,
+):
     time, _, chunk = s_ref.shape
     halves = decay_ref.shape[2] // chunk
     states = decay_ref.shape[1]
@@ -246,6 +285,33 @@
     at_once = max(1, 12 // groups)
     unroll = 8
     laps = time // unroll
+
+    pair = pl.ds(0 if axis == "col" else 2, 2)
+    copies = [
+        pltpu.make_async_copy(decay_hbm.at[pair], decay_ref, copied.at[0]),
+        pltpu.make_async_copy(skip_hbm, skip_raw_ref, copied.at[1]),
+    ]
+    for copy in copies:
+        copy.start()
+
+    piece = 32
+    row = lax.broadcasted_iota(jnp.int32, (2 * LANES, LANES), 0) & (LANES - 1)
+    taken = [jnp.where(row == 3 * RANK + n, 1.0, 0.0).astype(BF16) for n in range(2 * states)]
+
+    def spread(lap, _):
+        steps = pl.ds(lap * piece, piece)
+        coefs = coef_ref[steps].reshape(piece * SLOTS, LANES)
+        high = coefs.astype(BF16)
+        both = jnp.concatenate([high, (coefs - high.astype(F32)).astype(BF16)], axis=1)
+        for n in range(0, 2 * states, 4):
+            found = dot(both, jnp.concatenate(taken[n : n + 4], axis=1))
+            for k in range(4):
+                spread_ref[steps, n + k] = found[:, k * LANES : (k + 1) * LANES].reshape(piece, SLOTS, LANES)
+        return 0
+
+    lax.fori_loop(0, time // piece, spread, 0)
+    for copy in copies:
+        copy.wait()
     for first in range(0, states, at_once):
         rates = []
         for n in range(first, first + at_once):
@@ -261,7 +327,7 @@
                 by_slot(
                     halves,
                     lambda half, way: skip_raw_ref[
-                        way : way + 1, half * chunk + g * LANES : half * chunk + (g + 1) * LANES
+                        pair.start + way : pair.start + way + 1, half * chunk + g * LANES : half * chunk + (g + 1) * LANES
                     ],
                 )
                 for g in range(groups)
@@ -271,13 +337,8 @@
             hidden = list(hidden)
             for sub in range(unroll):
                 t = lap * unroll + sub
-                coefs = coef_ref[t]
-
-                def spread(lane):
-                    return jnp.broadcast_to(coefs[:, lane : lane + 1], (SLOTS, LANES))
-
-                enter = [spread(3 * RANK + first + n) for n in range(at_once)]
-                leave = [spread(3 * RANK + states + first + n) for n in range(at_once)]
+                enter = [spread_ref[t, first + n] for n in range(at_once)]
+                leave = [spread_ref[t, states + first + n] for n in range(at_once)]
                 for g in range(groups):
                     cells = pl.ds(g * LANES, LANES)
                     step = s_ref[t, :, cells]
@@ -312,8 +373,7 @@
     row = rows_of(lines * time)
     line = (row >> bits(length)) & (lines - 1)
     part = row >> bits(lines * length)
-    if len(out_refs) > 1:
-        part = part ^ lax.axis_index(axis)
+    part = part ^ lax.axis_index(axis)
     now = (part << bits(length)) + (row & (length - 1))
     for half in range(halves):
         ahead = now * SLOTS + (half * 2 * slot_lines) + line
@@ -325,13 +385,12 @@
             at += out_ref.shape[0]
 
 
-def join(axis, scanned, parts, lines, length, width, after, apart):
-    count = parts if apart else 1
+def join(axis, scanned, parts, lines, length, width, after):
     return pl.pallas_call(
         functools.partial(join_kernel, parts, lines, axis),
-        out_shape=[jax.ShapeDtypeStruct((parts * lines * length // count, width), BF16)] * count,
+        out_shape=[jax.ShapeDtypeStruct((lines * length, width), BF16)] * parts,
         in_specs=[pl.BlockSpec(memory_space=pl.ANY), pl.BlockSpec(memory_space=pltpu.VMEM)],
-        out_specs=[pl.BlockSpec(memory_space=pltpu.VMEM)] * count,
+        out_specs=[pl.BlockSpec(memory_space=pltpu.VMEM)] * parts,
         compiler_params=pltpu.CompilerParams(vmem_limit_bytes=24 * 1024 * 1024),
     )(after, scanned)
 
@@ -340,7 +399,6 @@
 
 
 def prepare(axis, after, xs, seam, in_weight, conv, conv_bias, proj, step_weight, step_bias, decay_log, skip):
-    swapped = len(xs) > 1
     parts, length, channels = seam.shape
     reach = xs[0].shape[-3]
     lines = reach - 2
@@ -351,43 +409,32 @@
     halves = 1 if lines >= 4 else 2
     assert lines <= SLOTS // (2 * halves)
     chunk = width // halves
-    way = 0 if axis == "col" else 1
-
-    def all_of(*shape):
-        return pl.BlockSpec(shape, lambda i: (0,) * len(shape))
-
-    def pair(*shape):
-        return pl.BlockSpec((2,) + shape, lambda i: (way,) + (0,) * len(shape))
-
     vmem = pl.BlockSpec(memory_space=pltpu.VMEM)
+    hbm = pl.BlockSpec(memory_space=pltpu.HBM)
     flops = 2 * time * (reach * channels * width + SLOTS * width * 256)
     return pl.pallas_call(
-        functools.partial(prepare_kernel, lines, axis, swapped),
+        functools.partial(prepare_kernel, lines, axis),
         out_shape=[
             jax.ShapeDtypeStruct((time, SLOTS, LANES), F32),
             jax.ShapeDtypeStruct((time, SLOTS, chunk), F32),
             jax.ShapeDtypeStruct((time, SLOTS, chunk), F32),
         ],
-        grid=(1,),
-        in_specs=[pl.BlockSpec(memory_space=pl.ANY)]
-        + [all_of(*x.shape) for x in xs]
-        + [
-            all_of(parts, length, channels),
-            all_of(channels, width),
-            all_of(3, 3, width),
-            all_of(1, width),
-            pair(RANK + 2 * states, width),
-            pair(RANK, width),
-            pl.BlockSpec((None, 2, width), lambda i: (way, 0, 0)),
-        ],
+        in_specs=[pl.BlockSpec(memory_space=pl.ANY)] + [vmem] * (len(xs) + 1) + [hbm] * 6,
         out_specs=[vmem, vmem, vmem],
         scratch_shapes=[
+            pltpu.VMEM((channels, width), in_weight.dtype),
+            pltpu.VMEM(conv.shape, conv.dtype),
+            pltpu.VMEM(conv_bias.shape, conv_bias.dtype),
+            pltpu.VMEM((2, RANK + 2 * states, width), proj.dtype),
+            pltpu.VMEM((2, RANK, width), step_weight.dtype),
+            pltpu.VMEM(step_bias.shape, step_bias.dtype),
             pltpu.VMEM((reach * time, channels), BF16),
             pltpu.VMEM((reach, time // SLOTS + 2, SLOTS, width), F32),
             pltpu.VMEM((halves * lines * time, chunk), BF16),
             pltpu.VMEM((chunk, halves * 2 * LANES), BF16),
             pltpu.VMEM((halves * 2 * LANES, chunk), BF16),
             pltpu.VMEM((SLOTS, chunk), F32),
+            pltpu.SemaphoreType.DMA((6,)),
         ],
         compiler_params=pltpu.CompilerParams(vmem_limit_bytes=24 * 1024 * 1024),
         cost_estimate=pl.CostEstimate(flops=4 * flops, bytes_accessed=4 * 1024 * 1024, transcendentals=time * SLOTS * chunk),
@@ -397,53 +444,53 @@
         seam,
         in_weight,
         conv,
-        conv_bias.reshape(1, width),
+        conv_bias,
         jnp.swapaxes(proj, 1, 2),
         step_weight,
-        step_bias.reshape(2, 2, width),
+        step_bias,
     )
 
 
 def scan(axis, after, coefs, steps, u, decay_log, skip):
     time, _, chunk = steps.shape
     width, states = decay_log.shape[1:]
-    way = 0 if axis == "col" else 1
     vmem = pl.BlockSpec(memory_space=pltpu.VMEM)
+    hbm = pl.BlockSpec(memory_space=pltpu.HBM)
     return pl.pallas_call(
-        scan_kernel,
+        functools.partial(scan_kernel, axis),
         out_shape=jax.ShapeDtypeStruct((time * SLOTS, chunk), BF16),
-        grid=(1,),
-        in_specs=[
-            pl.BlockSpec(memory_space=pl.ANY),
-            vmem,
-            vmem,
-            vmem,
-            pl.BlockSpec((2, states, width), lambda i: (way, 0, 0)),
-            pl.BlockSpec((None, 2, width), lambda i: (way, 0, 0)),
+        in_specs=[pl.BlockSpec(memory_space=pl.ANY), vmem, vmem, vmem, hbm, hbm],
+        out_specs=vmem,
+        scratch_shapes=[
+            pltpu.VMEM((time, SLOTS, chunk), F32),
+            pltpu.VMEM((time, SLOTS, chunk), F32),
+            pltpu.VMEM((time, 2 * states, SLOTS, LANES), F32),
+            pltpu.VMEM((2, states, width), decay_log.dtype),
+            pltpu.VMEM(skip.shape, skip.dtype),
+            pltpu.SemaphoreType.DMA((2,)),
         ],
-        out_specs=vmem,
-        scratch_shapes=[pltpu.VMEM((time, SLOTS, chunk), F32), pltpu.VMEM((time, SLOTS, chunk), F32)],
-        compiler_params=pltpu.CompilerParams(vmem_limit_bytes=24 * 1024 * 1024),
+        compiler_params=pltpu.CompilerParams(vmem_limit_bytes=(8 << 20) + time * (136 << 10) + time * 20 * chunk),
         cost_estimate=pl.CostEstimate(
             flops=8 * time * SLOTS * chunk * states,
             bytes_accessed=4 * 1024 * 1024,
             transcendentals=time * SLOTS * chunk * states,
         ),
-    )(after, coefs, steps, u, jnp.swapaxes(decay_log, 1, 2), skip.reshape(2, 2, width))
-
-
-def end_kernel(cols_ref, gate_ref, gain_ref, weight_ref, *refs):
-    row_refs, out_ref, gated_ref = refs[:-2], refs[-2], refs[-1]
+    )(after, coefs, steps, u, jnp.swapaxes(decay_log, 1, 2), skip)
+
+
+def end_kernel(columns, gate_ref, gain_ref, weight_ref, *refs):
+    col_refs, row_refs, out_ref, gated_ref = refs[:columns], refs[columns:-2], refs[-2], refs[-1]
     height, width, channels = out_ref.shape
     size = row_refs[0].shape[0]
     lines = size // width
     swap = flip("col") ^ lax.axis_index("col")
-    turn = flip("row") * (width // lax.axis_size("row"))
+    turn = (flip("row") ^ lax.axis_index("row")) * (width // lax.axis_size("row"))
     row = rows_of(height * width)
     line = (row >> bits(width)) ^ (swap * lines)
     source = (((row & (width - 1)) ^ turn) << bits(height)) + line
     rows = jnp.concatenate([row_ref[...] for row_ref in row_refs], axis=0)
-    combined = layer_norm(rows.astype(F32) + dot(one_hot([source], height * width), cols_ref[...]), gain_ref[...][None])
+    columns = jnp.concatenate([col_ref[...] for col_ref in col_refs], axis=0)
+    combined = layer_norm(rows.astype(F32) + dot(one_hot([source], height * width), columns), gain_ref[...][None])
     for part in range(len(row_refs)):
         cells = pl.ds(pl.multiple_of((part ^ swap) * size, size), size)
         gate = gate_ref[cells].astype(F32)
@@ -454,22 +501,26 @@
 
 def swap_blocks(blocks, axis):
     count = lax.axis_size(axis)
-    blocks = list(blocks)
-    return blocks[:1] + [lax.ppermute(blocks[k], axis, [(i, i ^ k) for i in range(count)]) for k in range(1, count)]
-
-
-def pick_kernel(axis, after_ref, x_ref, out_ref):
+    found = {k: lax.ppermute(blocks[k], axis, [(i, i ^ k) for i in range(count)]) for k in range(count - 1, 0, -1)}
+    return [blocks[0]] + [found[k] for k in range(1, count)]
+
+
+def pick_kernel(axis, after_ref, *refs):
+    x_refs, out_ref = refs[:-1], refs[-1]
     place = lax.axis_index(axis) ^ flip(axis)
-    out_ref[...] = x_ref[:, jnp.where(place == 0, 1, x_ref.shape[1] - 2)]
-
-
-def pick(axis, after, x):
+    line = jnp.where(place == 0, 1, x_refs[0].shape[0] - 2)
+    for part, x_ref in enumerate(x_refs):
+        out_ref[part] = x_ref[line]
+
+
+def pick(axis, after, xs):
     return pl.pallas_call(
         functools.partial(pick_kernel, axis),
-        out_shape=jax.ShapeDtypeStruct((x.shape[0],) + x.shape[2:], x.dtype),
-        in_specs=[pl.BlockSpec(memory_space=pl.ANY), pl.BlockSpec(memory_space=pltpu.VMEM)],
+        out_shape=jax.ShapeDtypeStruct((len(xs),) + xs[0].shape[1:], xs[0].dtype),
+        in_specs=[pl.BlockSpec(memory_space=pl.ANY)] + [pl.BlockSpec(memory_space=pltpu.VMEM)] * len(xs),
         out_specs=pl.BlockSpec(memory_space=pltpu.VMEM),
-    )(after, x)
+        compiler_params=pltpu.CompilerParams(vmem_limit_bytes=4 * 1024 * 1024),
+    )(after, *xs)
 
 
 def seam_of(axis, line):
@@ -506,13 +557,17 @@
     col_lines = width // lax.axis_size("row")
 
     rows, cols = lax.axis_size("row"), lax.axis_size("col")
-    normed, col_send, *row_send = pl.pallas_call(
-        cut_kernel,
-        out_shape=[
-            jax.ShapeDtypeStruct((tokens, channels), BF16),
-            jax.ShapeDtypeStruct((rows, col_lines + 2, height, channels), BF16),
-        ]
+    vmem = pl.BlockSpec(memory_space=pltpu.VMEM)
+    normed, *sends = pl.pallas_call(
+        functools.partial(cut_kernel, rows),
+        out_shape=[jax.ShapeDtypeStruct((tokens, channels), BF16)]
+        + [jax.ShapeDtypeStruct((col_lines + 2, height, channels), BF16)] * rows
         + [jax.ShapeDtypeStruct((row_lines + 2, width, channels), BF16)] * cols,
+        in_specs=[pl.BlockSpec(features.shape, lambda: (0, 0, 0)), pl.BlockSpec((channels,), lambda: (0,))],
+        out_specs=[vmem] * (1 + rows + cols),
+        scratch_shapes=[pltpu.VMEM((tokens, channels), BF16)],
+        compiler_params=pltpu.CompilerParams(vmem_limit_bytes=12 * 1024 * 1024),
+        cost_estimate=pl.CostEstimate(flops=6_000_000_000, bytes_accessed=2 << 20, transcendentals=tokens),
     )(features, norm_gain)
     weights = (in_weight, conv_weight, conv_bias, proj_weight, step_weight, step_bias, decay_log, skip_gain)
     gate = pl.pallas_call(
@@ -524,26 +579,27 @@
             pl.BlockSpec((channels, inner), lambda i: (0, 1)),
         ],
         out_specs=pl.BlockSpec((tokens, inner), lambda i: (0, 0)),
+        compiler_params=pltpu.CompilerParams(vmem_limit_bytes=12 * 1024 * 1024),
         cost_estimate=pl.CostEstimate(flops=2 * tokens * channels * inner, bytes_accessed=1 << 20, transcendentals=0),
     )(normed, in_weight)
 
-    row_x = swap_blocks(row_send, "col")
-    col_x = lax.all_to_all(col_send, "row", 0, 0, tiled=True)
-    start = lax.axis_index("col") == flip("col")
-    row_seam = seam_of("col", jnp.stack([jnp.where(start, x[1], x[-2]) for x in row_x]))
+    row_x = swap_blocks(sends[rows:], "col")
+    col_x = swap_blocks(sends[:rows], "row")
+    row_seam = seam_of("col", pick("col", normed, row_x))
     row_steps = prepare("col", normed, row_x, row_seam, *weights)
     col_seam = seam_of("row", pick("row", row_steps[0], col_x))
-    col_steps = prepare("row", row_steps[0], [col_x], col_seam, *weights)
+    col_steps = prepare("row", row_steps[0], col_x, col_seam, *weights)
     col_y = scan("row", normed, *col_steps, decay_log, skip_gain)
-    (joined,) = join("row", col_y, rows, col_lines, height, inner, normed, False)
-    col_y = lax.all_to_all(joined.reshape(rows, -1, inner), "row", 0, 0, tiled=True)
-    row_y = scan("col", joined, *row_steps, decay_log, skip_gain)
-    row_y = swap_blocks(join("col", row_y, cols, row_lines, width, inner, col_y, True), "col")
+    joined = join("row", col_y, rows, col_lines, height, inner, normed)
+    col_y = swap_blocks(joined, "row")
+    row_y = scan("col", joined[0], *row_steps, decay_log, skip_gain)
+    row_y = swap_blocks(join("col", row_y, cols, row_lines, width, inner, col_y[-1]), "col")
     return pl.pallas_call(
-        end_kernel,
+        functools.partial(end_kernel, rows),
         out_shape=jax.ShapeDtypeStruct(features.shape, BF16),
         scratch_shapes=[pltpu.VMEM((tokens, inner), BF16)],
-    )(col_y.reshape(tokens, inner), gate, out_gain, out_weight, *row_y)
+        compiler_params=pltpu.CompilerParams(vmem_limit_bytes=16 * 1024 * 1024),
+    )(gate, out_gain, out_weight, *col_y, *row_y)
 
 
 def solution(mesh):

time: 87.1 us -> 74.9 us (0.86)
  local copies, waits for them, and re-layouts: 17 us -> 1.79 us
  starting transfers between devices: 24.7 us -> 36.6 us
  Pallas kernels: 40.5 us -> 33.5 us
    ppermute x6 -> x20, starting transfers between devices: 4.93 us -> 35 us  [swap_blocks(): lax.ppermute(blocks[k], axis, [(i, i ^ k) for i in range(count)])]
    all_to_all x2 -> x0, starting transfers between devices: 18.5 us -> none  [the longest x1 12.4 us: local(): lax.all_to_all(joined.reshape(rows, -1, inner), 'row', 0, 0, tiled=True)]
    unnamed x54 -> x24, local copies, waits for them, and re-layouts: 15.6 us -> 1.79 us
    pallas_call x6, Pallas kernels: 34.7 us -> 31.9 us  [the longest x2 19.6 us: scan(): pl.pallas_call(functools.partial(scan_kernel, axis), out_shape=jax.ShapeD...]
    pallas_call x1, Pallas kernels: 2.3 us -> 0.36 us  [local(): pl.pallas_call(gate_kernel, out_shape=jax.ShapeDtypeStruct((tokens, inner...]
    pallas_call x1 -> x2, Pallas kernels: 1.64 us -> 0.05 us  [pick(): pl.pallas_call(functools.partial(pick_kernel, axis), out_shape=jax.ShapeD...]
    reshape x3 -> x0, local copies, waits for them, and re-layouts: 1.44 us -> none  [the longest x1 0.73 us: prepare(): step_bias.reshape(2, 2, width)]
    ppermute x6 -> x20, waiting for transfers between devices: 2.79 us -> 2.56 us  [swap_blocks(): lax.ppermute(blocks[k], axis, [(i, i ^ k) for i in range(count)])]
  transfers between devices with their start and end apart: 10 -> 22, of which waited for: 2 -> 2; matrix products, arithmetic and copies ran while one was open for 3% -> 0% of each run, Pallas kernels for 17% -> 19%
where the time goes in v5:
time: 74.9 us; the launch traced here: 74.7 us
  starting transfers between devices  36.6 us (49%)
  Pallas kernels  33.5 us (45%)
  waiting for transfers between devices  2.57 us (3%)
  local copies, waits for them, and re-layouts  1.79 us (2%)
    ppermute x20, starting transfers between devices, swap_blocks(): lax.ppermute(blocks[k], axis, [(i, i ^ k) for i in range(count)])  35 us
    pallas_call x2, Pallas kernels, scan(): pl.pallas_call(functools.partial(scan_kernel, axis), out_shape=jax.ShapeD...  19.6 us
    pallas_call x2, Pallas kernels, prepare(): pl.pallas_call(functools.partial(prepare_kernel, lines, axis), out_shape=...  10.1 us
    ppermute x20, waiting for transfers between devices, swap_blocks(): lax.ppermute(blocks[k], axis, [(i, i ^ k) for i in range(count)])  2.56 us
    unnamed x24, local copies, waits for them, and re-layouts  1.79 us
    pallas_call x1, Pallas kernels, local(): pl.pallas_call(functools.partial(end_kernel, rows), out_shape=jax.ShapeDt...  1.73 us
    ppermute x2, starting transfers between devices, seam_of(): return lax.ppermute(line, ('row', 'col'), pairs)  1.64 us
  transfers between devices with their start and end apart: 22, of which 2 were waited for; matrix products, arithmetic and copies ran while one was open for 0% of the time, Pallas kernels for 19%

profile of v5, /device:TPU:0, one launch (start us, length us, event | category | flops | bytes accessed | tf_op | source)
XLA Modules:
  0.0 74.7 jit_solution(5606648539595682486)
XLA Ops:
  0.0 1.1 %copy-done.5 = bf16[16,16,384]{2,1,0:T(8,128)(2,1)S(1)} copy-done((bf16[16,16,384]{2,1,0:T(8,128)(2,1)S(1)}, bf16[16,16,384]{2,1,0:T(8,128)(2,1)}, u32[]{:S(2)}) %copy-start.5) | copy-done | bytes 196632
  1.1 0.7 copy-done.11
  2.8 2.6 %collective-permute-start.1 = (bf16[6,16,384]{2,1,0:T(8,128)(2,1)S(1)}, bf16[6,16,384]{2,1,0:T(8,128)(2,1)S(1)}, u32[]{:S(2)}, u32[]{:S(2)}) collective-permute-start(bf16[6,16,384]{2,1,0:T(8,128)(2,1)S(1)} %get-tuple-element.39), channel_id=1, source_target_pairs={{0,2},{1,3},{2,0},{3,1},{4,6},{5,7},{6,4},{7,5},{8,10},{9,11},{10,... | collective-permute-start | bytes 221192 | tf_op jit(solution)/shard_map/ppermute | solution.py:504
  5.4 4.8 %collective-permute-start.10 = (bf16[4,16,384]{2,1,0:T(8,128)(2,1)S(1)}, bf16[4,16,384]{2,1,0:T(8,128)(2,1)S(1)}, u32[]{:S(2)}, u32[]{:S(2)}) collective-permute-start(bf16[4,16,384]{2,1,0:T(8,128)(2,1)S(1)} %get-tuple-element.49), channel_id=1, source_target_pairs={{0,28},{4,24},{8,20},{12,16},{16,12},{20,8},{24,4},{28,0},{1,29},{... | collective-permute-start | bytes 147464 | tf_op jit(solution)/shard_map/ppermute | solution.py:504
  10.8 0.7 collective-permute-start.3
  11.4 4.3 %collective-permute-start.5 = (bf16[4,16,384]{2,1,0:T(8,128)(2,1)S(1)}, bf16[4,16,384]{2,1,0:T(8,128)(2,1)S(1)}, u32[]{:S(2)}, u32[]{:S(2)}) collective-permute-start(bf16[4,16,384]{2,1,0:T(8,128)(2,1)S(1)} %get-tuple-element.44), channel_id=1, source_target_pairs={{0,8},{4,12},{8,0},{12,4},{16,24},{20,28},{24,16},{28,20},{1,9},{5... | collective-permute-start | bytes 147464 | tf_op jit(solution)/shard_map/ppermute | solution.py:504
  15.7 0.6 collective-permute-start.6
  16.3 2.6 %collective-permute-start.7 = (bf16[4,16,384]{2,1,0:T(8,128)(2,1)S(1)}, bf16[4,16,384]{2,1,0:T(8,128)(2,1)S(1)}, u32[]{:S(2)}, u32[]{:S(2)}) collective-permute-start(bf16[4,16,384]{2,1,0:T(8,128)(2,1)S(1)} %get-tuple-element.46), channel_id=1, source_target_pairs={{0,16},{4,20},{8,24},{12,28},{16,0},{20,4},{24,8},{28,12},{1,17},{... | collective-permute-start | bytes 147464 | tf_op jit(solution)/shard_map/ppermute | solution.py:504
  18.9 0.7 collective-permute-start.8
  19.6 3.1 %collective-permute-start.9 = (bf16[4,16,384]{2,1,0:T(8,128)(2,1)S(1)}, bf16[4,16,384]{2,1,0:T(8,128)(2,1)S(1)}, u32[]{:S(2)}, u32[]{:S(2)}) collective-permute-start(bf16[4,16,384]{2,1,0:T(8,128)(2,1)S(1)} %get-tuple-element.48), channel_id=1, source_target_pairs={{0,24},{4,28},{8,16},{12,20},{16,8},{20,12},{24,0},{28,4},{1,25},{... | collective-permute-start | bytes 147464 | tf_op jit(solution)/shard_map/ppermute | solution.py:504
  22.7 4.3 %shard_map.121 = (f32[64,8,128]{2,1,0:T(8,128)S(1)}, f32[64,8,768]{2,1,0:T(8,128)S(1)}, f32[64,8,768]{2,1,0:T(8,128)S(1)}) custom-call(bf16[256,384]{1,0:T(8,128)(2,1)S(1)} %get-tuple-element.36.norm_ref.after_ref, bf16[6,16,384]{2,1,0:T(8,128)(2,1)S(1)} %get-tuple-element.37.refs_0_, bf16[6,16,384]{2,1,0:T(8,128)(2,1)S(1)} %collective-permute-done.refs_1_, ...), custom_call_target="tpu_custom_call" | custom-call | flops 1711276032 | bytes 4194304 | tf_op jit(solution)/shard_map/pallas_call | solution.py:415
  27.2 1.0 %collective-permute-start.11 = (bf16[8,16,384]{2,1,0:T(8,128)(2,1)S(1)}, bf16[8,16,384]{2,1,0:T(8,128)(2,1)S(1)}, u32[]{:S(2)}, u32[]{:S(2)}) collective-permute-start(bf16[8,16,384]{2,1,0:T(8,128)(2,1)S(1)} %shard_map.122), channel_id=1, source_target_pairs={{28,29},{1,2},{30,31},{29,28},{2,1},{31,30}} | collective-permute-start | bytes 294920 | tf_op jit(solution)/shard_map/ppermute | solution.py:536
  28.1 5.8 %shard_map.123 = (f32[128,8,128]{2,1,0:T(8,128)S(1)}, f32[128,8,384]{2,1,0:T(8,128)S(1)}, f32[128,8,384]{2,1,0:T(8,128)S(1)}) custom-call(f32[64,8,128]{2,1,0:T(8,128)S(1)} %get-tuple-element.41.after_ref.coef_ref, bf16[4,16,384]{2,1,0:T(8,128)(2,1)S(1)} %get-tuple-element.42.refs_0_, bf16[4,16,384]{2,1,0:T(8,128)(2,1)S(1)} %collective-permute-done.4.refs_1_, ...), custom_call_target="tpu_custom_call" | custom-call | flops 2818572288 | bytes 4194304 | tf_op jit(solution)/shard_map/pallas_call | solution.py:415
  34.0 10.5 %shard_map.124.scanned_ref = bf16[1024,384]{1,0:T(8,128)(2,1)S(1)} custom-call(bf16[256,384]{1,0:T(8,128)(2,1)S(1)} %get-tuple-element.36.norm_ref.after_ref, f32[128,8,128]{2,1,0:T(8,128)S(1)} %get-tuple-element.50.coef_ref, f32[128,8,384]{2,1,0:T(8,128)S(1)} %get-tuple-element.51.s_ref, f32[128,8,384]{2,1,0:T(8,128)S(1)} %get-tuple-element.52.u_ref, ...), custom_call_target="tpu_custom_call" | custom-call | flops 50331648 | bytes 4194304 | tf_op jit(solution)/shard_map/pallas_call | solution.py:459
  44.5 0.7 shard_map.125
  45.3 3.7 %collective-permute-start.18 = (bf16[32,768]{1,0:T(8,128)(2,1)S(1)}, bf16[32,768]{1,0:T(8,128)(2,1)S(1)}, u32[]{:S(2)}, u32[]{:S(2)}) collective-permute-start(bf16[32,768]{1,0:T(8,128)(2,1)S(1)} %get-tuple-element.60), channel_id=1, source_target_pairs={{0,28},{4,24},{8,20},{12,16},{16,12},{20,8},{24,4},{28,0},{1,29},{... | collective-permute-start | bytes 147464 | tf_op jit(solution)/shard_map/ppermute | solution.py:504
  48.9 3.5 %collective-permute-start.14 = (bf16[32,768]{1,0:T(8,128)(2,1)S(1)}, bf16[32,768]{1,0:T(8,128)(2,1)S(1)}, u32[]{:S(2)}, u32[]{:S(2)}) collective-permute-start(bf16[32,768]{1,0:T(8,128)(2,1)S(1)} %get-tuple-element.56), channel_id=1, source_target_pairs={{0,12},{4,8},{8,4},{12,0},{16,28},{20,24},{24,20},{28,16},{1,13},{... | collective-permute-start | bytes 147464 | tf_op jit(solution)/shard_map/ppermute | solution.py:504
  52.4 9.1 %shard_map.126.scanned_ref = bf16[512,768]{1,0:T(8,128)(2,1)S(1)} custom-call(bf16[32,768]{1,0:T(8,128)(2,1)S(1)} %get-tuple-element.53.after_ref.refs_0_, f32[64,8,128]{2,1,0:T(8,128)S(1)} %get-tuple-element.41.after_ref.coef_ref, f32[64,8,768]{2,1,0:T(8,128)S(1)} %get-tuple-element.61.s_ref, f32[64,8,768]{2,1,0:T(8,128)S(1)} %get-tuple-element.62.u_ref, ...), custom_call_target="tpu_custom_call" | custom-call | flops 50331648 | bytes 4194304 | tf_op jit(solution)/shard_map/pallas_call | solution.py:459
  62.0 2.6 %collective-permute-start.20 = (bf16[64,768]{1,0:T(8,128)(2,1)S(1)}, bf16[64,768]{1,0:T(8,128)(2,1)S(1)}, u32[]{:S(2)}, u32[]{:S(2)}) collective-permute-start(bf16[64,768]{1,0:T(8,128)(2,1)S(1)} %get-tuple-element.65), channel_id=1, source_target_pairs={{0,2},{1,3},{2,0},{3,1},{4,6},{5,7},{6,4},{7,5},{8,10},{9,11},{10,... | collective-permute-start | bytes 294920 | tf_op jit(solution)/shard_map/ppermute | solution.py:504
  64.8 1.5 %collective-permute-start.16 = (bf16[32,768]{1,0:T(8,128)(2,1)S(1)}, bf16[32,768]{1,0:T(8,128)(2,1)S(1)}, u32[]{:S(2)}, u32[]{:S(2)}) collective-permute-start(bf16[32,768]{1,0:T(8,128)(2,1)S(1)} %get-tuple-element.58), channel_id=1, source_target_pairs={{0,20},{4,16},{8,28},{12,24},{16,4},{20,0},{24,12},{28,8},{1,21},{... | collective-permute-start | bytes 147464 | tf_op jit(solution)/shard_map/ppermute | solution.py:504
  66.3 3.8 %collective-permute-start.17 = (bf16[32,768]{1,0:T(8,128)(2,1)S(1)}, bf16[32,768]{1,0:T(8,128)(2,1)S(1)}, u32[]{:S(2)}, u32[]{:S(2)}) collective-permute-start(bf16[32,768]{1,0:T(8,128)(2,1)S(1)} %get-tuple-element.59), channel_id=1, source_target_pairs={{0,24},{4,28},{8,16},{12,20},{16,8},{20,12},{24,0},{28,4},{1,25},{... | collective-permute-start | bytes 147464 | tf_op jit(solution)/shard_map/ppermute | solution.py:504
  70.4 1.6 %collective-permute-done.16.refs_5_ = bf16[32,768]{1,0:T(8,128)(2,1)S(1)} collective-permute-done((bf16[32,768]{1,0:T(8,128)(2,1)S(1)}, bf16[32,768]{1,0:T(8,128)(2,1)S(1)}, u32[]{:S(2)}, u32[]{:S(2)}) %collective-permute-start.16) | collective-permute-done | bytes 49184 | tf_op jit(solution)/shard_map/ppermute | solution.py:504
  72.0 0.9 %collective-permute-done.17.refs_6_ = bf16[32,768]{1,0:T(8,128)(2,1)S(1)} collective-permute-done((bf16[32,768]{1,0:T(8,128)(2,1)S(1)}, bf16[32,768]{1,0:T(8,128)(2,1)S(1)}, u32[]{:S(2)}, u32[]{:S(2)}) %collective-permute-start.17) | collective-permute-done | bytes 49184 | tf_op jit(solution)/shard_map/ppermute | solution.py:504
  73.0 1.7 %shard_map.128 = bf16[16,16,384]{2,1,0:T(8,128)(2,1)} custom-call(bf16[256,768]{1,0:T(8,128)(2,1)S(1)} %shard_map.119.gate_ref, f32[768]{0:T(1024)S(1)} %copy-done.2, bf16[768,384]{1,0:T(8,128)(2,1)S(1)} %copy-done.1, bf16[32,768]{1,0:T(8,128)(2,1)S(1)} %get-tuple-element.53.after_ref.refs_0_, bf16[32,768]{1,0:T(8,128)(2,1)S(1)} %collective-permute-done.12.refs_1_, ...), custom_call_target="tpu_custom_call" | custom-call | tf_op jit(solution)/shard_map/pallas_call | solution.py:597
  (55 shorter events, 2.7 us)
Async XLA Ops:
  0.0 22.7 %copy-start = (bf16[384,1536]{1,0:T(8,128)(2,1)S(1)}, bf16[384,1536]{1,0:T(8,128)(2,1)}, u32[]{:S(2)}) copy-start(bf16[384,1536]{1,0:T(8,128)(2,1)} %refs_9_.3) | copy-start | bytes 3538948
  0.0 22.7 %copy-start.4 = (f32[4,24,768]{2,1,0:T(8,128)S(1)}, f32[4,24,768]{2,1,0:T(8,128)}, u32[]{:S(2)}) copy-start(f32[4,24,768]{2,1,0:T(8,128)} %refs_13_.1) | copy-start | bytes 884740
  2.3 8.5 %collective-permute-start = (bf16[6,16,384]{2,1,0:T(8,128)(2,1)S(1)}, bf16[6,16,384]{2,1,0:T(8,128)(2,1)S(1)}, u32[]{:S(2)}, u32[]{:S(2)}) collective-permute-start(bf16[6,16,384]{2,1,0:T(8,128)(2,1)S(1)} %get-tuple-element.38), channel_id=1, source_target_pairs={{0,1},{1,0},{2,3},{3,2},{4,5},{5,4},{6,7},{7,6},{8,9},{9,8},{10,11... | collective-permute-start | bytes 221192 | tf_op jit(solution)/shard_map/ppermute | solution.py:504
  2.8 7.9 %collective-permute-start.1 = (bf16[6,16,384]{2,1,0:T(8,128)(2,1)S(1)}, bf16[6,16,384]{2,1,0:T(8,128)(2,1)S(1)}, u32[]{:S(2)}, u32[]{:S(2)}) collective-permute-start(bf16[6,16,384]{2,1,0:T(8,128)(2,1)S(1)} %get-tuple-element.39), channel_id=1, source_target_pairs={{0,2},{1,3},{2,0},{3,1},{4,6},{5,7},{6,4},{7,5},{8,10},{9,11},{10,... | collective-permute-start | bytes 221192 | tf_op jit(solution)/shard_map/ppermute | solution.py:504
  5.4 5.4 %collective-permute-start.2 = (bf16[6,16,384]{2,1,0:T(8,128)(2,1)S(1)}, bf16[6,16,384]{2,1,0:T(8,128)(2,1)S(1)}, u32[]{:S(2)}, u32[]{:S(2)}) collective-permute-start(bf16[6,16,384]{2,1,0:T(8,128)(2,1)S(1)} %get-tuple-element.40), channel_id=1, source_target_pairs={{0,3},{1,2},{2,1},{3,0},{4,7},{5,6},{6,5},{7,4},{8,11},{9,10},{10,... | collective-permute-start | bytes 221192 | tf_op jit(solution)/shard_map/ppermute | solution.py:504
  5.4 10.9 %collective-permute-start.10 = (bf16[4,16,384]{2,1,0:T(8,128)(2,1)S(1)}, bf16[4,16,384]{2,1,0:T(8,128)(2,1)S(1)}, u32[]{:S(2)}, u32[]{:S(2)}) collective-permute-start(bf16[4,16,384]{2,1,0:T(8,128)(2,1)S(1)} %get-tuple-element.49), channel_id=1, source_target_pairs={{0,28},{4,24},{8,20},{12,16},{16,12},{20,8},{24,4},{28,0},{1,29},{... | collective-permute-start | bytes 147464 | tf_op jit(solution)/shard_map/ppermute | solution.py:504
  10.2 8.7 %collective-permute-start.4 = (bf16[4,16,384]{2,1,0:T(8,128)(2,1)S(1)}, bf16[4,16,384]{2,1,0:T(8,128)(2,1)S(1)}, u32[]{:S(2)}, u32[]{:S(2)}) collective-permute-start(bf16[4,16,384]{2,1,0:T(8,128)(2,1)S(1)} %get-tuple-element.43), channel_id=1, source_target_pairs={{0,4},{4,0},{8,12},{12,8},{16,20},{20,16},{24,28},{28,24},{1,5},{5... | collective-permute-start | bytes 147464 | tf_op jit(solution)/shard_map/ppermute | solution.py:504
  10.8 8.9 %collective-permute-start.3 = (bf16[4,16,384]{2,1,0:T(8,128)(2,1)S(1)}, bf16[4,16,384]{2,1,0:T(8,128)(2,1)S(1)}, u32[]{:S(2)}, u32[]{:S(2)}) collective-permute-start(bf16[4,16,384]{2,1,0:T(8,128)(2,1)S(1)} %shard_map.120), channel_id=1, source_target_pairs={{3,7},{4,8},{11,15},{12,16},{19,23},{20,24},{27,31},{7,3},{8,4},{1... | collective-permute-start | bytes 147464 | tf_op jit(solution)/shard_map/ppermute | solution.py:536
  11.4 15.6 %collective-permute-start.5 = (bf16[4,16,384]{2,1,0:T(8,128)(2,1)S(1)}, bf16[4,16,384]{2,1,0:T(8,128)(2,1)S(1)}, u32[]{:S(2)}, u32[]{:S(2)}) collective-permute-start(bf16[4,16,384]{2,1,0:T(8,128)(2,1)S(1)} %get-tuple-element.44), channel_id=1, source_target_pairs={{0,8},{4,12},{8,0},{12,4},{16,24},{20,28},{24,16},{28,20},{1,9},{5... | collective-permute-start | bytes 147464 | tf_op jit(solution)/shard_map/ppermute | solution.py:504
  15.7 11.3 %collective-permute-start.6 = (bf16[4,16,384]{2,1,0:T(8,128)(2,1)S(1)}, bf16[4,16,384]{2,1,0:T(8,128)(2,1)S(1)}, u32[]{:S(2)}, u32[]{:S(2)}) collective-permute-start(bf16[4,16,384]{2,1,0:T(8,128)(2,1)S(1)} %get-tuple-element.45), channel_id=1, source_target_pairs={{0,12},{4,8},{8,4},{12,0},{16,28},{20,24},{24,20},{28,16},{1,13},{... | collective-permute-start | bytes 147464 | tf_op jit(solution)/shard_map/ppermute | solution.py:504
  16.3 10.7 %collective-permute-start.7 = (bf16[4,16,384]{2,1,0:T(8,128)(2,1)S(1)}, bf16[4,16,384]{2,1,0:T(8,128)(2,1)S(1)}, u32[]{:S(2)}, u32[]{:S(2)}) collective-permute-start(bf16[4,16,384]{2,1,0:T(8,128)(2,1)S(1)} %get-tuple-element.46), channel_id=1, source_target_pairs={{0,16},{4,20},{8,24},{12,28},{16,0},{20,4},{24,8},{28,12},{1,17},{... | collective-permute-start | bytes 147464 | tf_op jit(solution)/shard_map/ppermute | solution.py:504
  18.9 8.1 %collective-permute-start.8 = (bf16[4,16,384]{2,1,0:T(8,128)(2,1)S(1)}, bf16[4,16,384]{2,1,0:T(8,128)(2,1)S(1)}, u32[]{:S(2)}, u32[]{:S(2)}) collective-permute-start(bf16[4,16,384]{2,1,0:T(8,128)(2,1)S(1)} %get-tuple-element.47), channel_id=1, source_target_pairs={{0,20},{4,16},{8,28},{12,24},{16,4},{20,0},{24,12},{28,8},{1,21},{... | collective-permute-start | bytes 147464 | tf_op jit(solution)/shard_map/ppermute | solution.py:504
  19.6 7.4 %collective-permute-start.9 = (bf16[4,16,384]{2,1,0:T(8,128)(2,1)S(1)}, bf16[4,16,384]{2,1,0:T(8,128)(2,1)S(1)}, u32[]{:S(2)}, u32[]{:S(2)}) collective-permute-start(bf16[4,16,384]{2,1,0:T(8,128)(2,1)S(1)} %get-tuple-element.48), channel_id=1, source_target_pairs={{0,24},{4,28},{8,16},{12,20},{16,8},{20,12},{24,0},{28,4},{1,25},{... | collective-permute-start | bytes 147464 | tf_op jit(solution)/shard_map/ppermute | solution.py:504
  27.2 1.0 %collective-permute-start.11 = (bf16[8,16,384]{2,1,0:T(8,128)(2,1)S(1)}, bf16[8,16,384]{2,1,0:T(8,128)(2,1)S(1)}, u32[]{:S(2)}, u32[]{:S(2)}) collective-permute-start(bf16[8,16,384]{2,1,0:T(8,128)(2,1)S(1)} %shard_map.122), channel_id=1, source_target_pairs={{28,29},{1,2},{30,31},{29,28},{2,1},{31,30}} | collective-permute-start | bytes 294920 | tf_op jit(solution)/shard_map/ppermute | solution.py:536
  45.3 16.3 %collective-permute-start.18 = (bf16[32,768]{1,0:T(8,128)(2,1)S(1)}, bf16[32,768]{1,0:T(8,128)(2,1)S(1)}, u32[]{:S(2)}, u32[]{:S(2)}) collective-permute-start(bf16[32,768]{1,0:T(8,128)(2,1)S(1)} %get-tuple-element.60), channel_id=1, source_target_pairs={{0,28},{4,24},{8,20},{12,16},{16,12},{20,8},{24,4},{28,0},{1,29},{... | collective-permute-start | bytes 147464 | tf_op jit(solution)/shard_map/ppermute | solution.py:504
  48.9 13.1 %collective-permute-start.12 = (bf16[32,768]{1,0:T(8,128)(2,1)S(1)}, bf16[32,768]{1,0:T(8,128)(2,1)S(1)}, u32[]{:S(2)}, u32[]{:S(2)}) collective-permute-start(bf16[32,768]{1,0:T(8,128)(2,1)S(1)} %get-tuple-element.54), channel_id=1, source_target_pairs={{0,4},{4,0},{8,12},{12,8},{16,20},{20,16},{24,28},{28,24},{1,5},{5... | collective-permute-start | bytes 147464 | tf_op jit(solution)/shard_map/ppermute | solution.py:504
  48.9 15.7 %collective-permute-start.13 = (bf16[32,768]{1,0:T(8,128)(2,1)S(1)}, bf16[32,768]{1,0:T(8,128)(2,1)S(1)}, u32[]{:S(2)}, u32[]{:S(2)}) collective-permute-start(bf16[32,768]{1,0:T(8,128)(2,1)S(1)} %get-tuple-element.55), channel_id=1, source_target_pairs={{0,8},{4,12},{8,0},{12,4},{16,24},{20,28},{24,16},{28,20},{1,9},{5... | collective-permute-start | bytes 147464 | tf_op jit(solution)/shard_map/ppermute | solution.py:504
  48.9 15.9 %collective-permute-start.14 = (bf16[32,768]{1,0:T(8,128)(2,1)S(1)}, bf16[32,768]{1,0:T(8,128)(2,1)S(1)}, u32[]{:S(2)}, u32[]{:S(2)}) collective-permute-start(bf16[32,768]{1,0:T(8,128)(2,1)S(1)} %get-tuple-element.56), channel_id=1, source_target_pairs={{0,12},{4,8},{8,4},{12,0},{16,28},{20,24},{24,20},{28,16},{1,13},{... | collective-permute-start | bytes 147464 | tf_op jit(solution)/shard_map/ppermute | solution.py:504
  52.4 13.8 %collective-permute-start.15 = (bf16[32,768]{1,0:T(8,128)(2,1)S(1)}, bf16[32,768]{1,0:T(8,128)(2,1)S(1)}, u32[]{:S(2)}, u32[]{:S(2)}) collective-permute-start(bf16[32,768]{1,0:T(8,128)(2,1)S(1)} %get-tuple-element.57), channel_id=1, source_target_pairs={{0,16},{4,20},{8,24},{12,28},{16,0},{20,4},{24,8},{28,12},{1,17},{... | collective-permute-start | bytes 147464 | tf_op jit(solution)/shard_map/ppermute | solution.py:504
  62.0 11.0 %collective-permute-start.19 = (bf16[64,768]{1,0:T(8,128)(2,1)S(1)}, bf16[64,768]{1,0:T(8,128)(2,1)S(1)}, u32[]{:S(2)}, u32[]{:S(2)}) collective-permute-start(bf16[64,768]{1,0:T(8,128)(2,1)S(1)} %get-tuple-element.64), channel_id=1, source_target_pairs={{0,1},{1,0},{2,3},{3,2},{4,5},{5,4},{6,7},{7,6},{8,9},{9,8},{10,11... | collective-permute-start | bytes 294920 | tf_op jit(solution)/shard_map/ppermute | solution.py:504
  62.0 10.9 %collective-permute-start.20 = (bf16[64,768]{1,0:T(8,128)(2,1)S(1)}, bf16[64,768]{1,0:T(8,128)(2,1)S(1)}, u32[]{:S(2)}, u32[]{:S(2)}) collective-permute-start(bf16[64,768]{1,0:T(8,128)(2,1)S(1)} %get-tuple-element.65), channel_id=1, source_target_pairs={{0,2},{1,3},{2,0},{3,1},{4,6},{5,7},{6,4},{7,5},{8,10},{9,11},{10,... | collective-permute-start | bytes 294920 | tf_op jit(solution)/shard_map/ppermute | solution.py:504
  64.7 8.3 %collective-permute-start.21 = (bf16[64,768]{1,0:T(8,128)(2,1)S(1)}, bf16[64,768]{1,0:T(8,128)(2,1)S(1)}, u32[]{:S(2)}, u32[]{:S(2)}) collective-permute-start(bf16[64,768]{1,0:T(8,128)(2,1)S(1)} %get-tuple-element.66), channel_id=1, source_target_pairs={{0,3},{1,2},{2,1},{3,0},{4,7},{5,6},{6,5},{7,4},{8,11},{9,10},{10,... | collective-permute-start | bytes 294920 | tf_op jit(solution)/shard_map/ppermute | solution.py:504
  64.8 7.3 %collective-permute-start.16 = (bf16[32,768]{1,0:T(8,128)(2,1)S(1)}, bf16[32,768]{1,0:T(8,128)(2,1)S(1)}, u32[]{:S(2)}, u32[]{:S(2)}) collective-permute-start(bf16[32,768]{1,0:T(8,128)(2,1)S(1)} %get-tuple-element.58), channel_id=1, source_target_pairs={{0,20},{4,16},{8,28},{12,24},{16,4},{20,0},{24,12},{28,8},{1,21},{... | collective-permute-start | bytes 147464 | tf_op jit(solution)/shard_map/ppermute | solution.py:504
  66.3 6.7 %collective-permute-start.17 = (bf16[32,768]{1,0:T(8,128)(2,1)S(1)}, bf16[32,768]{1,0:T(8,128)(2,1)S(1)}, u32[]{:S(2)}, u32[]{:S(2)}) collective-permute-start(bf16[32,768]{1,0:T(8,128)(2,1)S(1)} %get-tuple-element.59), channel_id=1, source_target_pairs={{0,24},{4,28},{8,16},{12,20},{16,8},{20,12},{24,0},{28,4},{1,25},{... | collective-permute-start | bytes 147464 | tf_op jit(solution)/shard_map/ppermute | solution.py:504
  (10 other events, 124.0 us)

commit v6 on v5

--- a/solution.py
+++ b/solution.py
@@ -50,7 +50,7 @@
 
 
 def cut_kernel(columns, feat_ref, gain_ref, norm_ref, *refs):
-    col_refs, row_refs, turned_ref = refs[:columns], refs[columns:-1], refs[-1]
+    col_refs, beside_ref, row_refs, turned_ref = refs[: columns // 2], refs[columns // 2], refs[columns // 2 + 1 : -1], refs[-1]
     height, width, channels = feat_ref.shape
     tile = layer_norm(feat_ref[...].reshape(height * width, channels).astype(F32), gain_ref[...][None]).astype(BF16)
     norm_ref[...] = tile
@@ -67,14 +67,25 @@
     turned_ref[...] = turned
     reach = col_refs[0].shape[0]
     turn = flip("row") ^ lax.axis_index("row")
-    for part, col_ref in enumerate(col_refs):
+    for part in range(columns):
         for line in range(reach):
             at = jnp.clip((part ^ turn) * (reach - 2) + line - 1, 0, width - 1)
-            col_ref[line] = turned_ref[pl.ds(pl.multiple_of(at * height, height), height)]
+            found = turned_ref[pl.ds(pl.multiple_of(at * height, height), height)]
+            if part & 1:
+                beside_ref[part >> 1, line] = found
+            else:
+                col_refs[part >> 1][line] = found
 
 
 def gate_kernel(norm_ref, weight_ref, gate_ref):
     gate_ref[...] = dot(norm_ref[...], weight_ref[...]).astype(BF16)
+
+
+def views(refs, rank):
+    found = []
+    for ref in refs:
+        found += [ref] if len(ref.shape) == rank else [ref.at[k] for k in range(ref.shape[0])]
+    return found
 
 
 def by_slot(halves, rows):
@@ -93,54 +104,32 @@
     after_ref,
     *refs,
 ):
-    x_refs, refs = refs[:-23], refs[-23:]
+    x_refs, refs = views(refs[:-16], 3), refs[-16:]
     (
         seam_ref,
-        weight_hbm,
-        conv_hbm,
-        conv_bias_hbm,
-        proj_hbm,
-        step_hbm,
-        bias_hbm,
-        proj_out_ref,
-        s_ref,
-        v_ref,
         weight_ref,
         conv_ref,
         conv_bias_ref,
         proj_raw_ref,
         step_raw_ref,
         bias_raw_ref,
+        proj_out_ref,
+        s_ref,
+        v_ref,
         token_ref,
         inner_ref,
         active_ref,
         proj_ref,
         step_ref,
         bias_ref,
-        copied,
     ) = refs
-    pair = pl.ds(0 if axis == "col" else 2, 2)
-    copies = [
-        pltpu.make_async_copy(source, to, copied.at[k])
-        for k, (source, to) in enumerate(
-            [
-                (weight_hbm.at[:, pl.ds(0, weight_ref.shape[1])], weight_ref),
-                (conv_hbm, conv_ref),
-                (conv_bias_hbm, conv_bias_ref),
-                (proj_hbm.at[pair], proj_raw_ref),
-                (step_hbm.at[pair], step_raw_ref),
-                (bias_hbm, bias_raw_ref),
-            ]
-        )
-    ]
-    for copy in copies:
-        copy.start()
+    ks = (0, 1) if axis == "col" else (2, 3)
     parts, length, channels = seam_ref.shape
     reach = lines + 2
     states = (proj_raw_ref.shape[1] - RANK) // 2
     time = parts * length
     low = time // SLOTS
-    width = weight_ref.shape[1]
+    width = weight_ref.shape[1] // 2
     chunk = s_ref.shape[2]
     halves = width // chunk
     slot_lines = SLOTS // (2 * halves)
@@ -160,9 +149,7 @@
             missing = place == (0 if line == 0 else lax.axis_size(axis) - 1)
             x = jnp.where(missing, seam_ref[...].reshape(time, channels), x)
         token_ref[line * time : (line + 1) * time] = dot(order, x).astype(BF16)
-    for copy in copies:
-        copy.wait()
-    inner = dot(token_ref[...], weight_ref[...]).astype(BF16).astype(F32)
+    inner = dot(token_ref[...], weight_ref[:, :width]).astype(BF16).astype(F32)
     inner_ref[:, 1 : low + 1] = inner.reshape(reach, low, SLOTS, width)
     place = lax.broadcasted_iota(jnp.int32, (SLOTS, width), 0)
     for line in range(reach):
@@ -201,17 +188,17 @@
 
     lax.fori_loop(0, low // 2, convolve, 0)
 
-    bias_ref[...] = by_slot(halves, lambda half, way: bias_raw_ref[pair.start + way : pair.start + way + 1, half * chunk : (half + 1) * chunk])
+    bias_ref[...] = by_slot(halves, lambda half, way: bias_raw_ref[ks[way] : ks[way] + 1, half * chunk : (half + 1) * chunk])
     for half in range(halves):
         cells = slice(half * chunk, (half + 1) * chunk)
         for way in range(2):
             kind = slice((half * 2 + way) * LANES, (half * 2 + way + 1) * LANES)
-            w = proj_raw_ref[way, :, cells].astype(F32)
+            w = proj_raw_ref[ks[way], :, cells].astype(F32)
             ranks = w[:RANK]
             rest = jnp.zeros((LANES - 3 * RANK - 2 * states, chunk), F32)
             w = jnp.concatenate([ranks, ranks, ranks, w[RANK:], rest], axis=0)
             proj_ref[:, kind] = w.T.astype(BF16)
-            w = step_raw_ref[way, :, cells]
+            w = step_raw_ref[ks[way], :, cells]
             high = w.astype(BF16).astype(F32)
             rest = jnp.zeros((LANES - 3 * RANK, chunk), F32)
             step_ref[kind, :] = jnp.concatenate([high, high, w - high, rest], axis=0).astype(BF16)
@@ -268,32 +255,24 @@
     coef_ref,
     s_ref,
     u_ref,
-    decay_hbm,
-    skip_hbm,
+    decay_ref,
+    skip_raw_ref,
     out_ref,
     v_ref,
     y_ref,
     spread_ref,
-    decay_ref,
-    skip_raw_ref,
-    copied,
 ):
     time, _, chunk = s_ref.shape
     halves = decay_ref.shape[2] // chunk
     states = decay_ref.shape[1]
     groups = chunk // LANES
     at_once = max(1, 12 // groups)
-    unroll = 8
+    unroll = 16 if axis == "col" else 8
     laps = time // unroll
-
-    pair = pl.ds(0 if axis == "col" else 2, 2)
-    copies = [
-        pltpu.make_async_copy(decay_hbm.at[pair], decay_ref, copied.at[0]),
-        pltpu.make_async_copy(skip_hbm, skip_raw_ref, copied.at[1]),
-    ]
-    for copy in copies:
-        copy.start()
-
+    base2 = axis == "col"
+    power = jnp.exp2 if base2 else jnp.exp
+
+    ks = (0, 1) if axis == "col" else (2, 3)
     piece = 32
     row = lax.broadcasted_iota(jnp.int32, (2 * LANES, LANES), 0) & (LANES - 1)
     taken = [jnp.where(row == 3 * RANK + n, 1.0, 0.0).astype(BF16) for n in range(2 * states)]
@@ -310,8 +289,6 @@
         return 0
 
     lax.fori_loop(0, time // piece, spread, 0)
-    for copy in copies:
-        copy.wait()
     for first in range(0, states, at_once):
         rates = []
         for n in range(first, first + at_once):
@@ -319,15 +296,15 @@
             for g in range(groups):
                 rate = by_slot(
                     halves,
-                    lambda half, way: decay_ref[way, n : n + 1, half * chunk + g * LANES : half * chunk + (g + 1) * LANES],
+                    lambda half, way: decay_ref[ks[way], n : n + 1, half * chunk + g * LANES : half * chunk + (g + 1) * LANES],
                 )
-                rates[-1].append(-LOG2E * jnp.exp(rate))
+                rates[-1].append((-LOG2E if base2 else -1.0) * jnp.exp(rate))
         if first == 0:
             skips = [
                 by_slot(
                     halves,
                     lambda half, way: skip_raw_ref[
-                        pair.start + way : pair.start + way + 1, half * chunk + g * LANES : half * chunk + (g + 1) * LANES
+                        ks[way] : ks[way] + 1, half * chunk + g * LANES : half * chunk + (g + 1) * LANES
                     ],
                 )
                 for g in range(groups)
@@ -352,7 +329,7 @@
                         y = y_ref[t, :, cells]
                     for n in range(at_once):
                         k = n * groups + g
-                        h = jnp.exp2(step * rates[n][g]) * hidden[k] + value * enter[n]
+                        h = power(step * rates[n][g]) * hidden[k] + value * enter[n]
                         hidden[k] = h
                         y = y + h * leave[n]
                     y_ref[t, :, cells] = y
@@ -365,10 +342,10 @@
 
 
 def join_kernel(parts, lines, axis, after_ref, scanned_ref, *out_refs):
-    length = sum(out_ref.shape[0] for out_ref in out_refs) // (parts * lines)
+    length = out_refs[0].shape[-2] // lines
     time = parts * length
     chunk = scanned_ref.shape[1]
-    halves = out_refs[0].shape[1] // chunk
+    halves = out_refs[0].shape[-1] // chunk
     slot_lines = SLOTS // (2 * halves)
     row = rows_of(lines * time)
     line = (row >> bits(length)) & (lines - 1)
@@ -379,18 +356,23 @@
         ahead = now * SLOTS + (half * 2 * slot_lines) + line
         behind = (time - 1 - now) * SLOTS + (half * 2 * slot_lines + slot_lines) + line
         joined = dot(one_hot([ahead, behind], time * SLOTS), scanned_ref[...]).astype(BF16)
-        at = 0
-        for out_ref in out_refs:
-            out_ref[:, half * chunk : (half + 1) * chunk] = joined[at : at + out_ref.shape[0]]
-            at += out_ref.shape[0]
+        size = lines * length
+        for part in range(parts):
+            found = joined[part * size : (part + 1) * size]
+            if len(out_refs) < parts:
+                out_refs[part >> 1][part & 1, :, half * chunk : (half + 1) * chunk] = found
+            else:
+                out_refs[part][:, half * chunk : (half + 1) * chunk] = found
 
 
 def join(axis, scanned, parts, lines, length, width, after):
+    size = (lines * length, width)
+    shapes = [size] * parts if axis == "col" else [(2,) + size] * (parts // 2)
     return pl.pallas_call(
         functools.partial(join_kernel, parts, lines, axis),
-        out_shape=[jax.ShapeDtypeStruct((lines * length, width), BF16)] * parts,
+        out_shape=[jax.ShapeDtypeStruct(shape, BF16) for shape in shapes],
         in_specs=[pl.BlockSpec(memory_space=pl.ANY), pl.BlockSpec(memory_space=pltpu.VMEM)],
-        out_specs=[pl.BlockSpec(memory_space=pltpu.VMEM)] * parts,
+        out_specs=[pl.BlockSpec(memory_space=pltpu.VMEM)] * len(shapes),
         compiler_params=pltpu.CompilerParams(vmem_limit_bytes=24 * 1024 * 1024),
     )(after, scanned)
 
@@ -405,12 +387,11 @@
     time = parts * length
     width = conv.shape[2]
     states = decay_log.shape[2]
-    assert step_weight.shape[1] == RANK
+    assert step_weight.shape[1] == RANK and in_weight.shape[1] == 2 * width
     halves = 1 if lines >= 4 else 2
     assert lines <= SLOTS // (2 * halves)
     chunk = width // halves
     vmem = pl.BlockSpec(memory_space=pltpu.VMEM)
-    hbm = pl.BlockSpec(memory_space=pltpu.HBM)
     flops = 2 * time * (reach * channels * width + SLOTS * width * 256)
     return pl.pallas_call(
         functools.partial(prepare_kernel, lines, axis),
@@ -419,22 +400,15 @@
             jax.ShapeDtypeStruct((time, SLOTS, chunk), F32),
             jax.ShapeDtypeStruct((time, SLOTS, chunk), F32),
         ],
-        in_specs=[pl.BlockSpec(memory_space=pl.ANY)] + [vmem] * (len(xs) + 1) + [hbm] * 6,
+        in_specs=[pl.BlockSpec(memory_space=pl.ANY)] + [vmem] * (len(xs) + 7),
         out_specs=[vmem, vmem, vmem],
         scratch_shapes=[
-            pltpu.VMEM((channels, width), in_weight.dtype),
-            pltpu.VMEM(conv.shape, conv.dtype),
-            pltpu.VMEM(conv_bias.shape, conv_bias.dtype),
-            pltpu.VMEM((2, RANK + 2 * states, width), proj.dtype),
-            pltpu.VMEM((2, RANK, width), step_weight.dtype),
-            pltpu.VMEM(step_bias.shape, step_bias.dtype),
             pltpu.VMEM((reach * time, channels), BF16),
             pltpu.VMEM((reach, time // SLOTS + 2, SLOTS, width), F32),
             pltpu.VMEM((halves * lines * time, chunk), BF16),
             pltpu.VMEM((chunk, halves * 2 * LANES), BF16),
             pltpu.VMEM((halves * 2 * LANES, chunk), BF16),
             pltpu.VMEM((SLOTS, chunk), F32),
-            pltpu.SemaphoreType.DMA((6,)),
         ],
         compiler_params=pltpu.CompilerParams(vmem_limit_bytes=24 * 1024 * 1024),
         cost_estimate=pl.CostEstimate(flops=4 * flops, bytes_accessed=4 * 1024 * 1024, transcendentals=time * SLOTS * chunk),
@@ -455,19 +429,15 @@
     time, _, chunk = steps.shape
     width, states = decay_log.shape[1:]
     vmem = pl.BlockSpec(memory_space=pltpu.VMEM)
-    hbm = pl.BlockSpec(memory_space=pltpu.HBM)
     return pl.pallas_call(
         functools.partial(scan_kernel, axis),
         out_shape=jax.ShapeDtypeStruct((time * SLOTS, chunk), BF16),
-        in_specs=[pl.BlockSpec(memory_space=pl.ANY), vmem, vmem, vmem, hbm, hbm],
+        in_specs=[pl.BlockSpec(memory_space=pl.ANY), vmem, vmem, vmem, vmem, vmem],
         out_specs=vmem,
         scratch_shapes=[
             pltpu.VMEM((time, SLOTS, chunk), F32),
             pltpu.VMEM((time, SLOTS, chunk), F32),
             pltpu.VMEM((time, 2 * states, SLOTS, LANES), F32),
-            pltpu.VMEM((2, states, width), decay_log.dtype),
-            pltpu.VMEM(skip.shape, skip.dtype),
-            pltpu.SemaphoreType.DMA((2,)),
         ],
         compiler_params=pltpu.CompilerParams(vmem_limit_bytes=(8 << 20) + time * (136 << 10) + time * 20 * chunk),
         cost_estimate=pl.CostEstimate(
@@ -479,7 +449,7 @@
 
 
 def end_kernel(columns, gate_ref, gain_ref, weight_ref, *refs):
-    col_refs, row_refs, out_ref, gated_ref = refs[:columns], refs[columns:-2], refs[-2], refs[-1]
+    pair_refs, beside_ref, row_refs, out_ref, gated_ref = refs[:columns], refs[columns], refs[columns + 1 : -2], refs[-2], refs[-1]
     height, width, channels = out_ref.shape
     size = row_refs[0].shape[0]
     lines = size // width
@@ -489,7 +459,10 @@
     line = (row >> bits(width)) ^ (swap * lines)
     source = (((row & (width - 1)) ^ turn) << bits(height)) + line
     rows = jnp.concatenate([row_ref[...] for row_ref in row_refs], axis=0)
-    columns = jnp.concatenate([col_ref[...] for col_ref in col_refs], axis=0)
+    blocks = []
+    for part in range(columns):
+        blocks += [pair_refs[part][0], beside_ref[part]]
+    columns = jnp.concatenate(blocks, axis=0)
     combined = layer_norm(rows.astype(F32) + dot(one_hot([source], height * width), columns), gain_ref[...][None])
     for part in range(len(row_refs)):
         cells = pl.ds(pl.multiple_of((part ^ swap) * size, size), size)
@@ -499,6 +472,57 @@
     out_ref[...] = out.reshape(height, width, channels)
 
 
+def pair_kernel(*refs):
+    count = len(refs) // 2
+    own_refs, beside_ref, out_refs = refs[:count], refs[count], refs[count + 1 :]
+    for k in range(count):
+        out_refs[k][0] = own_refs[k][...]
+        out_refs[k][1] = beside_ref[k + 1]
+
+
+def first_kernel(own_ref, beside_ref, out_ref):
+    out_ref[0] = own_ref[...]
+    out_ref[1] = beside_ref[0]
+
+
+def collect_kernel(after_ref, *refs):
+    out_ref = refs[-1]
+    for k in range(len(refs) - 1):
+        out_ref[k] = refs[k][1]
+
+
+def simple(kernel, shapes, *arrays, after=None):
+    vmem = pl.BlockSpec(memory_space=pltpu.VMEM)
+    first = [] if after is None else [after]
+    many = isinstance(shapes, list)
+    return pl.pallas_call(
+        kernel,
+        out_shape=shapes,
+        in_specs=[pl.BlockSpec(memory_space=pl.ANY)] * len(first) + [vmem] * len(arrays),
+        out_specs=[vmem] * len(shapes) if many else vmem,
+        compiler_params=pltpu.CompilerParams(vmem_limit_bytes=4 * 1024 * 1024),
+        cost_estimate=pl.CostEstimate(flops=0, bytes_accessed=2 << 20, transcendentals=0),
+    )(*first, *arrays)
+
+
+def swap(block, axis, k):
+    return lax.ppermute(block, axis, [(i, i ^ k) for i in range(lax.axis_size(axis))])
+
+
+def swap_out(own, beside):
+    beside = swap(beside, "row", 1)
+    shape = jax.ShapeDtypeStruct((2,) + own[0].shape, own[0].dtype)
+    pairs = simple(pair_kernel, [shape] * (len(own) - 1), *own[1:], beside)
+    found = {k: swap(pairs[k - 1], "row", 2 * k) for k in range(len(own) - 1, 0, -1)}
+    first = simple(first_kernel, jax.ShapeDtypeStruct((2,) + own[0].shape, own[0].dtype), own[0], beside)
+    return [first] + [found[k] for k in range(1, len(own))]
+
+
+def swap_back_far(pairs):
+    found = {k: swap(pairs[k], "row", 2 * k) for k in range(len(pairs) - 1, 0, -1)}
+    return [pairs[0]] + [found[k] for k in range(1, len(pairs))]
+
+
 def swap_blocks(blocks, axis):
     count = lax.axis_size(axis)
     found = {k: lax.ppermute(blocks[k], axis, [(i, i ^ k) for i in range(count)]) for k in range(count - 1, 0, -1)}
@@ -506,7 +530,7 @@
 
 
 def pick_kernel(axis, after_ref, *refs):
-    x_refs, out_ref = refs[:-1], refs[-1]
+    x_refs, out_ref = views(refs[:-1], 3), refs[-1]
     place = lax.axis_index(axis) ^ flip(axis)
     line = jnp.where(place == 0, 1, x_refs[0].shape[0] - 2)
     for part, x_ref in enumerate(x_refs):
@@ -516,7 +540,7 @@
 def pick(axis, after, xs):
     return pl.pallas_call(
         functools.partial(pick_kernel, axis),
-        out_shape=jax.ShapeDtypeStruct((len(xs),) + xs[0].shape[1:], xs[0].dtype),
+        out_shape=jax.ShapeDtypeStruct((lax.axis_size("col" if axis == "col" else "row"),) + xs[-1].shape[-2:], xs[-1].dtype),
         in_specs=[pl.BlockSpec(memory_space=pl.ANY)] + [pl.BlockSpec(memory_space=pltpu.VMEM)] * len(xs),
         out_specs=pl.BlockSpec(memory_space=pltpu.VMEM),
         compiler_params=pltpu.CompilerParams(vmem_limit_bytes=4 * 1024 * 1024),
@@ -561,10 +585,11 @@
     normed, *sends = pl.pallas_call(
         functools.partial(cut_kernel, rows),
         out_shape=[jax.ShapeDtypeStruct((tokens, channels), BF16)]
-        + [jax.ShapeDtypeStruct((col_lines + 2, height, channels), BF16)] * rows
+        + [jax.ShapeDtypeStruct((col_lines + 2, height, channels), BF16)] * (rows // 2)
+        + [jax.ShapeDtypeStruct((rows // 2, col_lines + 2, height, channels), BF16)]
         + [jax.ShapeDtypeStruct((row_lines + 2, width, channels), BF16)] * cols,
         in_specs=[pl.BlockSpec(features.shape, lambda: (0, 0, 0)), pl.BlockSpec((channels,), lambda: (0,))],
-        out_specs=[vmem] * (1 + rows + cols),
+        out_specs=[vmem] * (2 + rows // 2 + cols),
         scratch_shapes=[pltpu.VMEM((tokens, channels), BF16)],
         compiler_params=pltpu.CompilerParams(vmem_limit_bytes=12 * 1024 * 1024),
         cost_estimate=pl.CostEstimate(flops=6_000_000_000, bytes_accessed=2 << 20, transcendentals=tokens),
@@ -583,23 +608,27 @@
         cost_estimate=pl.CostEstimate(flops=2 * tokens * channels * inner, bytes_accessed=1 << 20, transcendentals=0),
     )(normed, in_weight)
 
-    row_x = swap_blocks(sends[rows:], "col")
-    col_x = swap_blocks(sends[:rows], "row")
+    half = rows // 2
+    row_x = swap_blocks(sends[half + 1 :], "col")
+    col_x = swap_out(sends[:half], sends[half])
     row_seam = seam_of("col", pick("col", normed, row_x))
     row_steps = prepare("col", normed, row_x, row_seam, *weights)
     col_seam = seam_of("row", pick("row", row_steps[0], col_x))
     col_steps = prepare("row", row_steps[0], col_x, col_seam, *weights)
     col_y = scan("row", normed, *col_steps, decay_log, skip_gain)
     joined = join("row", col_y, rows, col_lines, height, inner, normed)
-    col_y = swap_blocks(joined, "row")
+    col_y = swap_back_far(joined)
     row_y = scan("col", joined[0], *row_steps, decay_log, skip_gain)
-    row_y = swap_blocks(join("col", row_y, cols, row_lines, width, inner, col_y[-1]), "col")
+    beside = jax.ShapeDtypeStruct((half,) + joined[0].shape[1:], BF16)
+    beside = simple(collect_kernel, beside, *col_y, after=row_y)
+    row_y = swap_blocks(join("col", row_y, cols, row_lines, width, inner, beside), "col")
+    beside = swap(beside, "row", 1)
     return pl.pallas_call(
-        functools.partial(end_kernel, rows),
+        functools.partial(end_kernel, half),
         out_shape=jax.ShapeDtypeStruct(features.shape, BF16),
         scratch_shapes=[pltpu.VMEM((tokens, inner), BF16)],
         compiler_params=pltpu.CompilerParams(vmem_limit_bytes=16 * 1024 * 1024),
-    )(gate, out_gain, out_weight, *col_y, *row_y)
+    )(gate, out_gain, out_weight, *col_y, beside, *row_y)
 
 
 def solution(mesh):

time: 74.9 us -> 68.1 us (0.909)
  starting transfers between devices: 36.6 us -> 21.6 us
  waiting for transfers between devices: 2.57 us -> 12.4 us
  Pallas kernels: 33.5 us -> 31.9 us
    ppermute x20 -> x6, starting transfers between devices: 35 us -> 4.94 us  [swap_blocks(): lax.ppermute(blocks[k], axis, [(i, i ^ k) for i in range(count)])]
    ppermute x0 -> x8, starting transfers between devices: none -> 15 us  [swap(): lax.ppermute(block, axis, [(i, i ^ k) for i in range(lax.axis_size(axis))])]
    ppermute x20 -> x6, waiting for transfers between devices: 2.56 us -> 8.97 us  [swap_blocks(): lax.ppermute(blocks[k], axis, [(i, i ^ k) for i in range(count)])]
    ppermute x0 -> x8, waiting for transfers between devices: none -> 3.44 us  [swap(): lax.ppermute(block, axis, [(i, i ^ k) for i in range(lax.axis_size(axis))])]
    pallas_call x2, Pallas kernels: 10.1 us -> 8.6 us  [prepare(): pl.pallas_call(functools.partial(prepare_kernel, lines, axis), out_shape=...]
    pallas_call x1 -> x4, Pallas kernels: 1.73 us -> 1.78 us  [the longest x1 1.73 us: local(): pl.pallas_call(functools.partial(end_kernel, half), out_shape=jax.ShapeDt...]
  transfers between devices with their start and end apart: 22 -> 16, of which waited for: 2 -> 5; matrix products, arithmetic and copies ran while one was open for 0% -> 0% of each run, Pallas kernels for 19% -> 19%
where the time goes in v6:
time: 68.1 us; the launch traced here: 67.9 us
  Pallas kernels  31.9 us (47%)
  starting transfers between devices  21.6 us (32%)
  waiting for transfers between devices  12.4 us (18%)
  local copies, waits for them, and re-layouts  1.79 us (3%)
    pallas_call x2, Pallas kernels, scan(): pl.pallas_call(functools.partial(scan_kernel, axis), out_shape=jax.ShapeD...  19.5 us
    ppermute x8, starting transfers between devices, swap(): lax.ppermute(block, axis, [(i, i ^ k) for i in range(lax.axis_size(axis))])  15 us
    ppermute x6, waiting for transfers between devices, swap_blocks(): lax.ppermute(blocks[k], axis, [(i, i ^ k) for i in range(count)])  8.97 us
    pallas_call x2, Pallas kernels, prepare(): pl.pallas_call(functools.partial(prepare_kernel, lines, axis), out_shape=...  8.6 us
    ppermute x6, starting transfers between devices, swap_blocks(): lax.ppermute(blocks[k], axis, [(i, i ^ k) for i in range(count)])  4.94 us
    ppermute x8, waiting for transfers between devices, swap(): lax.ppermute(block, axis, [(i, i ^ k) for i in range(lax.axis_size(axis))])  3.44 us
    unnamed x24, local copies, waits for them, and re-layouts  1.79 us
    pallas_call x1, Pallas kernels, local(): pl.pallas_call(functools.partial(end_kernel, half), out_shape=jax.ShapeDt...  1.73 us
  transfers between devices with their start and end apart: 16, of which 5 were waited for; matrix products, arithmetic and copies ran while one was open for 0% of the time, Pallas kernels for 19%

profile of v6, /device:TPU:0, one launch (start us, length us, event | category | flops | bytes accessed | tf_op | source)
XLA Modules:
  0.0 67.9 jit_solution(10554668331071748016)
XLA Ops:
  0.0 1.1 %copy-done.5 = bf16[16,16,384]{2,1,0:T(8,128)(2,1)S(1)} copy-done((bf16[16,16,384]{2,1,0:T(8,128)(2,1)S(1)}, bf16[16,16,384]{2,1,0:T(8,128)(2,1)}, u32[]{:S(2)}) %copy-start.5) | copy-done | bytes 196632
  1.1 0.7 %copy-done.11 = f32[384]{0:T(512)S(1)} copy-done((f32[384]{0:T(512)S(1)}, f32[384]{0:T(512)}, u32[]{:S(2)}) %copy-start.11) | copy-done | bytes 1560
  1.8 0.5 shard_map.118
  2.3 3.0 %collective-permute-start.4 = (bf16[4,4,16,384]{3,2,1,0:T(8,128)(2,1)S(1)}, bf16[4,4,16,384]{3,2,1,0:T(8,128)(2,1)S(1)}, u32[]{:S(2)}, u32[]{:S(2)}) collective-permute-start(bf16[4,4,16,384]{3,2,1,0:T(8,128)(2,1)S(1)} %get-tuple-element.39), channel_id=1, source_target_pairs={{0,4},{4,0},{8,12},{12,8},{16,20},{20,16},{24,28},{28,24},{1,5},{5... | collective-permute-start | bytes 589832 | tf_op jit(solution)/shard_map/ppermute | solution.py:509
  5.3 1.5 %collective-permute-start.1 = (bf16[6,16,384]{2,1,0:T(8,128)(2,1)S(1)}, bf16[6,16,384]{2,1,0:T(8,128)(2,1)S(1)}, u32[]{:S(2)}, u32[]{:S(2)}) collective-permute-start(bf16[6,16,384]{2,1,0:T(8,128)(2,1)S(1)} %get-tuple-element.35), channel_id=1, source_target_pairs={{0,2},{1,3},{2,0},{3,1},{4,6},{5,7},{6,4},{7,5},{8,10},{9,11},{10,... | collective-permute-start | bytes 221192 | tf_op jit(solution)/shard_map/ppermute | solution.py:528
  7.2 3.0 %collective-permute-done.1.refs_2_ = bf16[6,16,384]{2,1,0:T(8,128)(2,1)S(1)} collective-permute-done((bf16[6,16,384]{2,1,0:T(8,128)(2,1)S(1)}, bf16[6,16,384]{2,1,0:T(8,128)(2,1)S(1)}, u32[]{:S(2)}, u32[]{:S(2)}) %collective-permute-start.1) | collective-permute-done | bytes 73760 | tf_op jit(solution)/shard_map/ppermute | solution.py:528
  10.2 1.2 %collective-permute-done.2.refs_3_ = bf16[6,16,384]{2,1,0:T(8,128)(2,1)S(1)} collective-permute-done((bf16[6,16,384]{2,1,0:T(8,128)(2,1)S(1)}, bf16[6,16,384]{2,1,0:T(8,128)(2,1)S(1)}, u32[]{:S(2)}, u32[]{:S(2)}) %collective-permute-start.2) | collective-permute-done | bytes 73760 | tf_op jit(solution)/shard_map/ppermute | solution.py:528
  11.4 0.7 collective-permute-start.3
  12.1 3.0 %collective-permute-start.5 = (bf16[2,4,16,384]{3,2,1,0:T(8,128)(2,1)S(1)}, bf16[2,4,16,384]{3,2,1,0:T(8,128)(2,1)S(1)}, u32[]{:S(2)}, u32[]{:S(2)}) collective-permute-start(bf16[2,4,16,384]{3,2,1,0:T(8,128)(2,1)S(1)} %get-tuple-element.43), channel_id=1, source_target_pairs={{0,8},{4,12},{8,0},{12,4},{16,24},{20,28},{24,16},{28,20},{1,9},{5... | collective-permute-start | bytes 294920 | tf_op jit(solution)/shard_map/ppermute | solution.py:509
  15.0 2.9 %collective-permute-start.6 = (bf16[2,4,16,384]{3,2,1,0:T(8,128)(2,1)S(1)}, bf16[2,4,16,384]{3,2,1,0:T(8,128)(2,1)S(1)}, u32[]{:S(2)}, u32[]{:S(2)}) collective-permute-start(bf16[2,4,16,384]{3,2,1,0:T(8,128)(2,1)S(1)} %get-tuple-element.44), channel_id=1, source_target_pairs={{0,16},{4,20},{8,24},{12,28},{16,0},{20,4},{24,8},{28,12},{1,17},{... | collective-permute-start | bytes 294920 | tf_op jit(solution)/shard_map/ppermute | solution.py:509
  18.0 3.5 %shard_map.121 = (f32[64,8,128]{2,1,0:T(8,128)S(1)}, f32[64,8,768]{2,1,0:T(8,128)S(1)}, f32[64,8,768]{2,1,0:T(8,128)S(1)}) custom-call(bf16[256,384]{1,0:T(8,128)(2,1)S(1)} %get-tuple-element.32.norm_ref.after_ref, bf16[6,16,384]{2,1,0:T(8,128)(2,1)S(1)} %get-tuple-element.33.refs_0_, bf16[6,16,384]{2,1,0:T(8,128)(2,1)S(1)} %collective-permute-done.refs_1_, ...), custom_call_target="tpu_custom_call" | custom-call | flops 1711276032 | bytes 4194304 | tf_op jit(solution)/shard_map/pallas_call | solution.py:396
  21.6 3.4 %collective-permute-done.6.refs_2_ = bf16[2,4,16,384]{3,2,1,0:T(8,128)(2,1)S(1)} collective-permute-done((bf16[2,4,16,384]{3,2,1,0:T(8,128)(2,1)S(1)}, bf16[2,4,16,384]{3,2,1,0:T(8,128)(2,1)S(1)}, u32[]{:S(2)}, u32[]{:S(2)}) %collective-permute-start.6) | collective-permute-done | bytes 98336 | tf_op jit(solution)/shard_map/ppermute | solution.py:509
  25.0 1.0 %collective-permute-start.8 = (bf16[8,16,384]{2,1,0:T(8,128)(2,1)S(1)}, bf16[8,16,384]{2,1,0:T(8,128)(2,1)S(1)}, u32[]{:S(2)}, u32[]{:S(2)}) collective-permute-start(bf16[8,16,384]{2,1,0:T(8,128)(2,1)S(1)} %shard_map.124), channel_id=1, source_target_pairs={{28,29},{1,2},{30,31},{29,28},{2,1},{31,30}} | collective-permute-start | bytes 294920 | tf_op jit(solution)/shard_map/ppermute | solution.py:560
  26.0 5.1 %shard_map.125 = (f32[128,8,128]{2,1,0:T(8,128)S(1)}, f32[128,8,384]{2,1,0:T(8,128)S(1)}, f32[128,8,384]{2,1,0:T(8,128)S(1)}) custom-call(f32[64,8,128]{2,1,0:T(8,128)S(1)} %get-tuple-element.37.after_ref.coef_ref, bf16[2,4,16,384]{3,2,1,0:T(8,128)(2,1)S(1)} %shard_map.122.refs_0_, bf16[2,4,16,384]{3,2,1,0:T(8,128)(2,1)S(1)} %collective-permute-done.5.refs_1_, ...), custom_call_target="tpu_custom_call" | custom-call | flops 2818572288 | bytes 4194304 | tf_op jit(solution)/shard_map/pallas_call | solution.py:396
  31.1 10.9 %shard_map.126.scanned_ref = bf16[1024,384]{1,0:T(8,128)(2,1)S(1)} custom-call(bf16[256,384]{1,0:T(8,128)(2,1)S(1)} %get-tuple-element.32.norm_ref.after_ref, f32[128,8,128]{2,1,0:T(8,128)S(1)} %get-tuple-element.46.coef_ref, f32[128,8,384]{2,1,0:T(8,128)S(1)} %get-tuple-element.47.s_ref, f32[128,8,384]{2,1,0:T(8,128)S(1)} %get-tuple-element.48.u_ref, ...), custom_call_target="tpu_custom_call" | custom-call | flops 50331648 | bytes 4194304 | tf_op jit(solution)/shard_map/pallas_call | solution.py:432
  42.0 0.7 %shard_map.127 = (bf16[2,32,768]{2,1,0:T(8,128)(2,1)S(1)}, bf16[2,32,768]{2,1,0:T(8,128)(2,1)S(1)}, bf16[2,32,768]{2,1,0:T(8,128)(2,1)S(1)}, bf16[2,32,768]{2,1,0:T(8,128)(2,1)S(1)}) custom-call(bf16[256,384]{1,0:T(8,128)(2,1)S(1)} %get-tuple-element.32.norm_ref.after_ref, bf16[1024,384]{1,0:T(8,128)(2,1)S(1)} %shard_map.126.scanned_ref), custom_call_target="tpu_custom_call" | custom-call | tf_op jit(solution)/shard_map/pallas_call | solution.py:371
  42.7 2.2 %collective-permute-start.10 = (bf16[2,32,768]{2,1,0:T(8,128)(2,1)S(1)}, bf16[2,32,768]{2,1,0:T(8,128)(2,1)S(1)}, u32[]{:S(2)}, u32[]{:S(2)}) collective-permute-start(bf16[2,32,768]{2,1,0:T(8,128)(2,1)S(1)} %get-tuple-element.51), channel_id=1, source_target_pairs={{0,16},{4,20},{8,24},{12,28},{16,0},{20,4},{24,8},{28,12},{1,17},{... | collective-permute-start | bytes 294920 | tf_op jit(solution)/shard_map/ppermute | solution.py:509
  44.9 1.9 %collective-permute-start.11 = (bf16[2,32,768]{2,1,0:T(8,128)(2,1)S(1)}, bf16[2,32,768]{2,1,0:T(8,128)(2,1)S(1)}, u32[]{:S(2)}, u32[]{:S(2)}) collective-permute-start(bf16[2,32,768]{2,1,0:T(8,128)(2,1)S(1)} %get-tuple-element.52), channel_id=1, source_target_pairs={{0,24},{4,28},{8,16},{12,20},{16,8},{20,12},{24,0},{28,4},{1,25},{... | collective-permute-start | bytes 294920 | tf_op jit(solution)/shard_map/ppermute | solution.py:509
  46.8 8.6 %shard_map.128.after_ref.scanned_ref = bf16[512,768]{1,0:T(8,128)(2,1)S(1)} custom-call(bf16[2,32,768]{2,1,0:T(8,128)(2,1)S(1)} %get-tuple-element.49.after_ref.refs_0_, f32[64,8,128]{2,1,0:T(8,128)S(1)} %get-tuple-element.37.after_ref.coef_ref, f32[64,8,768]{2,1,0:T(8,128)S(1)} %get-tuple-element.53.s_ref, f32[64,8,768]{2,1,0:T(8,128)S(1)} %get-tuple-element.54.u_ref, ...), custom_call_target="tpu_custom_call" | custom-call | flops 50331648 | bytes 4194304 | tf_op jit(solution)/shard_map/pallas_call | solution.py:432
  55.5 2.0 %collective-permute-start.12 = (bf16[4,32,768]{2,1,0:T(8,128)(2,1)S(1)}, bf16[4,32,768]{2,1,0:T(8,128)(2,1)S(1)}, u32[]{:S(2)}, u32[]{:S(2)}) collective-permute-start(bf16[4,32,768]{2,1,0:T(8,128)(2,1)S(1)} %shard_map.129.after_ref), channel_id=1, source_target_pairs={{0,4},{4,0},{8,12},{12,8},{16,20},{20,16},{24,28},{28,24},{1,5},{5... | collective-permute-start | bytes 589832 | tf_op jit(solution)/shard_map/ppermute | solution.py:509
  58.4 2.5 %collective-permute-start.14 = (bf16[64,768]{1,0:T(8,128)(2,1)S(1)}, bf16[64,768]{1,0:T(8,128)(2,1)S(1)}, u32[]{:S(2)}, u32[]{:S(2)}) collective-permute-start(bf16[64,768]{1,0:T(8,128)(2,1)S(1)} %get-tuple-element.57), channel_id=1, source_target_pairs={{0,2},{1,3},{2,0},{3,1},{4,6},{5,7},{6,4},{7,5},{8,10},{9,11},{10,... | collective-permute-start | bytes 294920 | tf_op jit(solution)/shard_map/ppermute | solution.py:528
  61.4 3.2 %collective-permute-done.14.refs_7_ = bf16[64,768]{1,0:T(8,128)(2,1)S(1)} collective-permute-done((bf16[64,768]{1,0:T(8,128)(2,1)S(1)}, bf16[64,768]{1,0:T(8,128)(2,1)S(1)}, u32[]{:S(2)}, u32[]{:S(2)}) %collective-permute-start.14) | collective-permute-done | bytes 98336 | tf_op jit(solution)/shard_map/ppermute | solution.py:528
  64.6 1.6 %collective-permute-done.15.refs_8_ = bf16[64,768]{1,0:T(8,128)(2,1)S(1)} collective-permute-done((bf16[64,768]{1,0:T(8,128)(2,1)S(1)}, bf16[64,768]{1,0:T(8,128)(2,1)S(1)}, u32[]{:S(2)}, u32[]{:S(2)}) %collective-permute-start.15) | collective-permute-done | bytes 98336 | tf_op jit(solution)/shard_map/ppermute | solution.py:528
  66.2 1.7 %shard_map.131 = bf16[16,16,384]{2,1,0:T(8,128)(2,1)} custom-call(bf16[256,768]{1,0:T(8,128)(2,1)S(1)} %shard_map.119.gate_ref, f32[768]{0:T(1024)S(1)} %copy-done.2, bf16[768,384]{1,0:T(8,128)(2,1)S(1)} %copy-done.1, bf16[2,32,768]{2,1,0:T(8,128)(2,1)S(1)} %get-tuple-element.49.after_ref.refs_0_, bf16[2,32,768]{2,1,0:T(8,128)(2,1)S(1)} %collective-permute-done.9.refs_1_, ...), custom_call_target="tpu_custom_call" | custom-call | tf_op jit(solution)/shard_map/pallas_call | solution.py:626
  (46 shorter events, 1.9 us)
Async XLA Ops:
  0.0 17.9 %copy-start.3 = (bf16[4,768,56]{1,2,0:T(8,128)(2,1)S(1)}, bf16[4,768,56]{1,2,0:T(8,128)(2,1)}, u32[]{:S(2)}) copy-start(bf16[4,768,56]{1,2,0:T(8,128)(2,1)} %param.17) | copy-start | bytes 1032196
  0.0 17.9 %copy-start = (bf16[384,1536]{1,0:T(8,128)(2,1)S(1)}, bf16[384,1536]{1,0:T(8,128)(2,1)}, u32[]{:S(2)}) copy-start(bf16[384,1536]{1,0:T(8,128)(2,1)} %refs_5_.3) | copy-start | bytes 3538948
  0.0 18.0 %copy-start.4 = (f32[4,24,768]{2,1,0:T(8,128)S(1)}, f32[4,24,768]{2,1,0:T(8,128)}, u32[]{:S(2)}) copy-start(f32[4,24,768]{2,1,0:T(8,128)} %refs_9_.3) | copy-start | bytes 884740
  1.7 16.2 %copy-start.7 = (f32[3,3,768]{2,1,0:T(4,128)S(1)}, f32[3,3,768]{2,1,0:T(4,128)}, u32[]{:S(2)}) copy-start(f32[3,3,768]{2,1,0:T(4,128)} %refs_6_.3) | copy-start | bytes 82948
  1.8 16.2 %copy-start.8 = (f32[4,768]{1,0:T(4,128)S(1)}, f32[4,768]{1,0:T(4,128)}, u32[]{:S(2)}) copy-start(f32[4,768]{1,0:T(4,128)} %refs_10_.3) | copy-start | bytes 36868
  1.8 16.2 %copy-start.10 = (f32[768]{0:T(1024)S(1)}, f32[768]{0:T(1024)}, u32[]{:S(2)}) copy-start(f32[768]{0:T(1024)} %refs_7_.3) | copy-start | bytes 9220
  2.3 9.8 %collective-permute-start.4 = (bf16[4,4,16,384]{3,2,1,0:T(8,128)(2,1)S(1)}, bf16[4,4,16,384]{3,2,1,0:T(8,128)(2,1)S(1)}, u32[]{:S(2)}, u32[]{:S(2)}) collective-permute-start(bf16[4,4,16,384]{3,2,1,0:T(8,128)(2,1)S(1)} %get-tuple-element.39), channel_id=1, source_target_pairs={{0,4},{4,0},{8,12},{12,8},{16,20},{20,16},{24,28},{28,24},{1,5},{5... | collective-permute-start | bytes 589832 | tf_op jit(solution)/shard_map/ppermute | solution.py:509
  5.3 1.9 %collective-permute-start = (bf16[6,16,384]{2,1,0:T(8,128)(2,1)S(1)}, bf16[6,16,384]{2,1,0:T(8,128)(2,1)S(1)}, u32[]{:S(2)}, u32[]{:S(2)}) collective-permute-start(bf16[6,16,384]{2,1,0:T(8,128)(2,1)S(1)} %get-tuple-element.34), channel_id=1, source_target_pairs={{0,1},{1,0},{2,3},{3,2},{4,5},{5,4},{6,7},{7,6},{8,9},{9,8},{10,11... | collective-permute-start | bytes 221192 | tf_op jit(solution)/shard_map/ppermute | solution.py:528
  5.3 4.9 %collective-permute-start.1 = (bf16[6,16,384]{2,1,0:T(8,128)(2,1)S(1)}, bf16[6,16,384]{2,1,0:T(8,128)(2,1)S(1)}, u32[]{:S(2)}, u32[]{:S(2)}) collective-permute-start(bf16[6,16,384]{2,1,0:T(8,128)(2,1)S(1)} %get-tuple-element.35), channel_id=1, source_target_pairs={{0,2},{1,3},{2,0},{3,1},{4,6},{5,7},{6,4},{7,5},{8,10},{9,11},{10,... | collective-permute-start | bytes 221192 | tf_op jit(solution)/shard_map/ppermute | solution.py:528
  6.8 4.5 %collective-permute-start.2 = (bf16[6,16,384]{2,1,0:T(8,128)(2,1)S(1)}, bf16[6,16,384]{2,1,0:T(8,128)(2,1)S(1)}, u32[]{:S(2)}, u32[]{:S(2)}) collective-permute-start(bf16[6,16,384]{2,1,0:T(8,128)(2,1)S(1)} %get-tuple-element.36), channel_id=1, source_target_pairs={{0,3},{1,2},{2,1},{3,0},{4,7},{5,6},{6,5},{7,4},{8,11},{9,10},{10,... | collective-permute-start | bytes 221192 | tf_op jit(solution)/shard_map/ppermute | solution.py:528
  11.4 6.6 %collective-permute-start.3 = (bf16[4,16,384]{2,1,0:T(8,128)(2,1)S(1)}, bf16[4,16,384]{2,1,0:T(8,128)(2,1)S(1)}, u32[]{:S(2)}, u32[]{:S(2)}) collective-permute-start(bf16[4,16,384]{2,1,0:T(8,128)(2,1)S(1)} %shard_map.120), channel_id=1, source_target_pairs={{3,7},{4,8},{11,15},{12,16},{19,23},{20,24},{27,31},{7,3},{8,4},{1... | collective-permute-start | bytes 147464 | tf_op jit(solution)/shard_map/ppermute | solution.py:560
  12.1 9.5 %collective-permute-start.5 = (bf16[2,4,16,384]{3,2,1,0:T(8,128)(2,1)S(1)}, bf16[2,4,16,384]{3,2,1,0:T(8,128)(2,1)S(1)}, u32[]{:S(2)}, u32[]{:S(2)}) collective-permute-start(bf16[2,4,16,384]{3,2,1,0:T(8,128)(2,1)S(1)} %get-tuple-element.43), channel_id=1, source_target_pairs={{0,8},{4,12},{8,0},{12,4},{16,24},{20,28},{24,16},{28,20},{1,9},{5... | collective-permute-start | bytes 294920 | tf_op jit(solution)/shard_map/ppermute | solution.py:509
  15.0 9.9 %collective-permute-start.6 = (bf16[2,4,16,384]{3,2,1,0:T(8,128)(2,1)S(1)}, bf16[2,4,16,384]{3,2,1,0:T(8,128)(2,1)S(1)}, u32[]{:S(2)}, u32[]{:S(2)}) collective-permute-start(bf16[2,4,16,384]{3,2,1,0:T(8,128)(2,1)S(1)} %get-tuple-element.44), channel_id=1, source_target_pairs={{0,16},{4,20},{8,24},{12,28},{16,0},{20,4},{24,8},{28,12},{1,17},{... | collective-permute-start | bytes 294920 | tf_op jit(solution)/shard_map/ppermute | solution.py:509
  17.9 7.0 %collective-permute-start.7 = (bf16[2,4,16,384]{3,2,1,0:T(8,128)(2,1)S(1)}, bf16[2,4,16,384]{3,2,1,0:T(8,128)(2,1)S(1)}, u32[]{:S(2)}, u32[]{:S(2)}) collective-permute-start(bf16[2,4,16,384]{3,2,1,0:T(8,128)(2,1)S(1)} %get-tuple-element.45), channel_id=1, source_target_pairs={{0,24},{4,28},{8,16},{12,20},{16,8},{20,12},{24,0},{28,4},{1,25},{... | collective-permute-start | bytes 294920 | tf_op jit(solution)/shard_map/ppermute | solution.py:509
  25.0 1.0 %collective-permute-start.8 = (bf16[8,16,384]{2,1,0:T(8,128)(2,1)S(1)}, bf16[8,16,384]{2,1,0:T(8,128)(2,1)S(1)}, u32[]{:S(2)}, u32[]{:S(2)}) collective-permute-start(bf16[8,16,384]{2,1,0:T(8,128)(2,1)S(1)} %shard_map.124), channel_id=1, source_target_pairs={{28,29},{1,2},{30,31},{29,28},{2,1},{31,30}} | collective-permute-start | bytes 294920 | tf_op jit(solution)/shard_map/ppermute | solution.py:560
  42.7 12.7 %collective-permute-start.10 = (bf16[2,32,768]{2,1,0:T(8,128)(2,1)S(1)}, bf16[2,32,768]{2,1,0:T(8,128)(2,1)S(1)}, u32[]{:S(2)}, u32[]{:S(2)}) collective-permute-start(bf16[2,32,768]{2,1,0:T(8,128)(2,1)S(1)} %get-tuple-element.51), channel_id=1, source_target_pairs={{0,16},{4,20},{8,24},{12,28},{16,0},{20,4},{24,8},{28,12},{1,17},{... | collective-permute-start | bytes 294920 | tf_op jit(solution)/shard_map/ppermute | solution.py:509
  44.9 10.5 %collective-permute-start.11 = (bf16[2,32,768]{2,1,0:T(8,128)(2,1)S(1)}, bf16[2,32,768]{2,1,0:T(8,128)(2,1)S(1)}, u32[]{:S(2)}, u32[]{:S(2)}) collective-permute-start(bf16[2,32,768]{2,1,0:T(8,128)(2,1)S(1)} %get-tuple-element.52), channel_id=1, source_target_pairs={{0,24},{4,28},{8,16},{12,20},{16,8},{20,12},{24,0},{28,4},{1,25},{... | collective-permute-start | bytes 294920 | tf_op jit(solution)/shard_map/ppermute | solution.py:509
  46.8 8.7 %collective-permute-start.9 = (bf16[2,32,768]{2,1,0:T(8,128)(2,1)S(1)}, bf16[2,32,768]{2,1,0:T(8,128)(2,1)S(1)}, u32[]{:S(2)}, u32[]{:S(2)}) collective-permute-start(bf16[2,32,768]{2,1,0:T(8,128)(2,1)S(1)} %get-tuple-element.50), channel_id=1, source_target_pairs={{0,8},{4,12},{8,0},{12,4},{16,24},{20,28},{24,16},{28,20},{1,9},{5... | collective-permute-start | bytes 294920 | tf_op jit(solution)/shard_map/ppermute | solution.py:509
  55.5 10.7 %copy-start.1 = (bf16[768,384]{1,0:T(8,128)(2,1)S(1)}, bf16[768,384]{1,0:T(8,128)(2,1)}, u32[]{:S(2)}) copy-start(bf16[768,384]{1,0:T(8,128)(2,1)} %weight_ref.3) | copy-start | bytes 1769476
  55.5 10.7 %copy-start.2 = (f32[768]{0:T(1024)S(1)}, f32[768]{0:T(1024)}, u32[]{:S(2)}) copy-start(f32[768]{0:T(1024)} %gain_ref.3) | copy-start | bytes 9220
  55.5 10.7 %collective-permute-start.12 = (bf16[4,32,768]{2,1,0:T(8,128)(2,1)S(1)}, bf16[4,32,768]{2,1,0:T(8,128)(2,1)S(1)}, u32[]{:S(2)}, u32[]{:S(2)}) collective-permute-start(bf16[4,32,768]{2,1,0:T(8,128)(2,1)S(1)} %shard_map.129.after_ref), channel_id=1, source_target_pairs={{0,4},{4,0},{8,12},{12,8},{16,20},{20,16},{24,28},{28,24},{1,5},{5... | collective-permute-start | bytes 589832 | tf_op jit(solution)/shard_map/ppermute | solution.py:509
  58.0 3.5 %collective-permute-start.13 = (bf16[64,768]{1,0:T(8,128)(2,1)S(1)}, bf16[64,768]{1,0:T(8,128)(2,1)S(1)}, u32[]{:S(2)}, u32[]{:S(2)}) collective-permute-start(bf16[64,768]{1,0:T(8,128)(2,1)S(1)} %get-tuple-element.56), channel_id=1, source_target_pairs={{0,1},{1,0},{2,3},{3,2},{4,5},{5,4},{6,7},{7,6},{8,9},{9,8},{10,11... | collective-permute-start | bytes 294920 | tf_op jit(solution)/shard_map/ppermute | solution.py:528
  58.4 6.2 %collective-permute-start.14 = (bf16[64,768]{1,0:T(8,128)(2,1)S(1)}, bf16[64,768]{1,0:T(8,128)(2,1)S(1)}, u32[]{:S(2)}, u32[]{:S(2)}) collective-permute-start(bf16[64,768]{1,0:T(8,128)(2,1)S(1)} %get-tuple-element.57), channel_id=1, source_target_pairs={{0,2},{1,3},{2,0},{3,1},{4,6},{5,7},{6,4},{7,5},{8,10},{9,11},{10,... | collective-permute-start | bytes 294920 | tf_op jit(solution)/shard_map/ppermute | solution.py:528
  61.0 5.2 %collective-permute-start.15 = (bf16[64,768]{1,0:T(8,128)(2,1)S(1)}, bf16[64,768]{1,0:T(8,128)(2,1)S(1)}, u32[]{:S(2)}, u32[]{:S(2)}) collective-permute-start(bf16[64,768]{1,0:T(8,128)(2,1)S(1)} %get-tuple-element.58), channel_id=1, source_target_pairs={{0,3},{1,2},{2,1},{3,0},{4,7},{5,6},{6,5},{7,4},{8,11},{9,10},{10,... | collective-permute-start | bytes 294920 | tf_op jit(solution)/shard_map/ppermute | solution.py:528
  (4 other events, 14.0 us)

commit v7 on v6

--- a/solution.py
+++ b/solution.py
@@ -260,35 +260,35 @@
     out_ref,
     v_ref,
     y_ref,
-    spread_ref,
+    *spread_refs,
 ):
     time, _, chunk = s_ref.shape
     halves = decay_ref.shape[2] // chunk
     states = decay_ref.shape[1]
     groups = chunk // LANES
     at_once = max(1, 12 // groups)
-    unroll = 16 if axis == "col" else 8
+    unroll = 16
     laps = time // unroll
-    base2 = axis == "col"
-    power = jnp.exp2 if base2 else jnp.exp
 
     ks = (0, 1) if axis == "col" else (2, 3)
-    piece = 32
     row = lax.broadcasted_iota(jnp.int32, (2 * LANES, LANES), 0) & (LANES - 1)
-    taken = [jnp.where(row == 3 * RANK + n, 1.0, 0.0).astype(BF16) for n in range(2 * states)]
-
-    def spread(lap, _):
-        steps = pl.ds(lap * piece, piece)
-        coefs = coef_ref[steps].reshape(piece * SLOTS, LANES)
+
+    def spread(lap, first, into_ref):
+        steps = pl.ds(lap * unroll, unroll)
+        coefs = coef_ref[steps].reshape(unroll * SLOTS, LANES)
         high = coefs.astype(BF16)
         both = jnp.concatenate([high, (coefs - high.astype(F32)).astype(BF16)], axis=1)
-        for n in range(0, 2 * states, 4):
-            found = dot(both, jnp.concatenate(taken[n : n + 4], axis=1))
-            for k in range(4):
-                spread_ref[steps, n + k] = found[:, k * LANES : (k + 1) * LANES].reshape(piece, SLOTS, LANES)
+        lanes = [3 * RANK + kind * states + first + n for kind in range(2) for n in range(at_once)]
+        taken = jnp.concatenate([jnp.where(row == lane, 1.0, 0.0).astype(BF16) for lane in lanes], axis=1)
+        found = dot(both, taken)
+        for k in range(2 * at_once):
+            into_ref[steps, k] = found[:, k * LANES : (k + 1) * LANES].reshape(unroll, SLOTS, LANES)
+
+    def begin(lap, _):
+        spread(lap, 0, spread_refs[0])
         return 0
 
-    lax.fori_loop(0, time // piece, spread, 0)
+    lax.fori_loop(0, laps, begin, 0)
     for first in range(0, states, at_once):
         rates = []
         for n in range(first, first + at_once):
@@ -298,7 +298,7 @@
                     halves,
                     lambda half, way: decay_ref[ks[way], n : n + 1, half * chunk + g * LANES : half * chunk + (g + 1) * LANES],
                 )
-                rates[-1].append((-LOG2E if base2 else -1.0) * jnp.exp(rate))
+                rates[-1].append(-LOG2E * jnp.exp(rate))
         if first == 0:
             skips = [
                 by_slot(
@@ -312,10 +312,13 @@
 
         def advance(lap, hidden):
             hidden = list(hidden)
+            if first + at_once < states:
+                spread(lap, first + at_once, spread_refs[(first // at_once + 1) & 1])
+            now_ref = spread_refs[(first // at_once) & 1]
             for sub in range(unroll):
                 t = lap * unroll + sub
-                enter = [spread_ref[t, first + n] for n in range(at_once)]
-                leave = [spread_ref[t, states + first + n] for n in range(at_once)]
+                enter = [now_ref[t, n] for n in range(at_once)]
+                leave = [now_ref[t, at_once + n] for n in range(at_once)]
                 for g in range(groups):
                     cells = pl.ds(g * LANES, LANES)
                     step = s_ref[t, :, cells]
@@ -329,7 +332,7 @@
                         y = y_ref[t, :, cells]
                     for n in range(at_once):
                         k = n * groups + g
-                        h = power(step * rates[n][g]) * hidden[k] + value * enter[n]
+                        h = jnp.exp2(step * rates[n][g]) * hidden[k] + value * enter[n]
                         hidden[k] = h
                         y = y + h * leave[n]
                     y_ref[t, :, cells] = y
@@ -428,6 +431,7 @@
 def scan(axis, after, coefs, steps, u, decay_log, skip):
     time, _, chunk = steps.shape
     width, states = decay_log.shape[1:]
+    at_once = max(1, 12 // (chunk // LANES))
     vmem = pl.BlockSpec(memory_space=pltpu.VMEM)
     return pl.pallas_call(
         functools.partial(scan_kernel, axis),
@@ -437,9 +441,10 @@
         scratch_shapes=[
             pltpu.VMEM((time, SLOTS, chunk), F32),
             pltpu.VMEM((time, SLOTS, chunk), F32),
-            pltpu.VMEM((time, 2 * states, SLOTS, LANES), F32),
+            pltpu.VMEM((time, 2 * at_once, SLOTS, LANES), F32),
+            pltpu.VMEM((time, 2 * at_once, SLOTS, LANES), F32),
         ],
-        compiler_params=pltpu.CompilerParams(vmem_limit_bytes=(8 << 20) + time * (136 << 10) + time * 20 * chunk),
+        compiler_params=pltpu.CompilerParams(vmem_limit_bytes=(8 << 20) + time * at_once * (16 << 10) + time * 80 * chunk),
         cost_estimate=pl.CostEstimate(
             flops=8 * time * SLOTS * chunk * states,
             bytes_accessed=4 * 1024 * 1024,

time: 68.1 us -> 74.1 us (1.088)
  Pallas kernels: 31.9 us -> 37.9 us
    pallas_call x2, Pallas kernels: 19.5 us -> 25.5 us  [scan(): pl.pallas_call(functools.partial(scan_kernel, axis), out_shape=jax.ShapeD...]
  transfers between devices with their start and end apart: 16 -> 16, of which waited for: 5 -> 5; matrix products, arithmetic and copies ran while one was open for 0% -> 0% of each run, Pallas kernels for 19% -> 22%
where the time goes in v7:
time: 74.1 us; the launch traced here: 73.9 us
  Pallas kernels  37.9 us (51%)
  starting transfers between devices  21.6 us (29%)
  waiting for transfers between devices  12.4 us (17%)
  local copies, waits for them, and re-layouts  1.79 us (2%)
    pallas_call x2, Pallas kernels, scan(): pl.pallas_call(functools.partial(scan_kernel, axis), out_shape=jax.ShapeD...  25.5 us
    ppermute x8, starting transfers between devices, swap(): lax.ppermute(block, axis, [(i, i ^ k) for i in range(lax.axis_size(axis))])  15 us
    ppermute x6, waiting for transfers between devices, swap_blocks(): lax.ppermute(blocks[k], axis, [(i, i ^ k) for i in range(count)])  8.97 us
    pallas_call x2, Pallas kernels, prepare(): pl.pallas_call(functools.partial(prepare_kernel, lines, axis), out_shape=...  8.59 us
    ppermute x6, starting transfers between devices, swap_blocks(): lax.ppermute(blocks[k], axis, [(i, i ^ k) for i in range(count)])  4.98 us
    ppermute x8, waiting for transfers between devices, swap(): lax.ppermute(block, axis, [(i, i ^ k) for i in range(lax.axis_size(axis))])  3.41 us
    unnamed x24, local copies, waits for them, and re-layouts  1.79 us
    pallas_call x1, Pallas kernels, local(): pl.pallas_call(functools.partial(end_kernel, half), out_shape=jax.ShapeDt...  1.73 us
  transfers between devices with their start and end apart: 16, of which 5 were waited for; matrix products, arithmetic and copies ran while one was open for 0% of the time, Pallas kernels for 22%

profile of v7, /device:TPU:0, one launch (start us, length us, event | category | flops | bytes accessed | tf_op | source)
XLA Modules:
  0.0 73.9 jit_solution(12809440142751763827)
XLA Ops:
  0.0 1.1 %copy-done.5 = bf16[16,16,384]{2,1,0:T(8,128)(2,1)S(1)} copy-done((bf16[16,16,384]{2,1,0:T(8,128)(2,1)S(1)}, bf16[16,16,384]{2,1,0:T(8,128)(2,1)}, u32[]{:S(2)}) %copy-start.5) | copy-done | bytes 196632
  1.1 0.7 copy-done.11
  1.8 0.5 shard_map.118
  2.3 3.0 %collective-permute-start.4 = (bf16[4,4,16,384]{3,2,1,0:T(8,128)(2,1)S(1)}, bf16[4,4,16,384]{3,2,1,0:T(8,128)(2,1)S(1)}, u32[]{:S(2)}, u32[]{:S(2)}) collective-permute-start(bf16[4,4,16,384]{3,2,1,0:T(8,128)(2,1)S(1)} %get-tuple-element.39), channel_id=1, source_target_pairs={{0,4},{4,0},{8,12},{12,8},{16,20},{20,16},{24,28},{28,24},{1,5},{5... | collective-permute-start | bytes 589832 | tf_op jit(solution)/shard_map/ppermute | solution.py:514
  5.3 1.5 %collective-permute-start.1 = (bf16[6,16,384]{2,1,0:T(8,128)(2,1)S(1)}, bf16[6,16,384]{2,1,0:T(8,128)(2,1)S(1)}, u32[]{:S(2)}, u32[]{:S(2)}) collective-permute-start(bf16[6,16,384]{2,1,0:T(8,128)(2,1)S(1)} %get-tuple-element.35), channel_id=1, source_target_pairs={{0,2},{1,3},{2,0},{3,1},{4,6},{5,7},{6,4},{7,5},{8,10},{9,11},{10,... | collective-permute-start | bytes 221192 | tf_op jit(solution)/shard_map/ppermute | solution.py:533
  7.2 3.0 %collective-permute-done.1.refs_2_ = bf16[6,16,384]{2,1,0:T(8,128)(2,1)S(1)} collective-permute-done((bf16[6,16,384]{2,1,0:T(8,128)(2,1)S(1)}, bf16[6,16,384]{2,1,0:T(8,128)(2,1)S(1)}, u32[]{:S(2)}, u32[]{:S(2)}) %collective-permute-start.1) | collective-permute-done | bytes 73760 | tf_op jit(solution)/shard_map/ppermute | solution.py:533
  10.2 1.2 %collective-permute-done.2.refs_3_ = bf16[6,16,384]{2,1,0:T(8,128)(2,1)S(1)} collective-permute-done((bf16[6,16,384]{2,1,0:T(8,128)(2,1)S(1)}, bf16[6,16,384]{2,1,0:T(8,128)(2,1)S(1)}, u32[]{:S(2)}, u32[]{:S(2)}) %collective-permute-start.2) | collective-permute-done | bytes 73760 | tf_op jit(solution)/shard_map/ppermute | solution.py:533
  11.4 0.7 collective-permute-start.3
  12.1 3.0 %collective-permute-start.5 = (bf16[2,4,16,384]{3,2,1,0:T(8,128)(2,1)S(1)}, bf16[2,4,16,384]{3,2,1,0:T(8,128)(2,1)S(1)}, u32[]{:S(2)}, u32[]{:S(2)}) collective-permute-start(bf16[2,4,16,384]{3,2,1,0:T(8,128)(2,1)S(1)} %get-tuple-element.43), channel_id=1, source_target_pairs={{0,8},{4,12},{8,0},{12,4},{16,24},{20,28},{24,16},{28,20},{1,9},{5... | collective-permute-start | bytes 294920 | tf_op jit(solution)/shard_map/ppermute | solution.py:514
  15.0 2.9 %collective-permute-start.6 = (bf16[2,4,16,384]{3,2,1,0:T(8,128)(2,1)S(1)}, bf16[2,4,16,384]{3,2,1,0:T(8,128)(2,1)S(1)}, u32[]{:S(2)}, u32[]{:S(2)}) collective-permute-start(bf16[2,4,16,384]{3,2,1,0:T(8,128)(2,1)S(1)} %get-tuple-element.44), channel_id=1, source_target_pairs={{0,16},{4,20},{8,24},{12,28},{16,0},{20,4},{24,8},{28,12},{1,17},{... | collective-permute-start | bytes 294920 | tf_op jit(solution)/shard_map/ppermute | solution.py:514
  18.0 3.5 %shard_map.121 = (f32[64,8,128]{2,1,0:T(8,128)S(1)}, f32[64,8,768]{2,1,0:T(8,128)S(1)}, f32[64,8,768]{2,1,0:T(8,128)S(1)}) custom-call(bf16[256,384]{1,0:T(8,128)(2,1)S(1)} %get-tuple-element.32.norm_ref.after_ref, bf16[6,16,384]{2,1,0:T(8,128)(2,1)S(1)} %get-tuple-element.33.refs_0_, bf16[6,16,384]{2,1,0:T(8,128)(2,1)S(1)} %collective-permute-done.refs_1_, ...), custom_call_target="tpu_custom_call" | custom-call | flops 1711276032 | bytes 4194304 | tf_op jit(solution)/shard_map/pallas_call | solution.py:399
  21.5 3.4 %collective-permute-done.6.refs_2_ = bf16[2,4,16,384]{3,2,1,0:T(8,128)(2,1)S(1)} collective-permute-done((bf16[2,4,16,384]{3,2,1,0:T(8,128)(2,1)S(1)}, bf16[2,4,16,384]{3,2,1,0:T(8,128)(2,1)S(1)}, u32[]{:S(2)}, u32[]{:S(2)}) %collective-permute-start.6) | collective-permute-done | bytes 98336 | tf_op jit(solution)/shard_map/ppermute | solution.py:514
  25.0 1.0 %collective-permute-start.8 = (bf16[8,16,384]{2,1,0:T(8,128)(2,1)S(1)}, bf16[8,16,384]{2,1,0:T(8,128)(2,1)S(1)}, u32[]{:S(2)}, u32[]{:S(2)}) collective-permute-start(bf16[8,16,384]{2,1,0:T(8,128)(2,1)S(1)} %shard_map.124), channel_id=1, source_target_pairs={{28,29},{1,2},{30,31},{29,28},{2,1},{31,30}} | collective-permute-start | bytes 294920 | tf_op jit(solution)/shard_map/ppermute | solution.py:565
  26.0 5.1 %shard_map.125 = (f32[128,8,128]{2,1,0:T(8,128)S(1)}, f32[128,8,384]{2,1,0:T(8,128)S(1)}, f32[128,8,384]{2,1,0:T(8,128)S(1)}) custom-call(f32[64,8,128]{2,1,0:T(8,128)S(1)} %get-tuple-element.37.after_ref.coef_ref, bf16[2,4,16,384]{3,2,1,0:T(8,128)(2,1)S(1)} %shard_map.122.refs_0_, bf16[2,4,16,384]{3,2,1,0:T(8,128)(2,1)S(1)} %collective-permute-done.5.refs_1_, ...), custom_call_target="tpu_custom_call" | custom-call | flops 2818572288 | bytes 4194304 | tf_op jit(solution)/shard_map/pallas_call | solution.py:399
  31.1 13.4 %shard_map.126.scanned_ref = bf16[1024,384]{1,0:T(8,128)(2,1)S(1)} custom-call(bf16[256,384]{1,0:T(8,128)(2,1)S(1)} %get-tuple-element.32.norm_ref.after_ref, f32[128,8,128]{2,1,0:T(8,128)S(1)} %get-tuple-element.46.coef_ref, f32[128,8,384]{2,1,0:T(8,128)S(1)} %get-tuple-element.47.s_ref, f32[128,8,384]{2,1,0:T(8,128)S(1)} %get-tuple-element.48.u_ref, ...), custom_call_target="tpu_custom_call" | custom-call | flops 50331648 | bytes 4194304 | tf_op jit(solution)/shard_map/pallas_call | solution.py:436
  44.5 0.7 shard_map.127
  45.3 2.2 %collective-permute-start.10 = (bf16[2,32,768]{2,1,0:T(8,128)(2,1)S(1)}, bf16[2,32,768]{2,1,0:T(8,128)(2,1)S(1)}, u32[]{:S(2)}, u32[]{:S(2)}) collective-permute-start(bf16[2,32,768]{2,1,0:T(8,128)(2,1)S(1)} %get-tuple-element.51), channel_id=1, source_target_pairs={{0,16},{4,20},{8,24},{12,28},{16,0},{20,4},{24,8},{28,12},{1,17},{... | collective-permute-start | bytes 294920 | tf_op jit(solution)/shard_map/ppermute | solution.py:514
  47.5 1.9 %collective-permute-start.11 = (bf16[2,32,768]{2,1,0:T(8,128)(2,1)S(1)}, bf16[2,32,768]{2,1,0:T(8,128)(2,1)S(1)}, u32[]{:S(2)}, u32[]{:S(2)}) collective-permute-start(bf16[2,32,768]{2,1,0:T(8,128)(2,1)S(1)} %get-tuple-element.52), channel_id=1, source_target_pairs={{0,24},{4,28},{8,16},{12,20},{16,8},{20,12},{24,0},{28,4},{1,25},{... | collective-permute-start | bytes 294920 | tf_op jit(solution)/shard_map/ppermute | solution.py:514
  49.3 12.0 %shard_map.128.after_ref.scanned_ref = bf16[512,768]{1,0:T(8,128)(2,1)S(1)} custom-call(bf16[2,32,768]{2,1,0:T(8,128)(2,1)S(1)} %get-tuple-element.49.after_ref.refs_0_, f32[64,8,128]{2,1,0:T(8,128)S(1)} %get-tuple-element.37.after_ref.coef_ref, f32[64,8,768]{2,1,0:T(8,128)S(1)} %get-tuple-element.53.s_ref, f32[64,8,768]{2,1,0:T(8,128)S(1)} %get-tuple-element.54.u_ref, ...), custom_call_target="tpu_custom_call" | custom-call | flops 50331648 | bytes 4194304 | tf_op jit(solution)/shard_map/pallas_call | solution.py:436
  61.4 2.0 %collective-permute-start.12 = (bf16[4,32,768]{2,1,0:T(8,128)(2,1)S(1)}, bf16[4,32,768]{2,1,0:T(8,128)(2,1)S(1)}, u32[]{:S(2)}, u32[]{:S(2)}) collective-permute-start(bf16[4,32,768]{2,1,0:T(8,128)(2,1)S(1)} %shard_map.129.after_ref), channel_id=1, source_target_pairs={{0,4},{4,0},{8,12},{12,8},{16,20},{20,16},{24,28},{28,24},{1,5},{5... | collective-permute-start | bytes 589832 | tf_op jit(solution)/shard_map/ppermute | solution.py:514
  64.4 2.5 %collective-permute-start.14 = (bf16[64,768]{1,0:T(8,128)(2,1)S(1)}, bf16[64,768]{1,0:T(8,128)(2,1)S(1)}, u32[]{:S(2)}, u32[]{:S(2)}) collective-permute-start(bf16[64,768]{1,0:T(8,128)(2,1)S(1)} %get-tuple-element.57), channel_id=1, source_target_pairs={{0,2},{1,3},{2,0},{3,1},{4,6},{5,7},{6,4},{7,5},{8,10},{9,11},{10,... | collective-permute-start | bytes 294920 | tf_op jit(solution)/shard_map/ppermute | solution.py:533
  67.4 3.2 %collective-permute-done.14.refs_7_ = bf16[64,768]{1,0:T(8,128)(2,1)S(1)} collective-permute-done((bf16[64,768]{1,0:T(8,128)(2,1)S(1)}, bf16[64,768]{1,0:T(8,128)(2,1)S(1)}, u32[]{:S(2)}, u32[]{:S(2)}) %collective-permute-start.14) | collective-permute-done | bytes 98336 | tf_op jit(solution)/shard_map/ppermute | solution.py:533
  70.6 1.6 %collective-permute-done.15.refs_8_ = bf16[64,768]{1,0:T(8,128)(2,1)S(1)} collective-permute-done((bf16[64,768]{1,0:T(8,128)(2,1)S(1)}, bf16[64,768]{1,0:T(8,128)(2,1)S(1)}, u32[]{:S(2)}, u32[]{:S(2)}) %collective-permute-start.15) | collective-permute-done | bytes 98336 | tf_op jit(solution)/shard_map/ppermute | solution.py:533
  72.2 1.7 %shard_map.131 = bf16[16,16,384]{2,1,0:T(8,128)(2,1)} custom-call(bf16[256,768]{1,0:T(8,128)(2,1)S(1)} %shard_map.119.gate_ref, f32[768]{0:T(1024)S(1)} %copy-done.2, bf16[768,384]{1,0:T(8,128)(2,1)S(1)} %copy-done.1, bf16[2,32,768]{2,1,0:T(8,128)(2,1)S(1)} %get-tuple-element.49.after_ref.refs_0_, bf16[2,32,768]{2,1,0:T(8,128)(2,1)S(1)} %collective-permute-done.9.refs_1_, ...), custom_call_target="tpu_custom_call" | custom-call | tf_op jit(solution)/shard_map/pallas_call | solution.py:631
  (46 shorter events, 1.9 us)
Async XLA Ops:
  0.0 17.9 %copy-start.3 = (bf16[4,768,56]{1,2,0:T(8,128)(2,1)S(1)}, bf16[4,768,56]{1,2,0:T(8,128)(2,1)}, u32[]{:S(2)}) copy-start(bf16[4,768,56]{1,2,0:T(8,128)(2,1)} %param.17) | copy-start | bytes 1032196
  0.0 17.9 %copy-start = (bf16[384,1536]{1,0:T(8,128)(2,1)S(1)}, bf16[384,1536]{1,0:T(8,128)(2,1)}, u32[]{:S(2)}) copy-start(bf16[384,1536]{1,0:T(8,128)(2,1)} %refs_5_.3) | copy-start | bytes 3538948
  0.0 18.0 %copy-start.4 = (f32[4,24,768]{2,1,0:T(8,128)S(1)}, f32[4,24,768]{2,1,0:T(8,128)}, u32[]{:S(2)}) copy-start(f32[4,24,768]{2,1,0:T(8,128)} %refs_9_.3) | copy-start | bytes 884740
  1.7 16.2 %copy-start.7 = (f32[3,3,768]{2,1,0:T(4,128)S(1)}, f32[3,3,768]{2,1,0:T(4,128)}, u32[]{:S(2)}) copy-start(f32[3,3,768]{2,1,0:T(4,128)} %refs_6_.3) | copy-start | bytes 82948
  1.8 16.2 %copy-start.8 = (f32[4,768]{1,0:T(4,128)S(1)}, f32[4,768]{1,0:T(4,128)}, u32[]{:S(2)}) copy-start(f32[4,768]{1,0:T(4,128)} %refs_10_.3) | copy-start | bytes 36868
  1.8 16.2 %copy-start.10 = (f32[768]{0:T(1024)S(1)}, f32[768]{0:T(1024)}, u32[]{:S(2)}) copy-start(f32[768]{0:T(1024)} %refs_7_.3) | copy-start | bytes 9220
  2.3 9.8 %collective-permute-start.4 = (bf16[4,4,16,384]{3,2,1,0:T(8,128)(2,1)S(1)}, bf16[4,4,16,384]{3,2,1,0:T(8,128)(2,1)S(1)}, u32[]{:S(2)}, u32[]{:S(2)}) collective-permute-start(bf16[4,4,16,384]{3,2,1,0:T(8,128)(2,1)S(1)} %get-tuple-element.39), channel_id=1, source_target_pairs={{0,4},{4,0},{8,12},{12,8},{16,20},{20,16},{24,28},{28,24},{1,5},{5... | collective-permute-start | bytes 589832 | tf_op jit(solution)/shard_map/ppermute | solution.py:514
  5.3 1.9 %collective-permute-start = (bf16[6,16,384]{2,1,0:T(8,128)(2,1)S(1)}, bf16[6,16,384]{2,1,0:T(8,128)(2,1)S(1)}, u32[]{:S(2)}, u32[]{:S(2)}) collective-permute-start(bf16[6,16,384]{2,1,0:T(8,128)(2,1)S(1)} %get-tuple-element.34), channel_id=1, source_target_pairs={{0,1},{1,0},{2,3},{3,2},{4,5},{5,4},{6,7},{7,6},{8,9},{9,8},{10,11... | collective-permute-start | bytes 221192 | tf_op jit(solution)/shard_map/ppermute | solution.py:533
  5.3 4.9 %collective-permute-start.1 = (bf16[6,16,384]{2,1,0:T(8,128)(2,1)S(1)}, bf16[6,16,384]{2,1,0:T(8,128)(2,1)S(1)}, u32[]{:S(2)}, u32[]{:S(2)}) collective-permute-start(bf16[6,16,384]{2,1,0:T(8,128)(2,1)S(1)} %get-tuple-element.35), channel_id=1, source_target_pairs={{0,2},{1,3},{2,0},{3,1},{4,6},{5,7},{6,4},{7,5},{8,10},{9,11},{10,... | collective-permute-start | bytes 221192 | tf_op jit(solution)/shard_map/ppermute | solution.py:533
  6.8 4.5 %collective-permute-start.2 = (bf16[6,16,384]{2,1,0:T(8,128)(2,1)S(1)}, bf16[6,16,384]{2,1,0:T(8,128)(2,1)S(1)}, u32[]{:S(2)}, u32[]{:S(2)}) collective-permute-start(bf16[6,16,384]{2,1,0:T(8,128)(2,1)S(1)} %get-tuple-element.36), channel_id=1, source_target_pairs={{0,3},{1,2},{2,1},{3,0},{4,7},{5,6},{6,5},{7,4},{8,11},{9,10},{10,... | collective-permute-start | bytes 221192 | tf_op jit(solution)/shard_map/ppermute | solution.py:533
  11.4 6.6 %collective-permute-start.3 = (bf16[4,16,384]{2,1,0:T(8,128)(2,1)S(1)}, bf16[4,16,384]{2,1,0:T(8,128)(2,1)S(1)}, u32[]{:S(2)}, u32[]{:S(2)}) collective-permute-start(bf16[4,16,384]{2,1,0:T(8,128)(2,1)S(1)} %shard_map.120), channel_id=1, source_target_pairs={{3,7},{4,8},{11,15},{12,16},{19,23},{20,24},{27,31},{7,3},{8,4},{1... | collective-permute-start | bytes 147464 | tf_op jit(solution)/shard_map/ppermute | solution.py:565
  12.1 9.5 %collective-permute-start.5 = (bf16[2,4,16,384]{3,2,1,0:T(8,128)(2,1)S(1)}, bf16[2,4,16,384]{3,2,1,0:T(8,128)(2,1)S(1)}, u32[]{:S(2)}, u32[]{:S(2)}) collective-permute-start(bf16[2,4,16,384]{3,2,1,0:T(8,128)(2,1)S(1)} %get-tuple-element.43), channel_id=1, source_target_pairs={{0,8},{4,12},{8,0},{12,4},{16,24},{20,28},{24,16},{28,20},{1,9},{5... | collective-permute-start | bytes 294920 | tf_op jit(solution)/shard_map/ppermute | solution.py:514
  15.0 9.9 %collective-permute-start.6 = (bf16[2,4,16,384]{3,2,1,0:T(8,128)(2,1)S(1)}, bf16[2,4,16,384]{3,2,1,0:T(8,128)(2,1)S(1)}, u32[]{:S(2)}, u32[]{:S(2)}) collective-permute-start(bf16[2,4,16,384]{3,2,1,0:T(8,128)(2,1)S(1)} %get-tuple-element.44), channel_id=1, source_target_pairs={{0,16},{4,20},{8,24},{12,28},{16,0},{20,4},{24,8},{28,12},{1,17},{... | collective-permute-start | bytes 294920 | tf_op jit(solution)/shard_map/ppermute | solution.py:514
  17.9 7.0 %collective-permute-start.7 = (bf16[2,4,16,384]{3,2,1,0:T(8,128)(2,1)S(1)}, bf16[2,4,16,384]{3,2,1,0:T(8,128)(2,1)S(1)}, u32[]{:S(2)}, u32[]{:S(2)}) collective-permute-start(bf16[2,4,16,384]{3,2,1,0:T(8,128)(2,1)S(1)} %get-tuple-element.45), channel_id=1, source_target_pairs={{0,24},{4,28},{8,16},{12,20},{16,8},{20,12},{24,0},{28,4},{1,25},{... | collective-permute-start | bytes 294920 | tf_op jit(solution)/shard_map/ppermute | solution.py:514
  25.0 1.0 %collective-permute-start.8 = (bf16[8,16,384]{2,1,0:T(8,128)(2,1)S(1)}, bf16[8,16,384]{2,1,0:T(8,128)(2,1)S(1)}, u32[]{:S(2)}, u32[]{:S(2)}) collective-permute-start(bf16[8,16,384]{2,1,0:T(8,128)(2,1)S(1)} %shard_map.124), channel_id=1, source_target_pairs={{28,29},{1,2},{30,31},{29,28},{2,1},{31,30}} | collective-permute-start | bytes 294920 | tf_op jit(solution)/shard_map/ppermute | solution.py:565
  45.3 16.1 %collective-permute-start.10 = (bf16[2,32,768]{2,1,0:T(8,128)(2,1)S(1)}, bf16[2,32,768]{2,1,0:T(8,128)(2,1)S(1)}, u32[]{:S(2)}, u32[]{:S(2)}) collective-permute-start(bf16[2,32,768]{2,1,0:T(8,128)(2,1)S(1)} %get-tuple-element.51), channel_id=1, source_target_pairs={{0,16},{4,20},{8,24},{12,28},{16,0},{20,4},{24,8},{28,12},{1,17},{... | collective-permute-start | bytes 294920 | tf_op jit(solution)/shard_map/ppermute | solution.py:514
  47.5 13.9 %collective-permute-start.11 = (bf16[2,32,768]{2,1,0:T(8,128)(2,1)S(1)}, bf16[2,32,768]{2,1,0:T(8,128)(2,1)S(1)}, u32[]{:S(2)}, u32[]{:S(2)}) collective-permute-start(bf16[2,32,768]{2,1,0:T(8,128)(2,1)S(1)} %get-tuple-element.52), channel_id=1, source_target_pairs={{0,24},{4,28},{8,16},{12,20},{16,8},{20,12},{24,0},{28,4},{1,25},{... | collective-permute-start | bytes 294920 | tf_op jit(solution)/shard_map/ppermute | solution.py:514
  49.3 12.1 %collective-permute-start.9 = (bf16[2,32,768]{2,1,0:T(8,128)(2,1)S(1)}, bf16[2,32,768]{2,1,0:T(8,128)(2,1)S(1)}, u32[]{:S(2)}, u32[]{:S(2)}) collective-permute-start(bf16[2,32,768]{2,1,0:T(8,128)(2,1)S(1)} %get-tuple-element.50), channel_id=1, source_target_pairs={{0,8},{4,12},{8,0},{12,4},{16,24},{20,28},{24,16},{28,20},{1,9},{5... | collective-permute-start | bytes 294920 | tf_op jit(solution)/shard_map/ppermute | solution.py:514
  61.4 10.8 %copy-start.1 = (bf16[768,384]{1,0:T(8,128)(2,1)S(1)}, bf16[768,384]{1,0:T(8,128)(2,1)}, u32[]{:S(2)}) copy-start(bf16[768,384]{1,0:T(8,128)(2,1)} %weight_ref.3) | copy-start | bytes 1769476
  61.4 10.7 %copy-start.2 = (f32[768]{0:T(1024)S(1)}, f32[768]{0:T(1024)}, u32[]{:S(2)}) copy-start(f32[768]{0:T(1024)} %gain_ref.3) | copy-start | bytes 9220
  61.4 10.7 %collective-permute-start.12 = (bf16[4,32,768]{2,1,0:T(8,128)(2,1)S(1)}, bf16[4,32,768]{2,1,0:T(8,128)(2,1)S(1)}, u32[]{:S(2)}, u32[]{:S(2)}) collective-permute-start(bf16[4,32,768]{2,1,0:T(8,128)(2,1)S(1)} %shard_map.129.after_ref), channel_id=1, source_target_pairs={{0,4},{4,0},{8,12},{12,8},{16,20},{20,16},{24,28},{28,24},{1,5},{5... | collective-permute-start | bytes 589832 | tf_op jit(solution)/shard_map/ppermute | solution.py:514
  63.9 3.5 %collective-permute-start.13 = (bf16[64,768]{1,0:T(8,128)(2,1)S(1)}, bf16[64,768]{1,0:T(8,128)(2,1)S(1)}, u32[]{:S(2)}, u32[]{:S(2)}) collective-permute-start(bf16[64,768]{1,0:T(8,128)(2,1)S(1)} %get-tuple-element.56), channel_id=1, source_target_pairs={{0,1},{1,0},{2,3},{3,2},{4,5},{5,4},{6,7},{7,6},{8,9},{9,8},{10,11... | collective-permute-start | bytes 294920 | tf_op jit(solution)/shard_map/ppermute | solution.py:533
  64.4 6.2 %collective-permute-start.14 = (bf16[64,768]{1,0:T(8,128)(2,1)S(1)}, bf16[64,768]{1,0:T(8,128)(2,1)S(1)}, u32[]{:S(2)}, u32[]{:S(2)}) collective-permute-start(bf16[64,768]{1,0:T(8,128)(2,1)S(1)} %get-tuple-element.57), channel_id=1, source_target_pairs={{0,2},{1,3},{2,0},{3,1},{4,6},{5,7},{6,4},{7,5},{8,10},{9,11},{10,... | collective-permute-start | bytes 294920 | tf_op jit(solution)/shard_map/ppermute | solution.py:533
  66.9 5.2 %collective-permute-start.15 = (bf16[64,768]{1,0:T(8,128)(2,1)S(1)}, bf16[64,768]{1,0:T(8,128)(2,1)S(1)}, u32[]{:S(2)}, u32[]{:S(2)}) collective-permute-start(bf16[64,768]{1,0:T(8,128)(2,1)S(1)} %get-tuple-element.58), channel_id=1, source_target_pairs={{0,3},{1,2},{2,1},{3,0},{4,7},{5,6},{6,5},{7,4},{8,11},{9,10},{10,... | collective-permute-start | bytes 294920 | tf_op jit(solution)/shard_map/ppermute | solution.py:533
  (4 other events, 14.0 us)

commit v8 on v6

--- a/solution.py
+++ b/solution.py
@@ -58,7 +58,7 @@
     turn = flip("col") ^ lax.axis_index("col")
     for part, row_ref in enumerate(row_refs):
         for line in range(reach):
-            at = jnp.clip((part ^ turn) * (reach - 2) + line - 1, 0, height - 1)
+            at = (part ^ turn) * reach + line
             row_ref[line] = norm_ref[pl.ds(pl.multiple_of(at * width, width), width)]
     row = rows_of(height * width)
     turned = dot(one_hot([((row & (height - 1)) << bits(width)) + (row >> bits(height))], height * width), tile).astype(
@@ -69,7 +69,7 @@
     turn = flip("row") ^ lax.axis_index("row")
     for part in range(columns):
         for line in range(reach):
-            at = jnp.clip((part ^ turn) * (reach - 2) + line - 1, 0, width - 1)
+            at = (part ^ turn) * reach + line
             found = turned_ref[pl.ds(pl.multiple_of(at * height, height), height)]
             if part & 1:
                 beside_ref[part >> 1, line] = found
@@ -104,9 +104,10 @@
     after_ref,
     *refs,
 ):
-    x_refs, refs = views(refs[:-16], 3), refs[-16:]
+    x_refs, refs = views(refs[:-17], 3), refs[-17:]
     (
-        seam_ref,
+        before_ref,
+        behind_ref,
         weight_ref,
         conv_ref,
         conv_bias_ref,
@@ -124,7 +125,7 @@
         bias_ref,
     ) = refs
     ks = (0, 1) if axis == "col" else (2, 3)
-    parts, length, channels = seam_ref.shape
+    parts, length, channels = before_ref.shape
     reach = lines + 2
     states = (proj_raw_ref.shape[1] - RANK) // 2
     time = parts * length
@@ -140,14 +141,14 @@
 
     row = rows_of(time)
     source = ((row & 7) << bits(low)) + (row >> 3)
-    source = source ^ (lax.axis_index(axis) << bits(length))
-    order = one_hot([source], time)
+    orders = [one_hot([source], time), one_hot([source ^ (lax.axis_index(axis) << bits(length))], time)]
     for line in range(reach):
-        x = jnp.concatenate([x_ref[line] for x_ref in x_refs], axis=0)
-        if line == 0 or line == reach - 1:
-            place = lax.axis_index(axis) ^ flip(axis)
-            missing = place == (0 if line == 0 else lax.axis_size(axis) - 1)
-            x = jnp.where(missing, seam_ref[...].reshape(time, channels), x)
+        if 0 < line < reach - 1:
+            x = jnp.concatenate([x_ref[line - 1] for x_ref in x_refs], axis=0)
+            order = orders[1]
+        else:
+            x = (behind_ref if line else before_ref)[...].reshape(time, channels)
+            order = orders[0]
         token_ref[line * time : (line + 1) * time] = dot(order, x).astype(BF16)
     inner = dot(token_ref[...], weight_ref[:, :width]).astype(BF16).astype(F32)
     inner_ref[:, 1 : low + 1] = inner.reshape(reach, low, SLOTS, width)
@@ -267,10 +268,8 @@
     states = decay_ref.shape[1]
     groups = chunk // LANES
     at_once = max(1, 12 // groups)
-    unroll = 16 if axis == "col" else 8
+    unroll = 16
     laps = time // unroll
-    base2 = axis == "col"
-    power = jnp.exp2 if base2 else jnp.exp
 
     ks = (0, 1) if axis == "col" else (2, 3)
     piece = 32
@@ -298,7 +297,7 @@
                     halves,
                     lambda half, way: decay_ref[ks[way], n : n + 1, half * chunk + g * LANES : half * chunk + (g + 1) * LANES],
                 )
-                rates[-1].append((-LOG2E if base2 else -1.0) * jnp.exp(rate))
+                rates[-1].append(-LOG2E * jnp.exp(rate))
         if first == 0:
             skips = [
                 by_slot(
@@ -310,18 +309,31 @@
                 for g in range(groups)
             ]
 
+        def decays(t):
+            found = []
+            for g in range(groups):
+                step = s_ref[t, :, g * LANES : (g + 1) * LANES]
+                found.append([jnp.exp2(step * rates[n][g]) for n in range(at_once)])
+            return found
+
         def advance(lap, hidden):
             hidden = list(hidden)
+            ahead = decays(lap * unroll) if axis == "col" else None
             for sub in range(unroll):
                 t = lap * unroll + sub
+                if axis == "col":
+                    decay = ahead
+                    if sub + 1 < unroll:
+                        ahead = decays(t + 1)
+                else:
+                    decay = decays(t)
                 enter = [spread_ref[t, first + n] for n in range(at_once)]
                 leave = [spread_ref[t, states + first + n] for n in range(at_once)]
                 for g in range(groups):
                     cells = pl.ds(g * LANES, LANES)
-                    step = s_ref[t, :, cells]
                     if first == 0:
                         u = u_ref[t, :, cells]
-                        value = step * u
+                        value = s_ref[t, :, cells] * u
                         v_ref[t, :, cells] = value
                         y = skips[g] * u
                     else:
@@ -329,7 +341,7 @@
                         y = y_ref[t, :, cells]
                     for n in range(at_once):
                         k = n * groups + g
-                        h = power(step * rates[n][g]) * hidden[k] + value * enter[n]
+                        h = decay[g][n] * hidden[k] + value * enter[n]
                         hidden[k] = h
                         y = y + h * leave[n]
                     y_ref[t, :, cells] = y
@@ -380,10 +392,10 @@
 RANK = 24
 
 
-def prepare(axis, after, xs, seam, in_weight, conv, conv_bias, proj, step_weight, step_bias, decay_log, skip):
-    parts, length, channels = seam.shape
-    reach = xs[0].shape[-3]
-    lines = reach - 2
+def prepare(axis, after, xs, seams, in_weight, conv, conv_bias, proj, step_weight, step_bias, decay_log, skip):
+    parts, length, channels = seams[0].shape
+    lines = xs[0].shape[-3]
+    reach = lines + 2
     time = parts * length
     width = conv.shape[2]
     states = decay_log.shape[2]
@@ -400,7 +412,7 @@
             jax.ShapeDtypeStruct((time, SLOTS, chunk), F32),
             jax.ShapeDtypeStruct((time, SLOTS, chunk), F32),
         ],
-        in_specs=[pl.BlockSpec(memory_space=pl.ANY)] + [vmem] * (len(xs) + 7),
+        in_specs=[pl.BlockSpec(memory_space=pl.ANY)] + [vmem] * (len(xs) + 8),
         out_specs=[vmem, vmem, vmem],
         scratch_shapes=[
             pltpu.VMEM((reach * time, channels), BF16),
@@ -415,7 +427,7 @@
     )(
         after,
         *xs,
-        seam,
+        *seams,
         in_weight,
         conv,
         conv_bias,
@@ -530,34 +542,34 @@
 
 
 def pick_kernel(axis, after_ref, *refs):
-    x_refs, out_ref = views(refs[:-1], 3), refs[-1]
-    place = lax.axis_index(axis) ^ flip(axis)
-    line = jnp.where(place == 0, 1, x_refs[0].shape[0] - 2)
-    for part, x_ref in enumerate(x_refs):
-        out_ref[part] = x_ref[line]
-
-
-def pick(axis, after, xs):
-    return pl.pallas_call(
+    x_refs, first_ref, last_ref = views(refs[:-2], 3), refs[-2], refs[-1]
+    place = lax.axis_index(axis)
+    for k, x_ref in enumerate(x_refs):
+        first_ref[k ^ place] = x_ref[0]
+        last_ref[k ^ place] = x_ref[x_ref.shape[0] - 1]
+
+
+def seams_of(axis, after, xs):
+    shape = jax.ShapeDtypeStruct((lax.axis_size(axis),) + xs[-1].shape[-2:], xs[-1].dtype)
+    vmem = pl.BlockSpec(memory_space=pltpu.VMEM)
+    first, last = pl.pallas_call(
         functools.partial(pick_kernel, axis),
-        out_shape=jax.ShapeDtypeStruct((lax.axis_size("col" if axis == "col" else "row"),) + xs[-1].shape[-2:], xs[-1].dtype),
-        in_specs=[pl.BlockSpec(memory_space=pl.ANY)] + [pl.BlockSpec(memory_space=pltpu.VMEM)] * len(xs),
-        out_specs=pl.BlockSpec(memory_space=pltpu.VMEM),
+        out_shape=[shape, shape],
+        in_specs=[pl.BlockSpec(memory_space=pl.ANY)] + [vmem] * len(xs),
+        out_specs=[vmem, vmem],
         compiler_params=pltpu.CompilerParams(vmem_limit_bytes=4 * 1024 * 1024),
     )(after, *xs)
-
-
-def seam_of(axis, line):
-    count = lax.axis_size(axis)
     height, breadth = lax.axis_size("row"), lax.axis_size("col")
+    chain = []
     if axis == "row":
-        at = lambda group: (0 if group & 1 else count - 1) * breadth
-        ends = [(at(c) + c, at(c) + c + 1) for c in range(breadth - 1)]
+        for c in range(breadth):
+            chain += [r * breadth + c for r in (range(height - 1, -1, -1) if c & 1 else range(height))]
     else:
-        at = lambda group: 0 if group & 1 else count - 1
-        ends = [(at(r) + r * breadth, at(r) + (r + 1) * breadth) for r in range(height - 1)]
-    pairs = ends + [(b, a) for a, b in ends]
-    return lax.ppermute(line, ("row", "col"), pairs)
+        for r in range(height):
+            chain += [r * breadth + c for c in (range(breadth - 1, -1, -1) if r & 1 else range(breadth))]
+    ahead = list(zip(chain[:-1], chain[1:]))
+    both = ("row", "col")
+    return lax.ppermute(last, both, ahead), lax.ppermute(first, both, [(b, a) for a, b in ahead])
 
 
 def local(
@@ -585,9 +597,9 @@
     normed, *sends = pl.pallas_call(
         functools.partial(cut_kernel, rows),
         out_shape=[jax.ShapeDtypeStruct((tokens, channels), BF16)]
-        + [jax.ShapeDtypeStruct((col_lines + 2, height, channels), BF16)] * (rows // 2)
-        + [jax.ShapeDtypeStruct((rows // 2, col_lines + 2, height, channels), BF16)]
-        + [jax.ShapeDtypeStruct((row_lines + 2, width, channels), BF16)] * cols,
+        + [jax.ShapeDtypeStruct((col_lines, height, channels), BF16)] * (rows // 2)
+        + [jax.ShapeDtypeStruct((rows // 2, col_lines, height, channels), BF16)]
+        + [jax.ShapeDtypeStruct((row_lines, width, channels), BF16)] * cols,
         in_specs=[pl.BlockSpec(features.shape, lambda: (0, 0, 0)), pl.BlockSpec((channels,), lambda: (0,))],
         out_specs=[vmem] * (2 + rows // 2 + cols),
         scratch_shapes=[pltpu.VMEM((tokens, channels), BF16)],
@@ -611,10 +623,8 @@
     half = rows // 2
     row_x = swap_blocks(sends[half + 1 :], "col")
     col_x = swap_out(sends[:half], sends[half])
-    row_seam = seam_of("col", pick("col", normed, row_x))
-    row_steps = prepare("col", normed, row_x, row_seam, *weights)
-    col_seam = seam_of("row", pick("row", row_steps[0], col_x))
-    col_steps = prepare("row", row_steps[0], col_x, col_seam, *weights)
+    row_steps = prepare("col", normed, row_x, seams_of("col", normed, row_x), *weights)
+    col_steps = prepare("row", row_steps[0], col_x, seams_of("row", row_steps[0], col_x), *weights)
     col_y = scan("row", normed, *col_steps, decay_log, skip_gain)
     joined = join("row", col_y, rows, col_lines, height, inner, normed)
     col_y = swap_back_far(joined)

time: 68.1 us -> 76.4 us (1.12)
  starting transfers between devices: 21.6 us -> 30.9 us
  Pallas kernels: 31.9 us -> 30.9 us
    ppermute x2 -> x4, starting transfers between devices: 1.63 us -> 9.5 us  [the longest x2 6.91 us: seams_of(): lax.ppermute(last, both, ahead)]
    ppermute x8, starting transfers between devices: 15 us -> 17.6 us  [swap(): lax.ppermute(block, axis, [(i, i ^ k) for i in range(lax.axis_size(axis))])]
    ppermute x2 -> x4, waiting for transfers between devices: 0.01 us -> 2.01 us  [the longest x2 1.7 us: seams_of(): lax.ppermute(last, both, ahead)]
    ppermute x6, starting transfers between devices: 4.94 us -> 3.79 us  [swap_blocks(): lax.ppermute(blocks[k], axis, [(i, i ^ k) for i in range(count)])]
    ppermute x8, waiting for transfers between devices: 3.44 us -> 2.29 us  [swap(): lax.ppermute(block, axis, [(i, i ^ k) for i in range(lax.axis_size(axis))])]
    ppermute x6, waiting for transfers between devices: 8.97 us -> 7.97 us  [swap_blocks(): lax.ppermute(blocks[k], axis, [(i, i ^ k) for i in range(count)])]
    pallas_call x2, Pallas kernels: 19.5 us -> 18.6 us  [scan(): pl.pallas_call(functools.partial(scan_kernel, axis), out_shape=jax.ShapeD...]
  transfers between devices with their start and end apart: 16 -> 18, of which waited for: 5 -> 7; matrix products, arithmetic and copies ran while one was open for 0% -> 0% of each run, Pallas kernels for 19% -> 17%
where the time goes in v8:
time: 76.4 us; the launch traced here: 76.2 us
  Pallas kernels  30.9 us (40%)
  starting transfers between devices  30.9 us (40%)
  waiting for transfers between devices  12.3 us (16%)
  local copies, waits for them, and re-layouts  1.79 us (2%)
    pallas_call x2, Pallas kernels, scan(): pl.pallas_call(functools.partial(scan_kernel, axis), out_shape=jax.ShapeD...  18.6 us
    ppermute x8, starting transfers between devices, swap(): lax.ppermute(block, axis, [(i, i ^ k) for i in range(lax.axis_size(axis))])  17.6 us
    pallas_call x2, Pallas kernels, prepare(): pl.pallas_call(functools.partial(prepare_kernel, lines, axis), out_shape=...  8.57 us
    ppermute x6, waiting for transfers between devices, swap_blocks(): lax.ppermute(blocks[k], axis, [(i, i ^ k) for i in range(count)])  7.97 us
    ppermute x2, starting transfers between devices, seams_of(): lax.ppermute(last, both, ahead)  6.91 us
    ppermute x6, starting transfers between devices, swap_blocks(): lax.ppermute(blocks[k], axis, [(i, i ^ k) for i in range(count)])  3.79 us
    ppermute x2, starting transfers between devices, seams_of(): lax.ppermute(first, both, [(b, a) for a, b in ahead])  2.58 us
    ppermute x8, waiting for transfers between devices, swap(): lax.ppermute(block, axis, [(i, i ^ k) for i in range(lax.axis_size(axis))])  2.29 us
  transfers between devices with their start and end apart: 18, of which 7 were waited for; matrix products, arithmetic and copies ran while one was open for 0% of the time, Pallas kernels for 17%

profile of v8, /device:TPU:0, one launch (start us, length us, event | category | flops | bytes accessed | tf_op | source)
XLA Modules:
  0.0 76.2 jit_solution(9224701118706060704)
XLA Ops:
  0.0 1.1 %copy-done.5 = bf16[16,16,384]{2,1,0:T(8,128)(2,1)S(1)} copy-done((bf16[16,16,384]{2,1,0:T(8,128)(2,1)S(1)}, bf16[16,16,384]{2,1,0:T(8,128)(2,1)}, u32[]{:S(2)}) %copy-start.5) | copy-done | bytes 196632
  2.2 3.0 %collective-permute-start.5 = (bf16[4,2,16,384]{3,2,1,0:T(8,128)(2,1)S(1)}, bf16[4,2,16,384]{3,2,1,0:T(8,128)(2,1)S(1)}, u32[]{:S(2)}, u32[]{:S(2)}) collective-permute-start(bf16[4,2,16,384]{3,2,1,0:T(8,128)(2,1)S(1)} %get-tuple-element.45), channel_id=1, source_target_pairs={{0,4},{4,0},{8,12},{12,8},{16,20},{20,16},{24,28},{28,24},{1,5},{5... | collective-permute-start | bytes 294920 | tf_op jit(solution)/shard_map/ppermute | solution.py:521
  5.3 1.5 %collective-permute-start.1 = (bf16[4,16,384]{2,1,0:T(8,128)(2,1)S(1)}, bf16[4,16,384]{2,1,0:T(8,128)(2,1)S(1)}, u32[]{:S(2)}, u32[]{:S(2)}) collective-permute-start(bf16[4,16,384]{2,1,0:T(8,128)(2,1)S(1)} %get-tuple-element.39), channel_id=1, source_target_pairs={{0,2},{1,3},{2,0},{3,1},{4,6},{5,7},{6,4},{7,5},{8,10},{9,11},{10,... | collective-permute-start | bytes 147464 | tf_op jit(solution)/shard_map/ppermute | solution.py:540
  7.1 2.3 %collective-permute-done.1.refs_2_ = bf16[4,16,384]{2,1,0:T(8,128)(2,1)S(1)} collective-permute-done((bf16[4,16,384]{2,1,0:T(8,128)(2,1)S(1)}, bf16[4,16,384]{2,1,0:T(8,128)(2,1)S(1)}, u32[]{:S(2)}, u32[]{:S(2)}) %collective-permute-start.1) | collective-permute-done | bytes 49184 | tf_op jit(solution)/shard_map/ppermute | solution.py:540
  9.4 1.1 %collective-permute-done.2.refs_3_ = bf16[4,16,384]{2,1,0:T(8,128)(2,1)S(1)} collective-permute-done((bf16[4,16,384]{2,1,0:T(8,128)(2,1)S(1)}, bf16[4,16,384]{2,1,0:T(8,128)(2,1)S(1)}, u32[]{:S(2)}, u32[]{:S(2)}) %collective-permute-start.2) | collective-permute-done | bytes 49184 | tf_op jit(solution)/shard_map/ppermute | solution.py:540
  10.5 2.1 %collective-permute-start.3 = (bf16[4,16,384]{2,1,0:T(8,128)(2,1)S(1)}, bf16[4,16,384]{2,1,0:T(8,128)(2,1)S(1)}, u32[]{:S(2)}, u32[]{:S(2)}) collective-permute-start(bf16[4,16,384]{2,1,0:T(8,128)(2,1)S(1)} %get-tuple-element.41), channel_id=1, source_target_pairs={{0,1},{1,2},{2,3},{3,7},{7,6},{6,5},{5,4},{4,8},{8,9},{9,10},{10,1... | collective-permute-start | bytes 147464 | tf_op jit(solution)/shard_map/ppermute | solution.py:572
  12.5 1.3 %collective-permute-start.4 = (bf16[4,16,384]{2,1,0:T(8,128)(2,1)S(1)}, bf16[4,16,384]{2,1,0:T(8,128)(2,1)S(1)}, u32[]{:S(2)}, u32[]{:S(2)}) collective-permute-start(bf16[4,16,384]{2,1,0:T(8,128)(2,1)S(1)} %get-tuple-element.42), channel_id=1, source_target_pairs={{1,0},{2,1},{3,2},{7,3},{6,7},{5,6},{4,5},{8,4},{9,8},{10,9},{11,1... | collective-permute-start | bytes 147464 | tf_op jit(solution)/shard_map/ppermute | solution.py:572
  13.9 5.0 %collective-permute-start.6 = (bf16[2,2,16,384]{3,2,1,0:T(8,128)(2,1)S(1)}, bf16[2,2,16,384]{3,2,1,0:T(8,128)(2,1)S(1)}, u32[]{:S(2)}, u32[]{:S(2)}) collective-permute-start(bf16[2,2,16,384]{3,2,1,0:T(8,128)(2,1)S(1)} %get-tuple-element.49), channel_id=1, source_target_pairs={{0,8},{4,12},{8,0},{12,4},{16,24},{20,28},{24,16},{28,20},{1,9},{5... | collective-permute-start | bytes 147464 | tf_op jit(solution)/shard_map/ppermute | solution.py:521
  18.9 2.6 %collective-permute-start.7 = (bf16[2,2,16,384]{3,2,1,0:T(8,128)(2,1)S(1)}, bf16[2,2,16,384]{3,2,1,0:T(8,128)(2,1)S(1)}, u32[]{:S(2)}, u32[]{:S(2)}) collective-permute-start(bf16[2,2,16,384]{3,2,1,0:T(8,128)(2,1)S(1)} %get-tuple-element.50), channel_id=1, source_target_pairs={{0,16},{4,20},{8,24},{12,28},{16,0},{20,4},{24,8},{28,12},{1,17},{... | collective-permute-start | bytes 147464 | tf_op jit(solution)/shard_map/ppermute | solution.py:521
  21.6 3.5 %shard_map.121 = (f32[64,8,128]{2,1,0:T(8,128)S(1)}, f32[64,8,768]{2,1,0:T(8,128)S(1)}, f32[64,8,768]{2,1,0:T(8,128)S(1)}) custom-call(bf16[256,384]{1,0:T(8,128)(2,1)S(1)} %get-tuple-element.36.norm_ref.after_ref, bf16[4,16,384]{2,1,0:T(8,128)(2,1)S(1)} %get-tuple-element.37.refs_0_, bf16[4,16,384]{2,1,0:T(8,128)(2,1)S(1)} %collective-permute-done.refs_1_, ...), custom_call_target="tpu_custom_call" | custom-call | flops 1711276032 | bytes 4194304 | tf_op jit(solution)/shard_map/pallas_call | solution.py:408
  25.1 2.3 %collective-permute-done.8.refs_3_ = bf16[2,2,16,384]{3,2,1,0:T(8,128)(2,1)S(1)} collective-permute-done((bf16[2,2,16,384]{3,2,1,0:T(8,128)(2,1)S(1)}, bf16[2,2,16,384]{3,2,1,0:T(8,128)(2,1)S(1)}, u32[]{:S(2)}, u32[]{:S(2)}) %collective-permute-start.8) | collective-permute-done | bytes 49184 | tf_op jit(solution)/shard_map/ppermute | solution.py:521
  27.4 1.3 %collective-permute-start.10 = (bf16[8,16,384]{2,1,0:T(8,128)(2,1)S(1)}, bf16[8,16,384]{2,1,0:T(8,128)(2,1)S(1)}, u32[]{:S(2)}, u32[]{:S(2)}) collective-permute-start(bf16[8,16,384]{2,1,0:T(8,128)(2,1)S(1)} %get-tuple-element.53), channel_id=1, source_target_pairs={{4,0},{8,4},{12,8},{16,12},{20,16},{24,20},{28,24},{29,28},{25,29}... | collective-permute-start | bytes 294920 | tf_op jit(solution)/shard_map/ppermute | solution.py:572
  28.8 4.9 %collective-permute-start.9 = (bf16[8,16,384]{2,1,0:T(8,128)(2,1)S(1)}, bf16[8,16,384]{2,1,0:T(8,128)(2,1)S(1)}, u32[]{:S(2)}, u32[]{:S(2)}) collective-permute-start(bf16[8,16,384]{2,1,0:T(8,128)(2,1)S(1)} %get-tuple-element.52), channel_id=1, source_target_pairs={{0,4},{4,8},{8,12},{12,16},{16,20},{20,24},{24,28},{28,29},{29,25}... | collective-permute-start | bytes 294920 | tf_op jit(solution)/shard_map/ppermute | solution.py:572
  33.9 1.7 %collective-permute-done.9.refs_4_ = bf16[8,16,384]{2,1,0:T(8,128)(2,1)S(1)} collective-permute-done((bf16[8,16,384]{2,1,0:T(8,128)(2,1)S(1)}, bf16[8,16,384]{2,1,0:T(8,128)(2,1)S(1)}, u32[]{:S(2)}, u32[]{:S(2)}) %collective-permute-start.9) | collective-permute-done | bytes 98336 | tf_op jit(solution)/shard_map/ppermute | solution.py:572
  35.6 5.1 %shard_map.125 = (f32[128,8,128]{2,1,0:T(8,128)S(1)}, f32[128,8,384]{2,1,0:T(8,128)S(1)}, f32[128,8,384]{2,1,0:T(8,128)S(1)}) custom-call(f32[64,8,128]{2,1,0:T(8,128)S(1)} %get-tuple-element.43.after_ref.coef_ref, bf16[2,2,16,384]{3,2,1,0:T(8,128)(2,1)S(1)} %shard_map.122.refs_0_, bf16[2,2,16,384]{3,2,1,0:T(8,128)(2,1)S(1)} %collective-permute-done.6.refs_1_, ...), custom_call_target="tpu_custom_call" | custom-call | flops 2818572288 | bytes 4194304 | tf_op jit(solution)/shard_map/pallas_call | solution.py:408
  40.7 9.9 %shard_map.126.scanned_ref = bf16[1024,384]{1,0:T(8,128)(2,1)S(1)} custom-call(bf16[256,384]{1,0:T(8,128)(2,1)S(1)} %get-tuple-element.36.norm_ref.after_ref, f32[128,8,128]{2,1,0:T(8,128)S(1)} %get-tuple-element.54.coef_ref, f32[128,8,384]{2,1,0:T(8,128)S(1)} %get-tuple-element.55.s_ref, f32[128,8,384]{2,1,0:T(8,128)S(1)} %get-tuple-element.56.u_ref, ...), custom_call_target="tpu_custom_call" | custom-call | flops 50331648 | bytes 4194304 | tf_op jit(solution)/shard_map/pallas_call | solution.py:444
  51.3 1.9 %collective-permute-start.11 = (bf16[2,32,768]{2,1,0:T(8,128)(2,1)S(1)}, bf16[2,32,768]{2,1,0:T(8,128)(2,1)S(1)}, u32[]{:S(2)}, u32[]{:S(2)}) collective-permute-start(bf16[2,32,768]{2,1,0:T(8,128)(2,1)S(1)} %get-tuple-element.58), channel_id=1, source_target_pairs={{0,8},{4,12},{8,0},{12,4},{16,24},{20,28},{24,16},{28,20},{1,9},{5... | collective-permute-start | bytes 294920 | tf_op jit(solution)/shard_map/ppermute | solution.py:521
  53.3 2.0 %collective-permute-start.12 = (bf16[2,32,768]{2,1,0:T(8,128)(2,1)S(1)}, bf16[2,32,768]{2,1,0:T(8,128)(2,1)S(1)}, u32[]{:S(2)}, u32[]{:S(2)}) collective-permute-start(bf16[2,32,768]{2,1,0:T(8,128)(2,1)S(1)} %get-tuple-element.59), channel_id=1, source_target_pairs={{0,16},{4,20},{8,24},{12,28},{16,0},{20,4},{24,8},{28,12},{1,17},{... | collective-permute-start | bytes 294920 | tf_op jit(solution)/shard_map/ppermute | solution.py:521
  55.8 8.7 %shard_map.128.after_ref.scanned_ref = bf16[512,768]{1,0:T(8,128)(2,1)S(1)} custom-call(bf16[2,32,768]{2,1,0:T(8,128)(2,1)S(1)} %get-tuple-element.57.after_ref.refs_0_, f32[64,8,128]{2,1,0:T(8,128)S(1)} %get-tuple-element.43.after_ref.coef_ref, f32[64,8,768]{2,1,0:T(8,128)S(1)} %get-tuple-element.61.s_ref, f32[64,8,768]{2,1,0:T(8,128)S(1)} %get-tuple-element.62.u_ref, ...), custom_call_target="tpu_custom_call" | custom-call | flops 50331648 | bytes 4194304 | tf_op jit(solution)/shard_map/pallas_call | solution.py:444
  64.6 2.5 %collective-permute-start.14 = (bf16[4,32,768]{2,1,0:T(8,128)(2,1)S(1)}, bf16[4,32,768]{2,1,0:T(8,128)(2,1)S(1)}, u32[]{:S(2)}, u32[]{:S(2)}) collective-permute-start(bf16[4,32,768]{2,1,0:T(8,128)(2,1)S(1)} %shard_map.129.after_ref), channel_id=1, source_target_pairs={{0,4},{4,0},{8,12},{12,8},{16,20},{20,16},{24,28},{28,24},{1,5},{5... | collective-permute-start | bytes 589832 | tf_op jit(solution)/shard_map/ppermute | solution.py:521
  67.7 1.8 %collective-permute-start.17 = (bf16[64,768]{1,0:T(8,128)(2,1)S(1)}, bf16[64,768]{1,0:T(8,128)(2,1)S(1)}, u32[]{:S(2)}, u32[]{:S(2)}) collective-permute-start(bf16[64,768]{1,0:T(8,128)(2,1)S(1)} %get-tuple-element.66), channel_id=1, source_target_pairs={{0,3},{1,2},{2,1},{3,0},{4,7},{5,6},{6,5},{7,4},{8,11},{9,10},{10,... | collective-permute-start | bytes 294920 | tf_op jit(solution)/shard_map/ppermute | solution.py:540
  69.8 3.4 %collective-permute-done.16.refs_7_ = bf16[64,768]{1,0:T(8,128)(2,1)S(1)} collective-permute-done((bf16[64,768]{1,0:T(8,128)(2,1)S(1)}, bf16[64,768]{1,0:T(8,128)(2,1)S(1)}, u32[]{:S(2)}, u32[]{:S(2)}) %collective-permute-start.16) | collective-permute-done | bytes 98336 | tf_op jit(solution)/shard_map/ppermute | solution.py:540
  73.2 1.2 %collective-permute-done.17.refs_8_ = bf16[64,768]{1,0:T(8,128)(2,1)S(1)} collective-permute-done((bf16[64,768]{1,0:T(8,128)(2,1)S(1)}, bf16[64,768]{1,0:T(8,128)(2,1)S(1)}, u32[]{:S(2)}, u32[]{:S(2)}) %collective-permute-start.17) | collective-permute-done | bytes 98336 | tf_op jit(solution)/shard_map/ppermute | solution.py:540
  74.5 1.7 %shard_map.131 = bf16[16,16,384]{2,1,0:T(8,128)(2,1)} custom-call(bf16[256,768]{1,0:T(8,128)(2,1)S(1)} %shard_map.119.gate_ref, f32[768]{0:T(1024)S(1)} %copy-done.2, bf16[768,384]{1,0:T(8,128)(2,1)S(1)} %copy-done.1, bf16[2,32,768]{2,1,0:T(8,128)(2,1)S(1)} %get-tuple-element.57.after_ref.refs_0_, bf16[2,32,768]{2,1,0:T(8,128)(2,1)S(1)} %collective-permute-done.11.refs_1_, ...), custom_call_target="tpu_custom_call" | custom-call | tf_op jit(solution)/shard_map/pallas_call | solution.py:636
  (50 shorter events, 4.2 us)
Async XLA Ops:
  0.0 21.5 %copy-start.3 = (bf16[4,768,56]{1,2,0:T(8,128)(2,1)S(1)}, bf16[4,768,56]{1,2,0:T(8,128)(2,1)}, u32[]{:S(2)}) copy-start(bf16[4,768,56]{1,2,0:T(8,128)(2,1)} %param.17) | copy-start | bytes 1032196
  0.0 21.5 %copy-start = (bf16[384,1536]{1,0:T(8,128)(2,1)S(1)}, bf16[384,1536]{1,0:T(8,128)(2,1)}, u32[]{:S(2)}) copy-start(bf16[384,1536]{1,0:T(8,128)(2,1)} %refs_6_.3) | copy-start | bytes 3538948
  0.0 21.5 %copy-start.4 = (f32[4,24,768]{2,1,0:T(8,128)S(1)}, f32[4,24,768]{2,1,0:T(8,128)}, u32[]{:S(2)}) copy-start(f32[4,24,768]{2,1,0:T(8,128)} %refs_10_.3) | copy-start | bytes 884740
  1.7 19.8 %copy-start.7 = (f32[3,3,768]{2,1,0:T(4,128)S(1)}, f32[3,3,768]{2,1,0:T(4,128)}, u32[]{:S(2)}) copy-start(f32[3,3,768]{2,1,0:T(4,128)} %refs_7_.3) | copy-start | bytes 82948
  1.8 19.8 %copy-start.8 = (f32[4,768]{1,0:T(4,128)S(1)}, f32[4,768]{1,0:T(4,128)}, u32[]{:S(2)}) copy-start(f32[4,768]{1,0:T(4,128)} %refs_11_.3) | copy-start | bytes 36868
  1.8 19.8 %copy-start.10 = (f32[768]{0:T(1024)S(1)}, f32[768]{0:T(1024)}, u32[]{:S(2)}) copy-start(f32[768]{0:T(1024)} %refs_8_.3) | copy-start | bytes 9220
  2.2 11.6 %collective-permute-start.5 = (bf16[4,2,16,384]{3,2,1,0:T(8,128)(2,1)S(1)}, bf16[4,2,16,384]{3,2,1,0:T(8,128)(2,1)S(1)}, u32[]{:S(2)}, u32[]{:S(2)}) collective-permute-start(bf16[4,2,16,384]{3,2,1,0:T(8,128)(2,1)S(1)} %get-tuple-element.45), channel_id=1, source_target_pairs={{0,4},{4,0},{8,12},{12,8},{16,20},{20,16},{24,28},{28,24},{1,5},{5... | collective-permute-start | bytes 294920 | tf_op jit(solution)/shard_map/ppermute | solution.py:521
  5.3 1.9 %collective-permute-start = (bf16[4,16,384]{2,1,0:T(8,128)(2,1)S(1)}, bf16[4,16,384]{2,1,0:T(8,128)(2,1)S(1)}, u32[]{:S(2)}, u32[]{:S(2)}) collective-permute-start(bf16[4,16,384]{2,1,0:T(8,128)(2,1)S(1)} %get-tuple-element.38), channel_id=1, source_target_pairs={{0,1},{1,0},{2,3},{3,2},{4,5},{5,4},{6,7},{7,6},{8,9},{9,8},{10,11... | collective-permute-start | bytes 147464 | tf_op jit(solution)/shard_map/ppermute | solution.py:540
  5.3 4.2 %collective-permute-start.1 = (bf16[4,16,384]{2,1,0:T(8,128)(2,1)S(1)}, bf16[4,16,384]{2,1,0:T(8,128)(2,1)S(1)}, u32[]{:S(2)}, u32[]{:S(2)}) collective-permute-start(bf16[4,16,384]{2,1,0:T(8,128)(2,1)S(1)} %get-tuple-element.39), channel_id=1, source_target_pairs={{0,2},{1,3},{2,0},{3,1},{4,6},{5,7},{6,4},{7,5},{8,10},{9,11},{10,... | collective-permute-start | bytes 147464 | tf_op jit(solution)/shard_map/ppermute | solution.py:540
  6.7 3.7 %collective-permute-start.2 = (bf16[4,16,384]{2,1,0:T(8,128)(2,1)S(1)}, bf16[4,16,384]{2,1,0:T(8,128)(2,1)S(1)}, u32[]{:S(2)}, u32[]{:S(2)}) collective-permute-start(bf16[4,16,384]{2,1,0:T(8,128)(2,1)S(1)} %get-tuple-element.40), channel_id=1, source_target_pairs={{0,3},{1,2},{2,1},{3,0},{4,7},{5,6},{6,5},{7,4},{8,11},{9,10},{10,... | collective-permute-start | bytes 147464 | tf_op jit(solution)/shard_map/ppermute | solution.py:540
  10.5 11.0 %collective-permute-start.3 = (bf16[4,16,384]{2,1,0:T(8,128)(2,1)S(1)}, bf16[4,16,384]{2,1,0:T(8,128)(2,1)S(1)}, u32[]{:S(2)}, u32[]{:S(2)}) collective-permute-start(bf16[4,16,384]{2,1,0:T(8,128)(2,1)S(1)} %get-tuple-element.41), channel_id=1, source_target_pairs={{0,1},{1,2},{2,3},{3,7},{7,6},{6,5},{5,4},{4,8},{8,9},{9,10},{10,1... | collective-permute-start | bytes 147464 | tf_op jit(solution)/shard_map/ppermute | solution.py:572
  12.5 9.0 %collective-permute-start.4 = (bf16[4,16,384]{2,1,0:T(8,128)(2,1)S(1)}, bf16[4,16,384]{2,1,0:T(8,128)(2,1)S(1)}, u32[]{:S(2)}, u32[]{:S(2)}) collective-permute-start(bf16[4,16,384]{2,1,0:T(8,128)(2,1)S(1)} %get-tuple-element.42), channel_id=1, source_target_pairs={{1,0},{2,1},{3,2},{7,3},{6,7},{5,6},{4,5},{8,4},{9,8},{10,9},{11,1... | collective-permute-start | bytes 147464 | tf_op jit(solution)/shard_map/ppermute | solution.py:572
  13.9 11.2 %collective-permute-start.6 = (bf16[2,2,16,384]{3,2,1,0:T(8,128)(2,1)S(1)}, bf16[2,2,16,384]{3,2,1,0:T(8,128)(2,1)S(1)}, u32[]{:S(2)}, u32[]{:S(2)}) collective-permute-start(bf16[2,2,16,384]{3,2,1,0:T(8,128)(2,1)S(1)} %get-tuple-element.49), channel_id=1, source_target_pairs={{0,8},{4,12},{8,0},{12,4},{16,24},{20,28},{24,16},{28,20},{1,9},{5... | collective-permute-start | bytes 147464 | tf_op jit(solution)/shard_map/ppermute | solution.py:521
  18.9 6.2 %collective-permute-start.7 = (bf16[2,2,16,384]{3,2,1,0:T(8,128)(2,1)S(1)}, bf16[2,2,16,384]{3,2,1,0:T(8,128)(2,1)S(1)}, u32[]{:S(2)}, u32[]{:S(2)}) collective-permute-start(bf16[2,2,16,384]{3,2,1,0:T(8,128)(2,1)S(1)} %get-tuple-element.50), channel_id=1, source_target_pairs={{0,16},{4,20},{8,24},{12,28},{16,0},{20,4},{24,8},{28,12},{1,17},{... | collective-permute-start | bytes 147464 | tf_op jit(solution)/shard_map/ppermute | solution.py:521
  21.5 5.9 %collective-permute-start.8 = (bf16[2,2,16,384]{3,2,1,0:T(8,128)(2,1)S(1)}, bf16[2,2,16,384]{3,2,1,0:T(8,128)(2,1)S(1)}, u32[]{:S(2)}, u32[]{:S(2)}) collective-permute-start(bf16[2,2,16,384]{3,2,1,0:T(8,128)(2,1)S(1)} %get-tuple-element.51), channel_id=1, source_target_pairs={{0,24},{4,28},{8,16},{12,20},{16,8},{20,12},{24,0},{28,4},{1,25},{... | collective-permute-start | bytes 147464 | tf_op jit(solution)/shard_map/ppermute | solution.py:521
  27.4 6.5 %collective-permute-start.10 = (bf16[8,16,384]{2,1,0:T(8,128)(2,1)S(1)}, bf16[8,16,384]{2,1,0:T(8,128)(2,1)S(1)}, u32[]{:S(2)}, u32[]{:S(2)}) collective-permute-start(bf16[8,16,384]{2,1,0:T(8,128)(2,1)S(1)} %get-tuple-element.53), channel_id=1, source_target_pairs={{4,0},{8,4},{12,8},{16,12},{20,16},{24,20},{28,24},{29,28},{25,29}... | collective-permute-start | bytes 294920 | tf_op jit(solution)/shard_map/ppermute | solution.py:572
  28.8 6.9 %collective-permute-start.9 = (bf16[8,16,384]{2,1,0:T(8,128)(2,1)S(1)}, bf16[8,16,384]{2,1,0:T(8,128)(2,1)S(1)}, u32[]{:S(2)}, u32[]{:S(2)}) collective-permute-start(bf16[8,16,384]{2,1,0:T(8,128)(2,1)S(1)} %get-tuple-element.52), channel_id=1, source_target_pairs={{0,4},{4,8},{8,12},{12,16},{16,20},{20,24},{24,28},{28,29},{29,25}... | collective-permute-start | bytes 294920 | tf_op jit(solution)/shard_map/ppermute | solution.py:572
  51.3 13.2 %collective-permute-start.11 = (bf16[2,32,768]{2,1,0:T(8,128)(2,1)S(1)}, bf16[2,32,768]{2,1,0:T(8,128)(2,1)S(1)}, u32[]{:S(2)}, u32[]{:S(2)}) collective-permute-start(bf16[2,32,768]{2,1,0:T(8,128)(2,1)S(1)} %get-tuple-element.58), channel_id=1, source_target_pairs={{0,8},{4,12},{8,0},{12,4},{16,24},{20,28},{24,16},{28,20},{1,9},{5... | collective-permute-start | bytes 294920 | tf_op jit(solution)/shard_map/ppermute | solution.py:521
  53.3 11.3 %collective-permute-start.12 = (bf16[2,32,768]{2,1,0:T(8,128)(2,1)S(1)}, bf16[2,32,768]{2,1,0:T(8,128)(2,1)S(1)}, u32[]{:S(2)}, u32[]{:S(2)}) collective-permute-start(bf16[2,32,768]{2,1,0:T(8,128)(2,1)S(1)} %get-tuple-element.59), channel_id=1, source_target_pairs={{0,16},{4,20},{8,24},{12,28},{16,0},{20,4},{24,8},{28,12},{1,17},{... | collective-permute-start | bytes 294920 | tf_op jit(solution)/shard_map/ppermute | solution.py:521
  55.3 9.3 %collective-permute-start.13 = (bf16[2,32,768]{2,1,0:T(8,128)(2,1)S(1)}, bf16[2,32,768]{2,1,0:T(8,128)(2,1)S(1)}, u32[]{:S(2)}, u32[]{:S(2)}) collective-permute-start(bf16[2,32,768]{2,1,0:T(8,128)(2,1)S(1)} %get-tuple-element.60), channel_id=1, source_target_pairs={{0,24},{4,28},{8,16},{12,20},{16,8},{20,12},{24,0},{28,4},{1,25},{... | collective-permute-start | bytes 294920 | tf_op jit(solution)/shard_map/ppermute | solution.py:521
  64.6 9.8 %collective-permute-start.14 = (bf16[4,32,768]{2,1,0:T(8,128)(2,1)S(1)}, bf16[4,32,768]{2,1,0:T(8,128)(2,1)S(1)}, u32[]{:S(2)}, u32[]{:S(2)}) collective-permute-start(bf16[4,32,768]{2,1,0:T(8,128)(2,1)S(1)} %shard_map.129.after_ref), channel_id=1, source_target_pairs={{0,4},{4,0},{8,12},{12,8},{16,20},{20,16},{24,28},{28,24},{1,5},{5... | collective-permute-start | bytes 589832 | tf_op jit(solution)/shard_map/ppermute | solution.py:521
  67.5 2.3 %collective-permute-start.15 = (bf16[64,768]{1,0:T(8,128)(2,1)S(1)}, bf16[64,768]{1,0:T(8,128)(2,1)S(1)}, u32[]{:S(2)}, u32[]{:S(2)}) collective-permute-start(bf16[64,768]{1,0:T(8,128)(2,1)S(1)} %get-tuple-element.64), channel_id=1, source_target_pairs={{0,1},{1,0},{2,3},{3,2},{4,5},{5,4},{6,7},{7,6},{8,9},{9,8},{10,11... | collective-permute-start | bytes 294920 | tf_op jit(solution)/shard_map/ppermute | solution.py:540
  67.6 5.7 %collective-permute-start.16 = (bf16[64,768]{1,0:T(8,128)(2,1)S(1)}, bf16[64,768]{1,0:T(8,128)(2,1)S(1)}, u32[]{:S(2)}, u32[]{:S(2)}) collective-permute-start(bf16[64,768]{1,0:T(8,128)(2,1)S(1)} %get-tuple-element.65), channel_id=1, source_target_pairs={{0,2},{1,3},{2,0},{3,1},{4,6},{5,7},{6,4},{7,5},{8,10},{9,11},{10,... | collective-permute-start | bytes 294920 | tf_op jit(solution)/shard_map/ppermute | solution.py:540
  67.7 6.8 %collective-permute-start.17 = (bf16[64,768]{1,0:T(8,128)(2,1)S(1)}, bf16[64,768]{1,0:T(8,128)(2,1)S(1)}, u32[]{:S(2)}, u32[]{:S(2)}) collective-permute-start(bf16[64,768]{1,0:T(8,128)(2,1)S(1)} %get-tuple-element.66), channel_id=1, source_target_pairs={{0,3},{1,2},{2,1},{3,0},{4,7},{5,6},{6,5},{7,4},{8,11},{9,10},{10,... | collective-permute-start | bytes 294920 | tf_op jit(solution)/shard_map/ppermute | solution.py:540
  (6 other events, 45.4 us)

commit v9 on v6

--- a/solution.py
+++ b/solution.py
@@ -203,7 +203,7 @@
             rest = jnp.zeros((LANES - 3 * RANK, chunk), F32)
             step_ref[kind, :] = jnp.concatenate([high, high, w - high, rest], axis=0).astype(BF16)
 
-    piece = 256
+    piece = 512
     for first in range(0, time * SLOTS, piece):
         row = rows_of(piece, first)
         now = row >> 3
@@ -266,14 +266,12 @@
     halves = decay_ref.shape[2] // chunk
     states = decay_ref.shape[1]
     groups = chunk // LANES
-    at_once = max(1, 12 // groups)
-    unroll = 16 if axis == "col" else 8
+    at_once = 4
+    unroll = 16 if axis == "col" else 32
     laps = time // unroll
-    base2 = axis == "col"
-    power = jnp.exp2 if base2 else jnp.exp
 
     ks = (0, 1) if axis == "col" else (2, 3)
-    piece = 32
+    piece = 64
     row = lax.broadcasted_iota(jnp.int32, (2 * LANES, LANES), 0) & (LANES - 1)
     taken = [jnp.where(row == 3 * RANK + n, 1.0, 0.0).astype(BF16) for n in range(2 * states)]
 
@@ -298,7 +296,7 @@
                     halves,
                     lambda half, way: decay_ref[ks[way], n : n + 1, half * chunk + g * LANES : half * chunk + (g + 1) * LANES],
                 )
-                rates[-1].append((-LOG2E if base2 else -1.0) * jnp.exp(rate))
+                rates[-1].append(-LOG2E * jnp.exp(rate))
         if first == 0:
             skips = [
                 by_slot(
@@ -316,12 +314,15 @@
                 t = lap * unroll + sub
                 enter = [spread_ref[t, first + n] for n in range(at_once)]
                 leave = [spread_ref[t, states + first + n] for n in range(at_once)]
+                decay = []
+                for g in range(groups):
+                    step = s_ref[t, :, g * LANES : (g + 1) * LANES]
+                    decay.append([jnp.exp2(step * rates[n][g]) for n in range(at_once)])
                 for g in range(groups):
                     cells = pl.ds(g * LANES, LANES)
-                    step = s_ref[t, :, cells]
                     if first == 0:
                         u = u_ref[t, :, cells]
-                        value = step * u
+                        value = s_ref[t, :, cells] * u
                         v_ref[t, :, cells] = value
                         y = skips[g] * u
                     else:
@@ -329,7 +330,7 @@
                         y = y_ref[t, :, cells]
                     for n in range(at_once):
                         k = n * groups + g
-                        h = power(step * rates[n][g]) * hidden[k] + value * enter[n]
+                        h = decay[g][n] * hidden[k] + value * enter[n]
                         hidden[k] = h
                         y = y + h * leave[n]
                     y_ref[t, :, cells] = y

time: 68.1 us -> 65.8 us (0.966)
  Pallas kernels: 31.9 us -> 29.5 us
    pallas_call x2, Pallas kernels: 19.5 us -> 17.9 us  [scan(): pl.pallas_call(functools.partial(scan_kernel, axis), out_shape=jax.ShapeD...]
    pallas_call x2, Pallas kernels: 8.6 us -> 7.75 us  [prepare(): pl.pallas_call(functools.partial(prepare_kernel, lines, axis), out_shape=...]
  transfers between devices with their start and end apart: 16 -> 16, of which waited for: 5 -> 6; matrix products, arithmetic and copies ran while one was open for 0% -> 0% of each run, Pallas kernels for 19% -> 19%
where the time goes in v9:
time: 65.8 us; the launch traced here: 65.6 us
  Pallas kernels  29.5 us (45%)
  starting transfers between devices  21.4 us (33%)
  waiting for transfers between devices  12.7 us (19%)
  local copies, waits for them, and re-layouts  1.79 us (3%)
    pallas_call x2, Pallas kernels, scan(): pl.pallas_call(functools.partial(scan_kernel, axis), out_shape=jax.ShapeD...  17.9 us
    ppermute x8, starting transfers between devices, swap(): lax.ppermute(block, axis, [(i, i ^ k) for i in range(lax.axis_size(axis))])  14.7 us
    ppermute x6, waiting for transfers between devices, swap_blocks(): lax.ppermute(blocks[k], axis, [(i, i ^ k) for i in range(count)])  8.97 us
    pallas_call x2, Pallas kernels, prepare(): pl.pallas_call(functools.partial(prepare_kernel, lines, axis), out_shape=...  7.75 us
    ppermute x6, starting transfers between devices, swap_blocks(): lax.ppermute(blocks[k], axis, [(i, i ^ k) for i in range(count)])  4.98 us
    ppermute x8, waiting for transfers between devices, swap(): lax.ppermute(block, axis, [(i, i ^ k) for i in range(lax.axis_size(axis))])  3.69 us
    unnamed x24, local copies, waits for them, and re-layouts  1.79 us
    pallas_call x1, Pallas kernels, local(): pl.pallas_call(functools.partial(end_kernel, half), out_shape=jax.ShapeDt...  1.73 us
  transfers between devices with their start and end apart: 16, of which 6 were waited for; matrix products, arithmetic and copies ran while one was open for 0% of the time, Pallas kernels for 19%

profile of v9, /device:TPU:0, one launch (start us, length us, event | category | flops | bytes accessed | tf_op | source)
XLA Modules:
  0.0 65.6 jit_solution(5041655646114470240)
XLA Ops:
  0.0 1.1 %copy-done.5 = bf16[16,16,384]{2,1,0:T(8,128)(2,1)S(1)} copy-done((bf16[16,16,384]{2,1,0:T(8,128)(2,1)S(1)}, bf16[16,16,384]{2,1,0:T(8,128)(2,1)}, u32[]{:S(2)}) %copy-start.5) | copy-done | bytes 196632
  1.1 0.7 %copy-done.11 = f32[384]{0:T(512)S(1)} copy-done((f32[384]{0:T(512)S(1)}, f32[384]{0:T(512)}, u32[]{:S(2)}) %copy-start.11) | copy-done | bytes 1560
  2.3 3.0 %collective-permute-start.4 = (bf16[4,4,16,384]{3,2,1,0:T(8,128)(2,1)S(1)}, bf16[4,4,16,384]{3,2,1,0:T(8,128)(2,1)S(1)}, u32[]{:S(2)}, u32[]{:S(2)}) collective-permute-start(bf16[4,4,16,384]{3,2,1,0:T(8,128)(2,1)S(1)} %get-tuple-element.39), channel_id=1, source_target_pairs={{0,4},{4,0},{8,12},{12,8},{16,20},{20,16},{24,28},{28,24},{1,5},{5... | collective-permute-start | bytes 589832 | tf_op jit(solution)/shard_map/ppermute | solution.py:510
  5.3 1.5 %collective-permute-start.1 = (bf16[6,16,384]{2,1,0:T(8,128)(2,1)S(1)}, bf16[6,16,384]{2,1,0:T(8,128)(2,1)S(1)}, u32[]{:S(2)}, u32[]{:S(2)}) collective-permute-start(bf16[6,16,384]{2,1,0:T(8,128)(2,1)S(1)} %get-tuple-element.35), channel_id=1, source_target_pairs={{0,2},{1,3},{2,0},{3,1},{4,6},{5,7},{6,4},{7,5},{8,10},{9,11},{10,... | collective-permute-start | bytes 221192 | tf_op jit(solution)/shard_map/ppermute | solution.py:529
  7.2 3.0 %collective-permute-done.1.refs_2_ = bf16[6,16,384]{2,1,0:T(8,128)(2,1)S(1)} collective-permute-done((bf16[6,16,384]{2,1,0:T(8,128)(2,1)S(1)}, bf16[6,16,384]{2,1,0:T(8,128)(2,1)S(1)}, u32[]{:S(2)}, u32[]{:S(2)}) %collective-permute-start.1) | collective-permute-done | bytes 73760 | tf_op jit(solution)/shard_map/ppermute | solution.py:529
  10.2 1.2 %collective-permute-done.2.refs_3_ = bf16[6,16,384]{2,1,0:T(8,128)(2,1)S(1)} collective-permute-done((bf16[6,16,384]{2,1,0:T(8,128)(2,1)S(1)}, bf16[6,16,384]{2,1,0:T(8,128)(2,1)S(1)}, u32[]{:S(2)}, u32[]{:S(2)}) %collective-permute-start.2) | collective-permute-done | bytes 73760 | tf_op jit(solution)/shard_map/ppermute | solution.py:529
  11.4 0.7 collective-permute-start.3
  12.1 3.0 %collective-permute-start.5 = (bf16[2,4,16,384]{3,2,1,0:T(8,128)(2,1)S(1)}, bf16[2,4,16,384]{3,2,1,0:T(8,128)(2,1)S(1)}, u32[]{:S(2)}, u32[]{:S(2)}) collective-permute-start(bf16[2,4,16,384]{3,2,1,0:T(8,128)(2,1)S(1)} %get-tuple-element.43), channel_id=1, source_target_pairs={{0,8},{4,12},{8,0},{12,4},{16,24},{20,28},{24,16},{28,20},{1,9},{5... | collective-permute-start | bytes 294920 | tf_op jit(solution)/shard_map/ppermute | solution.py:510
  15.0 2.9 %collective-permute-start.6 = (bf16[2,4,16,384]{3,2,1,0:T(8,128)(2,1)S(1)}, bf16[2,4,16,384]{3,2,1,0:T(8,128)(2,1)S(1)}, u32[]{:S(2)}, u32[]{:S(2)}) collective-permute-start(bf16[2,4,16,384]{3,2,1,0:T(8,128)(2,1)S(1)} %get-tuple-element.44), channel_id=1, source_target_pairs={{0,16},{4,20},{8,24},{12,28},{16,0},{20,4},{24,8},{28,12},{1,17},{... | collective-permute-start | bytes 294920 | tf_op jit(solution)/shard_map/ppermute | solution.py:510
  18.0 3.5 %shard_map.121 = (f32[64,8,128]{2,1,0:T(8,128)S(1)}, f32[64,8,768]{2,1,0:T(8,128)S(1)}, f32[64,8,768]{2,1,0:T(8,128)S(1)}) custom-call(bf16[256,384]{1,0:T(8,128)(2,1)S(1)} %get-tuple-element.32.norm_ref.after_ref, bf16[6,16,384]{2,1,0:T(8,128)(2,1)S(1)} %get-tuple-element.33.refs_0_, bf16[6,16,384]{2,1,0:T(8,128)(2,1)S(1)} %collective-permute-done.refs_1_, ...), custom_call_target="tpu_custom_call" | custom-call | flops 1711276032 | bytes 4194304 | tf_op jit(solution)/shard_map/pallas_call | solution.py:397
  21.5 3.4 %collective-permute-done.6.refs_2_ = bf16[2,4,16,384]{3,2,1,0:T(8,128)(2,1)S(1)} collective-permute-done((bf16[2,4,16,384]{3,2,1,0:T(8,128)(2,1)S(1)}, bf16[2,4,16,384]{3,2,1,0:T(8,128)(2,1)S(1)}, u32[]{:S(2)}, u32[]{:S(2)}) %collective-permute-start.6) | collective-permute-done | bytes 98336 | tf_op jit(solution)/shard_map/ppermute | solution.py:510
  25.0 1.0 %collective-permute-start.8 = (bf16[8,16,384]{2,1,0:T(8,128)(2,1)S(1)}, bf16[8,16,384]{2,1,0:T(8,128)(2,1)S(1)}, u32[]{:S(2)}, u32[]{:S(2)}) collective-permute-start(bf16[8,16,384]{2,1,0:T(8,128)(2,1)S(1)} %shard_map.124), channel_id=1, source_target_pairs={{28,29},{1,2},{30,31},{29,28},{2,1},{31,30}} | collective-permute-start | bytes 294920 | tf_op jit(solution)/shard_map/ppermute | solution.py:561
  26.0 4.3 %shard_map.125 = (f32[128,8,128]{2,1,0:T(8,128)S(1)}, f32[128,8,384]{2,1,0:T(8,128)S(1)}, f32[128,8,384]{2,1,0:T(8,128)S(1)}) custom-call(f32[64,8,128]{2,1,0:T(8,128)S(1)} %get-tuple-element.37.after_ref.coef_ref, bf16[2,4,16,384]{3,2,1,0:T(8,128)(2,1)S(1)} %shard_map.122.refs_0_, bf16[2,4,16,384]{3,2,1,0:T(8,128)(2,1)S(1)} %collective-permute-done.5.refs_1_, ...), custom_call_target="tpu_custom_call" | custom-call | flops 2818572288 | bytes 4194304 | tf_op jit(solution)/shard_map/pallas_call | solution.py:397
  30.3 9.5 %shard_map.126.scanned_ref = bf16[1024,384]{1,0:T(8,128)(2,1)S(1)} custom-call(bf16[256,384]{1,0:T(8,128)(2,1)S(1)} %get-tuple-element.32.norm_ref.after_ref, f32[128,8,128]{2,1,0:T(8,128)S(1)} %get-tuple-element.46.coef_ref, f32[128,8,384]{2,1,0:T(8,128)S(1)} %get-tuple-element.47.s_ref, f32[128,8,384]{2,1,0:T(8,128)S(1)} %get-tuple-element.48.u_ref, ...), custom_call_target="tpu_custom_call" | custom-call | flops 50331648 | bytes 4194304 | tf_op jit(solution)/shard_map/pallas_call | solution.py:433
  39.8 0.7 %shard_map.127 = (bf16[2,32,768]{2,1,0:T(8,128)(2,1)S(1)}, bf16[2,32,768]{2,1,0:T(8,128)(2,1)S(1)}, bf16[2,32,768]{2,1,0:T(8,128)(2,1)S(1)}, bf16[2,32,768]{2,1,0:T(8,128)(2,1)S(1)}) custom-call(bf16[256,384]{1,0:T(8,128)(2,1)S(1)} %get-tuple-element.32.norm_ref.after_ref, bf16[1024,384]{1,0:T(8,128)(2,1)S(1)} %shard_map.126.scanned_ref), custom_call_target="tpu_custom_call" | custom-call | tf_op jit(solution)/shard_map/pallas_call | solution.py:372
  40.6 2.1 %collective-permute-start.10 = (bf16[2,32,768]{2,1,0:T(8,128)(2,1)S(1)}, bf16[2,32,768]{2,1,0:T(8,128)(2,1)S(1)}, u32[]{:S(2)}, u32[]{:S(2)}) collective-permute-start(bf16[2,32,768]{2,1,0:T(8,128)(2,1)S(1)} %get-tuple-element.51), channel_id=1, source_target_pairs={{0,16},{4,20},{8,24},{12,28},{16,0},{20,4},{24,8},{28,12},{1,17},{... | collective-permute-start | bytes 294920 | tf_op jit(solution)/shard_map/ppermute | solution.py:510
  42.7 1.9 %collective-permute-start.11 = (bf16[2,32,768]{2,1,0:T(8,128)(2,1)S(1)}, bf16[2,32,768]{2,1,0:T(8,128)(2,1)S(1)}, u32[]{:S(2)}, u32[]{:S(2)}) collective-permute-start(bf16[2,32,768]{2,1,0:T(8,128)(2,1)S(1)} %get-tuple-element.52), channel_id=1, source_target_pairs={{0,24},{4,28},{8,16},{12,20},{16,8},{20,12},{24,0},{28,4},{1,25},{... | collective-permute-start | bytes 294920 | tf_op jit(solution)/shard_map/ppermute | solution.py:510
  44.6 8.4 %shard_map.128.after_ref.scanned_ref = bf16[512,768]{1,0:T(8,128)(2,1)S(1)} custom-call(bf16[2,32,768]{2,1,0:T(8,128)(2,1)S(1)} %get-tuple-element.49.after_ref.refs_0_, f32[64,8,128]{2,1,0:T(8,128)S(1)} %get-tuple-element.37.after_ref.coef_ref, f32[64,8,768]{2,1,0:T(8,128)S(1)} %get-tuple-element.53.s_ref, f32[64,8,768]{2,1,0:T(8,128)S(1)} %get-tuple-element.54.u_ref, ...), custom_call_target="tpu_custom_call" | custom-call | flops 50331648 | bytes 4194304 | tf_op jit(solution)/shard_map/pallas_call | solution.py:433
  53.3 1.8 %collective-permute-start.12 = (bf16[4,32,768]{2,1,0:T(8,128)(2,1)S(1)}, bf16[4,32,768]{2,1,0:T(8,128)(2,1)S(1)}, u32[]{:S(2)}, u32[]{:S(2)}) collective-permute-start(bf16[4,32,768]{2,1,0:T(8,128)(2,1)S(1)} %shard_map.129.after_ref), channel_id=1, source_target_pairs={{0,4},{4,0},{8,12},{12,8},{16,20},{20,16},{24,28},{28,24},{1,5},{5... | collective-permute-start | bytes 589832 | tf_op jit(solution)/shard_map/ppermute | solution.py:510
  55.5 0.5 collective-permute-start.13
  56.1 2.5 %collective-permute-start.14 = (bf16[64,768]{1,0:T(8,128)(2,1)S(1)}, bf16[64,768]{1,0:T(8,128)(2,1)S(1)}, u32[]{:S(2)}, u32[]{:S(2)}) collective-permute-start(bf16[64,768]{1,0:T(8,128)(2,1)S(1)} %get-tuple-element.57), channel_id=1, source_target_pairs={{0,2},{1,3},{2,0},{3,1},{4,6},{5,7},{6,4},{7,5},{8,10},{9,11},{10,... | collective-permute-start | bytes 294920 | tf_op jit(solution)/shard_map/ppermute | solution.py:529
  59.0 3.2 %collective-permute-done.14.refs_7_ = bf16[64,768]{1,0:T(8,128)(2,1)S(1)} collective-permute-done((bf16[64,768]{1,0:T(8,128)(2,1)S(1)}, bf16[64,768]{1,0:T(8,128)(2,1)S(1)}, u32[]{:S(2)}, u32[]{:S(2)}) %collective-permute-start.14) | collective-permute-done | bytes 98336 | tf_op jit(solution)/shard_map/ppermute | solution.py:529
  62.2 1.6 %collective-permute-done.15.refs_8_ = bf16[64,768]{1,0:T(8,128)(2,1)S(1)} collective-permute-done((bf16[64,768]{1,0:T(8,128)(2,1)S(1)}, bf16[64,768]{1,0:T(8,128)(2,1)S(1)}, u32[]{:S(2)}, u32[]{:S(2)}) %collective-permute-start.15) | collective-permute-done | bytes 98336 | tf_op jit(solution)/shard_map/ppermute | solution.py:529
  63.8 1.7 %shard_map.131 = bf16[16,16,384]{2,1,0:T(8,128)(2,1)} custom-call(bf16[256,768]{1,0:T(8,128)(2,1)S(1)} %shard_map.119.gate_ref, f32[768]{0:T(1024)S(1)} %copy-done.2, bf16[768,384]{1,0:T(8,128)(2,1)S(1)} %copy-done.1, bf16[2,32,768]{2,1,0:T(8,128)(2,1)S(1)} %get-tuple-element.49.after_ref.refs_0_, bf16[2,32,768]{2,1,0:T(8,128)(2,1)S(1)} %collective-permute-done.9.refs_1_, ...), custom_call_target="tpu_custom_call" | custom-call | tf_op jit(solution)/shard_map/pallas_call | solution.py:627
  (46 shorter events, 2.1 us)
Async XLA Ops:
  0.0 17.9 %copy-start.3 = (bf16[4,768,56]{1,2,0:T(8,128)(2,1)S(1)}, bf16[4,768,56]{1,2,0:T(8,128)(2,1)}, u32[]{:S(2)}) copy-start(bf16[4,768,56]{1,2,0:T(8,128)(2,1)} %param.17) | copy-start | bytes 1032196
  0.0 17.9 %copy-start = (bf16[384,1536]{1,0:T(8,128)(2,1)S(1)}, bf16[384,1536]{1,0:T(8,128)(2,1)}, u32[]{:S(2)}) copy-start(bf16[384,1536]{1,0:T(8,128)(2,1)} %refs_5_.3) | copy-start | bytes 3538948
  0.0 18.0 %copy-start.4 = (f32[4,24,768]{2,1,0:T(8,128)S(1)}, f32[4,24,768]{2,1,0:T(8,128)}, u32[]{:S(2)}) copy-start(f32[4,24,768]{2,1,0:T(8,128)} %refs_9_.3) | copy-start | bytes 884740
  1.7 16.2 %copy-start.7 = (f32[3,3,768]{2,1,0:T(4,128)S(1)}, f32[3,3,768]{2,1,0:T(4,128)}, u32[]{:S(2)}) copy-start(f32[3,3,768]{2,1,0:T(4,128)} %refs_6_.3) | copy-start | bytes 82948
  1.8 16.2 %copy-start.8 = (f32[4,768]{1,0:T(4,128)S(1)}, f32[4,768]{1,0:T(4,128)}, u32[]{:S(2)}) copy-start(f32[4,768]{1,0:T(4,128)} %refs_10_.3) | copy-start | bytes 36868
  1.8 16.2 %copy-start.10 = (f32[768]{0:T(1024)S(1)}, f32[768]{0:T(1024)}, u32[]{:S(2)}) copy-start(f32[768]{0:T(1024)} %refs_7_.3) | copy-start | bytes 9220
  2.3 9.8 %collective-permute-start.4 = (bf16[4,4,16,384]{3,2,1,0:T(8,128)(2,1)S(1)}, bf16[4,4,16,384]{3,2,1,0:T(8,128)(2,1)S(1)}, u32[]{:S(2)}, u32[]{:S(2)}) collective-permute-start(bf16[4,4,16,384]{3,2,1,0:T(8,128)(2,1)S(1)} %get-tuple-element.39), channel_id=1, source_target_pairs={{0,4},{4,0},{8,12},{12,8},{16,20},{20,16},{24,28},{28,24},{1,5},{5... | collective-permute-start | bytes 589832 | tf_op jit(solution)/shard_map/ppermute | solution.py:510
  5.3 1.9 %collective-permute-start = (bf16[6,16,384]{2,1,0:T(8,128)(2,1)S(1)}, bf16[6,16,384]{2,1,0:T(8,128)(2,1)S(1)}, u32[]{:S(2)}, u32[]{:S(2)}) collective-permute-start(bf16[6,16,384]{2,1,0:T(8,128)(2,1)S(1)} %get-tuple-element.34), channel_id=1, source_target_pairs={{0,1},{1,0},{2,3},{3,2},{4,5},{5,4},{6,7},{7,6},{8,9},{9,8},{10,11... | collective-permute-start | bytes 221192 | tf_op jit(solution)/shard_map/ppermute | solution.py:529
  5.3 4.9 %collective-permute-start.1 = (bf16[6,16,384]{2,1,0:T(8,128)(2,1)S(1)}, bf16[6,16,384]{2,1,0:T(8,128)(2,1)S(1)}, u32[]{:S(2)}, u32[]{:S(2)}) collective-permute-start(bf16[6,16,384]{2,1,0:T(8,128)(2,1)S(1)} %get-tuple-element.35), channel_id=1, source_target_pairs={{0,2},{1,3},{2,0},{3,1},{4,6},{5,7},{6,4},{7,5},{8,10},{9,11},{10,... | collective-permute-start | bytes 221192 | tf_op jit(solution)/shard_map/ppermute | solution.py:529
  6.8 4.5 %collective-permute-start.2 = (bf16[6,16,384]{2,1,0:T(8,128)(2,1)S(1)}, bf16[6,16,384]{2,1,0:T(8,128)(2,1)S(1)}, u32[]{:S(2)}, u32[]{:S(2)}) collective-permute-start(bf16[6,16,384]{2,1,0:T(8,128)(2,1)S(1)} %get-tuple-element.36), channel_id=1, source_target_pairs={{0,3},{1,2},{2,1},{3,0},{4,7},{5,6},{6,5},{7,4},{8,11},{9,10},{10,... | collective-permute-start | bytes 221192 | tf_op jit(solution)/shard_map/ppermute | solution.py:529
  11.4 6.6 %collective-permute-start.3 = (bf16[4,16,384]{2,1,0:T(8,128)(2,1)S(1)}, bf16[4,16,384]{2,1,0:T(8,128)(2,1)S(1)}, u32[]{:S(2)}, u32[]{:S(2)}) collective-permute-start(bf16[4,16,384]{2,1,0:T(8,128)(2,1)S(1)} %shard_map.120), channel_id=1, source_target_pairs={{3,7},{4,8},{11,15},{12,16},{19,23},{20,24},{27,31},{7,3},{8,4},{1... | collective-permute-start | bytes 147464 | tf_op jit(solution)/shard_map/ppermute | solution.py:561
  12.1 9.4 %collective-permute-start.5 = (bf16[2,4,16,384]{3,2,1,0:T(8,128)(2,1)S(1)}, bf16[2,4,16,384]{3,2,1,0:T(8,128)(2,1)S(1)}, u32[]{:S(2)}, u32[]{:S(2)}) collective-permute-start(bf16[2,4,16,384]{3,2,1,0:T(8,128)(2,1)S(1)} %get-tuple-element.43), channel_id=1, source_target_pairs={{0,8},{4,12},{8,0},{12,4},{16,24},{20,28},{24,16},{28,20},{1,9},{5... | collective-permute-start | bytes 294920 | tf_op jit(solution)/shard_map/ppermute | solution.py:510
  15.0 9.9 %collective-permute-start.6 = (bf16[2,4,16,384]{3,2,1,0:T(8,128)(2,1)S(1)}, bf16[2,4,16,384]{3,2,1,0:T(8,128)(2,1)S(1)}, u32[]{:S(2)}, u32[]{:S(2)}) collective-permute-start(bf16[2,4,16,384]{3,2,1,0:T(8,128)(2,1)S(1)} %get-tuple-element.44), channel_id=1, source_target_pairs={{0,16},{4,20},{8,24},{12,28},{16,0},{20,4},{24,8},{28,12},{1,17},{... | collective-permute-start | bytes 294920 | tf_op jit(solution)/shard_map/ppermute | solution.py:510
  17.9 7.0 %collective-permute-start.7 = (bf16[2,4,16,384]{3,2,1,0:T(8,128)(2,1)S(1)}, bf16[2,4,16,384]{3,2,1,0:T(8,128)(2,1)S(1)}, u32[]{:S(2)}, u32[]{:S(2)}) collective-permute-start(bf16[2,4,16,384]{3,2,1,0:T(8,128)(2,1)S(1)} %get-tuple-element.45), channel_id=1, source_target_pairs={{0,24},{4,28},{8,16},{12,20},{16,8},{20,12},{24,0},{28,4},{1,25},{... | collective-permute-start | bytes 294920 | tf_op jit(solution)/shard_map/ppermute | solution.py:510
  25.0 1.0 %collective-permute-start.8 = (bf16[8,16,384]{2,1,0:T(8,128)(2,1)S(1)}, bf16[8,16,384]{2,1,0:T(8,128)(2,1)S(1)}, u32[]{:S(2)}, u32[]{:S(2)}) collective-permute-start(bf16[8,16,384]{2,1,0:T(8,128)(2,1)S(1)} %shard_map.124), channel_id=1, source_target_pairs={{28,29},{1,2},{30,31},{29,28},{2,1},{31,30}} | collective-permute-start | bytes 294920 | tf_op jit(solution)/shard_map/ppermute | solution.py:561
  40.6 12.5 %collective-permute-start.10 = (bf16[2,32,768]{2,1,0:T(8,128)(2,1)S(1)}, bf16[2,32,768]{2,1,0:T(8,128)(2,1)S(1)}, u32[]{:S(2)}, u32[]{:S(2)}) collective-permute-start(bf16[2,32,768]{2,1,0:T(8,128)(2,1)S(1)} %get-tuple-element.51), channel_id=1, source_target_pairs={{0,16},{4,20},{8,24},{12,28},{16,0},{20,4},{24,8},{28,12},{1,17},{... | collective-permute-start | bytes 294920 | tf_op jit(solution)/shard_map/ppermute | solution.py:510
  42.7 10.3 %collective-permute-start.11 = (bf16[2,32,768]{2,1,0:T(8,128)(2,1)S(1)}, bf16[2,32,768]{2,1,0:T(8,128)(2,1)S(1)}, u32[]{:S(2)}, u32[]{:S(2)}) collective-permute-start(bf16[2,32,768]{2,1,0:T(8,128)(2,1)S(1)} %get-tuple-element.52), channel_id=1, source_target_pairs={{0,24},{4,28},{8,16},{12,20},{16,8},{20,12},{24,0},{28,4},{1,25},{... | collective-permute-start | bytes 294920 | tf_op jit(solution)/shard_map/ppermute | solution.py:510
  44.6 8.7 %collective-permute-start.9 = (bf16[2,32,768]{2,1,0:T(8,128)(2,1)S(1)}, bf16[2,32,768]{2,1,0:T(8,128)(2,1)S(1)}, u32[]{:S(2)}, u32[]{:S(2)}) collective-permute-start(bf16[2,32,768]{2,1,0:T(8,128)(2,1)S(1)} %get-tuple-element.50), channel_id=1, source_target_pairs={{0,8},{4,12},{8,0},{12,4},{16,24},{20,28},{24,16},{28,20},{1,9},{5... | collective-permute-start | bytes 294920 | tf_op jit(solution)/shard_map/ppermute | solution.py:510
  53.3 10.5 %copy-start.1 = (bf16[768,384]{1,0:T(8,128)(2,1)S(1)}, bf16[768,384]{1,0:T(8,128)(2,1)}, u32[]{:S(2)}) copy-start(bf16[768,384]{1,0:T(8,128)(2,1)} %weight_ref.3) | copy-start | bytes 1769476
  53.3 10.5 %copy-start.2 = (f32[768]{0:T(1024)S(1)}, f32[768]{0:T(1024)}, u32[]{:S(2)}) copy-start(f32[768]{0:T(1024)} %gain_ref.3) | copy-start | bytes 9220
  53.3 10.5 %collective-permute-start.12 = (bf16[4,32,768]{2,1,0:T(8,128)(2,1)S(1)}, bf16[4,32,768]{2,1,0:T(8,128)(2,1)S(1)}, u32[]{:S(2)}, u32[]{:S(2)}) collective-permute-start(bf16[4,32,768]{2,1,0:T(8,128)(2,1)S(1)} %shard_map.129.after_ref), channel_id=1, source_target_pairs={{0,4},{4,0},{8,12},{12,8},{16,20},{20,16},{24,28},{28,24},{1,5},{5... | collective-permute-start | bytes 589832 | tf_op jit(solution)/shard_map/ppermute | solution.py:510
  55.5 3.5 %collective-permute-start.13 = (bf16[64,768]{1,0:T(8,128)(2,1)S(1)}, bf16[64,768]{1,0:T(8,128)(2,1)S(1)}, u32[]{:S(2)}, u32[]{:S(2)}) collective-permute-start(bf16[64,768]{1,0:T(8,128)(2,1)S(1)} %get-tuple-element.56), channel_id=1, source_target_pairs={{0,1},{1,0},{2,3},{3,2},{4,5},{5,4},{6,7},{7,6},{8,9},{9,8},{10,11... | collective-permute-start | bytes 294920 | tf_op jit(solution)/shard_map/ppermute | solution.py:529
  56.1 6.2 %collective-permute-start.14 = (bf16[64,768]{1,0:T(8,128)(2,1)S(1)}, bf16[64,768]{1,0:T(8,128)(2,1)S(1)}, u32[]{:S(2)}, u32[]{:S(2)}) collective-permute-start(bf16[64,768]{1,0:T(8,128)(2,1)S(1)} %get-tuple-element.57), channel_id=1, source_target_pairs={{0,2},{1,3},{2,0},{3,1},{4,6},{5,7},{6,4},{7,5},{8,10},{9,11},{10,... | collective-permute-start | bytes 294920 | tf_op jit(solution)/shard_map/ppermute | solution.py:529
  58.6 5.2 %collective-permute-start.15 = (bf16[64,768]{1,0:T(8,128)(2,1)S(1)}, bf16[64,768]{1,0:T(8,128)(2,1)S(1)}, u32[]{:S(2)}, u32[]{:S(2)}) collective-permute-start(bf16[64,768]{1,0:T(8,128)(2,1)S(1)} %get-tuple-element.58), channel_id=1, source_target_pairs={{0,3},{1,2},{2,1},{3,0},{4,7},{5,6},{6,5},{7,4},{8,11},{9,10},{10,... | collective-permute-start | bytes 294920 | tf_op jit(solution)/shard_map/ppermute | solution.py:529
  (4 other events, 12.3 us)

commit v10 on v9

--- a/solution.py
+++ b/solution.py
@@ -49,28 +49,53 @@
     return (lax.axis_index(other) & 1) * (lax.axis_size(axis) - 1)
 
 
-def cut_kernel(columns, feat_ref, gain_ref, norm_ref, *refs):
-    col_refs, beside_ref, row_refs, turned_ref = refs[: columns // 2], refs[columns // 2], refs[columns // 2 + 1 : -1], refs[-1]
+def edge_kernel(feat_ref, *out_refs):
     height, width, channels = feat_ref.shape
-    tile = layer_norm(feat_ref[...].reshape(height * width, channels).astype(F32), gain_ref[...][None]).astype(BF16)
+    tile = feat_ref[...].reshape(height * width, channels)
+    for second in range(2):
+        odd = (lax.axis_index("row") + second) & 1
+        out_refs[second][...] = feat_ref[jnp.where(odd == 1, 0, height - 1)]
+        odd = (lax.axis_index("col") + second) & 1
+        picked = one_hot([(rows_of(height) << bits(width)) + jnp.where(odd == 1, 0, width - 1)], height * width)
+        out_refs[2 + second][...] = dot(picked, tile).astype(BF16)
+
+
+def cut_kernel(columns, feat_ref, gain_ref, *refs):
+    edge_refs, norm_ref, refs = refs[:4], refs[4], refs[5:]
+    col_refs, beside_ref, row_refs = refs[: columns // 2], refs[columns // 2], refs[columns // 2 + 1 : -2]
+    by_row_ref, by_col_ref = refs[-2:]
+    height, width, channels = feat_ref.shape
+    tokens = height * width
+    gain = gain_ref[...][None]
+
+    def normed(values):
+        return layer_norm(values.astype(F32), gain).astype(BF16)
+
+    tile = normed(feat_ref[...].reshape(tokens, channels))
     norm_ref[...] = tile
+    by_row_ref[width : width + tokens] = tile
+    row = rows_of(tokens)
+    turned = dot(one_hot([((row & (height - 1)) << bits(width)) + (row >> bits(height))], tokens), tile)
+    by_col_ref[height : height + tokens] = turned.astype(BF16)
+    for axis, ext_ref, size in (("row", by_row_ref, width), ("col", by_col_ref, height)):
+        first, second = edge_refs[:2] if axis == "row" else edge_refs[2:]
+        first, second = normed(first[...]), normed(second[...])
+        odd = (lax.axis_index(axis) & 1) == 1
+        ext_ref[0:size] = jnp.where(odd, first, second)
+        ext_ref[size + tokens : 2 * size + tokens] = jnp.where(odd, second, first)
+
     reach = row_refs[0].shape[0]
     turn = flip("col") ^ lax.axis_index("col")
     for part, row_ref in enumerate(row_refs):
         for line in range(reach):
-            at = jnp.clip((part ^ turn) * (reach - 2) + line - 1, 0, height - 1)
-            row_ref[line] = norm_ref[pl.ds(pl.multiple_of(at * width, width), width)]
-    row = rows_of(height * width)
-    turned = dot(one_hot([((row & (height - 1)) << bits(width)) + (row >> bits(height))], height * width), tile).astype(
-        BF16
-    )
-    turned_ref[...] = turned
+            at = (part ^ turn) * (reach - 2) + line
+            row_ref[line] = by_row_ref[pl.ds(pl.multiple_of(at * width, width), width)]
     reach = col_refs[0].shape[0]
     turn = flip("row") ^ lax.axis_index("row")
     for part in range(columns):
         for line in range(reach):
-            at = jnp.clip((part ^ turn) * (reach - 2) + line - 1, 0, width - 1)
-            found = turned_ref[pl.ds(pl.multiple_of(at * height, height), height)]
+            at = (part ^ turn) * (reach - 2) + line
+            found = by_col_ref[pl.ds(pl.multiple_of(at * height, height), height)]
             if part & 1:
                 beside_ref[part >> 1, line] = found
             else:
@@ -104,9 +129,8 @@
     after_ref,
     *refs,
 ):
-    x_refs, refs = views(refs[:-16], 3), refs[-16:]
+    x_refs, refs = views(refs[:-15], 3), refs[-15:]
     (
-        seam_ref,
         weight_ref,
         conv_ref,
         conv_bias_ref,
@@ -124,8 +148,8 @@
         bias_ref,
     ) = refs
     ks = (0, 1) if axis == "col" else (2, 3)
-    parts, length, channels = seam_ref.shape
-    reach = lines + 2
+    reach, length, channels = x_refs[0].shape
+    parts = len(x_refs)
     states = (proj_raw_ref.shape[1] - RANK) // 2
     time = parts * length
     low = time // SLOTS
@@ -144,10 +168,6 @@
     order = one_hot([source], time)
     for line in range(reach):
         x = jnp.concatenate([x_ref[line] for x_ref in x_refs], axis=0)
-        if line == 0 or line == reach - 1:
-            place = lax.axis_index(axis) ^ flip(axis)
-            missing = place == (0 if line == 0 else lax.axis_size(axis) - 1)
-            x = jnp.where(missing, seam_ref[...].reshape(time, channels), x)
         token_ref[line * time : (line + 1) * time] = dot(order, x).astype(BF16)
     inner = dot(token_ref[...], weight_ref[:, :width]).astype(BF16).astype(F32)
     inner_ref[:, 1 : low + 1] = inner.reshape(reach, low, SLOTS, width)
@@ -381,9 +401,9 @@
 RANK = 24
 
 
-def prepare(axis, after, xs, seam, in_weight, conv, conv_bias, proj, step_weight, step_bias, decay_log, skip):
-    parts, length, channels = seam.shape
-    reach = xs[0].shape[-3]
+def prepare(axis, after, xs, in_weight, conv, conv_bias, proj, step_weight, step_bias, decay_log, skip):
+    parts = lax.axis_size(axis)
+    reach, length, channels = xs[0].shape[-3:]
     lines = reach - 2
     time = parts * length
     width = conv.shape[2]
@@ -401,7 +421,7 @@
             jax.ShapeDtypeStruct((time, SLOTS, chunk), F32),
             jax.ShapeDtypeStruct((time, SLOTS, chunk), F32),
         ],
-        in_specs=[pl.BlockSpec(memory_space=pl.ANY)] + [vmem] * (len(xs) + 7),
+        in_specs=[pl.BlockSpec(memory_space=pl.ANY)] + [vmem] * (len(xs) + 6),
         out_specs=[vmem, vmem, vmem],
         scratch_shapes=[
             pltpu.VMEM((reach * time, channels), BF16),
@@ -416,7 +436,6 @@
     )(
         after,
         *xs,
-        seam,
         in_weight,
         conv,
         conv_bias,
@@ -530,35 +549,10 @@
     return [blocks[0]] + [found[k] for k in range(1, count)]
 
 
-def pick_kernel(axis, after_ref, *refs):
-    x_refs, out_ref = views(refs[:-1], 3), refs[-1]
-    place = lax.axis_index(axis) ^ flip(axis)
-    line = jnp.where(place == 0, 1, x_refs[0].shape[0] - 2)
-    for part, x_ref in enumerate(x_refs):
-        out_ref[part] = x_ref[line]
-
-
-def pick(axis, after, xs):
-    return pl.pallas_call(
-        functools.partial(pick_kernel, axis),
-        out_shape=jax.ShapeDtypeStruct((lax.axis_size("col" if axis == "col" else "row"),) + xs[-1].shape[-2:], xs[-1].dtype),
-        in_specs=[pl.BlockSpec(memory_space=pl.ANY)] + [pl.BlockSpec(memory_space=pltpu.VMEM)] * len(xs),
-        out_specs=pl.BlockSpec(memory_space=pltpu.VMEM),
-        compiler_params=pltpu.CompilerParams(vmem_limit_bytes=4 * 1024 * 1024),
-    )(after, *xs)
-
-
-def seam_of(axis, line):
+def neighbours(first, second, axis):
     count = lax.axis_size(axis)
-    height, breadth = lax.axis_size("row"), lax.axis_size("col")
-    if axis == "row":
-        at = lambda group: (0 if group & 1 else count - 1) * breadth
-        ends = [(at(c) + c, at(c) + c + 1) for c in range(breadth - 1)]
-    else:
-        at = lambda group: 0 if group & 1 else count - 1
-        ends = [(at(r) + r * breadth, at(r) + (r + 1) * breadth) for r in range(height - 1)]
-    pairs = ends + [(b, a) for a, b in ends]
-    return lax.ppermute(line, ("row", "col"), pairs)
+    pairs = [(i, i + 1) for i in range(1, count - 1, 2)]
+    return swap(first, axis, 1), lax.ppermute(second, axis, pairs + [(b, a) for a, b in pairs])
 
 
 def local(
@@ -583,18 +577,27 @@
 
     rows, cols = lax.axis_size("row"), lax.axis_size("col")
     vmem = pl.BlockSpec(memory_space=pltpu.VMEM)
+    edges = simple(
+        edge_kernel,
+        [jax.ShapeDtypeStruct((width, channels), BF16)] * 2 + [jax.ShapeDtypeStruct((height, channels), BF16)] * 2,
+        features,
+    )
+    edges = neighbours(*edges[:2], "row") + neighbours(*edges[2:], "col")
     normed, *sends = pl.pallas_call(
         functools.partial(cut_kernel, rows),
         out_shape=[jax.ShapeDtypeStruct((tokens, channels), BF16)]
         + [jax.ShapeDtypeStruct((col_lines + 2, height, channels), BF16)] * (rows // 2)
         + [jax.ShapeDtypeStruct((rows // 2, col_lines + 2, height, channels), BF16)]
         + [jax.ShapeDtypeStruct((row_lines + 2, width, channels), BF16)] * cols,
-        in_specs=[pl.BlockSpec(features.shape, lambda: (0, 0, 0)), pl.BlockSpec((channels,), lambda: (0,))],
+        in_specs=[vmem, pl.BlockSpec((channels,), lambda: (0,))] + [vmem] * 4,
         out_specs=[vmem] * (2 + rows // 2 + cols),
-        scratch_shapes=[pltpu.VMEM((tokens, channels), BF16)],
+        scratch_shapes=[
+            pltpu.VMEM((tokens + 2 * width, channels), BF16),
+            pltpu.VMEM((tokens + 2 * height, channels), BF16),
+        ],
         compiler_params=pltpu.CompilerParams(vmem_limit_bytes=12 * 1024 * 1024),
         cost_estimate=pl.CostEstimate(flops=6_000_000_000, bytes_accessed=2 << 20, transcendentals=tokens),
-    )(features, norm_gain)
+    )(features, norm_gain, *edges)
     weights = (in_weight, conv_weight, conv_bias, proj_weight, step_weight, step_bias, decay_log, skip_gain)
     gate = pl.pallas_call(
         gate_kernel,
@@ -612,10 +615,8 @@
     half = rows // 2
     row_x = swap_blocks(sends[half + 1 :], "col")
     col_x = swap_out(sends[:half], sends[half])
-    row_seam = seam_of("col", pick("col", normed, row_x))
-    row_steps = prepare("col", normed, row_x, row_seam, *weights)
-    col_seam = seam_of("row", pick("row", row_steps[0], col_x))
-    col_steps = prepare("row", row_steps[0], col_x, col_seam, *weights)
+    row_steps = prepare("col", normed, row_x, *weights)
+    col_steps = prepare("row", row_steps[0], col_x, *weights)
     col_y = scan("row", normed, *col_steps, decay_log, skip_gain)
     joined = join("row", col_y, rows, col_lines, height, inner, normed)
     col_y = swap_back_far(joined)

time: 65.8 us -> 69.3 us (1.053)
  starting transfers between devices: 21.4 us -> 27.4 us
  waiting for transfers between devices: 12.7 us -> 9.2 us
  local copies, waits for them, and re-layouts: 1.79 us -> 2.58 us
    ppermute x6, waiting for transfers between devices: 8.97 us -> 4.63 us  [swap_blocks(): lax.ppermute(blocks[k], axis, [(i, i ^ k) for i in range(count)])]
    ppermute x8 -> x10, starting transfers between devices: 14.7 us -> 18.8 us  [swap(): lax.ppermute(block, axis, [(i, i ^ k) for i in range(lax.axis_size(axis))])]
    ppermute x6, starting transfers between devices: 4.98 us -> 7.14 us  [swap_blocks(): lax.ppermute(blocks[k], axis, [(i, i ^ k) for i in range(count)])]
    ppermute x8 -> x10, waiting for transfers between devices: 3.69 us -> 4.56 us  [swap(): lax.ppermute(block, axis, [(i, i ^ k) for i in range(lax.axis_size(axis))])]
    unnamed x24 -> x26, local copies, waits for them, and re-layouts: 1.79 us -> 2.58 us
  transfers between devices with their start and end apart: 16 -> 18, of which waited for: 6 -> 6; matrix products, arithmetic and copies ran while one was open for 0% -> 0% of each run, Pallas kernels for 19% -> 18%
where the time goes in v10:
time: 69.3 us; the launch traced here: 69.1 us
  Pallas kernels  29.6 us (43%)
  starting transfers between devices  27.4 us (40%)
  waiting for transfers between devices  9.2 us (13%)
  local copies, waits for them, and re-layouts  2.58 us (4%)
    ppermute x10, starting transfers between devices, swap(): lax.ppermute(block, axis, [(i, i ^ k) for i in range(lax.axis_size(axis))])  18.8 us
    pallas_call x2, Pallas kernels, scan(): pl.pallas_call(functools.partial(scan_kernel, axis), out_shape=jax.ShapeD...  17.9 us
    pallas_call x2, Pallas kernels, prepare(): pl.pallas_call(functools.partial(prepare_kernel, lines, axis), out_shape=...  7.69 us
    ppermute x6, starting transfers between devices, swap_blocks(): lax.ppermute(blocks[k], axis, [(i, i ^ k) for i in range(count)])  7.14 us
    ppermute x6, waiting for transfers between devices, swap_blocks(): lax.ppermute(blocks[k], axis, [(i, i ^ k) for i in range(count)])  4.63 us
    ppermute x10, waiting for transfers between devices, swap(): lax.ppermute(block, axis, [(i, i ^ k) for i in range(lax.axis_size(axis))])  4.56 us
    unnamed x26, local copies, waits for them, and re-layouts  2.58 us
    pallas_call x1, Pallas kernels, local(): pl.pallas_call(functools.partial(end_kernel, half), out_shape=jax.ShapeDt...  1.73 us
  transfers between devices with their start and end apart: 18, of which 6 were waited for; matrix products, arithmetic and copies ran while one was open for 0% of the time, Pallas kernels for 18%

profile of v10, /device:TPU:0, one launch (start us, length us, event | category | flops | bytes accessed | tf_op | source)
XLA Modules:
  0.0 69.1 jit_solution(10951160016562396862)
XLA Ops:
  0.0 0.9 %copy-done.2 = bf16[16,16,384]{2,1,0:T(8,128)(2,1)S(1)} copy-done((bf16[16,16,384]{2,1,0:T(8,128)(2,1)S(1)}, bf16[16,16,384]{2,1,0:T(8,128)(2,1)}, u32[]{:S(2)}) %copy-start.2) | copy-done | bytes 196632
  1.1 3.0 %collective-permute-start = (bf16[16,384]{1,0:T(8,128)(2,1)S(1)}, bf16[16,384]{1,0:T(8,128)(2,1)S(1)}, u32[]{:S(2)}, u32[]{:S(2)}) collective-permute-start(bf16[16,384]{1,0:T(8,128)(2,1)S(1)} %get-tuple-element.36), channel_id=1, source_target_pairs={{0,4},{4,0},{8,12},{12,8},{16,20},{20,16},{24,28},{28,24},{1,5},{5... | collective-permute-start | bytes 36872 | tf_op jit(solution)/shard_map/ppermute | solution.py:529
  4.1 0.7 collective-permute-start.1
  4.9 0.8 %collective-permute-start.3 = (bf16[16,384]{1,0:T(8,128)(2,1)S(1)}, bf16[16,384]{1,0:T(8,128)(2,1)S(1)}, u32[]{:S(2)}, u32[]{:S(2)}) collective-permute-start(bf16[16,384]{1,0:T(8,128)(2,1)S(1)} %get-tuple-element.39), channel_id=1, source_target_pairs={{1,2},{2,1},{5,6},{6,5},{9,10},{10,9},{13,14},{14,13},{17,18},{18,... | collective-permute-start | bytes 36872 | tf_op jit(solution)/shard_map/ppermute | solution.py:555
  6.0 0.9 %copy-done.3 = bf16[16,16,384]{2,1,0:T(8,128)(2,1)S(1)} copy-done((bf16[16,16,384]{2,1,0:T(8,128)(2,1)S(1)}, bf16[16,16,384]{2,1,0:T(8,128)(2,1)}, u32[]{:S(2)}) %copy-start.3) | copy-done | bytes 196632
  6.9 0.7 copy-done.12
  8.2 4.8 %collective-permute-start.7 = (bf16[4,4,16,384]{3,2,1,0:T(8,128)(2,1)S(1)}, bf16[4,4,16,384]{3,2,1,0:T(8,128)(2,1)S(1)}, u32[]{:S(2)}, u32[]{:S(2)}) collective-permute-start(bf16[4,4,16,384]{3,2,1,0:T(8,128)(2,1)S(1)} %get-tuple-element.47), channel_id=1, source_target_pairs={{0,4},{4,0},{8,12},{12,8},{16,20},{20,16},{24,28},{28,24},{1,5},{5... | collective-permute-start | bytes 589832 | tf_op jit(solution)/shard_map/ppermute | solution.py:529
  12.9 3.8 %collective-permute-start.4 = (bf16[6,16,384]{2,1,0:T(8,128)(2,1)S(1)}, bf16[6,16,384]{2,1,0:T(8,128)(2,1)S(1)}, u32[]{:S(2)}, u32[]{:S(2)}) collective-permute-start(bf16[6,16,384]{2,1,0:T(8,128)(2,1)S(1)} %get-tuple-element.42), channel_id=1, source_target_pairs={{0,1},{1,0},{2,3},{3,2},{4,5},{5,4},{6,7},{7,6},{8,9},{9,8},{10,11... | collective-permute-start | bytes 221192 | tf_op jit(solution)/shard_map/ppermute | solution.py:548
  16.7 1.3 %collective-permute-start.5 = (bf16[6,16,384]{2,1,0:T(8,128)(2,1)S(1)}, bf16[6,16,384]{2,1,0:T(8,128)(2,1)S(1)}, u32[]{:S(2)}, u32[]{:S(2)}) collective-permute-start(bf16[6,16,384]{2,1,0:T(8,128)(2,1)S(1)} %get-tuple-element.43), channel_id=1, source_target_pairs={{0,2},{1,3},{2,0},{3,1},{4,6},{5,7},{6,4},{7,5},{8,10},{9,11},{10,... | collective-permute-start | bytes 221192 | tf_op jit(solution)/shard_map/ppermute | solution.py:548
  18.2 5.6 %collective-permute-start.10 = (bf16[2,4,16,384]{3,2,1,0:T(8,128)(2,1)S(1)}, bf16[2,4,16,384]{3,2,1,0:T(8,128)(2,1)S(1)}, u32[]{:S(2)}, u32[]{:S(2)}) collective-permute-start(bf16[2,4,16,384]{3,2,1,0:T(8,128)(2,1)S(1)} %get-tuple-element.53), channel_id=1, source_target_pairs={{0,24},{4,28},{8,16},{12,20},{16,8},{20,12},{24,0},{28,4},{1,25},{... | collective-permute-start | bytes 294920 | tf_op jit(solution)/shard_map/ppermute | solution.py:529
  24.5 3.5 %shard_map.121 = (f32[64,8,128]{2,1,0:T(8,128)S(1)}, f32[64,8,768]{2,1,0:T(8,128)S(1)}, f32[64,8,768]{2,1,0:T(8,128)S(1)}) custom-call(bf16[256,384]{1,0:T(8,128)(2,1)S(1)} %get-tuple-element.40.norm_ref.after_ref, bf16[6,16,384]{2,1,0:T(8,128)(2,1)S(1)} %get-tuple-element.41.refs_0_, bf16[6,16,384]{2,1,0:T(8,128)(2,1)S(1)} %collective-permute-done.4.refs_1_, ...), custom_call_target="tpu_custom_call" | custom-call | flops 1711276032 | bytes 4194304 | tf_op jit(solution)/shard_map/pallas_call | solution.py:417
  28.0 2.5 %collective-permute-done.8.refs_1_ = bf16[2,4,16,384]{3,2,1,0:T(8,128)(2,1)S(1)} collective-permute-done((bf16[2,4,16,384]{3,2,1,0:T(8,128)(2,1)S(1)}, bf16[2,4,16,384]{3,2,1,0:T(8,128)(2,1)S(1)}, u32[]{:S(2)}, u32[]{:S(2)}) %collective-permute-start.8) | collective-permute-done | bytes 98336 | tf_op jit(solution)/shard_map/ppermute | solution.py:529
  30.5 1.7 %collective-permute-done.9.refs_2_ = bf16[2,4,16,384]{3,2,1,0:T(8,128)(2,1)S(1)} collective-permute-done((bf16[2,4,16,384]{3,2,1,0:T(8,128)(2,1)S(1)}, bf16[2,4,16,384]{3,2,1,0:T(8,128)(2,1)S(1)}, u32[]{:S(2)}, u32[]{:S(2)}) %collective-permute-start.9) | collective-permute-done | bytes 98336 | tf_op jit(solution)/shard_map/ppermute | solution.py:529
  32.2 4.2 %shard_map.124 = (f32[128,8,128]{2,1,0:T(8,128)S(1)}, f32[128,8,384]{2,1,0:T(8,128)S(1)}, f32[128,8,384]{2,1,0:T(8,128)S(1)}) custom-call(f32[64,8,128]{2,1,0:T(8,128)S(1)} %get-tuple-element.45.after_ref.coef_ref, bf16[2,4,16,384]{3,2,1,0:T(8,128)(2,1)S(1)} %shard_map.122.refs_0_, bf16[2,4,16,384]{3,2,1,0:T(8,128)(2,1)S(1)} %collective-permute-done.8.refs_1_, ...), custom_call_target="tpu_custom_call" | custom-call | flops 2818572288 | bytes 4194304 | tf_op jit(solution)/shard_map/pallas_call | solution.py:417
  36.4 9.5 %shard_map.125.scanned_ref = bf16[1024,384]{1,0:T(8,128)(2,1)S(1)} custom-call(bf16[256,384]{1,0:T(8,128)(2,1)S(1)} %get-tuple-element.40.norm_ref.after_ref, f32[128,8,128]{2,1,0:T(8,128)S(1)} %get-tuple-element.54.coef_ref, f32[128,8,384]{2,1,0:T(8,128)S(1)} %get-tuple-element.55.s_ref, f32[128,8,384]{2,1,0:T(8,128)S(1)} %get-tuple-element.56.u_ref, ...), custom_call_target="tpu_custom_call" | custom-call | flops 50331648 | bytes 4194304 | tf_op jit(solution)/shard_map/pallas_call | solution.py:452
  46.0 0.7 %shard_map.126 = (bf16[2,32,768]{2,1,0:T(8,128)(2,1)S(1)}, bf16[2,32,768]{2,1,0:T(8,128)(2,1)S(1)}, bf16[2,32,768]{2,1,0:T(8,128)(2,1)S(1)}, bf16[2,32,768]{2,1,0:T(8,128)(2,1)S(1)}) custom-call(bf16[256,384]{1,0:T(8,128)(2,1)S(1)} %get-tuple-element.40.norm_ref.after_ref, bf16[1024,384]{1,0:T(8,128)(2,1)S(1)} %shard_map.125.scanned_ref), custom_call_target="tpu_custom_call" | custom-call | tf_op jit(solution)/shard_map/pallas_call | solution.py:392
  46.8 1.8 %collective-permute-start.12 = (bf16[2,32,768]{2,1,0:T(8,128)(2,1)S(1)}, bf16[2,32,768]{2,1,0:T(8,128)(2,1)S(1)}, u32[]{:S(2)}, u32[]{:S(2)}) collective-permute-start(bf16[2,32,768]{2,1,0:T(8,128)(2,1)S(1)} %get-tuple-element.59), channel_id=1, source_target_pairs={{0,16},{4,20},{8,24},{12,28},{16,0},{20,4},{24,8},{28,12},{1,17},{... | collective-permute-start | bytes 294920 | tf_op jit(solution)/shard_map/ppermute | solution.py:529
  48.6 2.6 %collective-permute-start.13 = (bf16[2,32,768]{2,1,0:T(8,128)(2,1)S(1)}, bf16[2,32,768]{2,1,0:T(8,128)(2,1)S(1)}, u32[]{:S(2)}, u32[]{:S(2)}) collective-permute-start(bf16[2,32,768]{2,1,0:T(8,128)(2,1)S(1)} %get-tuple-element.60), channel_id=1, source_target_pairs={{0,24},{4,28},{8,16},{12,20},{16,8},{20,12},{24,0},{28,4},{1,25},{... | collective-permute-start | bytes 294920 | tf_op jit(solution)/shard_map/ppermute | solution.py:529
  51.2 8.4 %shard_map.127.after_ref.scanned_ref = bf16[512,768]{1,0:T(8,128)(2,1)S(1)} custom-call(bf16[2,32,768]{2,1,0:T(8,128)(2,1)S(1)} %get-tuple-element.57.after_ref.refs_0_, f32[64,8,128]{2,1,0:T(8,128)S(1)} %get-tuple-element.45.after_ref.coef_ref, f32[64,8,768]{2,1,0:T(8,128)S(1)} %get-tuple-element.61.s_ref, f32[64,8,768]{2,1,0:T(8,128)S(1)} %get-tuple-element.62.u_ref, ...), custom_call_target="tpu_custom_call" | custom-call | flops 50331648 | bytes 4194304 | tf_op jit(solution)/shard_map/pallas_call | solution.py:452
  60.5 1.0 %collective-permute-start.16 = (bf16[64,768]{1,0:T(8,128)(2,1)S(1)}, bf16[64,768]{1,0:T(8,128)(2,1)S(1)}, u32[]{:S(2)}, u32[]{:S(2)}) collective-permute-start(bf16[64,768]{1,0:T(8,128)(2,1)S(1)} %get-tuple-element.65), channel_id=1, source_target_pairs={{0,2},{1,3},{2,0},{3,1},{4,6},{5,7},{6,4},{7,5},{8,10},{9,11},{10,... | collective-permute-start | bytes 294920 | tf_op jit(solution)/shard_map/ppermute | solution.py:548
  61.4 0.9 %collective-permute-start.17 = (bf16[64,768]{1,0:T(8,128)(2,1)S(1)}, bf16[64,768]{1,0:T(8,128)(2,1)S(1)}, u32[]{:S(2)}, u32[]{:S(2)}) collective-permute-start(bf16[64,768]{1,0:T(8,128)(2,1)S(1)} %get-tuple-element.66), channel_id=1, source_target_pairs={{0,3},{1,2},{2,1},{3,0},{4,7},{5,6},{6,5},{7,4},{8,11},{9,10},{10,... | collective-permute-start | bytes 294920 | tf_op jit(solution)/shard_map/ppermute | solution.py:548
  62.7 3.4 %collective-permute-done.16.refs_7_ = bf16[64,768]{1,0:T(8,128)(2,1)S(1)} collective-permute-done((bf16[64,768]{1,0:T(8,128)(2,1)S(1)}, bf16[64,768]{1,0:T(8,128)(2,1)S(1)}, u32[]{:S(2)}, u32[]{:S(2)}) %collective-permute-start.16) | collective-permute-done | bytes 98336 | tf_op jit(solution)/shard_map/ppermute | solution.py:548
  66.1 1.2 %collective-permute-done.17.refs_8_ = bf16[64,768]{1,0:T(8,128)(2,1)S(1)} collective-permute-done((bf16[64,768]{1,0:T(8,128)(2,1)S(1)}, bf16[64,768]{1,0:T(8,128)(2,1)S(1)}, u32[]{:S(2)}, u32[]{:S(2)}) %collective-permute-start.17) | collective-permute-done | bytes 98336 | tf_op jit(solution)/shard_map/ppermute | solution.py:548
  67.3 1.7 %shard_map.130 = bf16[16,16,384]{2,1,0:T(8,128)(2,1)} custom-call(bf16[256,768]{1,0:T(8,128)(2,1)S(1)} %shard_map.120.gate_ref, f32[768]{0:T(1024)S(1)} %copy-done.4, bf16[768,384]{1,0:T(8,128)(2,1)S(1)} %copy-done.1, bf16[2,32,768]{2,1,0:T(8,128)(2,1)S(1)} %get-tuple-element.57.after_ref.refs_0_, bf16[2,32,768]{2,1,0:T(8,128)(2,1)S(1)} %collective-permute-done.11.refs_1_, ...), custom_call_target="tpu_custom_call" | custom-call | tf_op jit(solution)/shard_map/pallas_call | solution.py:628
  (51 shorter events, 3.2 us)
Async XLA Ops:
  1.1 4.7 %collective-permute-start = (bf16[16,384]{1,0:T(8,128)(2,1)S(1)}, bf16[16,384]{1,0:T(8,128)(2,1)S(1)}, u32[]{:S(2)}, u32[]{:S(2)}) collective-permute-start(bf16[16,384]{1,0:T(8,128)(2,1)S(1)} %get-tuple-element.36), channel_id=1, source_target_pairs={{0,4},{4,0},{8,12},{12,8},{16,20},{20,16},{24,28},{28,24},{1,5},{5... | collective-permute-start | bytes 36872 | tf_op jit(solution)/shard_map/ppermute | solution.py:529
  4.1 1.7 %collective-permute-start.1 = (bf16[16,384]{1,0:T(8,128)(2,1)S(1)}, bf16[16,384]{1,0:T(8,128)(2,1)S(1)}, u32[]{:S(2)}, u32[]{:S(2)}) collective-permute-start(bf16[16,384]{1,0:T(8,128)(2,1)S(1)} %get-tuple-element.37), channel_id=1, source_target_pairs={{4,8},{12,16},{20,24},{8,4},{16,12},{24,20},{5,9},{13,17},{21,25},... | collective-permute-start | bytes 36872 | tf_op jit(solution)/shard_map/ppermute | solution.py:555
  4.8 1.2 %collective-permute-start.2 = (bf16[16,384]{1,0:T(8,128)(2,1)S(1)}, bf16[16,384]{1,0:T(8,128)(2,1)S(1)}, u32[]{:S(2)}, u32[]{:S(2)}) collective-permute-start(bf16[16,384]{1,0:T(8,128)(2,1)S(1)} %get-tuple-element.38), channel_id=1, source_target_pairs={{0,1},{1,0},{2,3},{3,2},{4,5},{5,4},{6,7},{7,6},{8,9},{9,8},{10,11... | collective-permute-start | bytes 36872 | tf_op jit(solution)/shard_map/ppermute | solution.py:529
  4.8 19.6 %copy-start = (bf16[384,1536]{1,0:T(8,128)(2,1)S(1)}, bf16[384,1536]{1,0:T(8,128)(2,1)}, u32[]{:S(2)}) copy-start(bf16[384,1536]{1,0:T(8,128)(2,1)} %refs_4_.3) | copy-start | bytes 3538948
  4.9 1.2 %collective-permute-start.3 = (bf16[16,384]{1,0:T(8,128)(2,1)S(1)}, bf16[16,384]{1,0:T(8,128)(2,1)S(1)}, u32[]{:S(2)}, u32[]{:S(2)}) collective-permute-start(bf16[16,384]{1,0:T(8,128)(2,1)S(1)} %get-tuple-element.39), channel_id=1, source_target_pairs={{1,2},{2,1},{5,6},{6,5},{9,10},{10,9},{13,14},{14,13},{17,18},{18,... | collective-permute-start | bytes 36872 | tf_op jit(solution)/shard_map/ppermute | solution.py:555
  7.6 16.8 %copy-start.5 = (bf16[4,768,56]{1,2,0:T(8,128)(2,1)S(1)}, bf16[4,768,56]{1,2,0:T(8,128)(2,1)}, u32[]{:S(2)}) copy-start(bf16[4,768,56]{1,2,0:T(8,128)(2,1)} %param.17) | copy-start | bytes 1032196
  7.6 16.8 %copy-start.6 = (f32[4,24,768]{2,1,0:T(8,128)S(1)}, f32[4,24,768]{2,1,0:T(8,128)}, u32[]{:S(2)}) copy-start(f32[4,24,768]{2,1,0:T(8,128)} %refs_8_.3) | copy-start | bytes 884740
  7.6 16.8 %copy-start.8 = (f32[3,3,768]{2,1,0:T(4,128)S(1)}, f32[3,3,768]{2,1,0:T(4,128)}, u32[]{:S(2)}) copy-start(f32[3,3,768]{2,1,0:T(4,128)} %refs_5_.3) | copy-start | bytes 82948
  7.6 16.8 %copy-start.9 = (f32[4,768]{1,0:T(4,128)S(1)}, f32[4,768]{1,0:T(4,128)}, u32[]{:S(2)}) copy-start(f32[4,768]{1,0:T(4,128)} %refs_9_.3) | copy-start | bytes 36868
  7.6 16.8 %copy-start.11 = (f32[768]{0:T(1024)S(1)}, f32[768]{0:T(1024)}, u32[]{:S(2)}) copy-start(f32[768]{0:T(1024)} %refs_6_.3) | copy-start | bytes 9220
  8.2 10.0 %collective-permute-start.7 = (bf16[4,4,16,384]{3,2,1,0:T(8,128)(2,1)S(1)}, bf16[4,4,16,384]{3,2,1,0:T(8,128)(2,1)S(1)}, u32[]{:S(2)}, u32[]{:S(2)}) collective-permute-start(bf16[4,4,16,384]{3,2,1,0:T(8,128)(2,1)S(1)} %get-tuple-element.47), channel_id=1, source_target_pairs={{0,4},{4,0},{8,12},{12,8},{16,20},{20,16},{24,28},{28,24},{1,5},{5... | collective-permute-start | bytes 589832 | tf_op jit(solution)/shard_map/ppermute | solution.py:529
  12.9 10.9 %collective-permute-start.4 = (bf16[6,16,384]{2,1,0:T(8,128)(2,1)S(1)}, bf16[6,16,384]{2,1,0:T(8,128)(2,1)S(1)}, u32[]{:S(2)}, u32[]{:S(2)}) collective-permute-start(bf16[6,16,384]{2,1,0:T(8,128)(2,1)S(1)} %get-tuple-element.42), channel_id=1, source_target_pairs={{0,1},{1,0},{2,3},{3,2},{4,5},{5,4},{6,7},{7,6},{8,9},{9,8},{10,11... | collective-permute-start | bytes 221192 | tf_op jit(solution)/shard_map/ppermute | solution.py:548
  16.7 7.7 %collective-permute-start.5 = (bf16[6,16,384]{2,1,0:T(8,128)(2,1)S(1)}, bf16[6,16,384]{2,1,0:T(8,128)(2,1)S(1)}, u32[]{:S(2)}, u32[]{:S(2)}) collective-permute-start(bf16[6,16,384]{2,1,0:T(8,128)(2,1)S(1)} %get-tuple-element.43), channel_id=1, source_target_pairs={{0,2},{1,3},{2,0},{3,1},{4,6},{5,7},{6,4},{7,5},{8,10},{9,11},{10,... | collective-permute-start | bytes 221192 | tf_op jit(solution)/shard_map/ppermute | solution.py:548
  18.0 6.4 %collective-permute-start.6 = (bf16[6,16,384]{2,1,0:T(8,128)(2,1)S(1)}, bf16[6,16,384]{2,1,0:T(8,128)(2,1)S(1)}, u32[]{:S(2)}, u32[]{:S(2)}) collective-permute-start(bf16[6,16,384]{2,1,0:T(8,128)(2,1)S(1)} %get-tuple-element.44), channel_id=1, source_target_pairs={{0,3},{1,2},{2,1},{3,0},{4,7},{5,6},{6,5},{7,4},{8,11},{9,10},{10,... | collective-permute-start | bytes 221192 | tf_op jit(solution)/shard_map/ppermute | solution.py:548
  18.2 9.8 %collective-permute-start.10 = (bf16[2,4,16,384]{3,2,1,0:T(8,128)(2,1)S(1)}, bf16[2,4,16,384]{3,2,1,0:T(8,128)(2,1)S(1)}, u32[]{:S(2)}, u32[]{:S(2)}) collective-permute-start(bf16[2,4,16,384]{3,2,1,0:T(8,128)(2,1)S(1)} %get-tuple-element.53), channel_id=1, source_target_pairs={{0,24},{4,28},{8,16},{12,20},{16,8},{20,12},{24,0},{28,4},{1,25},{... | collective-permute-start | bytes 294920 | tf_op jit(solution)/shard_map/ppermute | solution.py:529
  23.8 6.7 %collective-permute-start.8 = (bf16[2,4,16,384]{3,2,1,0:T(8,128)(2,1)S(1)}, bf16[2,4,16,384]{3,2,1,0:T(8,128)(2,1)S(1)}, u32[]{:S(2)}, u32[]{:S(2)}) collective-permute-start(bf16[2,4,16,384]{3,2,1,0:T(8,128)(2,1)S(1)} %get-tuple-element.51), channel_id=1, source_target_pairs={{0,8},{4,12},{8,0},{12,4},{16,24},{20,28},{24,16},{28,20},{1,9},{5... | collective-permute-start | bytes 294920 | tf_op jit(solution)/shard_map/ppermute | solution.py:529
  23.8 8.4 %collective-permute-start.9 = (bf16[2,4,16,384]{3,2,1,0:T(8,128)(2,1)S(1)}, bf16[2,4,16,384]{3,2,1,0:T(8,128)(2,1)S(1)}, u32[]{:S(2)}, u32[]{:S(2)}) collective-permute-start(bf16[2,4,16,384]{3,2,1,0:T(8,128)(2,1)S(1)} %get-tuple-element.52), channel_id=1, source_target_pairs={{0,16},{4,20},{8,24},{12,28},{16,0},{20,4},{24,8},{28,12},{1,17},{... | collective-permute-start | bytes 294920 | tf_op jit(solution)/shard_map/ppermute | solution.py:529
  46.7 12.9 %collective-permute-start.11 = (bf16[2,32,768]{2,1,0:T(8,128)(2,1)S(1)}, bf16[2,32,768]{2,1,0:T(8,128)(2,1)S(1)}, u32[]{:S(2)}, u32[]{:S(2)}) collective-permute-start(bf16[2,32,768]{2,1,0:T(8,128)(2,1)S(1)} %get-tuple-element.58), channel_id=1, source_target_pairs={{0,8},{4,12},{8,0},{12,4},{16,24},{20,28},{24,16},{28,20},{1,9},{5... | collective-permute-start | bytes 294920 | tf_op jit(solution)/shard_map/ppermute | solution.py:529
  46.8 12.8 %collective-permute-start.12 = (bf16[2,32,768]{2,1,0:T(8,128)(2,1)S(1)}, bf16[2,32,768]{2,1,0:T(8,128)(2,1)S(1)}, u32[]{:S(2)}, u32[]{:S(2)}) collective-permute-start(bf16[2,32,768]{2,1,0:T(8,128)(2,1)S(1)} %get-tuple-element.59), channel_id=1, source_target_pairs={{0,16},{4,20},{8,24},{12,28},{16,0},{20,4},{24,8},{28,12},{1,17},{... | collective-permute-start | bytes 294920 | tf_op jit(solution)/shard_map/ppermute | solution.py:529
  48.6 11.0 %collective-permute-start.13 = (bf16[2,32,768]{2,1,0:T(8,128)(2,1)S(1)}, bf16[2,32,768]{2,1,0:T(8,128)(2,1)S(1)}, u32[]{:S(2)}, u32[]{:S(2)}) collective-permute-start(bf16[2,32,768]{2,1,0:T(8,128)(2,1)S(1)} %get-tuple-element.60), channel_id=1, source_target_pairs={{0,24},{4,28},{8,16},{12,20},{16,8},{20,12},{24,0},{28,4},{1,25},{... | collective-permute-start | bytes 294920 | tf_op jit(solution)/shard_map/ppermute | solution.py:529
  59.7 7.7 %collective-permute-start.14 = (bf16[4,32,768]{2,1,0:T(8,128)(2,1)S(1)}, bf16[4,32,768]{2,1,0:T(8,128)(2,1)S(1)}, u32[]{:S(2)}, u32[]{:S(2)}) collective-permute-start(bf16[4,32,768]{2,1,0:T(8,128)(2,1)S(1)} %shard_map.128.after_ref), channel_id=1, source_target_pairs={{0,4},{4,0},{8,12},{12,8},{16,20},{20,16},{24,28},{28,24},{1,5},{5... | collective-permute-start | bytes 589832 | tf_op jit(solution)/shard_map/ppermute | solution.py:529
  60.4 2.3 %collective-permute-start.15 = (bf16[64,768]{1,0:T(8,128)(2,1)S(1)}, bf16[64,768]{1,0:T(8,128)(2,1)S(1)}, u32[]{:S(2)}, u32[]{:S(2)}) collective-permute-start(bf16[64,768]{1,0:T(8,128)(2,1)S(1)} %get-tuple-element.64), channel_id=1, source_target_pairs={{0,1},{1,0},{2,3},{3,2},{4,5},{5,4},{6,7},{7,6},{8,9},{9,8},{10,11... | collective-permute-start | bytes 294920 | tf_op jit(solution)/shard_map/ppermute | solution.py:548
  60.5 5.7 %collective-permute-start.16 = (bf16[64,768]{1,0:T(8,128)(2,1)S(1)}, bf16[64,768]{1,0:T(8,128)(2,1)S(1)}, u32[]{:S(2)}, u32[]{:S(2)}) collective-permute-start(bf16[64,768]{1,0:T(8,128)(2,1)S(1)} %get-tuple-element.65), channel_id=1, source_target_pairs={{0,2},{1,3},{2,0},{3,1},{4,6},{5,7},{6,4},{7,5},{8,10},{9,11},{10,... | collective-permute-start | bytes 294920 | tf_op jit(solution)/shard_map/ppermute | solution.py:548
  61.4 5.9 %collective-permute-start.17 = (bf16[64,768]{1,0:T(8,128)(2,1)S(1)}, bf16[64,768]{1,0:T(8,128)(2,1)S(1)}, u32[]{:S(2)}, u32[]{:S(2)}) collective-permute-start(bf16[64,768]{1,0:T(8,128)(2,1)S(1)} %get-tuple-element.66), channel_id=1, source_target_pairs={{0,3},{1,2},{2,1},{3,0},{4,7},{5,6},{6,5},{7,4},{8,11},{9,10},{10,... | collective-permute-start | bytes 294920 | tf_op jit(solution)/shard_map/ppermute | solution.py:548
  (7 other events, 26.4 us)

commit v11 on v9

--- a/solution.py
+++ b/solution.py
@@ -272,18 +272,17 @@
 
     ks = (0, 1) if axis == "col" else (2, 3)
     piece = 64
-    row = lax.broadcasted_iota(jnp.int32, (2 * LANES, LANES), 0) & (LANES - 1)
+    row = lax.broadcasted_iota(jnp.int32, (LANES, LANES), 0)
     taken = [jnp.where(row == 3 * RANK + n, 1.0, 0.0).astype(BF16) for n in range(2 * states)]
 
     def spread(lap, _):
         steps = pl.ds(lap * piece, piece)
-        coefs = coef_ref[steps].reshape(piece * SLOTS, LANES)
-        high = coefs.astype(BF16)
-        both = jnp.concatenate([high, (coefs - high.astype(F32)).astype(BF16)], axis=1)
+        coefs = coef_ref[steps].reshape(piece * SLOTS, LANES).astype(BF16)
         for n in range(0, 2 * states, 4):
-            found = dot(both, jnp.concatenate(taken[n : n + 4], axis=1))
-            for k in range(4):
-                spread_ref[steps, n + k] = found[:, k * LANES : (k + 1) * LANES].reshape(piece, SLOTS, LANES)
+            found = dot(coefs, jnp.concatenate(taken[n : n + 4], axis=1))
+            found = [found[:, k * LANES : (k + 1) * LANES].reshape(piece, SLOTS, LANES) for k in range(4)]
+            for k in range(0, 4, 2):
+                spread_ref[steps, (n + k) // 2] = jnp.concatenate(found[k : k + 2], axis=1).astype(BF16)
         return 0
 
     lax.fori_loop(0, time // piece, spread, 0)
@@ -312,8 +311,12 @@
             hidden = list(hidden)
             for sub in range(unroll):
                 t = lap * unroll + sub
-                enter = [spread_ref[t, first + n] for n in range(at_once)]
-                leave = [spread_ref[t, states + first + n] for n in range(at_once)]
+                enter, leave = [], []
+                for n in range(first, first + at_once, 2):
+                    both = spread_ref[t, n // 2].astype(F32)
+                    enter += [both[:SLOTS], both[SLOTS:]]
+                    both = spread_ref[t, (states + n) // 2].astype(F32)
+                    leave += [both[:SLOTS], both[SLOTS:]]
                 decay = []
                 for g in range(groups):
                     step = s_ref[t, :, g * LANES : (g + 1) * LANES]
@@ -438,7 +441,7 @@
         scratch_shapes=[
             pltpu.VMEM((time, SLOTS, chunk), F32),
             pltpu.VMEM((time, SLOTS, chunk), F32),
-            pltpu.VMEM((time, 2 * states, SLOTS, LANES), F32),
+            pltpu.VMEM((time, states, 2 * SLOTS, LANES), BF16),
         ],
         compiler_params=pltpu.CompilerParams(vmem_limit_bytes=(8 << 20) + time * (136 << 10) + time * 20 * chunk),
         cost_estimate=pl.CostEstimate(

time: 65.8 us -> 66.3 us (level)
  no operation moved by 1% of the time
where the time goes in v11:
time: 66.3 us; the launch traced here: 66.1 us
  Pallas kernels  30 us (45%)
  starting transfers between devices  21.5 us (32%)
  waiting for transfers between devices  12.5 us (19%)
  local copies, waits for them, and re-layouts  1.79 us (3%)
    pallas_call x2, Pallas kernels, scan(): pl.pallas_call(functools.partial(scan_kernel, axis), out_shape=jax.ShapeD...  18.5 us
    ppermute x8, starting transfers between devices, swap(): lax.ppermute(block, axis, [(i, i ^ k) for i in range(lax.axis_size(axis))])  14.9 us
    ppermute x6, waiting for transfers between devices, swap_blocks(): lax.ppermute(blocks[k], axis, [(i, i ^ k) for i in range(count)])  8.97 us
    pallas_call x2, Pallas kernels, prepare(): pl.pallas_call(functools.partial(prepare_kernel, lines, axis), out_shape=...  7.75 us
    ppermute x6, starting transfers between devices, swap_blocks(): lax.ppermute(blocks[k], axis, [(i, i ^ k) for i in range(count)])  4.98 us
    ppermute x8, waiting for transfers between devices, swap(): lax.ppermute(block, axis, [(i, i ^ k) for i in range(lax.axis_size(axis))])  3.56 us
    unnamed x24, local copies, waits for them, and re-layouts  1.79 us
    pallas_call x1, Pallas kernels, local(): pl.pallas_call(functools.partial(end_kernel, half), out_shape=jax.ShapeDt...  1.73 us
  transfers between devices with their start and end apart: 16, of which 6 were waited for; matrix products, arithmetic and copies ran while one was open for 0% of the time, Pallas kernels for 19%

profile of v11, /device:TPU:0, one launch (start us, length us, event | category | flops | bytes accessed | tf_op | source)
XLA Modules:
  0.0 66.1 jit_solution(8461729889518931579)
XLA Ops:
  0.0 1.1 %copy-done.5 = bf16[16,16,384]{2,1,0:T(8,128)(2,1)S(1)} copy-done((bf16[16,16,384]{2,1,0:T(8,128)(2,1)S(1)}, bf16[16,16,384]{2,1,0:T(8,128)(2,1)}, u32[]{:S(2)}) %copy-start.5) | copy-done | bytes 196632
  1.1 0.7 %copy-done.11 = f32[384]{0:T(512)S(1)} copy-done((f32[384]{0:T(512)S(1)}, f32[384]{0:T(512)}, u32[]{:S(2)}) %copy-start.11) | copy-done | bytes 1560
  2.3 3.0 %collective-permute-start.4 = (bf16[4,4,16,384]{3,2,1,0:T(8,128)(2,1)S(1)}, bf16[4,4,16,384]{3,2,1,0:T(8,128)(2,1)S(1)}, u32[]{:S(2)}, u32[]{:S(2)}) collective-permute-start(bf16[4,4,16,384]{3,2,1,0:T(8,128)(2,1)S(1)} %get-tuple-element.39), channel_id=1, source_target_pairs={{0,4},{4,0},{8,12},{12,8},{16,20},{20,16},{24,28},{28,24},{1,5},{5... | collective-permute-start | bytes 589832 | tf_op jit(solution)/shard_map/ppermute | solution.py:513
  5.3 1.5 %collective-permute-start.1 = (bf16[6,16,384]{2,1,0:T(8,128)(2,1)S(1)}, bf16[6,16,384]{2,1,0:T(8,128)(2,1)S(1)}, u32[]{:S(2)}, u32[]{:S(2)}) collective-permute-start(bf16[6,16,384]{2,1,0:T(8,128)(2,1)S(1)} %get-tuple-element.35), channel_id=1, source_target_pairs={{0,2},{1,3},{2,0},{3,1},{4,6},{5,7},{6,4},{7,5},{8,10},{9,11},{10,... | collective-permute-start | bytes 221192 | tf_op jit(solution)/shard_map/ppermute | solution.py:532
  7.2 3.0 %collective-permute-done.1.refs_2_ = bf16[6,16,384]{2,1,0:T(8,128)(2,1)S(1)} collective-permute-done((bf16[6,16,384]{2,1,0:T(8,128)(2,1)S(1)}, bf16[6,16,384]{2,1,0:T(8,128)(2,1)S(1)}, u32[]{:S(2)}, u32[]{:S(2)}) %collective-permute-start.1) | collective-permute-done | bytes 73760 | tf_op jit(solution)/shard_map/ppermute | solution.py:532
  10.2 1.2 %collective-permute-done.2.refs_3_ = bf16[6,16,384]{2,1,0:T(8,128)(2,1)S(1)} collective-permute-done((bf16[6,16,384]{2,1,0:T(8,128)(2,1)S(1)}, bf16[6,16,384]{2,1,0:T(8,128)(2,1)S(1)}, u32[]{:S(2)}, u32[]{:S(2)}) %collective-permute-start.2) | collective-permute-done | bytes 73760 | tf_op jit(solution)/shard_map/ppermute | solution.py:532
  11.4 0.7 collective-permute-start.3
  12.1 3.0 %collective-permute-start.5 = (bf16[2,4,16,384]{3,2,1,0:T(8,128)(2,1)S(1)}, bf16[2,4,16,384]{3,2,1,0:T(8,128)(2,1)S(1)}, u32[]{:S(2)}, u32[]{:S(2)}) collective-permute-start(bf16[2,4,16,384]{3,2,1,0:T(8,128)(2,1)S(1)} %get-tuple-element.43), channel_id=1, source_target_pairs={{0,8},{4,12},{8,0},{12,4},{16,24},{20,28},{24,16},{28,20},{1,9},{5... | collective-permute-start | bytes 294920 | tf_op jit(solution)/shard_map/ppermute | solution.py:513
  15.0 2.9 %collective-permute-start.6 = (bf16[2,4,16,384]{3,2,1,0:T(8,128)(2,1)S(1)}, bf16[2,4,16,384]{3,2,1,0:T(8,128)(2,1)S(1)}, u32[]{:S(2)}, u32[]{:S(2)}) collective-permute-start(bf16[2,4,16,384]{3,2,1,0:T(8,128)(2,1)S(1)} %get-tuple-element.44), channel_id=1, source_target_pairs={{0,16},{4,20},{8,24},{12,28},{16,0},{20,4},{24,8},{28,12},{1,17},{... | collective-permute-start | bytes 294920 | tf_op jit(solution)/shard_map/ppermute | solution.py:513
  18.0 3.5 %shard_map.121 = (f32[64,8,128]{2,1,0:T(8,128)S(1)}, f32[64,8,768]{2,1,0:T(8,128)S(1)}, f32[64,8,768]{2,1,0:T(8,128)S(1)}) custom-call(bf16[256,384]{1,0:T(8,128)(2,1)S(1)} %get-tuple-element.32.norm_ref.after_ref, bf16[6,16,384]{2,1,0:T(8,128)(2,1)S(1)} %get-tuple-element.33.refs_0_, bf16[6,16,384]{2,1,0:T(8,128)(2,1)S(1)} %collective-permute-done.refs_1_, ...), custom_call_target="tpu_custom_call" | custom-call | flops 1711276032 | bytes 4194304 | tf_op jit(solution)/shard_map/pallas_call | solution.py:400
  21.5 3.4 %collective-permute-done.6.refs_2_ = bf16[2,4,16,384]{3,2,1,0:T(8,128)(2,1)S(1)} collective-permute-done((bf16[2,4,16,384]{3,2,1,0:T(8,128)(2,1)S(1)}, bf16[2,4,16,384]{3,2,1,0:T(8,128)(2,1)S(1)}, u32[]{:S(2)}, u32[]{:S(2)}) %collective-permute-start.6) | collective-permute-done | bytes 98336 | tf_op jit(solution)/shard_map/ppermute | solution.py:513
  25.0 1.0 %collective-permute-start.8 = (bf16[8,16,384]{2,1,0:T(8,128)(2,1)S(1)}, bf16[8,16,384]{2,1,0:T(8,128)(2,1)S(1)}, u32[]{:S(2)}, u32[]{:S(2)}) collective-permute-start(bf16[8,16,384]{2,1,0:T(8,128)(2,1)S(1)} %shard_map.124), channel_id=1, source_target_pairs={{28,29},{1,2},{30,31},{29,28},{2,1},{31,30}} | collective-permute-start | bytes 294920 | tf_op jit(solution)/shard_map/ppermute | solution.py:564
  26.0 4.3 %shard_map.125 = (f32[128,8,128]{2,1,0:T(8,128)S(1)}, f32[128,8,384]{2,1,0:T(8,128)S(1)}, f32[128,8,384]{2,1,0:T(8,128)S(1)}) custom-call(f32[64,8,128]{2,1,0:T(8,128)S(1)} %get-tuple-element.37.after_ref.coef_ref, bf16[2,4,16,384]{3,2,1,0:T(8,128)(2,1)S(1)} %shard_map.122.refs_0_, bf16[2,4,16,384]{3,2,1,0:T(8,128)(2,1)S(1)} %collective-permute-done.5.refs_1_, ...), custom_call_target="tpu_custom_call" | custom-call | flops 2818572288 | bytes 4194304 | tf_op jit(solution)/shard_map/pallas_call | solution.py:400
  30.3 9.9 %shard_map.126.scanned_ref = bf16[1024,384]{1,0:T(8,128)(2,1)S(1)} custom-call(bf16[256,384]{1,0:T(8,128)(2,1)S(1)} %get-tuple-element.32.norm_ref.after_ref, f32[128,8,128]{2,1,0:T(8,128)S(1)} %get-tuple-element.46.coef_ref, f32[128,8,384]{2,1,0:T(8,128)S(1)} %get-tuple-element.47.s_ref, f32[128,8,384]{2,1,0:T(8,128)S(1)} %get-tuple-element.48.u_ref, ...), custom_call_target="tpu_custom_call" | custom-call | flops 50331648 | bytes 4194304 | tf_op jit(solution)/shard_map/pallas_call | solution.py:436
  40.2 0.7 %shard_map.127 = (bf16[2,32,768]{2,1,0:T(8,128)(2,1)S(1)}, bf16[2,32,768]{2,1,0:T(8,128)(2,1)S(1)}, bf16[2,32,768]{2,1,0:T(8,128)(2,1)S(1)}, bf16[2,32,768]{2,1,0:T(8,128)(2,1)S(1)}) custom-call(bf16[256,384]{1,0:T(8,128)(2,1)S(1)} %get-tuple-element.32.norm_ref.after_ref, bf16[1024,384]{1,0:T(8,128)(2,1)S(1)} %shard_map.126.scanned_ref), custom_call_target="tpu_custom_call" | custom-call | tf_op jit(solution)/shard_map/pallas_call | solution.py:375
  41.0 2.1 %collective-permute-start.10 = (bf16[2,32,768]{2,1,0:T(8,128)(2,1)S(1)}, bf16[2,32,768]{2,1,0:T(8,128)(2,1)S(1)}, u32[]{:S(2)}, u32[]{:S(2)}) collective-permute-start(bf16[2,32,768]{2,1,0:T(8,128)(2,1)S(1)} %get-tuple-element.51), channel_id=1, source_target_pairs={{0,16},{4,20},{8,24},{12,28},{16,0},{20,4},{24,8},{28,12},{1,17},{... | collective-permute-start | bytes 294920 | tf_op jit(solution)/shard_map/ppermute | solution.py:513
  43.1 1.9 %collective-permute-start.11 = (bf16[2,32,768]{2,1,0:T(8,128)(2,1)S(1)}, bf16[2,32,768]{2,1,0:T(8,128)(2,1)S(1)}, u32[]{:S(2)}, u32[]{:S(2)}) collective-permute-start(bf16[2,32,768]{2,1,0:T(8,128)(2,1)S(1)} %get-tuple-element.52), channel_id=1, source_target_pairs={{0,24},{4,28},{8,16},{12,20},{16,8},{20,12},{24,0},{28,4},{1,25},{... | collective-permute-start | bytes 294920 | tf_op jit(solution)/shard_map/ppermute | solution.py:513
  45.0 8.6 %shard_map.128.after_ref.scanned_ref = bf16[512,768]{1,0:T(8,128)(2,1)S(1)} custom-call(bf16[2,32,768]{2,1,0:T(8,128)(2,1)S(1)} %get-tuple-element.49.after_ref.refs_0_, f32[64,8,128]{2,1,0:T(8,128)S(1)} %get-tuple-element.37.after_ref.coef_ref, f32[64,8,768]{2,1,0:T(8,128)S(1)} %get-tuple-element.53.s_ref, f32[64,8,768]{2,1,0:T(8,128)S(1)} %get-tuple-element.54.u_ref, ...), custom_call_target="tpu_custom_call" | custom-call | flops 50331648 | bytes 4194304 | tf_op jit(solution)/shard_map/pallas_call | solution.py:436
  53.7 1.9 %collective-permute-start.12 = (bf16[4,32,768]{2,1,0:T(8,128)(2,1)S(1)}, bf16[4,32,768]{2,1,0:T(8,128)(2,1)S(1)}, u32[]{:S(2)}, u32[]{:S(2)}) collective-permute-start(bf16[4,32,768]{2,1,0:T(8,128)(2,1)S(1)} %shard_map.129.after_ref), channel_id=1, source_target_pairs={{0,4},{4,0},{8,12},{12,8},{16,20},{20,16},{24,28},{28,24},{1,5},{5... | collective-permute-start | bytes 589832 | tf_op jit(solution)/shard_map/ppermute | solution.py:513
  56.1 0.5 collective-permute-start.13
  56.6 2.5 %collective-permute-start.14 = (bf16[64,768]{1,0:T(8,128)(2,1)S(1)}, bf16[64,768]{1,0:T(8,128)(2,1)S(1)}, u32[]{:S(2)}, u32[]{:S(2)}) collective-permute-start(bf16[64,768]{1,0:T(8,128)(2,1)S(1)} %get-tuple-element.57), channel_id=1, source_target_pairs={{0,2},{1,3},{2,0},{3,1},{4,6},{5,7},{6,4},{7,5},{8,10},{9,11},{10,... | collective-permute-start | bytes 294920 | tf_op jit(solution)/shard_map/ppermute | solution.py:532
  59.6 3.2 %collective-permute-done.14.refs_7_ = bf16[64,768]{1,0:T(8,128)(2,1)S(1)} collective-permute-done((bf16[64,768]{1,0:T(8,128)(2,1)S(1)}, bf16[64,768]{1,0:T(8,128)(2,1)S(1)}, u32[]{:S(2)}, u32[]{:S(2)}) %collective-permute-start.14) | collective-permute-done | bytes 98336 | tf_op jit(solution)/shard_map/ppermute | solution.py:532
  62.8 1.6 %collective-permute-done.15.refs_8_ = bf16[64,768]{1,0:T(8,128)(2,1)S(1)} collective-permute-done((bf16[64,768]{1,0:T(8,128)(2,1)S(1)}, bf16[64,768]{1,0:T(8,128)(2,1)S(1)}, u32[]{:S(2)}, u32[]{:S(2)}) %collective-permute-start.15) | collective-permute-done | bytes 98336 | tf_op jit(solution)/shard_map/ppermute | solution.py:532
  64.4 1.7 %shard_map.131 = bf16[16,16,384]{2,1,0:T(8,128)(2,1)} custom-call(bf16[256,768]{1,0:T(8,128)(2,1)S(1)} %shard_map.119.gate_ref, f32[768]{0:T(1024)S(1)} %copy-done.2, bf16[768,384]{1,0:T(8,128)(2,1)S(1)} %copy-done.1, bf16[2,32,768]{2,1,0:T(8,128)(2,1)S(1)} %get-tuple-element.49.after_ref.refs_0_, bf16[2,32,768]{2,1,0:T(8,128)(2,1)S(1)} %collective-permute-done.9.refs_1_, ...), custom_call_target="tpu_custom_call" | custom-call | tf_op jit(solution)/shard_map/pallas_call | solution.py:630
  (46 shorter events, 2.0 us)
Async XLA Ops:
  0.0 17.9 %copy-start.3 = (bf16[4,768,56]{1,2,0:T(8,128)(2,1)S(1)}, bf16[4,768,56]{1,2,0:T(8,128)(2,1)}, u32[]{:S(2)}) copy-start(bf16[4,768,56]{1,2,0:T(8,128)(2,1)} %param.17) | copy-start | bytes 1032196
  0.0 17.9 %copy-start = (bf16[384,1536]{1,0:T(8,128)(2,1)S(1)}, bf16[384,1536]{1,0:T(8,128)(2,1)}, u32[]{:S(2)}) copy-start(bf16[384,1536]{1,0:T(8,128)(2,1)} %refs_5_.3) | copy-start | bytes 3538948
  0.0 18.0 %copy-start.4 = (f32[4,24,768]{2,1,0:T(8,128)S(1)}, f32[4,24,768]{2,1,0:T(8,128)}, u32[]{:S(2)}) copy-start(f32[4,24,768]{2,1,0:T(8,128)} %refs_9_.3) | copy-start | bytes 884740
  1.7 16.2 %copy-start.7 = (f32[3,3,768]{2,1,0:T(4,128)S(1)}, f32[3,3,768]{2,1,0:T(4,128)}, u32[]{:S(2)}) copy-start(f32[3,3,768]{2,1,0:T(4,128)} %refs_6_.3) | copy-start | bytes 82948
  1.8 16.2 %copy-start.8 = (f32[4,768]{1,0:T(4,128)S(1)}, f32[4,768]{1,0:T(4,128)}, u32[]{:S(2)}) copy-start(f32[4,768]{1,0:T(4,128)} %refs_10_.3) | copy-start | bytes 36868
  1.8 16.2 %copy-start.10 = (f32[768]{0:T(1024)S(1)}, f32[768]{0:T(1024)}, u32[]{:S(2)}) copy-start(f32[768]{0:T(1024)} %refs_7_.3) | copy-start | bytes 9220
  2.3 9.8 %collective-permute-start.4 = (bf16[4,4,16,384]{3,2,1,0:T(8,128)(2,1)S(1)}, bf16[4,4,16,384]{3,2,1,0:T(8,128)(2,1)S(1)}, u32[]{:S(2)}, u32[]{:S(2)}) collective-permute-start(bf16[4,4,16,384]{3,2,1,0:T(8,128)(2,1)S(1)} %get-tuple-element.39), channel_id=1, source_target_pairs={{0,4},{4,0},{8,12},{12,8},{16,20},{20,16},{24,28},{28,24},{1,5},{5... | collective-permute-start | bytes 589832 | tf_op jit(solution)/shard_map/ppermute | solution.py:513
  5.3 1.9 %collective-permute-start = (bf16[6,16,384]{2,1,0:T(8,128)(2,1)S(1)}, bf16[6,16,384]{2,1,0:T(8,128)(2,1)S(1)}, u32[]{:S(2)}, u32[]{:S(2)}) collective-permute-start(bf16[6,16,384]{2,1,0:T(8,128)(2,1)S(1)} %get-tuple-element.34), channel_id=1, source_target_pairs={{0,1},{1,0},{2,3},{3,2},{4,5},{5,4},{6,7},{7,6},{8,9},{9,8},{10,11... | collective-permute-start | bytes 221192 | tf_op jit(solution)/shard_map/ppermute | solution.py:532
  5.3 4.9 %collective-permute-start.1 = (bf16[6,16,384]{2,1,0:T(8,128)(2,1)S(1)}, bf16[6,16,384]{2,1,0:T(8,128)(2,1)S(1)}, u32[]{:S(2)}, u32[]{:S(2)}) collective-permute-start(bf16[6,16,384]{2,1,0:T(8,128)(2,1)S(1)} %get-tuple-element.35), channel_id=1, source_target_pairs={{0,2},{1,3},{2,0},{3,1},{4,6},{5,7},{6,4},{7,5},{8,10},{9,11},{10,... | collective-permute-start | bytes 221192 | tf_op jit(solution)/shard_map/ppermute | solution.py:532
  6.8 4.5 %collective-permute-start.2 = (bf16[6,16,384]{2,1,0:T(8,128)(2,1)S(1)}, bf16[6,16,384]{2,1,0:T(8,128)(2,1)S(1)}, u32[]{:S(2)}, u32[]{:S(2)}) collective-permute-start(bf16[6,16,384]{2,1,0:T(8,128)(2,1)S(1)} %get-tuple-element.36), channel_id=1, source_target_pairs={{0,3},{1,2},{2,1},{3,0},{4,7},{5,6},{6,5},{7,4},{8,11},{9,10},{10,... | collective-permute-start | bytes 221192 | tf_op jit(solution)/shard_map/ppermute | solution.py:532
  11.4 6.6 %collective-permute-start.3 = (bf16[4,16,384]{2,1,0:T(8,128)(2,1)S(1)}, bf16[4,16,384]{2,1,0:T(8,128)(2,1)S(1)}, u32[]{:S(2)}, u32[]{:S(2)}) collective-permute-start(bf16[4,16,384]{2,1,0:T(8,128)(2,1)S(1)} %shard_map.120), channel_id=1, source_target_pairs={{3,7},{4,8},{11,15},{12,16},{19,23},{20,24},{27,31},{7,3},{8,4},{1... | collective-permute-start | bytes 147464 | tf_op jit(solution)/shard_map/ppermute | solution.py:564
  12.1 9.4 %collective-permute-start.5 = (bf16[2,4,16,384]{3,2,1,0:T(8,128)(2,1)S(1)}, bf16[2,4,16,384]{3,2,1,0:T(8,128)(2,1)S(1)}, u32[]{:S(2)}, u32[]{:S(2)}) collective-permute-start(bf16[2,4,16,384]{3,2,1,0:T(8,128)(2,1)S(1)} %get-tuple-element.43), channel_id=1, source_target_pairs={{0,8},{4,12},{8,0},{12,4},{16,24},{20,28},{24,16},{28,20},{1,9},{5... | collective-permute-start | bytes 294920 | tf_op jit(solution)/shard_map/ppermute | solution.py:513
  15.0 9.9 %collective-permute-start.6 = (bf16[2,4,16,384]{3,2,1,0:T(8,128)(2,1)S(1)}, bf16[2,4,16,384]{3,2,1,0:T(8,128)(2,1)S(1)}, u32[]{:S(2)}, u32[]{:S(2)}) collective-permute-start(bf16[2,4,16,384]{3,2,1,0:T(8,128)(2,1)S(1)} %get-tuple-element.44), channel_id=1, source_target_pairs={{0,16},{4,20},{8,24},{12,28},{16,0},{20,4},{24,8},{28,12},{1,17},{... | collective-permute-start | bytes 294920 | tf_op jit(solution)/shard_map/ppermute | solution.py:513
  17.9 7.0 %collective-permute-start.7 = (bf16[2,4,16,384]{3,2,1,0:T(8,128)(2,1)S(1)}, bf16[2,4,16,384]{3,2,1,0:T(8,128)(2,1)S(1)}, u32[]{:S(2)}, u32[]{:S(2)}) collective-permute-start(bf16[2,4,16,384]{3,2,1,0:T(8,128)(2,1)S(1)} %get-tuple-element.45), channel_id=1, source_target_pairs={{0,24},{4,28},{8,16},{12,20},{16,8},{20,12},{24,0},{28,4},{1,25},{... | collective-permute-start | bytes 294920 | tf_op jit(solution)/shard_map/ppermute | solution.py:513
  25.0 1.0 %collective-permute-start.8 = (bf16[8,16,384]{2,1,0:T(8,128)(2,1)S(1)}, bf16[8,16,384]{2,1,0:T(8,128)(2,1)S(1)}, u32[]{:S(2)}, u32[]{:S(2)}) collective-permute-start(bf16[8,16,384]{2,1,0:T(8,128)(2,1)S(1)} %shard_map.124), channel_id=1, source_target_pairs={{28,29},{1,2},{30,31},{29,28},{2,1},{31,30}} | collective-permute-start | bytes 294920 | tf_op jit(solution)/shard_map/ppermute | solution.py:564
  41.0 12.6 %collective-permute-start.10 = (bf16[2,32,768]{2,1,0:T(8,128)(2,1)S(1)}, bf16[2,32,768]{2,1,0:T(8,128)(2,1)S(1)}, u32[]{:S(2)}, u32[]{:S(2)}) collective-permute-start(bf16[2,32,768]{2,1,0:T(8,128)(2,1)S(1)} %get-tuple-element.51), channel_id=1, source_target_pairs={{0,16},{4,20},{8,24},{12,28},{16,0},{20,4},{24,8},{28,12},{1,17},{... | collective-permute-start | bytes 294920 | tf_op jit(solution)/shard_map/ppermute | solution.py:513
  43.1 10.5 %collective-permute-start.11 = (bf16[2,32,768]{2,1,0:T(8,128)(2,1)S(1)}, bf16[2,32,768]{2,1,0:T(8,128)(2,1)S(1)}, u32[]{:S(2)}, u32[]{:S(2)}) collective-permute-start(bf16[2,32,768]{2,1,0:T(8,128)(2,1)S(1)} %get-tuple-element.52), channel_id=1, source_target_pairs={{0,24},{4,28},{8,16},{12,20},{16,8},{20,12},{24,0},{28,4},{1,25},{... | collective-permute-start | bytes 294920 | tf_op jit(solution)/shard_map/ppermute | solution.py:513
  45.0 8.7 %collective-permute-start.9 = (bf16[2,32,768]{2,1,0:T(8,128)(2,1)S(1)}, bf16[2,32,768]{2,1,0:T(8,128)(2,1)S(1)}, u32[]{:S(2)}, u32[]{:S(2)}) collective-permute-start(bf16[2,32,768]{2,1,0:T(8,128)(2,1)S(1)} %get-tuple-element.50), channel_id=1, source_target_pairs={{0,8},{4,12},{8,0},{12,4},{16,24},{20,28},{24,16},{28,20},{1,9},{5... | collective-permute-start | bytes 294920 | tf_op jit(solution)/shard_map/ppermute | solution.py:513
  53.7 10.7 %copy-start.1 = (bf16[768,384]{1,0:T(8,128)(2,1)S(1)}, bf16[768,384]{1,0:T(8,128)(2,1)}, u32[]{:S(2)}) copy-start(bf16[768,384]{1,0:T(8,128)(2,1)} %weight_ref.3) | copy-start | bytes 1769476
  53.7 10.7 %copy-start.2 = (f32[768]{0:T(1024)S(1)}, f32[768]{0:T(1024)}, u32[]{:S(2)}) copy-start(f32[768]{0:T(1024)} %gain_ref.3) | copy-start | bytes 9220
  53.7 10.6 %collective-permute-start.12 = (bf16[4,32,768]{2,1,0:T(8,128)(2,1)S(1)}, bf16[4,32,768]{2,1,0:T(8,128)(2,1)S(1)}, u32[]{:S(2)}, u32[]{:S(2)}) collective-permute-start(bf16[4,32,768]{2,1,0:T(8,128)(2,1)S(1)} %shard_map.129.after_ref), channel_id=1, source_target_pairs={{0,4},{4,0},{8,12},{12,8},{16,20},{20,16},{24,28},{28,24},{1,5},{5... | collective-permute-start | bytes 589832 | tf_op jit(solution)/shard_map/ppermute | solution.py:513
  56.1 3.5 %collective-permute-start.13 = (bf16[64,768]{1,0:T(8,128)(2,1)S(1)}, bf16[64,768]{1,0:T(8,128)(2,1)S(1)}, u32[]{:S(2)}, u32[]{:S(2)}) collective-permute-start(bf16[64,768]{1,0:T(8,128)(2,1)S(1)} %get-tuple-element.56), channel_id=1, source_target_pairs={{0,1},{1,0},{2,3},{3,2},{4,5},{5,4},{6,7},{7,6},{8,9},{9,8},{10,11... | collective-permute-start | bytes 294920 | tf_op jit(solution)/shard_map/ppermute | solution.py:532
  56.6 6.2 %collective-permute-start.14 = (bf16[64,768]{1,0:T(8,128)(2,1)S(1)}, bf16[64,768]{1,0:T(8,128)(2,1)S(1)}, u32[]{:S(2)}, u32[]{:S(2)}) collective-permute-start(bf16[64,768]{1,0:T(8,128)(2,1)S(1)} %get-tuple-element.57), channel_id=1, source_target_pairs={{0,2},{1,3},{2,0},{3,1},{4,6},{5,7},{6,4},{7,5},{8,10},{9,11},{10,... | collective-permute-start | bytes 294920 | tf_op jit(solution)/shard_map/ppermute | solution.py:532
  59.1 5.2 %collective-permute-start.15 = (bf16[64,768]{1,0:T(8,128)(2,1)S(1)}, bf16[64,768]{1,0:T(8,128)(2,1)S(1)}, u32[]{:S(2)}, u32[]{:S(2)}) collective-permute-start(bf16[64,768]{1,0:T(8,128)(2,1)S(1)} %get-tuple-element.58), channel_id=1, source_target_pairs={{0,3},{1,2},{2,1},{3,0},{4,7},{5,6},{6,5},{7,4},{8,11},{9,10},{10,... | collective-permute-start | bytes 294920 | tf_op jit(solution)/shard_map/ppermute | solution.py:532
  (4 other events, 12.3 us)

commit v12 on v9

--- a/solution.py
+++ b/solution.py
@@ -266,8 +266,8 @@
     halves = decay_ref.shape[2] // chunk
     states = decay_ref.shape[1]
     groups = chunk // LANES
-    at_once = 4
-    unroll = 16 if axis == "col" else 32
+    at_once = 4 if groups > 3 else 8
+    unroll = 32 if axis == "col" else 16
     laps = time // unroll
 
     ks = (0, 1) if axis == "col" else (2, 3)

time: 65.8 us -> 65.7 us (level)
  no operation moved by 1% of the time
where the time goes in v12:
time: 65.7 us; the launch traced here: 65.5 us
  Pallas kernels  29.4 us (45%)
  starting transfers between devices  21.3 us (32%)
  waiting for transfers between devices  12.7 us (19%)
  local copies, waits for them, and re-layouts  1.79 us (3%)
    pallas_call x2, Pallas kernels, scan(): pl.pallas_call(functools.partial(scan_kernel, axis), out_shape=jax.ShapeD...  17.9 us
    ppermute x8, starting transfers between devices, swap(): lax.ppermute(block, axis, [(i, i ^ k) for i in range(lax.axis_size(axis))])  14.7 us
    ppermute x6, waiting for transfers between devices, swap_blocks(): lax.ppermute(blocks[k], axis, [(i, i ^ k) for i in range(count)])  8.97 us
    pallas_call x2, Pallas kernels, prepare(): pl.pallas_call(functools.partial(prepare_kernel, lines, axis), out_shape=...  7.75 us
    ppermute x6, starting transfers between devices, swap_blocks(): lax.ppermute(blocks[k], axis, [(i, i ^ k) for i in range(count)])  4.98 us
    ppermute x8, waiting for transfers between devices, swap(): lax.ppermute(block, axis, [(i, i ^ k) for i in range(lax.axis_size(axis))])  3.76 us
    unnamed x24, local copies, waits for them, and re-layouts  1.79 us
    pallas_call x1, Pallas kernels, local(): pl.pallas_call(functools.partial(end_kernel, half), out_shape=jax.ShapeDt...  1.73 us
  transfers between devices with their start and end apart: 16, of which 6 were waited for; matrix products, arithmetic and copies ran while one was open for 0% of the time, Pallas kernels for 19%

profile of v12, /device:TPU:0, one launch (start us, length us, event | category | flops | bytes accessed | tf_op | source)
XLA Modules:
  0.0 65.5 jit_solution(6401052001063767277)
XLA Ops:
  0.0 1.1 %copy-done.5 = bf16[16,16,384]{2,1,0:T(8,128)(2,1)S(1)} copy-done((bf16[16,16,384]{2,1,0:T(8,128)(2,1)S(1)}, bf16[16,16,384]{2,1,0:T(8,128)(2,1)}, u32[]{:S(2)}) %copy-start.5) | copy-done | bytes 196632
  1.1 0.7 %copy-done.11 = f32[384]{0:T(512)S(1)} copy-done((f32[384]{0:T(512)S(1)}, f32[384]{0:T(512)}, u32[]{:S(2)}) %copy-start.11) | copy-done | bytes 1560
  2.3 3.0 %collective-permute-start.4 = (bf16[4,4,16,384]{3,2,1,0:T(8,128)(2,1)S(1)}, bf16[4,4,16,384]{3,2,1,0:T(8,128)(2,1)S(1)}, u32[]{:S(2)}, u32[]{:S(2)}) collective-permute-start(bf16[4,4,16,384]{3,2,1,0:T(8,128)(2,1)S(1)} %get-tuple-element.39), channel_id=1, source_target_pairs={{0,4},{4,0},{8,12},{12,8},{16,20},{20,16},{24,28},{28,24},{1,5},{5... | collective-permute-start | bytes 589832 | tf_op jit(solution)/shard_map/ppermute | solution.py:510
  5.3 1.5 %collective-permute-start.1 = (bf16[6,16,384]{2,1,0:T(8,128)(2,1)S(1)}, bf16[6,16,384]{2,1,0:T(8,128)(2,1)S(1)}, u32[]{:S(2)}, u32[]{:S(2)}) collective-permute-start(bf16[6,16,384]{2,1,0:T(8,128)(2,1)S(1)} %get-tuple-element.35), channel_id=1, source_target_pairs={{0,2},{1,3},{2,0},{3,1},{4,6},{5,7},{6,4},{7,5},{8,10},{9,11},{10,... | collective-permute-start | bytes 221192 | tf_op jit(solution)/shard_map/ppermute | solution.py:529
  7.2 3.0 %collective-permute-done.1.refs_2_ = bf16[6,16,384]{2,1,0:T(8,128)(2,1)S(1)} collective-permute-done((bf16[6,16,384]{2,1,0:T(8,128)(2,1)S(1)}, bf16[6,16,384]{2,1,0:T(8,128)(2,1)S(1)}, u32[]{:S(2)}, u32[]{:S(2)}) %collective-permute-start.1) | collective-permute-done | bytes 73760 | tf_op jit(solution)/shard_map/ppermute | solution.py:529
  10.2 1.2 %collective-permute-done.2.refs_3_ = bf16[6,16,384]{2,1,0:T(8,128)(2,1)S(1)} collective-permute-done((bf16[6,16,384]{2,1,0:T(8,128)(2,1)S(1)}, bf16[6,16,384]{2,1,0:T(8,128)(2,1)S(1)}, u32[]{:S(2)}, u32[]{:S(2)}) %collective-permute-start.2) | collective-permute-done | bytes 73760 | tf_op jit(solution)/shard_map/ppermute | solution.py:529
  11.4 0.7 collective-permute-start.3
  12.1 3.0 %collective-permute-start.5 = (bf16[2,4,16,384]{3,2,1,0:T(8,128)(2,1)S(1)}, bf16[2,4,16,384]{3,2,1,0:T(8,128)(2,1)S(1)}, u32[]{:S(2)}, u32[]{:S(2)}) collective-permute-start(bf16[2,4,16,384]{3,2,1,0:T(8,128)(2,1)S(1)} %get-tuple-element.43), channel_id=1, source_target_pairs={{0,8},{4,12},{8,0},{12,4},{16,24},{20,28},{24,16},{28,20},{1,9},{5... | collective-permute-start | bytes 294920 | tf_op jit(solution)/shard_map/ppermute | solution.py:510
  15.0 2.9 %collective-permute-start.6 = (bf16[2,4,16,384]{3,2,1,0:T(8,128)(2,1)S(1)}, bf16[2,4,16,384]{3,2,1,0:T(8,128)(2,1)S(1)}, u32[]{:S(2)}, u32[]{:S(2)}) collective-permute-start(bf16[2,4,16,384]{3,2,1,0:T(8,128)(2,1)S(1)} %get-tuple-element.44), channel_id=1, source_target_pairs={{0,16},{4,20},{8,24},{12,28},{16,0},{20,4},{24,8},{28,12},{1,17},{... | collective-permute-start | bytes 294920 | tf_op jit(solution)/shard_map/ppermute | solution.py:510
  18.0 3.5 %shard_map.121 = (f32[64,8,128]{2,1,0:T(8,128)S(1)}, f32[64,8,768]{2,1,0:T(8,128)S(1)}, f32[64,8,768]{2,1,0:T(8,128)S(1)}) custom-call(bf16[256,384]{1,0:T(8,128)(2,1)S(1)} %get-tuple-element.32.norm_ref.after_ref, bf16[6,16,384]{2,1,0:T(8,128)(2,1)S(1)} %get-tuple-element.33.refs_0_, bf16[6,16,384]{2,1,0:T(8,128)(2,1)S(1)} %collective-permute-done.refs_1_, ...), custom_call_target="tpu_custom_call" | custom-call | flops 1711276032 | bytes 4194304 | tf_op jit(solution)/shard_map/pallas_call | solution.py:397
  21.5 3.4 %collective-permute-done.6.refs_2_ = bf16[2,4,16,384]{3,2,1,0:T(8,128)(2,1)S(1)} collective-permute-done((bf16[2,4,16,384]{3,2,1,0:T(8,128)(2,1)S(1)}, bf16[2,4,16,384]{3,2,1,0:T(8,128)(2,1)S(1)}, u32[]{:S(2)}, u32[]{:S(2)}) %collective-permute-start.6) | collective-permute-done | bytes 98336 | tf_op jit(solution)/shard_map/ppermute | solution.py:510
  25.0 1.0 %collective-permute-start.8 = (bf16[8,16,384]{2,1,0:T(8,128)(2,1)S(1)}, bf16[8,16,384]{2,1,0:T(8,128)(2,1)S(1)}, u32[]{:S(2)}, u32[]{:S(2)}) collective-permute-start(bf16[8,16,384]{2,1,0:T(8,128)(2,1)S(1)} %shard_map.124), channel_id=1, source_target_pairs={{28,29},{1,2},{30,31},{29,28},{2,1},{31,30}} | collective-permute-start | bytes 294920 | tf_op jit(solution)/shard_map/ppermute | solution.py:561
  26.0 4.3 %shard_map.125 = (f32[128,8,128]{2,1,0:T(8,128)S(1)}, f32[128,8,384]{2,1,0:T(8,128)S(1)}, f32[128,8,384]{2,1,0:T(8,128)S(1)}) custom-call(f32[64,8,128]{2,1,0:T(8,128)S(1)} %get-tuple-element.37.after_ref.coef_ref, bf16[2,4,16,384]{3,2,1,0:T(8,128)(2,1)S(1)} %shard_map.122.refs_0_, bf16[2,4,16,384]{3,2,1,0:T(8,128)(2,1)S(1)} %collective-permute-done.5.refs_1_, ...), custom_call_target="tpu_custom_call" | custom-call | flops 2818572288 | bytes 4194304 | tf_op jit(solution)/shard_map/pallas_call | solution.py:397
  30.3 9.5 %shard_map.126.scanned_ref = bf16[1024,384]{1,0:T(8,128)(2,1)S(1)} custom-call(bf16[256,384]{1,0:T(8,128)(2,1)S(1)} %get-tuple-element.32.norm_ref.after_ref, f32[128,8,128]{2,1,0:T(8,128)S(1)} %get-tuple-element.46.coef_ref, f32[128,8,384]{2,1,0:T(8,128)S(1)} %get-tuple-element.47.s_ref, f32[128,8,384]{2,1,0:T(8,128)S(1)} %get-tuple-element.48.u_ref, ...), custom_call_target="tpu_custom_call" | custom-call | flops 50331648 | bytes 4194304 | tf_op jit(solution)/shard_map/pallas_call | solution.py:433
  39.8 0.7 %shard_map.127 = (bf16[2,32,768]{2,1,0:T(8,128)(2,1)S(1)}, bf16[2,32,768]{2,1,0:T(8,128)(2,1)S(1)}, bf16[2,32,768]{2,1,0:T(8,128)(2,1)S(1)}, bf16[2,32,768]{2,1,0:T(8,128)(2,1)S(1)}) custom-call(bf16[256,384]{1,0:T(8,128)(2,1)S(1)} %get-tuple-element.32.norm_ref.after_ref, bf16[1024,384]{1,0:T(8,128)(2,1)S(1)} %shard_map.126.scanned_ref), custom_call_target="tpu_custom_call" | custom-call | tf_op jit(solution)/shard_map/pallas_call | solution.py:372
  40.6 2.1 %collective-permute-start.10 = (bf16[2,32,768]{2,1,0:T(8,128)(2,1)S(1)}, bf16[2,32,768]{2,1,0:T(8,128)(2,1)S(1)}, u32[]{:S(2)}, u32[]{:S(2)}) collective-permute-start(bf16[2,32,768]{2,1,0:T(8,128)(2,1)S(1)} %get-tuple-element.51), channel_id=1, source_target_pairs={{0,16},{4,20},{8,24},{12,28},{16,0},{20,4},{24,8},{28,12},{1,17},{... | collective-permute-start | bytes 294920 | tf_op jit(solution)/shard_map/ppermute | solution.py:510
  42.7 1.9 %collective-permute-start.11 = (bf16[2,32,768]{2,1,0:T(8,128)(2,1)S(1)}, bf16[2,32,768]{2,1,0:T(8,128)(2,1)S(1)}, u32[]{:S(2)}, u32[]{:S(2)}) collective-permute-start(bf16[2,32,768]{2,1,0:T(8,128)(2,1)S(1)} %get-tuple-element.52), channel_id=1, source_target_pairs={{0,24},{4,28},{8,16},{12,20},{16,8},{20,12},{24,0},{28,4},{1,25},{... | collective-permute-start | bytes 294920 | tf_op jit(solution)/shard_map/ppermute | solution.py:510
  44.6 8.3 %shard_map.128.after_ref.scanned_ref = bf16[512,768]{1,0:T(8,128)(2,1)S(1)} custom-call(bf16[2,32,768]{2,1,0:T(8,128)(2,1)S(1)} %get-tuple-element.49.after_ref.refs_0_, f32[64,8,128]{2,1,0:T(8,128)S(1)} %get-tuple-element.37.after_ref.coef_ref, f32[64,8,768]{2,1,0:T(8,128)S(1)} %get-tuple-element.53.s_ref, f32[64,8,768]{2,1,0:T(8,128)S(1)} %get-tuple-element.54.u_ref, ...), custom_call_target="tpu_custom_call" | custom-call | flops 50331648 | bytes 4194304 | tf_op jit(solution)/shard_map/pallas_call | solution.py:433
  53.3 1.7 %collective-permute-start.12 = (bf16[4,32,768]{2,1,0:T(8,128)(2,1)S(1)}, bf16[4,32,768]{2,1,0:T(8,128)(2,1)S(1)}, u32[]{:S(2)}, u32[]{:S(2)}) collective-permute-start(bf16[4,32,768]{2,1,0:T(8,128)(2,1)S(1)} %shard_map.129.after_ref), channel_id=1, source_target_pairs={{0,4},{4,0},{8,12},{12,8},{16,20},{20,16},{24,28},{28,24},{1,5},{5... | collective-permute-start | bytes 589832 | tf_op jit(solution)/shard_map/ppermute | solution.py:510
  55.5 0.5 collective-permute-start.13
  56.0 2.5 %collective-permute-start.14 = (bf16[64,768]{1,0:T(8,128)(2,1)S(1)}, bf16[64,768]{1,0:T(8,128)(2,1)S(1)}, u32[]{:S(2)}, u32[]{:S(2)}) collective-permute-start(bf16[64,768]{1,0:T(8,128)(2,1)S(1)} %get-tuple-element.57), channel_id=1, source_target_pairs={{0,2},{1,3},{2,0},{3,1},{4,6},{5,7},{6,4},{7,5},{8,10},{9,11},{10,... | collective-permute-start | bytes 294920 | tf_op jit(solution)/shard_map/ppermute | solution.py:529
  59.0 3.2 %collective-permute-done.14.refs_7_ = bf16[64,768]{1,0:T(8,128)(2,1)S(1)} collective-permute-done((bf16[64,768]{1,0:T(8,128)(2,1)S(1)}, bf16[64,768]{1,0:T(8,128)(2,1)S(1)}, u32[]{:S(2)}, u32[]{:S(2)}) %collective-permute-start.14) | collective-permute-done | bytes 98336 | tf_op jit(solution)/shard_map/ppermute | solution.py:529
  62.2 1.6 %collective-permute-done.15.refs_8_ = bf16[64,768]{1,0:T(8,128)(2,1)S(1)} collective-permute-done((bf16[64,768]{1,0:T(8,128)(2,1)S(1)}, bf16[64,768]{1,0:T(8,128)(2,1)S(1)}, u32[]{:S(2)}, u32[]{:S(2)}) %collective-permute-start.15) | collective-permute-done | bytes 98336 | tf_op jit(solution)/shard_map/ppermute | solution.py:529
  63.8 1.7 %shard_map.131 = bf16[16,16,384]{2,1,0:T(8,128)(2,1)} custom-call(bf16[256,768]{1,0:T(8,128)(2,1)S(1)} %shard_map.119.gate_ref, f32[768]{0:T(1024)S(1)} %copy-done.2, bf16[768,384]{1,0:T(8,128)(2,1)S(1)} %copy-done.1, bf16[2,32,768]{2,1,0:T(8,128)(2,1)S(1)} %get-tuple-element.49.after_ref.refs_0_, bf16[2,32,768]{2,1,0:T(8,128)(2,1)S(1)} %collective-permute-done.9.refs_1_, ...), custom_call_target="tpu_custom_call" | custom-call | tf_op jit(solution)/shard_map/pallas_call | solution.py:627
  (46 shorter events, 2.2 us)
Async XLA Ops:
  0.0 17.9 %copy-start.3 = (bf16[4,768,56]{1,2,0:T(8,128)(2,1)S(1)}, bf16[4,768,56]{1,2,0:T(8,128)(2,1)}, u32[]{:S(2)}) copy-start(bf16[4,768,56]{1,2,0:T(8,128)(2,1)} %param.17) | copy-start | bytes 1032196
  0.0 17.9 %copy-start = (bf16[384,1536]{1,0:T(8,128)(2,1)S(1)}, bf16[384,1536]{1,0:T(8,128)(2,1)}, u32[]{:S(2)}) copy-start(bf16[384,1536]{1,0:T(8,128)(2,1)} %refs_5_.3) | copy-start | bytes 3538948
  0.0 18.0 %copy-start.4 = (f32[4,24,768]{2,1,0:T(8,128)S(1)}, f32[4,24,768]{2,1,0:T(8,128)}, u32[]{:S(2)}) copy-start(f32[4,24,768]{2,1,0:T(8,128)} %refs_9_.3) | copy-start | bytes 884740
  1.7 16.2 %copy-start.7 = (f32[3,3,768]{2,1,0:T(4,128)S(1)}, f32[3,3,768]{2,1,0:T(4,128)}, u32[]{:S(2)}) copy-start(f32[3,3,768]{2,1,0:T(4,128)} %refs_6_.3) | copy-start | bytes 82948
  1.8 16.2 %copy-start.8 = (f32[4,768]{1,0:T(4,128)S(1)}, f32[4,768]{1,0:T(4,128)}, u32[]{:S(2)}) copy-start(f32[4,768]{1,0:T(4,128)} %refs_10_.3) | copy-start | bytes 36868
  1.8 16.2 %copy-start.10 = (f32[768]{0:T(1024)S(1)}, f32[768]{0:T(1024)}, u32[]{:S(2)}) copy-start(f32[768]{0:T(1024)} %refs_7_.3) | copy-start | bytes 9220
  2.3 9.8 %collective-permute-start.4 = (bf16[4,4,16,384]{3,2,1,0:T(8,128)(2,1)S(1)}, bf16[4,4,16,384]{3,2,1,0:T(8,128)(2,1)S(1)}, u32[]{:S(2)}, u32[]{:S(2)}) collective-permute-start(bf16[4,4,16,384]{3,2,1,0:T(8,128)(2,1)S(1)} %get-tuple-element.39), channel_id=1, source_target_pairs={{0,4},{4,0},{8,12},{12,8},{16,20},{20,16},{24,28},{28,24},{1,5},{5... | collective-permute-start | bytes 589832 | tf_op jit(solution)/shard_map/ppermute | solution.py:510
  5.3 1.9 %collective-permute-start = (bf16[6,16,384]{2,1,0:T(8,128)(2,1)S(1)}, bf16[6,16,384]{2,1,0:T(8,128)(2,1)S(1)}, u32[]{:S(2)}, u32[]{:S(2)}) collective-permute-start(bf16[6,16,384]{2,1,0:T(8,128)(2,1)S(1)} %get-tuple-element.34), channel_id=1, source_target_pairs={{0,1},{1,0},{2,3},{3,2},{4,5},{5,4},{6,7},{7,6},{8,9},{9,8},{10,11... | collective-permute-start | bytes 221192 | tf_op jit(solution)/shard_map/ppermute | solution.py:529
  5.3 4.9 %collective-permute-start.1 = (bf16[6,16,384]{2,1,0:T(8,128)(2,1)S(1)}, bf16[6,16,384]{2,1,0:T(8,128)(2,1)S(1)}, u32[]{:S(2)}, u32[]{:S(2)}) collective-permute-start(bf16[6,16,384]{2,1,0:T(8,128)(2,1)S(1)} %get-tuple-element.35), channel_id=1, source_target_pairs={{0,2},{1,3},{2,0},{3,1},{4,6},{5,7},{6,4},{7,5},{8,10},{9,11},{10,... | collective-permute-start | bytes 221192 | tf_op jit(solution)/shard_map/ppermute | solution.py:529
  6.8 4.5 %collective-permute-start.2 = (bf16[6,16,384]{2,1,0:T(8,128)(2,1)S(1)}, bf16[6,16,384]{2,1,0:T(8,128)(2,1)S(1)}, u32[]{:S(2)}, u32[]{:S(2)}) collective-permute-start(bf16[6,16,384]{2,1,0:T(8,128)(2,1)S(1)} %get-tuple-element.36), channel_id=1, source_target_pairs={{0,3},{1,2},{2,1},{3,0},{4,7},{5,6},{6,5},{7,4},{8,11},{9,10},{10,... | collective-permute-start | bytes 221192 | tf_op jit(solution)/shard_map/ppermute | solution.py:529
  11.4 6.6 %collective-permute-start.3 = (bf16[4,16,384]{2,1,0:T(8,128)(2,1)S(1)}, bf16[4,16,384]{2,1,0:T(8,128)(2,1)S(1)}, u32[]{:S(2)}, u32[]{:S(2)}) collective-permute-start(bf16[4,16,384]{2,1,0:T(8,128)(2,1)S(1)} %shard_map.120), channel_id=1, source_target_pairs={{3,7},{4,8},{11,15},{12,16},{19,23},{20,24},{27,31},{7,3},{8,4},{1... | collective-permute-start | bytes 147464 | tf_op jit(solution)/shard_map/ppermute | solution.py:561
  12.1 9.4 %collective-permute-start.5 = (bf16[2,4,16,384]{3,2,1,0:T(8,128)(2,1)S(1)}, bf16[2,4,16,384]{3,2,1,0:T(8,128)(2,1)S(1)}, u32[]{:S(2)}, u32[]{:S(2)}) collective-permute-start(bf16[2,4,16,384]{3,2,1,0:T(8,128)(2,1)S(1)} %get-tuple-element.43), channel_id=1, source_target_pairs={{0,8},{4,12},{8,0},{12,4},{16,24},{20,28},{24,16},{28,20},{1,9},{5... | collective-permute-start | bytes 294920 | tf_op jit(solution)/shard_map/ppermute | solution.py:510
  15.0 9.9 %collective-permute-start.6 = (bf16[2,4,16,384]{3,2,1,0:T(8,128)(2,1)S(1)}, bf16[2,4,16,384]{3,2,1,0:T(8,128)(2,1)S(1)}, u32[]{:S(2)}, u32[]{:S(2)}) collective-permute-start(bf16[2,4,16,384]{3,2,1,0:T(8,128)(2,1)S(1)} %get-tuple-element.44), channel_id=1, source_target_pairs={{0,16},{4,20},{8,24},{12,28},{16,0},{20,4},{24,8},{28,12},{1,17},{... | collective-permute-start | bytes 294920 | tf_op jit(solution)/shard_map/ppermute | solution.py:510
  17.9 7.0 %collective-permute-start.7 = (bf16[2,4,16,384]{3,2,1,0:T(8,128)(2,1)S(1)}, bf16[2,4,16,384]{3,2,1,0:T(8,128)(2,1)S(1)}, u32[]{:S(2)}, u32[]{:S(2)}) collective-permute-start(bf16[2,4,16,384]{3,2,1,0:T(8,128)(2,1)S(1)} %get-tuple-element.45), channel_id=1, source_target_pairs={{0,24},{4,28},{8,16},{12,20},{16,8},{20,12},{24,0},{28,4},{1,25},{... | collective-permute-start | bytes 294920 | tf_op jit(solution)/shard_map/ppermute | solution.py:510
  25.0 1.0 %collective-permute-start.8 = (bf16[8,16,384]{2,1,0:T(8,128)(2,1)S(1)}, bf16[8,16,384]{2,1,0:T(8,128)(2,1)S(1)}, u32[]{:S(2)}, u32[]{:S(2)}) collective-permute-start(bf16[8,16,384]{2,1,0:T(8,128)(2,1)S(1)} %shard_map.124), channel_id=1, source_target_pairs={{28,29},{1,2},{30,31},{29,28},{2,1},{31,30}} | collective-permute-start | bytes 294920 | tf_op jit(solution)/shard_map/ppermute | solution.py:561
  40.6 12.4 %collective-permute-start.10 = (bf16[2,32,768]{2,1,0:T(8,128)(2,1)S(1)}, bf16[2,32,768]{2,1,0:T(8,128)(2,1)S(1)}, u32[]{:S(2)}, u32[]{:S(2)}) collective-permute-start(bf16[2,32,768]{2,1,0:T(8,128)(2,1)S(1)} %get-tuple-element.51), channel_id=1, source_target_pairs={{0,16},{4,20},{8,24},{12,28},{16,0},{20,4},{24,8},{28,12},{1,17},{... | collective-permute-start | bytes 294920 | tf_op jit(solution)/shard_map/ppermute | solution.py:510
  42.7 10.3 %collective-permute-start.11 = (bf16[2,32,768]{2,1,0:T(8,128)(2,1)S(1)}, bf16[2,32,768]{2,1,0:T(8,128)(2,1)S(1)}, u32[]{:S(2)}, u32[]{:S(2)}) collective-permute-start(bf16[2,32,768]{2,1,0:T(8,128)(2,1)S(1)} %get-tuple-element.52), channel_id=1, source_target_pairs={{0,24},{4,28},{8,16},{12,20},{16,8},{20,12},{24,0},{28,4},{1,25},{... | collective-permute-start | bytes 294920 | tf_op jit(solution)/shard_map/ppermute | solution.py:510
  44.6 8.7 %collective-permute-start.9 = (bf16[2,32,768]{2,1,0:T(8,128)(2,1)S(1)}, bf16[2,32,768]{2,1,0:T(8,128)(2,1)S(1)}, u32[]{:S(2)}, u32[]{:S(2)}) collective-permute-start(bf16[2,32,768]{2,1,0:T(8,128)(2,1)S(1)} %get-tuple-element.50), channel_id=1, source_target_pairs={{0,8},{4,12},{8,0},{12,4},{16,24},{20,28},{24,16},{28,20},{1,9},{5... | collective-permute-start | bytes 294920 | tf_op jit(solution)/shard_map/ppermute | solution.py:510
  53.3 10.5 %copy-start.1 = (bf16[768,384]{1,0:T(8,128)(2,1)S(1)}, bf16[768,384]{1,0:T(8,128)(2,1)}, u32[]{:S(2)}) copy-start(bf16[768,384]{1,0:T(8,128)(2,1)} %weight_ref.3) | copy-start | bytes 1769476
  53.3 10.4 %copy-start.2 = (f32[768]{0:T(1024)S(1)}, f32[768]{0:T(1024)}, u32[]{:S(2)}) copy-start(f32[768]{0:T(1024)} %gain_ref.3) | copy-start | bytes 9220
  53.3 10.4 %collective-permute-start.12 = (bf16[4,32,768]{2,1,0:T(8,128)(2,1)S(1)}, bf16[4,32,768]{2,1,0:T(8,128)(2,1)S(1)}, u32[]{:S(2)}, u32[]{:S(2)}) collective-permute-start(bf16[4,32,768]{2,1,0:T(8,128)(2,1)S(1)} %shard_map.129.after_ref), channel_id=1, source_target_pairs={{0,4},{4,0},{8,12},{12,8},{16,20},{20,16},{24,28},{28,24},{1,5},{5... | collective-permute-start | bytes 589832 | tf_op jit(solution)/shard_map/ppermute | solution.py:510
  55.5 3.5 %collective-permute-start.13 = (bf16[64,768]{1,0:T(8,128)(2,1)S(1)}, bf16[64,768]{1,0:T(8,128)(2,1)S(1)}, u32[]{:S(2)}, u32[]{:S(2)}) collective-permute-start(bf16[64,768]{1,0:T(8,128)(2,1)S(1)} %get-tuple-element.56), channel_id=1, source_target_pairs={{0,1},{1,0},{2,3},{3,2},{4,5},{5,4},{6,7},{7,6},{8,9},{9,8},{10,11... | collective-permute-start | bytes 294920 | tf_op jit(solution)/shard_map/ppermute | solution.py:529
  56.0 6.2 %collective-permute-start.14 = (bf16[64,768]{1,0:T(8,128)(2,1)S(1)}, bf16[64,768]{1,0:T(8,128)(2,1)S(1)}, u32[]{:S(2)}, u32[]{:S(2)}) collective-permute-start(bf16[64,768]{1,0:T(8,128)(2,1)S(1)} %get-tuple-element.57), channel_id=1, source_target_pairs={{0,2},{1,3},{2,0},{3,1},{4,6},{5,7},{6,4},{7,5},{8,10},{9,11},{10,... | collective-permute-start | bytes 294920 | tf_op jit(solution)/shard_map/ppermute | solution.py:529
  58.5 5.2 %collective-permute-start.15 = (bf16[64,768]{1,0:T(8,128)(2,1)S(1)}, bf16[64,768]{1,0:T(8,128)(2,1)S(1)}, u32[]{:S(2)}, u32[]{:S(2)}) collective-permute-start(bf16[64,768]{1,0:T(8,128)(2,1)S(1)} %get-tuple-element.58), channel_id=1, source_target_pairs={{0,3},{1,2},{2,1},{3,0},{4,7},{5,6},{6,5},{7,4},{8,11},{9,10},{10,... | collective-permute-start | bytes 294920 | tf_op jit(solution)/shard_map/ppermute | solution.py:529
  (4 other events, 12.3 us)

commit v13 on v9

--- a/solution.py
+++ b/solution.py
@@ -203,7 +203,7 @@
             rest = jnp.zeros((LANES - 3 * RANK, chunk), F32)
             step_ref[kind, :] = jnp.concatenate([high, high, w - high, rest], axis=0).astype(BF16)
 
-    piece = 512
+    piece = min(1024, time * SLOTS)
     for first in range(0, time * SLOTS, piece):
         row = rows_of(piece, first)
         now = row >> 3
@@ -267,7 +267,7 @@
     states = decay_ref.shape[1]
     groups = chunk // LANES
     at_once = 4
-    unroll = 16 if axis == "col" else 32
+    unroll = 32
     laps = time // unroll
 
     ks = (0, 1) if axis == "col" else (2, 3)

time: 65.8 us -> 65.7 us (level)
  no operation moved by 1% of the time
where the time goes in v13:
time: 65.7 us; the launch traced here: 65.5 us
  Pallas kernels  29.5 us (45%)
  starting transfers between devices  21.3 us (32%)
  waiting for transfers between devices  12.7 us (19%)
  local copies, waits for them, and re-layouts  1.79 us (3%)
    pallas_call x2, Pallas kernels, scan(): pl.pallas_call(functools.partial(scan_kernel, axis), out_shape=jax.ShapeD...  17.9 us
    ppermute x8, starting transfers between devices, swap(): lax.ppermute(block, axis, [(i, i ^ k) for i in range(lax.axis_size(axis))])  14.7 us
    ppermute x6, waiting for transfers between devices, swap_blocks(): lax.ppermute(blocks[k], axis, [(i, i ^ k) for i in range(count)])  8.97 us
    pallas_call x2, Pallas kernels, prepare(): pl.pallas_call(functools.partial(prepare_kernel, lines, axis), out_shape=...  7.77 us
    ppermute x6, starting transfers between devices, swap_blocks(): lax.ppermute(blocks[k], axis, [(i, i ^ k) for i in range(count)])  4.98 us
    ppermute x8, waiting for transfers between devices, swap(): lax.ppermute(block, axis, [(i, i ^ k) for i in range(lax.axis_size(axis))])  3.76 us
    unnamed x24, local copies, waits for them, and re-layouts  1.79 us
    pallas_call x1, Pallas kernels, local(): pl.pallas_call(functools.partial(end_kernel, half), out_shape=jax.ShapeDt...  1.73 us
  transfers between devices with their start and end apart: 16, of which 6 were waited for; matrix products, arithmetic and copies ran while one was open for 0% of the time, Pallas kernels for 19%

profile of v13, /device:TPU:0, one launch (start us, length us, event | category | flops | bytes accessed | tf_op | source)
XLA Modules:
  0.0 65.5 jit_solution(2202553829285906267)
XLA Ops:
  0.0 1.1 %copy-done.5 = bf16[16,16,384]{2,1,0:T(8,128)(2,1)S(1)} copy-done((bf16[16,16,384]{2,1,0:T(8,128)(2,1)S(1)}, bf16[16,16,384]{2,1,0:T(8,128)(2,1)}, u32[]{:S(2)}) %copy-start.5) | copy-done | bytes 196632
  1.1 0.7 %copy-done.11 = f32[384]{0:T(512)S(1)} copy-done((f32[384]{0:T(512)S(1)}, f32[384]{0:T(512)}, u32[]{:S(2)}) %copy-start.11) | copy-done | bytes 1560
  2.3 3.0 %collective-permute-start.4 = (bf16[4,4,16,384]{3,2,1,0:T(8,128)(2,1)S(1)}, bf16[4,4,16,384]{3,2,1,0:T(8,128)(2,1)S(1)}, u32[]{:S(2)}, u32[]{:S(2)}) collective-permute-start(bf16[4,4,16,384]{3,2,1,0:T(8,128)(2,1)S(1)} %get-tuple-element.39), channel_id=1, source_target_pairs={{0,4},{4,0},{8,12},{12,8},{16,20},{20,16},{24,28},{28,24},{1,5},{5... | collective-permute-start | bytes 589832 | tf_op jit(solution)/shard_map/ppermute | solution.py:510
  5.3 1.5 %collective-permute-start.1 = (bf16[6,16,384]{2,1,0:T(8,128)(2,1)S(1)}, bf16[6,16,384]{2,1,0:T(8,128)(2,1)S(1)}, u32[]{:S(2)}, u32[]{:S(2)}) collective-permute-start(bf16[6,16,384]{2,1,0:T(8,128)(2,1)S(1)} %get-tuple-element.35), channel_id=1, source_target_pairs={{0,2},{1,3},{2,0},{3,1},{4,6},{5,7},{6,4},{7,5},{8,10},{9,11},{10,... | collective-permute-start | bytes 221192 | tf_op jit(solution)/shard_map/ppermute | solution.py:529
  7.2 3.0 %collective-permute-done.1.refs_2_ = bf16[6,16,384]{2,1,0:T(8,128)(2,1)S(1)} collective-permute-done((bf16[6,16,384]{2,1,0:T(8,128)(2,1)S(1)}, bf16[6,16,384]{2,1,0:T(8,128)(2,1)S(1)}, u32[]{:S(2)}, u32[]{:S(2)}) %collective-permute-start.1) | collective-permute-done | bytes 73760 | tf_op jit(solution)/shard_map/ppermute | solution.py:529
  10.2 1.2 %collective-permute-done.2.refs_3_ = bf16[6,16,384]{2,1,0:T(8,128)(2,1)S(1)} collective-permute-done((bf16[6,16,384]{2,1,0:T(8,128)(2,1)S(1)}, bf16[6,16,384]{2,1,0:T(8,128)(2,1)S(1)}, u32[]{:S(2)}, u32[]{:S(2)}) %collective-permute-start.2) | collective-permute-done | bytes 73760 | tf_op jit(solution)/shard_map/ppermute | solution.py:529
  11.4 0.7 collective-permute-start.3
  12.1 3.0 %collective-permute-start.5 = (bf16[2,4,16,384]{3,2,1,0:T(8,128)(2,1)S(1)}, bf16[2,4,16,384]{3,2,1,0:T(8,128)(2,1)S(1)}, u32[]{:S(2)}, u32[]{:S(2)}) collective-permute-start(bf16[2,4,16,384]{3,2,1,0:T(8,128)(2,1)S(1)} %get-tuple-element.43), channel_id=1, source_target_pairs={{0,8},{4,12},{8,0},{12,4},{16,24},{20,28},{24,16},{28,20},{1,9},{5... | collective-permute-start | bytes 294920 | tf_op jit(solution)/shard_map/ppermute | solution.py:510
  15.0 2.9 %collective-permute-start.6 = (bf16[2,4,16,384]{3,2,1,0:T(8,128)(2,1)S(1)}, bf16[2,4,16,384]{3,2,1,0:T(8,128)(2,1)S(1)}, u32[]{:S(2)}, u32[]{:S(2)}) collective-permute-start(bf16[2,4,16,384]{3,2,1,0:T(8,128)(2,1)S(1)} %get-tuple-element.44), channel_id=1, source_target_pairs={{0,16},{4,20},{8,24},{12,28},{16,0},{20,4},{24,8},{28,12},{1,17},{... | collective-permute-start | bytes 294920 | tf_op jit(solution)/shard_map/ppermute | solution.py:510
  18.0 3.5 %shard_map.121 = (f32[64,8,128]{2,1,0:T(8,128)S(1)}, f32[64,8,768]{2,1,0:T(8,128)S(1)}, f32[64,8,768]{2,1,0:T(8,128)S(1)}) custom-call(bf16[256,384]{1,0:T(8,128)(2,1)S(1)} %get-tuple-element.32.norm_ref.after_ref, bf16[6,16,384]{2,1,0:T(8,128)(2,1)S(1)} %get-tuple-element.33.refs_0_, bf16[6,16,384]{2,1,0:T(8,128)(2,1)S(1)} %collective-permute-done.refs_1_, ...), custom_call_target="tpu_custom_call" | custom-call | flops 1711276032 | bytes 4194304 | tf_op jit(solution)/shard_map/pallas_call | solution.py:397
  21.5 3.4 %collective-permute-done.6.refs_2_ = bf16[2,4,16,384]{3,2,1,0:T(8,128)(2,1)S(1)} collective-permute-done((bf16[2,4,16,384]{3,2,1,0:T(8,128)(2,1)S(1)}, bf16[2,4,16,384]{3,2,1,0:T(8,128)(2,1)S(1)}, u32[]{:S(2)}, u32[]{:S(2)}) %collective-permute-start.6) | collective-permute-done | bytes 98336 | tf_op jit(solution)/shard_map/ppermute | solution.py:510
  25.0 1.0 %collective-permute-start.8 = (bf16[8,16,384]{2,1,0:T(8,128)(2,1)S(1)}, bf16[8,16,384]{2,1,0:T(8,128)(2,1)S(1)}, u32[]{:S(2)}, u32[]{:S(2)}) collective-permute-start(bf16[8,16,384]{2,1,0:T(8,128)(2,1)S(1)} %shard_map.124), channel_id=1, source_target_pairs={{28,29},{1,2},{30,31},{29,28},{2,1},{31,30}} | collective-permute-start | bytes 294920 | tf_op jit(solution)/shard_map/ppermute | solution.py:561
  26.0 4.3 %shard_map.125 = (f32[128,8,128]{2,1,0:T(8,128)S(1)}, f32[128,8,384]{2,1,0:T(8,128)S(1)}, f32[128,8,384]{2,1,0:T(8,128)S(1)}) custom-call(f32[64,8,128]{2,1,0:T(8,128)S(1)} %get-tuple-element.37.after_ref.coef_ref, bf16[2,4,16,384]{3,2,1,0:T(8,128)(2,1)S(1)} %shard_map.122.refs_0_, bf16[2,4,16,384]{3,2,1,0:T(8,128)(2,1)S(1)} %collective-permute-done.5.refs_1_, ...), custom_call_target="tpu_custom_call" | custom-call | flops 2818572288 | bytes 4194304 | tf_op jit(solution)/shard_map/pallas_call | solution.py:397
  30.3 9.5 %shard_map.126.scanned_ref = bf16[1024,384]{1,0:T(8,128)(2,1)S(1)} custom-call(bf16[256,384]{1,0:T(8,128)(2,1)S(1)} %get-tuple-element.32.norm_ref.after_ref, f32[128,8,128]{2,1,0:T(8,128)S(1)} %get-tuple-element.46.coef_ref, f32[128,8,384]{2,1,0:T(8,128)S(1)} %get-tuple-element.47.s_ref, f32[128,8,384]{2,1,0:T(8,128)S(1)} %get-tuple-element.48.u_ref, ...), custom_call_target="tpu_custom_call" | custom-call | flops 50331648 | bytes 4194304 | tf_op jit(solution)/shard_map/pallas_call | solution.py:433
  39.8 0.7 %shard_map.127 = (bf16[2,32,768]{2,1,0:T(8,128)(2,1)S(1)}, bf16[2,32,768]{2,1,0:T(8,128)(2,1)S(1)}, bf16[2,32,768]{2,1,0:T(8,128)(2,1)S(1)}, bf16[2,32,768]{2,1,0:T(8,128)(2,1)S(1)}) custom-call(bf16[256,384]{1,0:T(8,128)(2,1)S(1)} %get-tuple-element.32.norm_ref.after_ref, bf16[1024,384]{1,0:T(8,128)(2,1)S(1)} %shard_map.126.scanned_ref), custom_call_target="tpu_custom_call" | custom-call | tf_op jit(solution)/shard_map/pallas_call | solution.py:372
  40.6 2.1 %collective-permute-start.10 = (bf16[2,32,768]{2,1,0:T(8,128)(2,1)S(1)}, bf16[2,32,768]{2,1,0:T(8,128)(2,1)S(1)}, u32[]{:S(2)}, u32[]{:S(2)}) collective-permute-start(bf16[2,32,768]{2,1,0:T(8,128)(2,1)S(1)} %get-tuple-element.51), channel_id=1, source_target_pairs={{0,16},{4,20},{8,24},{12,28},{16,0},{20,4},{24,8},{28,12},{1,17},{... | collective-permute-start | bytes 294920 | tf_op jit(solution)/shard_map/ppermute | solution.py:510
  42.7 1.9 %collective-permute-start.11 = (bf16[2,32,768]{2,1,0:T(8,128)(2,1)S(1)}, bf16[2,32,768]{2,1,0:T(8,128)(2,1)S(1)}, u32[]{:S(2)}, u32[]{:S(2)}) collective-permute-start(bf16[2,32,768]{2,1,0:T(8,128)(2,1)S(1)} %get-tuple-element.52), channel_id=1, source_target_pairs={{0,24},{4,28},{8,16},{12,20},{16,8},{20,12},{24,0},{28,4},{1,25},{... | collective-permute-start | bytes 294920 | tf_op jit(solution)/shard_map/ppermute | solution.py:510
  44.6 8.3 %shard_map.128.after_ref.scanned_ref = bf16[512,768]{1,0:T(8,128)(2,1)S(1)} custom-call(bf16[2,32,768]{2,1,0:T(8,128)(2,1)S(1)} %get-tuple-element.49.after_ref.refs_0_, f32[64,8,128]{2,1,0:T(8,128)S(1)} %get-tuple-element.37.after_ref.coef_ref, f32[64,8,768]{2,1,0:T(8,128)S(1)} %get-tuple-element.53.s_ref, f32[64,8,768]{2,1,0:T(8,128)S(1)} %get-tuple-element.54.u_ref, ...), custom_call_target="tpu_custom_call" | custom-call | flops 50331648 | bytes 4194304 | tf_op jit(solution)/shard_map/pallas_call | solution.py:433
  53.3 1.7 %collective-permute-start.12 = (bf16[4,32,768]{2,1,0:T(8,128)(2,1)S(1)}, bf16[4,32,768]{2,1,0:T(8,128)(2,1)S(1)}, u32[]{:S(2)}, u32[]{:S(2)}) collective-permute-start(bf16[4,32,768]{2,1,0:T(8,128)(2,1)S(1)} %shard_map.129.after_ref), channel_id=1, source_target_pairs={{0,4},{4,0},{8,12},{12,8},{16,20},{20,16},{24,28},{28,24},{1,5},{5... | collective-permute-start | bytes 589832 | tf_op jit(solution)/shard_map/ppermute | solution.py:510
  55.5 0.5 collective-permute-start.13
  56.0 2.5 %collective-permute-start.14 = (bf16[64,768]{1,0:T(8,128)(2,1)S(1)}, bf16[64,768]{1,0:T(8,128)(2,1)S(1)}, u32[]{:S(2)}, u32[]{:S(2)}) collective-permute-start(bf16[64,768]{1,0:T(8,128)(2,1)S(1)} %get-tuple-element.57), channel_id=1, source_target_pairs={{0,2},{1,3},{2,0},{3,1},{4,6},{5,7},{6,4},{7,5},{8,10},{9,11},{10,... | collective-permute-start | bytes 294920 | tf_op jit(solution)/shard_map/ppermute | solution.py:529
  59.0 3.2 %collective-permute-done.14.refs_7_ = bf16[64,768]{1,0:T(8,128)(2,1)S(1)} collective-permute-done((bf16[64,768]{1,0:T(8,128)(2,1)S(1)}, bf16[64,768]{1,0:T(8,128)(2,1)S(1)}, u32[]{:S(2)}, u32[]{:S(2)}) %collective-permute-start.14) | collective-permute-done | bytes 98336 | tf_op jit(solution)/shard_map/ppermute | solution.py:529
  62.2 1.6 %collective-permute-done.15.refs_8_ = bf16[64,768]{1,0:T(8,128)(2,1)S(1)} collective-permute-done((bf16[64,768]{1,0:T(8,128)(2,1)S(1)}, bf16[64,768]{1,0:T(8,128)(2,1)S(1)}, u32[]{:S(2)}, u32[]{:S(2)}) %collective-permute-start.15) | collective-permute-done | bytes 98336 | tf_op jit(solution)/shard_map/ppermute | solution.py:529
  63.8 1.7 %shard_map.131 = bf16[16,16,384]{2,1,0:T(8,128)(2,1)} custom-call(bf16[256,768]{1,0:T(8,128)(2,1)S(1)} %shard_map.119.gate_ref, f32[768]{0:T(1024)S(1)} %copy-done.2, bf16[768,384]{1,0:T(8,128)(2,1)S(1)} %copy-done.1, bf16[2,32,768]{2,1,0:T(8,128)(2,1)S(1)} %get-tuple-element.49.after_ref.refs_0_, bf16[2,32,768]{2,1,0:T(8,128)(2,1)S(1)} %collective-permute-done.9.refs_1_, ...), custom_call_target="tpu_custom_call" | custom-call | tf_op jit(solution)/shard_map/pallas_call | solution.py:627
  (46 shorter events, 2.2 us)
Async XLA Ops:
  0.0 17.9 %copy-start.3 = (bf16[4,768,56]{1,2,0:T(8,128)(2,1)S(1)}, bf16[4,768,56]{1,2,0:T(8,128)(2,1)}, u32[]{:S(2)}) copy-start(bf16[4,768,56]{1,2,0:T(8,128)(2,1)} %param.17) | copy-start | bytes 1032196
  0.0 17.9 %copy-start = (bf16[384,1536]{1,0:T(8,128)(2,1)S(1)}, bf16[384,1536]{1,0:T(8,128)(2,1)}, u32[]{:S(2)}) copy-start(bf16[384,1536]{1,0:T(8,128)(2,1)} %refs_5_.3) | copy-start | bytes 3538948
  0.0 18.0 %copy-start.4 = (f32[4,24,768]{2,1,0:T(8,128)S(1)}, f32[4,24,768]{2,1,0:T(8,128)}, u32[]{:S(2)}) copy-start(f32[4,24,768]{2,1,0:T(8,128)} %refs_9_.3) | copy-start | bytes 884740
  1.7 16.2 %copy-start.7 = (f32[3,3,768]{2,1,0:T(4,128)S(1)}, f32[3,3,768]{2,1,0:T(4,128)}, u32[]{:S(2)}) copy-start(f32[3,3,768]{2,1,0:T(4,128)} %refs_6_.3) | copy-start | bytes 82948
  1.8 16.2 %copy-start.8 = (f32[4,768]{1,0:T(4,128)S(1)}, f32[4,768]{1,0:T(4,128)}, u32[]{:S(2)}) copy-start(f32[4,768]{1,0:T(4,128)} %refs_10_.3) | copy-start | bytes 36868
  1.8 16.2 %copy-start.10 = (f32[768]{0:T(1024)S(1)}, f32[768]{0:T(1024)}, u32[]{:S(2)}) copy-start(f32[768]{0:T(1024)} %refs_7_.3) | copy-start | bytes 9220
  2.3 9.8 %collective-permute-start.4 = (bf16[4,4,16,384]{3,2,1,0:T(8,128)(2,1)S(1)}, bf16[4,4,16,384]{3,2,1,0:T(8,128)(2,1)S(1)}, u32[]{:S(2)}, u32[]{:S(2)}) collective-permute-start(bf16[4,4,16,384]{3,2,1,0:T(8,128)(2,1)S(1)} %get-tuple-element.39), channel_id=1, source_target_pairs={{0,4},{4,0},{8,12},{12,8},{16,20},{20,16},{24,28},{28,24},{1,5},{5... | collective-permute-start | bytes 589832 | tf_op jit(solution)/shard_map/ppermute | solution.py:510
  5.3 1.9 %collective-permute-start = (bf16[6,16,384]{2,1,0:T(8,128)(2,1)S(1)}, bf16[6,16,384]{2,1,0:T(8,128)(2,1)S(1)}, u32[]{:S(2)}, u32[]{:S(2)}) collective-permute-start(bf16[6,16,384]{2,1,0:T(8,128)(2,1)S(1)} %get-tuple-element.34), channel_id=1, source_target_pairs={{0,1},{1,0},{2,3},{3,2},{4,5},{5,4},{6,7},{7,6},{8,9},{9,8},{10,11... | collective-permute-start | bytes 221192 | tf_op jit(solution)/shard_map/ppermute | solution.py:529
  5.3 4.9 %collective-permute-start.1 = (bf16[6,16,384]{2,1,0:T(8,128)(2,1)S(1)}, bf16[6,16,384]{2,1,0:T(8,128)(2,1)S(1)}, u32[]{:S(2)}, u32[]{:S(2)}) collective-permute-start(bf16[6,16,384]{2,1,0:T(8,128)(2,1)S(1)} %get-tuple-element.35), channel_id=1, source_target_pairs={{0,2},{1,3},{2,0},{3,1},{4,6},{5,7},{6,4},{7,5},{8,10},{9,11},{10,... | collective-permute-start | bytes 221192 | tf_op jit(solution)/shard_map/ppermute | solution.py:529
  6.8 4.5 %collective-permute-start.2 = (bf16[6,16,384]{2,1,0:T(8,128)(2,1)S(1)}, bf16[6,16,384]{2,1,0:T(8,128)(2,1)S(1)}, u32[]{:S(2)}, u32[]{:S(2)}) collective-permute-start(bf16[6,16,384]{2,1,0:T(8,128)(2,1)S(1)} %get-tuple-element.36), channel_id=1, source_target_pairs={{0,3},{1,2},{2,1},{3,0},{4,7},{5,6},{6,5},{7,4},{8,11},{9,10},{10,... | collective-permute-start | bytes 221192 | tf_op jit(solution)/shard_map/ppermute | solution.py:529
  11.4 6.6 %collective-permute-start.3 = (bf16[4,16,384]{2,1,0:T(8,128)(2,1)S(1)}, bf16[4,16,384]{2,1,0:T(8,128)(2,1)S(1)}, u32[]{:S(2)}, u32[]{:S(2)}) collective-permute-start(bf16[4,16,384]{2,1,0:T(8,128)(2,1)S(1)} %shard_map.120), channel_id=1, source_target_pairs={{3,7},{4,8},{11,15},{12,16},{19,23},{20,24},{27,31},{7,3},{8,4},{1... | collective-permute-start | bytes 147464 | tf_op jit(solution)/shard_map/ppermute | solution.py:561
  12.1 9.4 %collective-permute-start.5 = (bf16[2,4,16,384]{3,2,1,0:T(8,128)(2,1)S(1)}, bf16[2,4,16,384]{3,2,1,0:T(8,128)(2,1)S(1)}, u32[]{:S(2)}, u32[]{:S(2)}) collective-permute-start(bf16[2,4,16,384]{3,2,1,0:T(8,128)(2,1)S(1)} %get-tuple-element.43), channel_id=1, source_target_pairs={{0,8},{4,12},{8,0},{12,4},{16,24},{20,28},{24,16},{28,20},{1,9},{5... | collective-permute-start | bytes 294920 | tf_op jit(solution)/shard_map/ppermute | solution.py:510
  15.0 9.9 %collective-permute-start.6 = (bf16[2,4,16,384]{3,2,1,0:T(8,128)(2,1)S(1)}, bf16[2,4,16,384]{3,2,1,0:T(8,128)(2,1)S(1)}, u32[]{:S(2)}, u32[]{:S(2)}) collective-permute-start(bf16[2,4,16,384]{3,2,1,0:T(8,128)(2,1)S(1)} %get-tuple-element.44), channel_id=1, source_target_pairs={{0,16},{4,20},{8,24},{12,28},{16,0},{20,4},{24,8},{28,12},{1,17},{... | collective-permute-start | bytes 294920 | tf_op jit(solution)/shard_map/ppermute | solution.py:510
  17.9 7.0 %collective-permute-start.7 = (bf16[2,4,16,384]{3,2,1,0:T(8,128)(2,1)S(1)}, bf16[2,4,16,384]{3,2,1,0:T(8,128)(2,1)S(1)}, u32[]{:S(2)}, u32[]{:S(2)}) collective-permute-start(bf16[2,4,16,384]{3,2,1,0:T(8,128)(2,1)S(1)} %get-tuple-element.45), channel_id=1, source_target_pairs={{0,24},{4,28},{8,16},{12,20},{16,8},{20,12},{24,0},{28,4},{1,25},{... | collective-permute-start | bytes 294920 | tf_op jit(solution)/shard_map/ppermute | solution.py:510
  25.0 1.0 %collective-permute-start.8 = (bf16[8,16,384]{2,1,0:T(8,128)(2,1)S(1)}, bf16[8,16,384]{2,1,0:T(8,128)(2,1)S(1)}, u32[]{:S(2)}, u32[]{:S(2)}) collective-permute-start(bf16[8,16,384]{2,1,0:T(8,128)(2,1)S(1)} %shard_map.124), channel_id=1, source_target_pairs={{28,29},{1,2},{30,31},{29,28},{2,1},{31,30}} | collective-permute-start | bytes 294920 | tf_op jit(solution)/shard_map/ppermute | solution.py:561
  40.6 12.4 %collective-permute-start.10 = (bf16[2,32,768]{2,1,0:T(8,128)(2,1)S(1)}, bf16[2,32,768]{2,1,0:T(8,128)(2,1)S(1)}, u32[]{:S(2)}, u32[]{:S(2)}) collective-permute-start(bf16[2,32,768]{2,1,0:T(8,128)(2,1)S(1)} %get-tuple-element.51), channel_id=1, source_target_pairs={{0,16},{4,20},{8,24},{12,28},{16,0},{20,4},{24,8},{28,12},{1,17},{... | collective-permute-start | bytes 294920 | tf_op jit(solution)/shard_map/ppermute | solution.py:510
  42.7 10.3 %collective-permute-start.11 = (bf16[2,32,768]{2,1,0:T(8,128)(2,1)S(1)}, bf16[2,32,768]{2,1,0:T(8,128)(2,1)S(1)}, u32[]{:S(2)}, u32[]{:S(2)}) collective-permute-start(bf16[2,32,768]{2,1,0:T(8,128)(2,1)S(1)} %get-tuple-element.52), channel_id=1, source_target_pairs={{0,24},{4,28},{8,16},{12,20},{16,8},{20,12},{24,0},{28,4},{1,25},{... | collective-permute-start | bytes 294920 | tf_op jit(solution)/shard_map/ppermute | solution.py:510
  44.6 8.7 %collective-permute-start.9 = (bf16[2,32,768]{2,1,0:T(8,128)(2,1)S(1)}, bf16[2,32,768]{2,1,0:T(8,128)(2,1)S(1)}, u32[]{:S(2)}, u32[]{:S(2)}) collective-permute-start(bf16[2,32,768]{2,1,0:T(8,128)(2,1)S(1)} %get-tuple-element.50), channel_id=1, source_target_pairs={{0,8},{4,12},{8,0},{12,4},{16,24},{20,28},{24,16},{28,20},{1,9},{5... | collective-permute-start | bytes 294920 | tf_op jit(solution)/shard_map/ppermute | solution.py:510
  53.3 10.5 %copy-start.1 = (bf16[768,384]{1,0:T(8,128)(2,1)S(1)}, bf16[768,384]{1,0:T(8,128)(2,1)}, u32[]{:S(2)}) copy-start(bf16[768,384]{1,0:T(8,128)(2,1)} %weight_ref.3) | copy-start | bytes 1769476
  53.3 10.5 %copy-start.2 = (f32[768]{0:T(1024)S(1)}, f32[768]{0:T(1024)}, u32[]{:S(2)}) copy-start(f32[768]{0:T(1024)} %gain_ref.3) | copy-start | bytes 9220
  53.3 10.4 %collective-permute-start.12 = (bf16[4,32,768]{2,1,0:T(8,128)(2,1)S(1)}, bf16[4,32,768]{2,1,0:T(8,128)(2,1)S(1)}, u32[]{:S(2)}, u32[]{:S(2)}) collective-permute-start(bf16[4,32,768]{2,1,0:T(8,128)(2,1)S(1)} %shard_map.129.after_ref), channel_id=1, source_target_pairs={{0,4},{4,0},{8,12},{12,8},{16,20},{20,16},{24,28},{28,24},{1,5},{5... | collective-permute-start | bytes 589832 | tf_op jit(solution)/shard_map/ppermute | solution.py:510
  55.5 3.5 %collective-permute-start.13 = (bf16[64,768]{1,0:T(8,128)(2,1)S(1)}, bf16[64,768]{1,0:T(8,128)(2,1)S(1)}, u32[]{:S(2)}, u32[]{:S(2)}) collective-permute-start(bf16[64,768]{1,0:T(8,128)(2,1)S(1)} %get-tuple-element.56), channel_id=1, source_target_pairs={{0,1},{1,0},{2,3},{3,2},{4,5},{5,4},{6,7},{7,6},{8,9},{9,8},{10,11... | collective-permute-start | bytes 294920 | tf_op jit(solution)/shard_map/ppermute | solution.py:529
  56.0 6.2 %collective-permute-start.14 = (bf16[64,768]{1,0:T(8,128)(2,1)S(1)}, bf16[64,768]{1,0:T(8,128)(2,1)S(1)}, u32[]{:S(2)}, u32[]{:S(2)}) collective-permute-start(bf16[64,768]{1,0:T(8,128)(2,1)S(1)} %get-tuple-element.57), channel_id=1, source_target_pairs={{0,2},{1,3},{2,0},{3,1},{4,6},{5,7},{6,4},{7,5},{8,10},{9,11},{10,... | collective-permute-start | bytes 294920 | tf_op jit(solution)/shard_map/ppermute | solution.py:529
  58.5 5.2 %collective-permute-start.15 = (bf16[64,768]{1,0:T(8,128)(2,1)S(1)}, bf16[64,768]{1,0:T(8,128)(2,1)S(1)}, u32[]{:S(2)}, u32[]{:S(2)}) collective-permute-start(bf16[64,768]{1,0:T(8,128)(2,1)S(1)} %get-tuple-element.58), channel_id=1, source_target_pairs={{0,3},{1,2},{2,1},{3,0},{4,7},{5,6},{6,5},{7,4},{8,11},{9,10},{10,... | collective-permute-start | bytes 294920 | tf_op jit(solution)/shard_map/ppermute | solution.py:529
  (4 other events, 12.4 us)
